TPU v7x, 32 devices: a whole 2x2x4 slice. The times are simulated.
32 devices in a mesh: view: 4 (over z), gx: 4 (over y, x), gy: 2 (over core).
Axes of the slice: x: 2, y: 2, z: 4, core: 2. Of those that a mesh axis runs over, the one named last changes fastest.
Arguments:
- velocity: float32 [3, 128, 256, 512], P(None, 'gx', 'gy', 'view'), may hold values from -6 to 6
- occupied: int32 [16, 32, 4], P('gx', 'gy', 'view'), may hold values 0 or 1
- q_floor: float32 [1], replicated, may hold values from -1 to 0
- q_span: float32 [1], replicated, may hold values from 1 to 4
Outputs:
- image: float32 [4, 2, 4, 32, 128], P('gx', 'gy', None, 'view')
All inputs are finite; a program needn't handle non-finite values. No bound on the sum of `occupied` on one device may be relied on, other than what follows from the above.
Results may differ from a plain program's by a relative error of at most 0.0003.
Values sent between devices are 32-bit elements; how exact they have to be, the bound alone decides.
No kernel may reach another device: no remote copies, remote signals or barrier semaphores. Data moves between devices by JAX's collectives and lax.ppermute only.
A program may use at most 128 MiB of HBM per device.

v0:
```python
import jax
import jax.numpy as jnp
from jax import lax
from jax.sharding import PartitionSpec as P

SUB = 8


def extended(cells, sides, width):
    for axis, dim in sides:
        count = lax.axis_size(axis)
        head = lax.slice_in_dim(cells, 0, width, axis=dim)
        tail = lax.slice_in_dim(cells, cells.shape[dim] - width, cells.shape[dim], axis=dim)
        cells = jnp.concatenate(
            [
                lax.ppermute(tail, axis, [(i, (i + 1) % count) for i in range(count)]),
                cells,
                lax.ppermute(head, axis, [((i + 1) % count, i) for i in range(count)]),
            ],
            axis=dim,
        )
    return cells


def partner(block, axis, apart):
    count = lax.axis_size(axis)
    route = []
    for low in range(count):
        high = low | 1 << apart
        if high != low and high < count:
            route += [(low, high), (high, low)]
    return lax.ppermute(block, axis, route)


def derivative(padded_field, direction):
    length_inner = padded_field.shape[direction] - 4

    def shifted(offset):
        return lax.slice_in_dim(padded_field, offset, offset + length_inner, axis=direction)

    return (shifted(0) - 8.0 * shifted(1) + 8.0 * shifted(3) - shifted(4)) / 12.0


def criterion(padded_sets):
    gradient = [
        [derivative(padded_sets[column][component], column) for column in range(3)]
        for component in range(3)
    ]
    diagonal_part = (
        gradient[0][0] * gradient[0][0]
        + gradient[1][1] * gradient[1][1]
        + gradient[2][2] * gradient[2][2]
    )
    cross_part = (
        gradient[0][1] * gradient[1][0]
        + gradient[0][2] * gradient[2][0]
        + gradient[1][2] * gradient[2][1]
    )
    return -0.5 * diagonal_part - cross_part


def composite(front_image, back_image):
    colour_part = front_image[:3] + front_image[3:] * back_image[:3]
    passing_part = front_image[3:] * back_image[3:]
    return jnp.concatenate([colour_part, passing_part], axis=0)


def local(velocity, occupied, q_floor, q_span):
    brick_x, brick_y, brick_z = (velocity.shape[1], velocity.shape[2], velocity.shape[3])
    view_count = lax.axis_size("view")
    density = 5.0 / (brick_z * view_count)
    pad_across = extended(velocity, (("gx", 1),), 2)
    pad_down = extended(velocity, (("gy", 2),), 2)
    pad_depth = extended(velocity, (("view", 3),), 2)
    padded_sets = (pad_across, pad_down, pad_depth)
    qvalue = criterion(padded_sets)
    occupancy = occupied[:, :, 0].astype(jnp.float32)
    shade_level = jnp.clip((qvalue - q_floor[0]) / q_span[0], 0.0, 1.0)
    shade_level = shade_level.reshape(brick_x // SUB, SUB, brick_y // SUB, SUB, brick_z)
    shade_level = (shade_level * occupancy[:, None, :, None, None]).reshape(
        brick_x, brick_y, brick_z
    )
    optical = density * shade_level
    coverage = 1.0 - jnp.exp(-optical)
    steps_row = lax.broadcasted_iota(jnp.int32, (brick_z, brick_z), 0)
    steps_col = lax.broadcasted_iota(jnp.int32, (brick_z, brick_z), 1)
    strict_upper = (steps_row < steps_col).astype(jnp.float32)
    before = jnp.dot(
        optical.reshape(brick_x * brick_y, brick_z), strict_upper, precision=lax.Precision.HIGHEST
    )
    weight = jnp.exp(-before.reshape(brick_x, brick_y, brick_z)) * coverage
    red = jnp.sum(weight * shade_level, axis=-1)
    green = jnp.sum(weight * 4.0 * shade_level * (1.0 - shade_level), axis=-1)
    blue = jnp.sum(weight * (1.0 - shade_level), axis=-1)
    through = jnp.exp(-jnp.sum(optical, axis=-1))
    partial_value = jnp.stack([red, green, blue, through], axis=0)
    block_rows = brick_x // view_count
    holding = partial_value.reshape(4, view_count, block_rows, brick_y)
    view_index = lax.axis_index("view")
    for level_bit in range(view_count.bit_length() - 1):
        half_count = holding.shape[1] // 2
        paired = holding.reshape(4, half_count, 2, block_rows, brick_y)
        own_bit = view_index >> level_bit & 1
        kept_half = lax.dynamic_index_in_dim(paired, own_bit, 2, keepdims=False)
        sent_half = lax.dynamic_index_in_dim(paired, 1 - own_bit, 2, keepdims=False)
        got_half = partner(sent_half, "view", level_bit)
        front_half = jnp.where(own_bit == 0, kept_half, got_half)
        back_half = jnp.where(own_bit == 0, got_half, kept_half)
        holding = composite(front_half, back_half)
    finished = jnp.concatenate([holding[:3], 1.0 - holding[3:]], axis=0)
    return finished.reshape(1, 1, 4, block_rows, brick_y)


def solution(mesh):
    placed = (P(None, "gx", "gy", "view"), P("gx", "gy", "view"), P(), P())
    return jax.shard_map(
        local,
        mesh=mesh,
        in_specs=placed,
        out_specs=P("gx", "gy", None, "view", None),
        check_vma=False,
    )
```

profile of v0, /device:TPU:0, one launch (start us, length us, event | category | flops | bytes accessed | tf_op | source)
XLA Modules:
  0.0 132.3 jit_solution(2567992347919057332)
XLA Ops:
  0.0 1.2 fusion.78
  1.2 0.5 collective-permute-start.3
  1.7 0.0 copy-start
  1.7 0.1 collective-permute-start.2
  1.9 6.6 %copy.38 = f32[3,32,128,128]{2,3,1,0:T(8,128)} copy(f32[3,32,128,128]{3,2,1,0:T(8,128)} %param.4) | data formatting | bytes 12582912 | tf_op args[0]
  8.5 1.9 %fusion.77 = (f32[3,32,128,2]{2,3,1,0:T(2,128)}, f32[3,32,128,2]{2,3,1,0:T(2,128)}) fusion(f32[3,32,128,128]{2,3,1,0:T(8,128)} %copy.38), kind=kLoop, calls=%fused_computation.147 | loop fusion | bytes 393216 | tf_op jit(solution)/shard_map/slice | solution.py:13
  10.3 5.0 %collective-permute-start.5 = (f32[3,32,128,2]{2,3,1,0:T(2,128)}, f32[3,32,128,2]{2,3,1,0:T(2,128)}, u32[]{:S(2)}, u32[]{:S(2)}) collective-permute-start(f32[3,32,128,2]{2,3,1,0:T(2,128)} %get-tuple-element.18), channel_id=1, source_target_pairs={{8,0},{16,8},{24,16},{0,24},{9,1},{17,9},{25,17},{1,25},{10,2},{18... | collective-permute-start | bytes 294920 | tf_op jit(solution)/shard_map/ppermute | solution.py:18
  15.4 0.0 collective-permute-start.4
  15.4 2.1 %fusion.76 = (f32[3,2,128,128]{2,3,1,0:T(8,128)}, f32[3,2,128,128]{2,3,1,0:T(8,128)}) fusion(f32[3,32,128,128]{2,3,1,0:T(8,128)} %copy.38), kind=kLoop, calls=%fused_computation.146 | loop fusion | bytes 1572864 | tf_op jit(solution)/shard_map/slice | solution.py:13
  17.4 2.4 %collective-permute-start.1 = (f32[3,2,128,128]{2,3,1,0:T(8,128)}, f32[3,2,128,128]{2,3,1,0:T(8,128)S(1)}, u32[]{:S(2)}, u32[]{:S(2)}) collective-permute-start(f32[3,2,128,128]{2,3,1,0:T(8,128)} %get-tuple-element.16), channel_id=1, source_target_pairs={{2,0},{4,2},{6,4},{0,6},{3,1},{5,3},{7,5},{1,7},{10,8},{12,10},{14... | collective-permute-start | bytes 1179656 | tf_op jit(solution)/shard_map/ppermute | solution.py:18
  19.9 0.0 copy-done
  19.9 0.1 mul.176
  20.0 0.1 mul.177
  21.4 0.0 collective-permute-done.3
  21.4 0.1 collective-permute-start
  21.5 4.0 %copy.46 = f32[3,32,2,128]{2,3,1,0:T(8,128)} copy(f32[3,32,2,128]{3,1,2,0:T(8,128)S(1)} %collective-permute-done.3) | data formatting | bytes 196608 | tf_op jit(solution)/shard_map/ppermute | solution.py:18
  25.5 0.0 collective-permute-done.2
  25.5 0.0 slice-start
  25.5 4.0 %copy.44 = f32[3,32,2,128]{2,3,1,0:T(8,128)} copy(f32[3,32,2,128]{3,1,2,0:T(8,128)S(1)} %collective-permute-done.2) | data formatting | bytes 196608 | tf_op jit(solution)/shard_map/ppermute | solution.py:16
  29.5 0.0 slice-start.1
  29.5 14.8 %pad_maximum_fusion = f32[3,32,132,128]{2,3,1,0:T(8,128)} fusion(f32[3,32,2,128]{2,3,1,0:T(8,128)} %copy.46, f32[3,32,128,128]{2,3,1,0:T(8,128)} %copy.38, f32[3,32,2,128]{2,3,1,0:T(8,128)} %copy.44), kind=kLoop, calls=%fused_computation.10 | loop fusion | flops 3244032 | bytes 12976128 | tf_op jit(solution)/shard_map/concatenate | solution.py:14
  44.2 9.7 %slice_bitcast_fusion.2 = (f32[32,132,128]{1,2,0:T(8,128)}, f32[32,132,128]{1,2,0:T(8,128)}, f32[32,132,128]{1,2,0:T(8,128)}) fusion(f32[3,32,132,128]{2,3,1,0:T(8,128)} %pad_maximum_fusion), kind=kLoop, calls=%fused_computation.24 | loop fusion | bytes 12976128 | tf_op jit(solution)/shard_map/squeeze | solution.py:46
  53.9 0.0 collective-permute-done.5
  53.9 0.0 collective-permute-done.4
  53.9 0.0 slice-done
  53.9 0.0 slice-done.1
  53.9 2.0 %pad_maximum_fusion.1 = f32[3,32,128,132]{2,3,1,0:T(8,128)S(1)} fusion(f32[3,32,128,2]{2,3,1,0:T(2,128)} %collective-permute-done.5, f32[3,32,128,128]{2,3,1,0:T(8,128)S(1)} %bitcast.118, f32[3,32,128,2]{2,3,1,0:T(2,128)} %collective-permute-done.4), kind=kLoop, calls=%fused_computation.11 | loop fusion | flops 3244032 | bytes 12976128 | tf_op jit(solution)/shard_map/concatenate | solution.py:14
  55.9 2.5 %slice_bitcast_fusion.5 = (f32[32,128,132]{1,2,0:T(8,128)S(1)}, f32[32,128,132]{1,2,0:T(8,128)}, f32[32,128,132]{1,2,0:T(8,128)}) fusion(f32[3,32,128,132]{2,3,1,0:T(8,128)S(1)} %pad_maximum_fusion.1), kind=kLoop, calls=%fused_computation.27 | loop fusion | bytes 12976128 | tf_op jit(solution)/shard_map/squeeze | solution.py:46
  58.4 0.0 collective-permute-done.1
  58.4 0.0 collective-permute-done
  58.4 32.0 %fusion.66.clone.5 = f32[32,128,128]{1,2,0:T(8,128)} fusion(f32[32,128]{1,0:T(8,128)S(1)} %mul.177, f32[]{:T(128)} %bitcast.116, f32[]{:T(128)} %bitcast.114, f32[32,132,128]{1,2,0:T(8,128)} %get-tuple-element.10, f32[32,128,132]{1,2,0:T(8,128)} %get-tuple-element.13, f32[3,2,128,128]{2,3,1,0:T(8,128)S(1)} %collective-permute-done.1, ...), kind=kLoop, calls=%fused_computation.118.clone.clone.clone.clone.clone.2 | loop fusion | flops 43515904 | bytes 59523080 | tf_op jit(solution)/shard_map/reduce_sum | solution.py:92
  90.4 32.4 %multiply_reduce_fusion.2 = (f32[32,128]{1,0:T(8,128)S(1)}, f32[32,128]{1,0:T(8,128)S(1)}, f32[32,128]{1,0:T(8,128)S(1)}, f32[32,128]{1,0:T(8,128)S(1)}) fusion(f32[32,128]{1,0:T(8,128)S(1)} %mul.177, f32[]{:T(128)} %bitcast.115, f32[]{:T(128)} %bitcast.113, f32[32,132,128]{1,2,0:T(8,128)} %get-tuple-element.10, f32[32,128,132]{1,2,0:T(8,128)} %get-tuple-element.13, ...), kind=kOutput, calls=%fused_computation.113 | convolution fusion | flops 856162304 | bytes 59588616 | tf_op jit(solution)/shard_map/dot_general | solution.py:88
  122.9 0.1 collective-permute-start.6
  123.0 3.9 %collective-permute-done.6 = f32[4,2,8,128]{3,2,1,0:T(8,128)S(1)} collective-permute-done((f32[4,2,8,128]{3,2,1,0:T(8,128)S(1)}, f32[4,2,8,128]{3,2,1,0:T(8,128)S(1)}, u32[]{:S(2)}, u32[]{:S(2)}) %collective-permute-start.6) | collective-permute-done | bytes 32800 | tf_op jit(solution)/shard_map/ppermute | solution.py:32
  126.9 2.4 %collective-permute-start.7 = (f32[4,1,8,128]{3,2,1,0:T(8,128)S(1)}, f32[4,1,8,128]{3,2,1,0:T(8,128)S(1)}, u32[]{:S(2)}, u32[]{:S(2)}) collective-permute-start(f32[4,1,8,128]{3,2,1,0:T(8,128)S(1)} %fusion.71), channel_id=1, source_target_pairs={{0,16},{16,0},{8,24},{24,8},{1,17},{17,1},{9,25},{25,9},{2,18},{18... | collective-permute-start | bytes 49160 | tf_op jit(solution)/shard_map/ppermute | solution.py:32
  129.4 2.3 %collective-permute-done.7 = f32[4,1,8,128]{3,2,1,0:T(8,128)S(1)} collective-permute-done((f32[4,1,8,128]{3,2,1,0:T(8,128)S(1)}, f32[4,1,8,128]{3,2,1,0:T(8,128)S(1)}, u32[]{:S(2)}, u32[]{:S(2)}) %collective-permute-start.7) | collective-permute-done | bytes 16416 | tf_op jit(solution)/shard_map/ppermute | solution.py:32
  131.7 0.6 maximum_bitcast_fusion
  (14 shorter events, 0.1 us)
Async XLA Ops:
  1.2 20.2 %collective-permute-start.3 = (f32[3,32,2,128]{3,1,2,0:T(8,128)S(1)}, f32[3,32,2,128]{3,1,2,0:T(8,128)S(1)}, u32[]{:S(2)}, u32[]{:S(2)}) collective-permute-start(f32[3,32,2,128]{3,1,2,0:T(8,128)S(1)} %copy.53), channel_id=1, source_target_pairs={{1,0},{0,1},{3,2},{2,3},{5,4},{4,5},{7,6},{6,7},{9,8},{8,9},{11,10... | collective-permute-start | bytes 294920 | tf_op jit(solution)/shard_map/ppermute | solution.py:18
  1.7 18.2 %copy-start = (s32[4,16,1]{1,2,0:T(1,128)S(1)}, s32[4,16,1]{1,2,0:T(1,128)}, u32[]{:S(2)}) copy-start(s32[4,16,1]{1,2,0:T(1,128)} %param.5) | copy-start | bytes 772
  1.7 23.7 %collective-permute-start.2 = (f32[3,32,2,128]{3,1,2,0:T(8,128)S(1)}, f32[3,32,2,128]{3,1,2,0:T(8,128)S(1)}, u32[]{:S(2)}, u32[]{:S(2)}) collective-permute-start(f32[3,32,2,128]{3,1,2,0:T(8,128)S(1)} %copy.52), channel_id=1, source_target_pairs={{0,1},{1,0},{2,3},{3,2},{4,5},{5,4},{6,7},{7,6},{8,9},{9,8},{10,11... | collective-permute-start | bytes 294920 | tf_op jit(solution)/shard_map/ppermute | solution.py:16
  10.3 43.6 %collective-permute-start.5 = (f32[3,32,128,2]{2,3,1,0:T(2,128)}, f32[3,32,128,2]{2,3,1,0:T(2,128)}, u32[]{:S(2)}, u32[]{:S(2)}) collective-permute-start(f32[3,32,128,2]{2,3,1,0:T(2,128)} %get-tuple-element.18), channel_id=1, source_target_pairs={{8,0},{16,8},{24,16},{0,24},{9,1},{17,9},{25,17},{1,25},{10,2},{18... | collective-permute-start | bytes 294920 | tf_op jit(solution)/shard_map/ppermute | solution.py:18
  15.4 38.5 %collective-permute-start.4 = (f32[3,32,128,2]{2,3,1,0:T(2,128)}, f32[3,32,128,2]{2,3,1,0:T(2,128)}, u32[]{:S(2)}, u32[]{:S(2)}) collective-permute-start(f32[3,32,128,2]{2,3,1,0:T(2,128)} %get-tuple-element.17), channel_id=1, source_target_pairs={{0,8},{8,16},{16,24},{24,0},{1,9},{9,17},{17,25},{25,1},{2,10},{10... | collective-permute-start | bytes 294920 | tf_op jit(solution)/shard_map/ppermute | solution.py:16
  17.4 41.0 %collective-permute-start.1 = (f32[3,2,128,128]{2,3,1,0:T(8,128)}, f32[3,2,128,128]{2,3,1,0:T(8,128)S(1)}, u32[]{:S(2)}, u32[]{:S(2)}) collective-permute-start(f32[3,2,128,128]{2,3,1,0:T(8,128)} %get-tuple-element.16), channel_id=1, source_target_pairs={{2,0},{4,2},{6,4},{0,6},{3,1},{5,3},{7,5},{1,7},{10,8},{12,10},{14... | collective-permute-start | bytes 1179656 | tf_op jit(solution)/shard_map/ppermute | solution.py:18
  21.4 37.0 %collective-permute-start = (f32[3,2,128,128]{2,3,1,0:T(8,128)}, f32[3,2,128,128]{2,3,1,0:T(8,128)}, u32[]{:S(2)}, u32[]{:S(2)}) collective-permute-start(f32[3,2,128,128]{2,3,1,0:T(8,128)} %get-tuple-element.15), channel_id=1, source_target_pairs={{0,2},{2,4},{4,6},{6,0},{1,3},{3,5},{5,7},{7,1},{8,10},{10,12},{12... | collective-permute-start | bytes 1179656 | tf_op jit(solution)/shard_map/ppermute | solution.py:16
  25.5 28.4 %slice-start = ((s8[6291456]{0:T(1024)(128)(4,1)}), s8[2097152]{0:T(1024)(128)(4,1)S(1)}, s32[]{:S(2)}) async-start(s8[6291456]{0:T(1024)(128)(4,1)} %bitcast.117), calls=%async_computation | async-start | bytes 4194304
  29.5 24.5 %slice-start.1 = ((s8[6291456]{0:T(1024)(128)(4,1)}), s8[4194304]{0:T(1024)(128)(4,1)S(1)}, s32[]{:S(2)}) async-start(s8[6291456]{0:T(1024)(128)(4,1)} %bitcast.117), calls=%async_computation.1 | async-start | bytes 8388608
  122.9 4.0 %collective-permute-start.6 = (f32[4,2,8,128]{3,2,1,0:T(8,128)S(1)}, f32[4,2,8,128]{3,2,1,0:T(8,128)S(1)}, u32[]{:S(2)}, u32[]{:S(2)}) collective-permute-start(f32[4,2,8,128]{3,2,1,0:T(8,128)S(1)} %dynamic-slice_bitcast_fusion), channel_id=1, source_target_pairs={{0,8},{8,0},{16,24},{24,16},{1,9},{9,1},{17,25},{25,17},{2,10},{10... | collective-permute-start | bytes 98312 | tf_op jit(solution)/shard_map/ppermute | solution.py:32
  126.9 4.7 %collective-permute-start.7 = (f32[4,1,8,128]{3,2,1,0:T(8,128)S(1)}, f32[4,1,8,128]{3,2,1,0:T(8,128)S(1)}, u32[]{:S(2)}, u32[]{:S(2)}) collective-permute-start(f32[4,1,8,128]{3,2,1,0:T(8,128)S(1)} %fusion.71), channel_id=1, source_target_pairs={{0,16},{16,0},{8,24},{24,8},{1,17},{17,1},{9,25},{25,9},{2,18},{18... | collective-permute-start | bytes 49160 | tf_op jit(solution)/shard_map/ppermute | solution.py:32
where the time goes:
time: 133 us; the launch traced here: 132 us
  other arithmetic  49.5 us (37%)
  matrix products  32.4 us (24%)
  local copies, waits for them, and re-layouts  32.1 us (24%)
  starting transfers between devices  10.7 us (8%)
  waiting for transfers between devices  6.18 us (5%)
  between operations  1.47 us (1%)
    dot_general x1, matrix products, local(): jnp.dot(optical.reshape(brick_x * brick_y, brick_z), strict_upper, precis...  32.4 us
    reduce_sum x1, other arithmetic, local(): red = jnp.sum(weight * shade_level, axis=-1)  32 us
    concatenate x2, other arithmetic, extended(): jnp.concatenate([lax.ppermute(tail, axis, [(i, (i + 1) % count) for i in...  16.8 us
    squeeze x2, local copies, waits for them, and re-layouts, criterion(): padded_sets[column][component]  12.1 us
    ppermute x3, starting transfers between devices, extended(): lax.ppermute(head, axis, [((i + 1) % count, i) for i in range(count)])  8.01 us
    unnamed x9, local copies, waits for them, and re-layouts  6.61 us
    ppermute x2, waiting for transfers between devices, partner(): return lax.ppermute(block, axis, route)  6.16 us
    slice x3, local copies, waits for them, and re-layouts, extended(): lax.slice_in_dim(cells, cells.shape[dim] - width, cells.shape[dim], axis=...  5.12 us
  transfers between devices with their start and end apart: 8, of which 2 were waited for; matrix products, arithmetic and copies ran while one was open for 36% of the time, Pallas kernels for 0%

commit v1 on v0

v1 whole, which is shorter than its diff:
```python
import functools

import jax
import jax.numpy as jnp
from jax import lax
from jax.experimental import pallas as pl
from jax.experimental.pallas import tpu as pltpu
from jax.sharding import PartitionSpec as P

SUB = 8
PAD = 8
ROWS = 32


def faces_kernel(u_hbm, yface_ref, zface_ref, u_ref, turned_ref, sems):
    comps, nx, ny, nz = u_ref.shape
    copies = [pltpu.make_async_copy(u_hbm.at[c], u_ref.at[c], sems.at[c]) for c in range(comps)]
    for copy in copies:
        copy.start()
    lane = lax.broadcasted_iota(jnp.int32, (8, nz), 1)
    for c in range(comps):
        copies[c].wait()
        for x in range(nx):
            yface_ref[0, c, pl.ds(2 * x, 2), :] = u_ref[c, x, pl.ds(ny - 2, 2), :]
            yface_ref[1, c, pl.ds(2 * x, 2), :] = u_ref[c, x, pl.ds(0, 2), :]

        def gather(group, carry):
            rows = pl.ds(pl.multiple_of(group * 8, 8), 8)
            packed = jnp.zeros((8, nz), jnp.float32)
            for x in range(nx):
                moved = pltpu.roll(u_ref[c, x, rows, :], (4 * x + 2) % nz, 1)
                packed = jnp.where((lane >= 4 * x) & (lane < 4 * x + 4), moved, packed)
            turned_ref[rows, :] = packed
            return carry

        lax.fori_loop(0, ny // 8, gather, 0)
        turned_ref[...] = turned_ref[...].T
        for layer in range(4):
            zface_ref[layer // 2, c, layer % 2] = turned_ref[pl.ds(layer, nx, stride=4), :]


def faces(u):
    comps, nx, ny, nz = u.shape
    return pl.pallas_call(
        faces_kernel,
        out_shape=(
            jax.ShapeDtypeStruct((2, comps, 2 * nx, nz), jnp.float32),
            jax.ShapeDtypeStruct((2, comps, 2, nx, ny), jnp.float32),
        ),
        in_specs=[pl.BlockSpec(memory_space=pl.ANY)],
        out_specs=(pl.BlockSpec(memory_space=pltpu.VMEM), pl.BlockSpec(memory_space=pltpu.VMEM)),
        scratch_shapes=[
            pltpu.VMEM(u.shape, jnp.float32),
            pltpu.VMEM((ny, nz), jnp.float32),
            pltpu.SemaphoreType.DMA((comps,)),
        ],
        compiler_params=pltpu.CompilerParams(vmem_limit_bytes=32 << 20),
        cost_estimate=pl.CostEstimate(flops=4 * u.size, bytes_accessed=4 * u.size, transcendentals=0),
    )(u)


def border_corrections(own_ref, left_ref, right_ref, corr_ref):
    comps, _, nx, ny = left_ref.shape
    for c in range(comps):
        right0 = right_ref[c, 0] - own_ref[1, c, 0]
        right1 = right_ref[c, 1] - own_ref[1, c, 1]
        left0 = left_ref[c, 0] - own_ref[0, c, 0]
        left1 = left_ref[c, 1] - own_ref[0, c, 1]
        corr_ref[c, pl.ds(0, nx, stride=4), :] = -right0
        corr_ref[c, pl.ds(1, nx, stride=4), :] = 8.0 * right0 - right1
        corr_ref[c, pl.ds(2, nx, stride=4), :] = left0 - 8.0 * left1
        corr_ref[c, pl.ds(3, nx, stride=4), :] = left1
        corr_ref[c] = corr_ref[c].T


def shade_row(pad_ref, slot, x, corr_ref, scale_ref, offset_ref, level_ref):
    comps, _, padded, nz = pad_ref.shape
    ny = padded - 2 * PAD
    lane = lax.broadcasted_iota(jnp.int32, (ROWS, nz), 1)
    border = (lane >= nz - 2) | (lane < 2)
    shift = lax.rem(2 * nz - 2 - 4 * x, nz)
    for y in range(0, ny, ROWS):
        across, down, depth = [], [], []
        for c in range(comps):
            def at(dx, dy):
                return pad_ref[c, slot + dx, pl.ds(PAD + y + dy, ROWS), :]

            across.append(8.0 * (at(1, 0) - at(-1, 0)) - (at(2, 0) - at(-2, 0)))
            down.append(8.0 * (at(0, 1) - at(0, -1)) - (at(0, 2) - at(0, -2)))
            here = at(0, 0)
            step = here - pltpu.roll(here, 2, 1)
            wrapped = 8.0 * pltpu.roll(step, nz - 1, 1) - pltpu.roll(step, nz - 2, 1) - step
            fix = pltpu.roll(corr_ref[c, pl.ds(y, ROWS), :], shift, 1)
            depth.append(wrapped + jnp.where(border, fix, 0.0))
        total = 0.5 * (across[0] * across[0] + down[1] * down[1] + depth[2] * depth[2])
        total = total + across[1] * down[0] + across[2] * depth[0] + down[2] * depth[1]
        block = x // SUB
        level = total * scale_ref[block, pl.ds(y, ROWS), :] + offset_ref[block, pl.ds(y, ROWS), :]
        level_ref[pl.ds(y, ROWS), :] = jnp.clip(level, 0.0, 1.0)


def blend_row(density, level_ref, store):
    ny, nz = level_ref.shape
    row = lax.broadcasted_iota(jnp.int32, (2 * nz, nz), 0)
    col = lax.broadcasted_iota(jnp.int32, (2 * nz, nz), 1)
    before = jnp.where((row < col) | ((row >= nz) & (row < col + nz)), -1.0, 0.0).astype(jnp.bfloat16)
    level = level_ref[...]
    optical = density * level
    high = optical.astype(jnp.bfloat16)
    low = (optical - high.astype(jnp.float32)).astype(jnp.bfloat16)
    parts = jnp.concatenate([high, low], axis=1)
    passing = jnp.exp(jnp.dot(parts, before, preferred_element_type=jnp.float32))
    weight = passing * (1.0 - jnp.exp(-optical))
    first = weight * level
    second = first * level
    lane_group = lax.broadcasted_iota(jnp.int32, (8, ny), 1) // 8
    eye = lax.broadcasted_iota(jnp.int32, (8, ny), 1) % 8 == lax.broadcasted_iota(jnp.int32, (8, ny), 0)

    def lanes(cells):
        total = jnp.zeros((8, ny), jnp.float32)
        for group in range(ny // 8):
            part = jnp.sum(cells[8 * group : 8 * group + 8], axis=1, keepdims=True)
            total = jnp.where(lane_group == group, part, total)
        return jnp.sum(jnp.where(eye, total, 0.0), axis=0, keepdims=True)

    red = lanes(first)
    square = lanes(second)
    through = jnp.exp(-density * lanes(level))
    store(jnp.concatenate([red, 4.0 * (red - square), 1.0 - through - red, through], axis=0))


def inner_kernel(
    density, u_hbm, yleft_ref, yright_ref, zown_ref, zleft_ref, zright_ref, scale_ref, offset_ref,
    image_ref, pad_ref, corr_ref, level0_ref, level1_ref, sems,
):
    comps, nx, padded, nz = pad_ref.shape
    ny = padded - 2 * PAD
    chunks = sems.shape[1]
    size = nx // chunks
    copies = [
        [
            pltpu.make_async_copy(
                u_hbm.at[c, pl.ds(k * size, size)],
                pad_ref.at[c, pl.ds(k * size, size), pl.ds(PAD, ny)],
                sems.at[c, k],
            )
            for c in range(comps)
        ]
        for k in range(chunks)
    ]
    for chunk in copies:
        for copy in chunk:
            copy.start()
    for c in range(comps):
        for x in range(nx):
            pad_ref[c, x, pl.ds(PAD - 2, 2), :] = yleft_ref[c, pl.ds(2 * x, 2), :]
            pad_ref[c, x, pl.ds(PAD + ny, 2), :] = yright_ref[c, pl.ds(2 * x, 2), :]
    border_corrections(zown_ref, zleft_ref, zright_ref, corr_ref)
    for chunk in copies:
        for copy in chunk:
            copy.wait()
    image_ref[...] = jnp.zeros(image_ref.shape, jnp.float32)

    def store(x):
        def put(values):
            for k in range(4):
                image_ref[k, pl.ds(x, 1), :] = values[k : k + 1]

        return put

    def pair(i, carry):
        x = 2 * i + 2
        shade_row(pad_ref, x, x, corr_ref, scale_ref, offset_ref, level0_ref)
        blend_row(density, level0_ref, store(x))
        shade_row(pad_ref, x + 1, x + 1, corr_ref, scale_ref, offset_ref, level1_ref)
        blend_row(density, level1_ref, store(x + 1))
        return carry

    lax.fori_loop(0, (nx - 4) // 2, pair, 0)


def inner(density, u, yleft, yright, zown, zleft, zright, scale, offset):
    comps, nx, ny, nz = u.shape
    chunks = 4
    vmem = pl.BlockSpec(memory_space=pltpu.VMEM)
    return pl.pallas_call(
        functools.partial(inner_kernel, density),
        out_shape=jax.ShapeDtypeStruct((4, nx, ny), jnp.float32),
        in_specs=[pl.BlockSpec(memory_space=pl.ANY)] + [vmem] * 7,
        out_specs=vmem,
        scratch_shapes=[
            pltpu.VMEM((comps, nx, ny + 2 * PAD, nz), jnp.float32),
            pltpu.VMEM((comps, 4 * nx, ny), jnp.float32),
            pltpu.VMEM((ny, nz), jnp.float32),
            pltpu.VMEM((ny, nz), jnp.float32),
            pltpu.SemaphoreType.DMA((comps, chunks)),
        ],
        compiler_params=pltpu.CompilerParams(vmem_limit_bytes=32 << 20),
        cost_estimate=pl.CostEstimate(flops=100 * u.size, bytes_accessed=4 * u.size, transcendentals=2 * u.size),
    )(u, yleft, yright, zown, zleft, zright, scale, offset)


def edge_kernel(
    density, u_hbm, xleft_hbm, xright_hbm, yleft_ref, yright_ref, zown_ref, zleft_ref, zright_ref, scale_ref, offset_ref,
    image_ref, pad_ref, corr_ref, level0_ref, level1_ref, sems,
):
    comps, _, padded, nz = pad_ref.shape
    ny = padded - 2 * PAD
    nx = zown_ref.shape[3]
    parts = (
        (u_hbm, 0, 4, 2),
        (u_hbm, nx - 4, 4, 6),
        (xleft_hbm, 0, 2, 0),
        (xright_hbm, 0, 2, 10),
    )
    copies = [
        pltpu.make_async_copy(
            source.at[c, pl.ds(start, count)], pad_ref.at[c, pl.ds(slot, count), pl.ds(PAD, ny)], sems.at[c, k]
        )
        for k, (source, start, count, slot) in enumerate(parts)
        for c in range(comps)
    ]
    for copy in copies:
        copy.start()
    places = ((2, 0), (3, 1), (8, nx - 2), (9, nx - 1))
    for c in range(comps):
        for slot, x in places:
            pad_ref[c, slot, pl.ds(PAD - 2, 2), :] = yleft_ref[c, pl.ds(2 * x, 2), :]
            pad_ref[c, slot, pl.ds(PAD + ny, 2), :] = yright_ref[c, pl.ds(2 * x, 2), :]
    border_corrections(zown_ref, zleft_ref, zright_ref, corr_ref)
    for copy in copies:
        copy.wait()

    def store(place):
        def put(values):
            for k in range(4):
                image_ref[k, place : place + 1, :] = values[k : k + 1]

        return put

    for place, (slot, x) in enumerate(places):
        level_ref = (level0_ref, level1_ref)[place % 2]
        shade_row(pad_ref, slot, x, corr_ref, scale_ref, offset_ref, level_ref)
        blend_row(density, level_ref, store(place))


def edge(density, u, xleft, xright, yleft, yright, zown, zleft, zright, scale, offset):
    comps, nx, ny, nz = u.shape
    vmem = pl.BlockSpec(memory_space=pltpu.VMEM)
    hbm = pl.BlockSpec(memory_space=pl.ANY)
    return pl.pallas_call(
        functools.partial(edge_kernel, density),
        out_shape=jax.ShapeDtypeStruct((4, 4, ny), jnp.float32),
        in_specs=[hbm] * 3 + [vmem] * 7,
        out_specs=vmem,
        scratch_shapes=[
            pltpu.VMEM((comps, 12, ny + 2 * PAD, nz), jnp.float32),
            pltpu.VMEM((comps, 4 * nx, ny), jnp.float32),
            pltpu.VMEM((ny, nz), jnp.float32),
            pltpu.VMEM((ny, nz), jnp.float32),
            pltpu.SemaphoreType.DMA((comps, 4)),
        ],
        compiler_params=pltpu.CompilerParams(vmem_limit_bytes=32 << 20),
        cost_estimate=pl.CostEstimate(flops=12 * u.size, bytes_accessed=2 * u.size, transcendentals=u.size // 4),
    )(u, xleft, xright, yleft, yright, zown, zleft, zright, scale, offset)


def turn(block, axis, by):
    count = lax.axis_size(axis)
    return lax.ppermute(block, axis, [(i, (i + by) % count) for i in range(count)])


def both_sides(tail_head, axis):
    if lax.axis_size(axis) == 2:
        other = turn(tail_head, axis, 1)
        return other[0], other[1]
    return turn(tail_head[0], axis, 1), turn(tail_head[1], axis, -1)


def local(velocity, occupied, q_floor, q_span):
    comps, nx, ny, nz = velocity.shape
    views = lax.axis_size("view")
    density = 5.0 / (nz * views)
    xleft = turn(velocity[:, nx - 2 :], "gx", 1)
    xright = turn(velocity[:, :2], "gx", -1)
    yface, zface = faces(velocity)
    yleft, yright = both_sides(yface, "gy")
    zleft = turn(zface[0], "view", 1)
    zright = turn(zface[1], "view", -1)
    zown = zface
    mask = jnp.repeat(occupied[:, :, 0].astype(jnp.float32), SUB, axis=1)
    spread = (nx // SUB, ny, nz)
    scale = jnp.broadcast_to((mask * (-1.0 / 144.0 / q_span[0]))[:, :, None], spread)
    offset = jnp.broadcast_to((mask * (-q_floor[0] / q_span[0]))[:, :, None], spread)
    middle = inner(density, velocity, yleft, yright, zown, zleft, zright, scale, offset)
    border = edge(density, velocity, xleft, xright, yleft, yright, zown, zleft, zright, scale, offset)
    partial_image = jnp.concatenate([border[:, :2], middle[:, 2:-2], border[:, 2:]], axis=1)
    rows = nx // views
    blocks = partial_image.reshape(4, views, rows, ny)
    me = lax.axis_index("view")
    sources, images = [me], [lax.dynamic_index_in_dim(blocks, me, 1, keepdims=False)]
    for by in range(1, views):
        sent = lax.dynamic_index_in_dim(blocks, (me + by) % views, 1, keepdims=False)
        images.append(turn(sent, "view", by))
        sources.append((me - by) % views)
    colour = jnp.zeros((3, rows, ny), jnp.float32)
    through = jnp.ones((rows, ny), jnp.float32)
    for source, image in zip(sources, images):
        passing = jnp.ones((rows, ny), jnp.float32)
        for other, behind in zip(sources, images):
            passing = passing * jnp.where(other < source, behind[3], 1.0)
        colour = colour + passing * image[:3]
        through = through * image[3]
    finished = jnp.concatenate([colour, 1.0 - through[None]], axis=0)
    return finished.reshape(1, 1, 4, rows, ny)


def solution(mesh):
    placed = (P(None, "gx", "gy", "view"), P("gx", "gy", "view"), P(), P())
    return jax.shard_map(
        local,
        mesh=mesh,
        in_specs=placed,
        out_specs=P("gx", "gy", None, "view", None),
        check_vma=False,
    )
```

time: 133 us -> 59.8 us (0.45)
  other arithmetic: 49.5 us -> 0.67 us
  matrix products: 32.4 us -> 0 us
  Pallas kernels: 0 us -> 30.4 us
  local copies, waits for them, and re-layouts: 32.1 us -> 7.39 us
  waiting for transfers between devices: 6.18 us -> 7.95 us
    dot_general x1 -> x0, matrix products: 32.4 us -> none  [local(): jnp.dot(optical.reshape(brick_x * brick_y, brick_z), strict_upper, precis...]
    reduce_sum x1 -> x0, other arithmetic: 32 us -> none  [local(): red = jnp.sum(weight * shade_level, axis=-1)]
    pallas_call x0 -> x3, Pallas kernels: none -> 30.4 us  [the longest x1 19.9 us: inner(): pl.pallas_call(functools.partial(inner_kernel, density), out_shape=jax.Sh...]
    concatenate x3 -> x0, other arithmetic: 16.8 us -> none  [the longest x2 16.8 us: extended(): jnp.concatenate([lax.ppermute(tail, axis, [(i, (i + 1) % count) for i in...]
    squeeze x3, local copies, waits for them, and re-layouts: 12.1 us -> 0.05 us  [the longest x1 0.02 us: local(): lax.dynamic_index_in_dim(blocks, (me + by) % views, 1, keepdims=False)]
    ppermute x2 -> x0, local copies, waits for them, and re-layouts: 7.95 us -> none  [the longest x1 3.98 us: extended(): lax.ppermute(tail, axis, [(i, (i + 1) % count) for i in range(count)])]
    slice x3, local copies, waits for them, and re-layouts: 5.12 us -> 1.19 us  [the longest x1 1.18 us: local(): xright = turn(velocity[:, :2], 'gx', -1)]
    ppermute x8, waiting for transfers between devices: 6.18 us -> 7.95 us  [turn(): lax.ppermute(block, axis, [(i, (i + by) % count) for i in range(count)])]
  transfers between devices with their start and end apart: 8 -> 8, of which waited for: 2 -> 5; matrix products, arithmetic and copies ran while one was open for 36% -> 1% of each run, Pallas kernels for 0% -> 43%
where the time goes in v1:
time: 59.8 us; the launch traced here: 59.6 us
  Pallas kernels  30.4 us (51%)
  starting transfers between devices  11.6 us (19%)
  waiting for transfers between devices  7.95 us (13%)
  local copies, waits for them, and re-layouts  7.39 us (12%)
  between operations  1.57 us (3%)
  other arithmetic  0.67 us (1%)
    pallas_call x1, Pallas kernels, inner(): pl.pallas_call(functools.partial(inner_kernel, density), out_shape=jax.Sh...  19.9 us
    ppermute x8, starting transfers between devices, turn(): lax.ppermute(block, axis, [(i, (i + by) % count) for i in range(count)])  11.6 us
    ppermute x8, waiting for transfers between devices, turn(): lax.ppermute(block, axis, [(i, (i + by) % count) for i in range(count)])  7.95 us
    pallas_call x1, Pallas kernels, faces(): pl.pallas_call(faces_kernel, out_shape=(jax.ShapeDtypeStruct((2, comps, 2...  5.84 us
    unnamed x6, local copies, waits for them, and re-layouts  5.57 us
    pallas_call x1, Pallas kernels, edge(): pl.pallas_call(functools.partial(edge_kernel, density), out_shape=jax.Sha...  4.65 us
  transfers between devices with their start and end apart: 8, of which 5 were waited for; matrix products, arithmetic and copies ran while one was open for 1% of the time, Pallas kernels for 43%

profile of v1, /device:TPU:0, one launch (start us, length us, event | category | flops | bytes accessed | tf_op | source)
XLA Modules:
  0.0 59.6 jit_solution(3889363577636673021)
XLA Ops:
  0.0 0.0 copy-start.2
  0.0 1.2 %fusion.4 = (f32[3,2,128,128]{3,2,1,0:T(8,128)S(1)}, f32[3,2,128,128]{3,2,1,0:T(8,128)S(1)}) fusion(f32[3,32,128,128]{3,2,1,0:T(8,128)} %u_hbm.5), kind=kLoop, calls=%fused_computation.25 | loop fusion | bytes 1572864 | tf_op jit(solution)/shard_map/slice | solution.py:285
  1.2 3.0 %collective-permute-start = (f32[3,2,128,128]{3,2,1,0:T(8,128)S(1)}, f32[3,2,128,128]{3,2,1,0:T(8,128)S(1)}, u32[]{:S(2)}, u32[]{:S(2)}) collective-permute-start(f32[3,2,128,128]{3,2,1,0:T(8,128)S(1)} %get-tuple-element.10), channel_id=1, source_target_pairs={{0,2},{2,4},{4,6},{6,0},{1,3},{3,5},{5,7},{7,1},{8,10},{10,12},{12... | collective-permute-start | bytes 1179656 | tf_op jit(solution)/shard_map/ppermute | solution.py:270
  4.2 1.0 %collective-permute-start.1 = (f32[3,2,128,128]{3,2,1,0:T(8,128)S(1)}, f32[3,2,128,128]{3,2,1,0:T(8,128)S(1)}, u32[]{:S(2)}, u32[]{:S(2)}) collective-permute-start(f32[3,2,128,128]{3,2,1,0:T(8,128)S(1)} %get-tuple-element.9), channel_id=1, source_target_pairs={{0,6},{2,0},{4,2},{6,4},{1,7},{3,1},{5,3},{7,5},{8,14},{10,8},{12,... | collective-permute-start | bytes 1179656 | tf_op jit(solution)/shard_map/ppermute | solution.py:270
  5.2 0.0 copy-start
  5.2 2.8 %copy-done = f32[3,32,128,128]{3,2,1,0:T(8,128)S(1)} copy-done((f32[3,32,128,128]{3,2,1,0:T(8,128)S(1)}, f32[3,32,128,128]{3,2,1,0:T(8,128)}, u32[]{:S(2)}) %copy-start) | copy-done | bytes 6291480
  8.0 5.8 %shard_map.46 = (f32[2,3,64,128]{3,2,1,0:T(8,128)S(1)}, f32[2,3,2,32,128]{4,3,2,1,0:T(8,128)S(1)}) custom-call(f32[3,32,128,128]{3,2,1,0:T(8,128)S(1)} %copy-done), custom_call_target="tpu_custom_call" | custom-call | flops 6291456 | bytes 6291456 | tf_op jit(solution)/shard_map/pallas_call | solution.py:44
  13.8 0.1 collective-permute-start.2
  13.9 2.0 %collective-permute-start.3 = (f32[3,2,32,128]{3,2,1,0:T(8,128)S(1)}, f32[3,2,32,128]{3,2,1,0:T(8,128)S(1)}, u32[]{:S(2)}, u32[]{:S(2)}) collective-permute-start(f32[3,2,32,128]{3,2,1,0:T(8,128)S(1)} %get-tuple-element.12), channel_id=1, source_target_pairs={{0,8},{8,16},{16,24},{24,0},{1,9},{9,17},{17,25},{25,1},{2,10},{10... | collective-permute-start | bytes 294920 | tf_op jit(solution)/shard_map/ppermute | solution.py:270
  16.0 2.1 %collective-permute-start.4 = (f32[3,2,32,128]{3,2,1,0:T(8,128)S(1)}, f32[3,2,32,128]{3,2,1,0:T(8,128)S(1)}, u32[]{:S(2)}, u32[]{:S(2)}) collective-permute-start(f32[3,2,32,128]{3,2,1,0:T(8,128)S(1)} %get-tuple-element.11), channel_id=1, source_target_pairs={{0,24},{8,0},{16,8},{24,16},{1,25},{9,1},{17,9},{25,17},{2,26},{10... | collective-permute-start | bytes 294920 | tf_op jit(solution)/shard_map/ppermute | solution.py:270
  19.4 0.0 copy-done.2
  19.5 0.1 broadcast_in_dim.41
  19.5 0.1 mul.125
  19.6 0.1 broadcast_in_dim.43
  19.7 0.1 mul.129
  19.8 0.0 collective-permute-done.2
  19.9 1.8 %collective-permute-done.3.zleft_ref = f32[3,2,32,128]{3,2,1,0:T(8,128)S(1)} collective-permute-done((f32[3,2,32,128]{3,2,1,0:T(8,128)S(1)}, f32[3,2,32,128]{3,2,1,0:T(8,128)S(1)}, u32[]{:S(2)}, u32[]{:S(2)}) %collective-permute-start.3) | collective-permute-done | bytes 98336 | tf_op jit(solution)/shard_map/ppermute | solution.py:270
  21.6 1.3 %collective-permute-done.4.zright_ref = f32[3,2,32,128]{3,2,1,0:T(8,128)S(1)} collective-permute-done((f32[3,2,32,128]{3,2,1,0:T(8,128)S(1)}, f32[3,2,32,128]{3,2,1,0:T(8,128)S(1)}, u32[]{:S(2)}, u32[]{:S(2)}) %collective-permute-start.4) | collective-permute-done | bytes 98336 | tf_op jit(solution)/shard_map/ppermute | solution.py:270
  23.0 0.1 broadcast_in_dim.42.scale_ref
  23.1 0.1 broadcast_in_dim.44.offset_ref
  23.3 0.0 copy-start.1
  23.3 2.8 %copy-done.1 = f32[3,32,128,128]{3,2,1,0:T(8,128)S(1)} copy-done((f32[3,32,128,128]{3,2,1,0:T(8,128)S(1)}, f32[3,32,128,128]{3,2,1,0:T(8,128)}, u32[]{:S(2)}) %copy-start.1) | copy-done | bytes 6291480
  26.0 19.9 %shard_map.48 = f32[4,32,128]{2,1,0:T(8,128)S(1)} custom-call(f32[3,32,128,128]{3,2,1,0:T(8,128)S(1)} %copy-done.1, f32[3,64,128]{2,1,0:T(8,128)S(1)} %get-tuple-element.14.yleft_ref, f32[3,64,128]{2,1,0:T(8,128)S(1)} %get-tuple-element.13.yright_ref, f32[2,3,2,32,128]{4,3,2,1,0:T(8,128)S(1)} %get-tuple-element.8.zown_ref, ...), custom_call_target="tpu_custom_call" | custom-call | flops 157286400 | bytes 6291456 | tf_op jit(solution)/shard_map/pallas_call | solution.py:186
  46.0 0.0 collective-permute-done.xleft_hbm
  46.0 0.0 collective-permute-done.1.xright_hbm
  46.0 4.7 %shard_map.47 = f32[4,4,128]{2,1,0:T(4,128)S(1)} custom-call(f32[3,32,128,128]{3,2,1,0:T(8,128)S(1)} %copy-done.1, f32[3,2,128,128]{3,2,1,0:T(8,128)S(1)} %collective-permute-done.xleft_hbm, f32[3,2,128,128]{3,2,1,0:T(8,128)S(1)} %collective-permute-done.1.xright_hbm, f32[3,64,128]{2,1,0:T(8,128)S(1)} %get-tuple-element.14.yleft_ref, ...), custom_call_target="tpu_custom_call" | custom-call | flops 18874368 | bytes 3145728 | tf_op jit(solution)/shard_map/pallas_call | solution.py:251
  50.7 2.4 %collective-permute-start.7 = (f32[4,8,128]{2,1,0:T(8,128)S(1)}, f32[4,8,128]{2,1,0:T(8,128)S(1)}, u32[]{:S(2)}, u32[]{:S(2)}) collective-permute-start(f32[4,8,128]{2,1,0:T(8,128)S(1)} %get-tuple-element.19), channel_id=1, source_target_pairs={{0,24},{8,0},{16,8},{24,16},{1,25},{9,1},{17,9},{25,17},{2,26},{10... | collective-permute-start | bytes 49160 | tf_op jit(solution)/shard_map/ppermute | solution.py:270
  53.1 0.3 collective-permute-start.6
  53.4 0.7 %collective-permute-start.5 = (f32[4,8,128]{2,1,0:T(8,128)S(1)}, f32[4,8,128]{2,1,0:T(8,128)S(1)}, u32[]{:S(2)}, u32[]{:S(2)}) collective-permute-start(f32[4,8,128]{2,1,0:T(8,128)S(1)} %get-tuple-element.18), channel_id=1, source_target_pairs={{0,8},{8,16},{16,24},{24,0},{1,9},{9,17},{17,25},{25,1},{2,10},{10... | collective-permute-start | bytes 49160 | tf_op jit(solution)/shard_map/ppermute | solution.py:270
  54.1 0.4 collective-permute-done.7
  54.5 3.2 %collective-permute-done.6 = f32[4,8,128]{2,1,0:T(8,128)S(1)} collective-permute-done((f32[4,8,128]{2,1,0:T(8,128)S(1)}, f32[4,8,128]{2,1,0:T(8,128)S(1)}, u32[]{:S(2)}, u32[]{:S(2)}) %collective-permute-start.6) | collective-permute-done | bytes 16416 | tf_op jit(solution)/shard_map/ppermute | solution.py:270
  57.7 1.2 %collective-permute-done.5 = f32[4,8,128]{2,1,0:T(8,128)S(1)} collective-permute-done((f32[4,8,128]{2,1,0:T(8,128)S(1)}, f32[4,8,128]{2,1,0:T(8,128)S(1)}, u32[]{:S(2)}, u32[]{:S(2)}) %collective-permute-start.5) | collective-permute-done | bytes 16416 | tf_op jit(solution)/shard_map/ppermute | solution.py:270
  59.0 0.6 %maximum_bitcast_fusion.1 = f32[1,1,4,8,128]{4,3,2,1,0:T(8,128)} fusion(f32[1,8,128]{2,1,0:T(8,128)S(1)} %get-tuple-element.16, f32[3,8,128]{2,1,0:T(8,128)S(1)} %fusion), kind=kLoop, calls=%fused_computation.5 | loop fusion | flops 4096 | bytes 32768 | tf_op jit(solution)/shard_map/reshape | solution.py:315
  (10 shorter events, 0.1 us)
Async XLA Ops:
  0.0 19.4 %copy-start.2 = (s32[4,16,1]{1,2,0:T(1,128)S(1)}, s32[4,16,1]{1,2,0:T(1,128)}, u32[]{:S(2)}) copy-start(s32[4,16,1]{1,2,0:T(1,128)} %param.5) | copy-start | bytes 772
  1.2 44.8 %collective-permute-start = (f32[3,2,128,128]{3,2,1,0:T(8,128)S(1)}, f32[3,2,128,128]{3,2,1,0:T(8,128)S(1)}, u32[]{:S(2)}, u32[]{:S(2)}) collective-permute-start(f32[3,2,128,128]{3,2,1,0:T(8,128)S(1)} %get-tuple-element.10), channel_id=1, source_target_pairs={{0,2},{2,4},{4,6},{6,0},{1,3},{3,5},{5,7},{7,1},{8,10},{10,12},{12... | collective-permute-start | bytes 1179656 | tf_op jit(solution)/shard_map/ppermute | solution.py:270
  4.2 41.8 %collective-permute-start.1 = (f32[3,2,128,128]{3,2,1,0:T(8,128)S(1)}, f32[3,2,128,128]{3,2,1,0:T(8,128)S(1)}, u32[]{:S(2)}, u32[]{:S(2)}) collective-permute-start(f32[3,2,128,128]{3,2,1,0:T(8,128)S(1)} %get-tuple-element.9), channel_id=1, source_target_pairs={{0,6},{2,0},{4,2},{6,4},{1,7},{3,1},{5,3},{7,5},{8,14},{10,8},{12,... | collective-permute-start | bytes 1179656 | tf_op jit(solution)/shard_map/ppermute | solution.py:270
  5.2 2.8 %copy-start = (f32[3,32,128,128]{3,2,1,0:T(8,128)S(1)}, f32[3,32,128,128]{3,2,1,0:T(8,128)}, u32[]{:S(2)}) copy-start(f32[3,32,128,128]{3,2,1,0:T(8,128)} %u_hbm.5) | copy-start | bytes 18874372
  13.8 6.0 %collective-permute-start.2 = (f32[2,3,64,128]{3,2,1,0:T(8,128)S(1)}, f32[2,3,64,128]{3,2,1,0:T(8,128)S(1)}, u32[]{:S(2)}, u32[]{:S(2)}) collective-permute-start(f32[2,3,64,128]{3,2,1,0:T(8,128)S(1)} %get-tuple-element.7), channel_id=1, source_target_pairs={{0,1},{1,0},{2,3},{3,2},{4,5},{5,4},{6,7},{7,6},{8,9},{9,8},{10,11... | collective-permute-start | bytes 589832 | tf_op jit(solution)/shard_map/ppermute | solution.py:270
  13.9 7.7 %collective-permute-start.3 = (f32[3,2,32,128]{3,2,1,0:T(8,128)S(1)}, f32[3,2,32,128]{3,2,1,0:T(8,128)S(1)}, u32[]{:S(2)}, u32[]{:S(2)}) collective-permute-start(f32[3,2,32,128]{3,2,1,0:T(8,128)S(1)} %get-tuple-element.12), channel_id=1, source_target_pairs={{0,8},{8,16},{16,24},{24,0},{1,9},{9,17},{17,25},{25,1},{2,10},{10... | collective-permute-start | bytes 294920 | tf_op jit(solution)/shard_map/ppermute | solution.py:270
  16.0 7.0 %collective-permute-start.4 = (f32[3,2,32,128]{3,2,1,0:T(8,128)S(1)}, f32[3,2,32,128]{3,2,1,0:T(8,128)S(1)}, u32[]{:S(2)}, u32[]{:S(2)}) collective-permute-start(f32[3,2,32,128]{3,2,1,0:T(8,128)S(1)} %get-tuple-element.11), channel_id=1, source_target_pairs={{0,24},{8,0},{16,8},{24,16},{1,25},{9,1},{17,9},{25,17},{2,26},{10... | collective-permute-start | bytes 294920 | tf_op jit(solution)/shard_map/ppermute | solution.py:270
  23.3 2.8 %copy-start.1 = (f32[3,32,128,128]{3,2,1,0:T(8,128)S(1)}, f32[3,32,128,128]{3,2,1,0:T(8,128)}, u32[]{:S(2)}) copy-start(f32[3,32,128,128]{3,2,1,0:T(8,128)} %u_hbm.5) | copy-start | bytes 18874372
  50.7 3.8 %collective-permute-start.7 = (f32[4,8,128]{2,1,0:T(8,128)S(1)}, f32[4,8,128]{2,1,0:T(8,128)S(1)}, u32[]{:S(2)}, u32[]{:S(2)}) collective-permute-start(f32[4,8,128]{2,1,0:T(8,128)S(1)} %get-tuple-element.19), channel_id=1, source_target_pairs={{0,24},{8,0},{16,8},{24,16},{1,25},{9,1},{17,9},{25,17},{2,26},{10... | collective-permute-start | bytes 49160 | tf_op jit(solution)/shard_map/ppermute | solution.py:270
  53.1 4.6 %collective-permute-start.6 = (f32[4,8,128]{2,1,0:T(8,128)S(1)}, f32[4,8,128]{2,1,0:T(8,128)S(1)}, u32[]{:S(2)}, u32[]{:S(2)}) collective-permute-start(f32[4,8,128]{2,1,0:T(8,128)S(1)} %get-tuple-element.20), channel_id=1, source_target_pairs={{0,16},{8,24},{16,0},{24,8},{1,17},{9,25},{17,1},{25,9},{2,18},{10... | collective-permute-start | bytes 49160 | tf_op jit(solution)/shard_map/ppermute | solution.py:270
  53.4 5.5 %collective-permute-start.5 = (f32[4,8,128]{2,1,0:T(8,128)S(1)}, f32[4,8,128]{2,1,0:T(8,128)S(1)}, u32[]{:S(2)}, u32[]{:S(2)}) collective-permute-start(f32[4,8,128]{2,1,0:T(8,128)S(1)} %get-tuple-element.18), channel_id=1, source_target_pairs={{0,8},{8,16},{16,24},{24,0},{1,9},{9,17},{17,25},{25,1},{2,10},{10... | collective-permute-start | bytes 49160 | tf_op jit(solution)/shard_map/ppermute | solution.py:270

commit v2 on v0

v2 whole, which is shorter than its diff:
```python
import functools
import math

import jax
import jax.numpy as jnp
from jax import lax
from jax.experimental import pallas as pl
from jax.experimental.pallas import tpu as pltpu
from jax.sharding import PartitionSpec as P

SUB = 8
ROWS = 32
VMEM = pl.BlockSpec(memory_space=pltpu.VMEM)
HBM = pl.BlockSpec(memory_space=pl.ANY)
PARAMS = pltpu.CompilerParams(vmem_limit_bytes=32 << 20)


def split(values):
    high = values.astype(jnp.bfloat16)
    low = (values - high.astype(jnp.float32)).astype(jnp.bfloat16)
    return high, low


def iota(shape, dim):
    return lax.broadcasted_iota(jnp.int32, shape, dim)


def faces_kernel(u_hbm, u_ref, yface_ref, tail_ref, head_ref, sems):
    comps, nx, ny, nz = u_ref.shape
    quarters = sems.shape[1]
    rows = ny // quarters

    def fetch(c, k):
        span = pl.ds(k * rows if isinstance(k, int) else pl.multiple_of(k * rows, rows), rows)
        return pltpu.make_async_copy(u_hbm.at[c, :, span], u_ref.at[c, :, span], sems.at[c, k])

    for k in range(quarters):
        for c in (0, 1):
            fetch(c, k).start()
    for k in range(quarters):
        fetch(2, k).start()
    pair = iota((8, nz), 1) // 2

    def pack(members, y, out, first):
        out_rows = pl.ds(out, 8)
        tail = jnp.zeros((8, nz), jnp.float32)
        head = jnp.zeros((8, nz), jnp.float32)
        for c, base in members:
            for x in range(nx):
                place = base // 2 + x
                moved = pltpu.roll(u_ref[c, x, pl.ds(y, 8), :], (base + 2 * x + 2) % nz, 1)
                tail = jnp.where(pair == place, moved, tail)
                head = jnp.where(pair == (place + 1) % (nz // 2), moved, head)
        head = pltpu.roll(head, nz - 2, 1)
        if first:
            tail_ref[out_rows, :] = tail
            head_ref[out_rows, :] = head
        else:
            half = pair < nz // 4
            tail_ref[out_rows, :] = jnp.where(half, tail_ref[out_rows, :], tail)
            head_ref[out_rows, :] = jnp.where(half, head_ref[out_rows, :], head)

    def both(k, carry):
        fetch(0, k).wait()
        fetch(1, k).wait()
        for part in range(rows // 8):
            y = pl.multiple_of(k * rows + part * 8, 8)
            pack(((0, 0), (1, nz // 2)), y, y, True)
        return carry

    lax.fori_loop(0, quarters, both, 0)

    def last(base, offset, first):
        def step(k, carry):
            fetch(2, k).wait()
            for part in range(rows // 8):
                y = pl.multiple_of(k * rows + part * 8, 8)
                pack(((2, base),), y, pl.multiple_of(y + offset, 8), first)
            return carry

        return step

    lax.fori_loop(0, quarters // 2, last(0, ny, True), 0)
    lax.fori_loop(quarters // 2, quarters, last(nz // 2, ny // 2, False), 0)
    for c in range(comps):
        for x in range(nx):
            end = u_ref[c, x, pl.ds(ny - 8, 8), :]
            start = u_ref[c, x, pl.ds(0, 8), :]
            yface_ref[0, c, pl.ds(2 * x, 2), :] = jnp.concatenate([end[6:7] - 8.0 * end[7:8], end[7:8]], axis=0)
            yface_ref[1, c, pl.ds(2 * x, 2), :] = jnp.concatenate([-start[0:1], 8.0 * start[0:1] - start[1:2]], axis=0)


def faces(u):
    comps, nx, ny, nz = u.shape
    packed = jax.ShapeDtypeStruct((ny + ny // 2, nz), jnp.float32)
    return pl.pallas_call(
        faces_kernel,
        out_shape=(
            jax.ShapeDtypeStruct(u.shape, jnp.float32),
            jax.ShapeDtypeStruct((2, comps, 2 * nx, nz), jnp.float32),
            packed,
            packed,
        ),
        in_specs=[HBM],
        out_specs=(VMEM,) * 4,
        scratch_shapes=[pltpu.SemaphoreType.DMA((comps, 4))],
        compiler_params=pltpu.CompilerParams(vmem_limit_bytes=52 << 20),
        cost_estimate=pl.CostEstimate(flops=4 * u.size, bytes_accessed=4 * u.size, transcendentals=0),
    )(u)


def stencil(far):
    one = jnp.where(far == 1, 8.0, 0.0) - jnp.where(far == -1, 8.0, 0.0)
    return (one - jnp.where(far == 2, 1.0, 0.0) + jnp.where(far == -2, 1.0, 0.0)).astype(jnp.bfloat16)


def prepare(u_shape, yleft_ref, yright_ref, zleft_ref, zright_ref, top_ref, low_ref, fix_ref, dz_ref, dy_ref, sum_ref):
    comps, nx, ny, nz = u_shape
    dz_ref[...] = stencil(iota((2 * nz, nz), 0) % nz - iota((2 * nz, nz), 1))
    dy_ref[...] = stencil(iota((ny, 2 * ny), 1) % ny - iota((ny, 2 * ny), 0))
    row = iota((2 * nz, 2 * nz), 0) % nz
    col = iota((2 * nz, 2 * nz), 1)
    sum_ref[...] = jnp.where((row < col) & (col < nz) | (row <= col - nz), -1.0, 0.0).astype(jnp.bfloat16)
    source, target = iota((2 * nz, nz), 0) % nz, iota((2 * nz, nz), 1)
    side, place, layer = source // (2 * nx), source % (2 * nx) // 2, source % 2
    where = jnp.where(place == target // 4, 4 * side + 2 * layer, -1000) + 10 * (target % 4)
    weights = jnp.zeros((2 * nz, nz), jnp.float32)
    for value, (s, l, t) in (
        (1.0, (0, 0, 2)),
        (-8.0, (0, 1, 2)),
        (1.0, (0, 1, 3)),
        (-1.0, (1, 0, 0)),
        (8.0, (1, 0, 1)),
        (-1.0, (1, 1, 1)),
    ):
        weights = jnp.where(where == 4 * s + 2 * l + 10 * t, value, weights)
    weights = weights.astype(jnp.bfloat16)
    first = iota((ny, nz), 1) < nz // 2
    left, right = zleft_ref[:ny], zright_ref[:ny]
    left2, right2 = zleft_ref[ny:], zright_ref[ny:]
    turned_left2, turned_right2 = pltpu.roll(left2, nz // 2, 1), pltpu.roll(right2, nz // 2, 1)
    ghosts = (
        jnp.where(first, left, pltpu.roll(right, nz // 2, 1)),
        jnp.where(first, pltpu.roll(left, nz // 2, 1), right),
        jnp.where(
            first,
            jnp.concatenate([left2, turned_left2], axis=0),
            jnp.concatenate([turned_right2, right2], axis=0),
        ),
    )
    for c in range(comps):
        parts = jnp.concatenate(split(ghosts[c]), axis=1)
        fix_ref[c] = jnp.dot(parts, weights, preferred_element_type=jnp.float32)
    sub = iota((8, nz), 0)
    for c in range(comps):
        for group in range(nx // 4):
            left8 = yleft_ref[c, pl.ds(8 * group, 8), :]
            right8 = yright_ref[c, pl.ds(8 * group, 8), :]
            for k in range(4):
                top = left8 if k == 0 else pltpu.roll(left8, 8 - 2 * k, 0)
                low = right8 if k == 3 else pltpu.roll(right8, 6 - 2 * k, 0)
                top_ref[c, 4 * group + k] = jnp.where(sub < 2, top, 0.0)
                low_ref[c, 4 * group + k] = jnp.where(sub >= 6, low, 0.0)


def slopes(slab, x, refs, slope_ref):
    top_ref, low_ref, fix_ref, dz_ref, dy_ref = refs
    comps, ny, nz = slope_ref.shape[1:]
    lane = iota((ny, nz), 1)
    border = (lane >= nz - 2) | (lane < 2)
    shift = (2 * nz - 2 - 4 * x) % nz if isinstance(x, int) else lax.rem(2 * nz - 2 - 4 * x, nz)
    for c in range(comps):
        high, low = split(slab(c))
        depth = jnp.dot(jnp.concatenate([high, low], axis=1), dz_ref[...], preferred_element_type=jnp.float32)
        fix = pltpu.roll(fix_ref[c], shift, 1)
        slope_ref[1, c] = depth + jnp.where(border, fix, 0.0)
        down = jnp.dot(dy_ref[...], jnp.concatenate([high, low], axis=0), preferred_element_type=jnp.float32)
        slope_ref[0, c, pl.ds(0, 8), :] = down[:8] + top_ref[c, x]
        slope_ref[0, c, pl.ds(8, ny - 16), :] = down[8 : ny - 8]
        slope_ref[0, c, pl.ds(ny - 8, 8), :] = down[ny - 8 :] + low_ref[c, x]


def shade(near, x, slope_ref, scale_ref, offset_ref, level_ref):
    comps, ny, nz = slope_ref.shape[1:]
    block = x // SUB
    for y in range(0, ny, ROWS):
        rows = pl.ds(y, ROWS)
        across = [
            8.0 * (near(c, 1, rows) - near(c, -1, rows)) - (near(c, 2, rows) - near(c, -2, rows)) for c in range(comps)
        ]
        down = [slope_ref[0, c, rows, :] for c in range(comps)]
        depth = [slope_ref[1, c, rows, :] for c in range(comps)]
        total = 0.5 * (across[0] * across[0] + down[1] * down[1] + depth[2] * depth[2])
        total = total + across[1] * down[0] + across[2] * depth[0] + down[2] * depth[1]
        level = total * scale_ref[block, rows, :] + offset_ref[block, rows, :]
        level_ref[rows, :] = jnp.clip(level, 0.0, 1.0)


def blend(density, level_ref, sum_ref, store):
    ny, nz = level_ref.shape
    level = level_ref[...]
    binary = density / math.log(2.0)
    parts = jnp.concatenate(split(binary * level), axis=1)
    sums = jnp.dot(parts, sum_ref[...], preferred_element_type=jnp.float32)
    first = (jnp.exp2(sums[:, :nz]) - jnp.exp2(sums[:, nz:])) * level
    second = first * level
    lane_group = iota((8, ny), 1) // 8
    eye = iota((8, ny), 1) % 8 == iota((8, ny), 0)

    def lanes(cells):
        total = jnp.zeros((8, ny), jnp.float32)
        for group in range(ny // 8):
            part = jnp.sum(cells[8 * group : 8 * group + 8], axis=1, keepdims=True)
            total = jnp.where(lane_group == group, part, total)
        return jnp.sum(jnp.where(eye, total, 0.0), axis=0, keepdims=True)

    red = lanes(first)
    square = lanes(second)
    through = jnp.exp2(-binary * lanes(level))
    store(red, 4.0 * (red - square), 1.0 - through - red, through)


def put(image_ref, row):
    def store(*channels):
        for k, values in enumerate(channels):
            image_ref[k, pl.ds(row, 1), :] = values

    return store


def inner_kernel(
    density, u_ref, yleft_ref, yright_ref, zleft_ref, zright_ref, scale_ref, offset_ref,
    image_ref, top_ref, low_ref, fix_ref, dz_ref, dy_ref, sum_ref, slope0_ref, slope1_ref, level0_ref, level1_ref,
):
    comps, nx, ny, nz = u_ref.shape
    prepare(u_ref.shape, yleft_ref, yright_ref, zleft_ref, zright_ref, top_ref, low_ref, fix_ref, dz_ref, dy_ref, sum_ref)
    refs = (top_ref, low_ref, fix_ref, dz_ref, dy_ref)
    level1_ref[...] = jnp.zeros(level1_ref.shape, jnp.float32)

    def slab(x):
        return lambda c: u_ref[c, x]

    def near(x):
        return lambda c, d, rows: u_ref[c, x + d, rows, :]

    slopes(slab(2), 2, refs, slope0_ref)

    def pair(i, carry):
        x = 2 * i + 2
        slopes(slab(x + 1), x + 1, refs, slope1_ref)
        shade(near(x), x, slope0_ref, scale_ref, offset_ref, level0_ref)
        blend(density, level1_ref, sum_ref, put(image_ref, x - 1))
        slopes(slab(x + 2), x + 2, refs, slope0_ref)
        shade(near(x + 1), x + 1, slope1_ref, scale_ref, offset_ref, level1_ref)
        blend(density, level0_ref, sum_ref, put(image_ref, x))
        return carry

    lax.fori_loop(0, (nx - 4) // 2, pair, 0)
    blend(density, level1_ref, sum_ref, put(image_ref, nx - 3))


def tables(u):
    comps, nx, ny, nz = u.shape
    return [
        pltpu.VMEM((comps, nx, 8, nz), jnp.float32),
        pltpu.VMEM((comps, nx, 8, nz), jnp.float32),
        pltpu.VMEM((comps, ny, nz), jnp.float32),
        pltpu.VMEM((2 * nz, nz), jnp.bfloat16),
        pltpu.VMEM((ny, 2 * ny), jnp.bfloat16),
        pltpu.VMEM((2 * nz, 2 * nz), jnp.bfloat16),
        pltpu.VMEM((2, comps, ny, nz), jnp.float32),
        pltpu.VMEM((2, comps, ny, nz), jnp.float32),
        pltpu.VMEM((ny, nz), jnp.float32),
        pltpu.VMEM((ny, nz), jnp.float32),
    ]


def inner(density, u, *rest):
    comps, nx, ny, nz = u.shape
    return pl.pallas_call(
        functools.partial(inner_kernel, density),
        out_shape=jax.ShapeDtypeStruct((4, nx, ny), jnp.float32),
        in_specs=[VMEM] * 7,
        out_specs=VMEM,
        scratch_shapes=tables(u),
        compiler_params=PARAMS,
        cost_estimate=pl.CostEstimate(flops=100 * u.size, bytes_accessed=4 * u.size, transcendentals=2 * u.size),
    )(u, *rest)


def edge_kernel(
    density, u_ref, xleft_ref, xright_ref, yleft_ref, yright_ref, zleft_ref, zright_ref, scale_ref, offset_ref,
    image_ref, top_ref, low_ref, fix_ref, dz_ref, dy_ref, sum_ref, slope0_ref, slope1_ref, level0_ref, level1_ref,
):
    comps, nx, ny, nz = u_ref.shape
    prepare(u_ref.shape, yleft_ref, yright_ref, zleft_ref, zright_ref, top_ref, low_ref, fix_ref, dz_ref, dy_ref, sum_ref)
    refs = (top_ref, low_ref, fix_ref, dz_ref, dy_ref)

    def near(x):
        def read(c, d, rows):
            if x + d < 0:
                return xleft_ref[c, x + d + 2, rows, :]
            if x + d >= nx:
                return xright_ref[c, x + d - nx, rows, :]
            return u_ref[c, x + d, rows, :]

        return read

    def slab(x):
        return lambda c: u_ref[c, x]

    for place, x in enumerate((0, 1, nx - 2, nx - 1)):
        slope_ref = (slope0_ref, slope1_ref)[place % 2]
        level_ref = (level0_ref, level1_ref)[place % 2]
        slopes(slab(x), x, refs, slope_ref)
        shade(near(x), x, slope_ref, scale_ref, offset_ref, level_ref)
        blend(density, level_ref, sum_ref, put(image_ref, place))


def edge(density, u, *rest):
    comps, nx, ny, nz = u.shape
    return pl.pallas_call(
        functools.partial(edge_kernel, density),
        out_shape=jax.ShapeDtypeStruct((4, 4, ny), jnp.float32),
        in_specs=[VMEM] * 9,
        out_specs=VMEM,
        scratch_shapes=tables(u),
        compiler_params=PARAMS,
        cost_estimate=pl.CostEstimate(flops=12 * u.size, bytes_accessed=2 * u.size, transcendentals=u.size // 4),
    )(u, *rest)


def turn(block, axis, by):
    count = lax.axis_size(axis)
    return lax.ppermute(block, axis, [(i, (i + by) % count) for i in range(count)])


def both_sides(tail_head, axis):
    if lax.axis_size(axis) == 2:
        other = turn(tail_head, axis, 1)
        return other[0], other[1]
    return turn(tail_head[0], axis, 1), turn(tail_head[1], axis, -1)


def local(velocity, occupied, q_floor, q_span):
    comps, nx, ny, nz = velocity.shape
    views = lax.axis_size("view")
    density = 5.0 / (nz * views)
    xleft = turn(velocity[:, nx - 2 :], "gx", 1)
    xright = turn(velocity[:, :2], "gx", -1)
    u, yface, tail, head = faces(velocity)
    yleft, yright = both_sides(yface, "gy")
    zleft = turn(tail, "view", 1)
    zright = turn(head, "view", -1)
    mask = jnp.repeat(occupied[:, :, 0].astype(jnp.float32), SUB, axis=1)
    spread = (nx // SUB, ny, nz)
    scale = jnp.broadcast_to((mask * (-1.0 / 144.0 / q_span[0]))[:, :, None], spread)
    offset = jnp.broadcast_to((mask * (-q_floor[0] / q_span[0]))[:, :, None], spread)
    middle = inner(density, u, yleft, yright, zleft, zright, scale, offset)
    border = edge(density, u, xleft, xright, yleft, yright, zleft, zright, scale, offset)
    partial_image = jnp.concatenate([border[:, :2], middle[:, 2:-2], border[:, 2:]], axis=1)
    rows = nx // views
    blocks = partial_image.reshape(4, views, rows, ny)
    me = lax.axis_index("view")
    sources, images = [me], [lax.dynamic_index_in_dim(blocks, me, 1, keepdims=False)]
    for by in range(1, views):
        sent = lax.dynamic_index_in_dim(blocks, (me + by) % views, 1, keepdims=False)
        images.append(turn(sent, "view", by))
        sources.append((me - by) % views)
    colour = jnp.zeros((3, rows, ny), jnp.float32)
    through = jnp.ones((rows, ny), jnp.float32)
    for source, image in zip(sources, images):
        passing = jnp.ones((rows, ny), jnp.float32)
        for other, behind in zip(sources, images):
            passing = passing * jnp.where(other < source, behind[3], 1.0)
        colour = colour + passing * image[:3]
        through = through * image[3]
    finished = jnp.concatenate([colour, 1.0 - through[None]], axis=0)
    return finished.reshape(1, 1, 4, rows, ny)


def solution(mesh):
    placed = (P(None, "gx", "gy", "view"), P("gx", "gy", "view"), P(), P())
    return jax.shard_map(
        local,
        mesh=mesh,
        in_specs=placed,
        out_specs=P("gx", "gy", None, "view", None),
        check_vma=False,
    )
```

time: 133 us -> 43.7 us (0.33)
  other arithmetic: 49.5 us -> 0.67 us
  matrix products: 32.4 us -> 0 us
  local copies, waits for them, and re-layouts: 32.1 us -> 4.59 us
  Pallas kernels: 0 us -> 17.2 us
  waiting for transfers between devices: 6.18 us -> 7.87 us
    dot_general x1 -> x0, matrix products: 32.4 us -> none  [local(): jnp.dot(optical.reshape(brick_x * brick_y, brick_z), strict_upper, precis...]
    reduce_sum x1 -> x0, other arithmetic: 32 us -> none  [local(): red = jnp.sum(weight * shade_level, axis=-1)]
    pallas_call x0 -> x3, Pallas kernels: none -> 17.2 us  [the longest x1 8.75 us: inner(): pl.pallas_call(functools.partial(inner_kernel, density), out_shape=jax.Sh...]
    concatenate x3 -> x0, other arithmetic: 16.8 us -> none  [the longest x2 16.8 us: extended(): jnp.concatenate([lax.ppermute(tail, axis, [(i, (i + 1) % count) for i in...]
    squeeze x3 -> x2, local copies, waits for them, and re-layouts: 12.1 us -> 0.03 us  [the longest x1 0.02 us: local(): lax.dynamic_index_in_dim(blocks, (me + by) % views, 1, keepdims=False)]
    ppermute x2 -> x0, local copies, waits for them, and re-layouts: 7.95 us -> none  [the longest x1 3.98 us: extended(): lax.ppermute(tail, axis, [(i, (i + 1) % count) for i in range(count)])]
    slice x3, local copies, waits for them, and re-layouts: 5.12 us -> 1.19 us  [the longest x1 1.18 us: local(): xright = turn(velocity[:, :2], 'gx', -1)]
    unnamed x9 -> x4, local copies, waits for them, and re-layouts: 6.61 us -> 2.79 us
  transfers between devices with their start and end apart: 8 -> 8, of which waited for: 2 -> 5; matrix products, arithmetic and copies ran while one was open for 36% -> 1% of each run, Pallas kernels for 0% -> 36%
where the time goes in v2:
time: 43.7 us; the launch traced here: 43.5 us
  Pallas kernels  17.2 us (39%)
  starting transfers between devices  11.6 us (27%)
  waiting for transfers between devices  7.87 us (18%)
  local copies, waits for them, and re-layouts  4.59 us (11%)
  between operations  1.56 us (4%)
  other arithmetic  0.67 us (2%)
    ppermute x8, starting transfers between devices, turn(): lax.ppermute(block, axis, [(i, (i + by) % count) for i in range(count)])  11.6 us
    pallas_call x1, Pallas kernels, inner(): pl.pallas_call(functools.partial(inner_kernel, density), out_shape=jax.Sh...  8.75 us
    ppermute x8, waiting for transfers between devices, turn(): lax.ppermute(block, axis, [(i, (i + by) % count) for i in range(count)])  7.87 us
    pallas_call x1, Pallas kernels, faces(): pl.pallas_call(faces_kernel, out_shape=(jax.ShapeDtypeStruct(u.shape, jnp...  6.91 us
    unnamed x4, local copies, waits for them, and re-layouts  2.79 us
    pallas_call x1, Pallas kernels, edge(): pl.pallas_call(functools.partial(edge_kernel, density), out_shape=jax.Sha...  1.51 us
    slice x1, local copies, waits for them, and re-layouts, local(): xright = turn(velocity[:, :2], 'gx', -1)  1.18 us
  transfers between devices with their start and end apart: 8, of which 5 were waited for; matrix products, arithmetic and copies ran while one was open for 1% of the time, Pallas kernels for 36%

profile of v2, /device:TPU:0, one launch (start us, length us, event | category | flops | bytes accessed | tf_op | source)
XLA Modules:
  0.0 43.5 jit_solution(1851985733524909297)
XLA Ops:
  0.0 0.0 copy-start.1
  0.0 1.2 %fusion.4 = (f32[3,2,128,128]{3,2,1,0:T(8,128)S(1)}, f32[3,2,128,128]{3,2,1,0:T(8,128)S(1)}) fusion(f32[3,32,128,128]{3,2,1,0:T(8,128)} %u_hbm.1), kind=kLoop, calls=%fused_computation.23 | loop fusion | bytes 1572864 | tf_op jit(solution)/shard_map/slice | solution.py:350
  1.2 3.0 %collective-permute-start = (f32[3,2,128,128]{3,2,1,0:T(8,128)S(1)}, f32[3,2,128,128]{3,2,1,0:T(8,128)S(1)}, u32[]{:S(2)}, u32[]{:S(2)}) collective-permute-start(f32[3,2,128,128]{3,2,1,0:T(8,128)S(1)} %get-tuple-element.14), channel_id=1, source_target_pairs={{0,2},{2,4},{4,6},{6,0},{1,3},{3,5},{5,7},{7,1},{8,10},{10,12},{12... | collective-permute-start | bytes 1179656 | tf_op jit(solution)/shard_map/ppermute | solution.py:335
  4.2 1.0 %collective-permute-start.1 = (f32[3,2,128,128]{3,2,1,0:T(8,128)S(1)}, f32[3,2,128,128]{3,2,1,0:T(8,128)S(1)}, u32[]{:S(2)}, u32[]{:S(2)}) collective-permute-start(f32[3,2,128,128]{3,2,1,0:T(8,128)S(1)} %get-tuple-element.13), channel_id=1, source_target_pairs={{0,6},{2,0},{4,2},{6,4},{1,7},{3,1},{5,3},{7,5},{8,14},{10,8},{12,... | collective-permute-start | bytes 1179656 | tf_op jit(solution)/shard_map/ppermute | solution.py:335
  5.2 6.9 %shard_map.46 = (f32[3,32,128,128]{3,2,1,0:T(8,128)}, f32[2,3,64,128]{3,2,1,0:T(8,128)S(1)}, f32[192,128]{1,0:T(8,128)S(1)}, f32[192,128]{1,0:T(8,128)S(1)}) custom-call(f32[3,32,128,128]{3,2,1,0:T(8,128)} %u_hbm.1), custom_call_target="tpu_custom_call" | custom-call | flops 6291456 | bytes 6291456 | tf_op jit(solution)/shard_map/pallas_call | solution.py:96
  12.1 0.1 collective-permute-start.2
  12.2 2.0 %collective-permute-start.3 = (f32[192,128]{1,0:T(8,128)S(1)}, f32[192,128]{1,0:T(8,128)S(1)}, u32[]{:S(2)}, u32[]{:S(2)}) collective-permute-start(f32[192,128]{1,0:T(8,128)S(1)} %get-tuple-element.11), channel_id=1, source_target_pairs={{0,8},{8,16},{16,24},{24,0},{1,9},{9,17},{17,25},{25,1},{2,10},{10... | collective-permute-start | bytes 294920 | tf_op jit(solution)/shard_map/ppermute | solution.py:335
  14.2 2.1 %collective-permute-start.4 = (f32[192,128]{1,0:T(8,128)S(1)}, f32[192,128]{1,0:T(8,128)S(1)}, u32[]{:S(2)}, u32[]{:S(2)}) collective-permute-start(f32[192,128]{1,0:T(8,128)S(1)} %get-tuple-element.12), channel_id=1, source_target_pairs={{0,24},{8,0},{16,8},{24,16},{1,25},{9,1},{17,9},{25,17},{2,26},{10... | collective-permute-start | bytes 294920 | tf_op jit(solution)/shard_map/ppermute | solution.py:335
  17.7 0.0 copy-done.1
  17.8 0.1 broadcast_in_dim.41
  17.8 0.1 mul.125
  17.9 0.1 broadcast_in_dim.43
  18.0 0.1 mul.129
  18.1 0.0 collective-permute-done.2
  18.1 1.8 %collective-permute-done.3.zleft_ref = f32[192,128]{1,0:T(8,128)S(1)} collective-permute-done((f32[192,128]{1,0:T(8,128)S(1)}, f32[192,128]{1,0:T(8,128)S(1)}, u32[]{:S(2)}, u32[]{:S(2)}) %collective-permute-start.3) | collective-permute-done | bytes 98336 | tf_op jit(solution)/shard_map/ppermute | solution.py:335
  19.9 1.3 %collective-permute-done.4.zright_ref = f32[192,128]{1,0:T(8,128)S(1)} collective-permute-done((f32[192,128]{1,0:T(8,128)S(1)}, f32[192,128]{1,0:T(8,128)S(1)}, u32[]{:S(2)}, u32[]{:S(2)}) %collective-permute-start.4) | collective-permute-done | bytes 98336 | tf_op jit(solution)/shard_map/ppermute | solution.py:335
  21.2 0.1 broadcast_in_dim.42.scale_ref
  21.3 0.1 broadcast_in_dim.44.offset_ref
  21.5 0.0 copy-start
  21.5 2.8 %copy-done = f32[3,32,128,128]{3,2,1,0:T(8,128)S(1)} copy-done((f32[3,32,128,128]{3,2,1,0:T(8,128)S(1)}, f32[3,32,128,128]{3,2,1,0:T(8,128)}, u32[]{:S(2)}) %copy-start) | copy-done | bytes 6291480
  24.3 8.7 %shard_map.48 = f32[4,32,128]{2,1,0:T(8,128)S(1)} custom-call(f32[3,32,128,128]{3,2,1,0:T(8,128)S(1)} %copy-done, f32[3,64,128]{2,1,0:T(8,128)S(1)} %get-tuple-element.16.yleft_ref, f32[3,64,128]{2,1,0:T(8,128)S(1)} %get-tuple-element.15.yright_ref, f32[192,128]{1,0:T(8,128)S(1)} %collective-permute-done.3.zleft_ref, ...), custom_call_target="tpu_custom_call" | custom-call | flops 157286400 | bytes 6291456 | tf_op jit(solution)/shard_map/pallas_call | solution.py:280
  33.0 0.0 collective-permute-done.xleft_ref
  33.0 0.0 collective-permute-done.1.xright_ref
  33.1 1.5 %shard_map.47 = f32[4,4,128]{2,1,0:T(4,128)S(1)} custom-call(f32[3,32,128,128]{3,2,1,0:T(8,128)S(1)} %copy-done, f32[3,2,128,128]{3,2,1,0:T(8,128)S(1)} %collective-permute-done.xleft_ref, f32[3,2,128,128]{3,2,1,0:T(8,128)S(1)} %collective-permute-done.1.xright_ref, f32[3,64,128]{2,1,0:T(8,128)S(1)} %get-tuple-element.16.yleft_ref, ...), custom_call_target="tpu_custom_call" | custom-call | flops 18874368 | bytes 3145728 | tf_op jit(solution)/shard_map/pallas_call | solution.py:322
  34.6 2.4 %collective-permute-start.7 = (f32[4,8,128]{2,1,0:T(8,128)S(1)}, f32[4,8,128]{2,1,0:T(8,128)S(1)}, u32[]{:S(2)}, u32[]{:S(2)}) collective-permute-start(f32[4,8,128]{2,1,0:T(8,128)S(1)} %get-tuple-element.21), channel_id=1, source_target_pairs={{0,24},{8,0},{16,8},{24,16},{1,25},{9,1},{17,9},{25,17},{2,26},{10... | collective-permute-start | bytes 49160 | tf_op jit(solution)/shard_map/ppermute | solution.py:335
  37.0 0.3 collective-permute-start.6
  37.3 0.7 %collective-permute-start.5 = (f32[4,8,128]{2,1,0:T(8,128)S(1)}, f32[4,8,128]{2,1,0:T(8,128)S(1)}, u32[]{:S(2)}, u32[]{:S(2)}) collective-permute-start(f32[4,8,128]{2,1,0:T(8,128)S(1)} %get-tuple-element.20), channel_id=1, source_target_pairs={{0,8},{8,16},{16,24},{24,0},{1,9},{9,17},{17,25},{25,1},{2,10},{10... | collective-permute-start | bytes 49160 | tf_op jit(solution)/shard_map/ppermute | solution.py:335
  38.0 0.4 collective-permute-done.7
  38.4 3.2 %collective-permute-done.6 = f32[4,8,128]{2,1,0:T(8,128)S(1)} collective-permute-done((f32[4,8,128]{2,1,0:T(8,128)S(1)}, f32[4,8,128]{2,1,0:T(8,128)S(1)}, u32[]{:S(2)}, u32[]{:S(2)}) %collective-permute-start.6) | collective-permute-done | bytes 16416 | tf_op jit(solution)/shard_map/ppermute | solution.py:335
  41.6 1.2 %collective-permute-done.5 = f32[4,8,128]{2,1,0:T(8,128)S(1)} collective-permute-done((f32[4,8,128]{2,1,0:T(8,128)S(1)}, f32[4,8,128]{2,1,0:T(8,128)S(1)}, u32[]{:S(2)}, u32[]{:S(2)}) %collective-permute-start.5) | collective-permute-done | bytes 16416 | tf_op jit(solution)/shard_map/ppermute | solution.py:335
  42.9 0.6 %maximum_bitcast_fusion.1 = f32[1,1,4,8,128]{4,3,2,1,0:T(8,128)} fusion(f32[1,8,128]{2,1,0:T(8,128)S(1)} %get-tuple-element.18, f32[3,8,128]{2,1,0:T(8,128)S(1)} %fusion), kind=kLoop, calls=%fused_computation.3 | loop fusion | flops 4096 | bytes 32768 | tf_op jit(solution)/shard_map/reshape | solution.py:379
  (9 shorter events, 0.1 us)
Async XLA Ops:
  0.0 17.7 %copy-start.1 = (s32[4,16,1]{1,2,0:T(1,128)S(1)}, s32[4,16,1]{1,2,0:T(1,128)}, u32[]{:S(2)}) copy-start(s32[4,16,1]{1,2,0:T(1,128)} %param.5) | copy-start | bytes 772
  1.2 31.9 %collective-permute-start = (f32[3,2,128,128]{3,2,1,0:T(8,128)S(1)}, f32[3,2,128,128]{3,2,1,0:T(8,128)S(1)}, u32[]{:S(2)}, u32[]{:S(2)}) collective-permute-start(f32[3,2,128,128]{3,2,1,0:T(8,128)S(1)} %get-tuple-element.14), channel_id=1, source_target_pairs={{0,2},{2,4},{4,6},{6,0},{1,3},{3,5},{5,7},{7,1},{8,10},{10,12},{12... | collective-permute-start | bytes 1179656 | tf_op jit(solution)/shard_map/ppermute | solution.py:335
  4.2 28.9 %collective-permute-start.1 = (f32[3,2,128,128]{3,2,1,0:T(8,128)S(1)}, f32[3,2,128,128]{3,2,1,0:T(8,128)S(1)}, u32[]{:S(2)}, u32[]{:S(2)}) collective-permute-start(f32[3,2,128,128]{3,2,1,0:T(8,128)S(1)} %get-tuple-element.13), channel_id=1, source_target_pairs={{0,6},{2,0},{4,2},{6,4},{1,7},{3,1},{5,3},{7,5},{8,14},{10,8},{12,... | collective-permute-start | bytes 1179656 | tf_op jit(solution)/shard_map/ppermute | solution.py:335
  12.1 6.0 %collective-permute-start.2 = (f32[2,3,64,128]{3,2,1,0:T(8,128)S(1)}, f32[2,3,64,128]{3,2,1,0:T(8,128)S(1)}, u32[]{:S(2)}, u32[]{:S(2)}) collective-permute-start(f32[2,3,64,128]{3,2,1,0:T(8,128)S(1)} %get-tuple-element.10), channel_id=1, source_target_pairs={{0,1},{1,0},{2,3},{3,2},{4,5},{5,4},{6,7},{7,6},{8,9},{9,8},{10,11... | collective-permute-start | bytes 589832 | tf_op jit(solution)/shard_map/ppermute | solution.py:335
  12.2 7.7 %collective-permute-start.3 = (f32[192,128]{1,0:T(8,128)S(1)}, f32[192,128]{1,0:T(8,128)S(1)}, u32[]{:S(2)}, u32[]{:S(2)}) collective-permute-start(f32[192,128]{1,0:T(8,128)S(1)} %get-tuple-element.11), channel_id=1, source_target_pairs={{0,8},{8,16},{16,24},{24,0},{1,9},{9,17},{17,25},{25,1},{2,10},{10... | collective-permute-start | bytes 294920 | tf_op jit(solution)/shard_map/ppermute | solution.py:335
  14.2 7.0 %collective-permute-start.4 = (f32[192,128]{1,0:T(8,128)S(1)}, f32[192,128]{1,0:T(8,128)S(1)}, u32[]{:S(2)}, u32[]{:S(2)}) collective-permute-start(f32[192,128]{1,0:T(8,128)S(1)} %get-tuple-element.12), channel_id=1, source_target_pairs={{0,24},{8,0},{16,8},{24,16},{1,25},{9,1},{17,9},{25,17},{2,26},{10... | collective-permute-start | bytes 294920 | tf_op jit(solution)/shard_map/ppermute | solution.py:335
  21.5 2.8 %copy-start = (f32[3,32,128,128]{3,2,1,0:T(8,128)S(1)}, f32[3,32,128,128]{3,2,1,0:T(8,128)}, u32[]{:S(2)}) copy-start(f32[3,32,128,128]{3,2,1,0:T(8,128)} %get-tuple-element.9.u_ref) | copy-start | bytes 18874372
  34.6 3.8 %collective-permute-start.7 = (f32[4,8,128]{2,1,0:T(8,128)S(1)}, f32[4,8,128]{2,1,0:T(8,128)S(1)}, u32[]{:S(2)}, u32[]{:S(2)}) collective-permute-start(f32[4,8,128]{2,1,0:T(8,128)S(1)} %get-tuple-element.21), channel_id=1, source_target_pairs={{0,24},{8,0},{16,8},{24,16},{1,25},{9,1},{17,9},{25,17},{2,26},{10... | collective-permute-start | bytes 49160 | tf_op jit(solution)/shard_map/ppermute | solution.py:335
  37.0 4.6 %collective-permute-start.6 = (f32[4,8,128]{2,1,0:T(8,128)S(1)}, f32[4,8,128]{2,1,0:T(8,128)S(1)}, u32[]{:S(2)}, u32[]{:S(2)}) collective-permute-start(f32[4,8,128]{2,1,0:T(8,128)S(1)} %get-tuple-element.22), channel_id=1, source_target_pairs={{0,16},{8,24},{16,0},{24,8},{1,17},{9,25},{17,1},{25,9},{2,18},{10... | collective-permute-start | bytes 49160 | tf_op jit(solution)/shard_map/ppermute | solution.py:335
  37.3 5.5 %collective-permute-start.5 = (f32[4,8,128]{2,1,0:T(8,128)S(1)}, f32[4,8,128]{2,1,0:T(8,128)S(1)}, u32[]{:S(2)}, u32[]{:S(2)}) collective-permute-start(f32[4,8,128]{2,1,0:T(8,128)S(1)} %get-tuple-element.20), channel_id=1, source_target_pairs={{0,8},{8,16},{16,24},{24,0},{1,9},{9,17},{17,25},{25,1},{2,10},{10... | collective-permute-start | bytes 49160 | tf_op jit(solution)/shard_map/ppermute | solution.py:335

commit v3 on v2

v3 whole, which is shorter than its diff:
```python
import functools
import math

import jax
import jax.numpy as jnp
from jax import lax
from jax.experimental import pallas as pl
from jax.experimental.pallas import tpu as pltpu
from jax.sharding import PartitionSpec as P

SUB = 8
ROWS = 32
VMEM = pl.BlockSpec(memory_space=pltpu.VMEM)
HBM = pl.BlockSpec(memory_space=pltpu.HBM)
COST = pl.CostEstimate(flops=1 << 20, bytes_accessed=1 << 20, transcendentals=0)
PARAMS = pltpu.CompilerParams(vmem_limit_bytes=32 << 20)


def split(values):
    high = values.astype(jnp.bfloat16)
    low = (values - high.astype(jnp.float32)).astype(jnp.bfloat16)
    return high, low


def iota(shape, dim):
    return lax.broadcasted_iota(jnp.int32, shape, dim)


def faces_kernel(
    u_hbm, u_ref, xtail_ref, xhead_ref, yface_ref, tail_ref, head_ref, sems, side_sems
):
    comps, nx, ny, nz = u_ref.shape
    sides = [
        pltpu.make_async_copy(source, target, side_sems.at[k])
        for k, (source, target) in enumerate(
            (
                (u_hbm.at[:, pl.ds(nx - 2, 2)], xtail_ref),
                (u_hbm.at[:, pl.ds(0, 2)], xhead_ref),
            )
        )
    ]
    quarters = sems.shape[1]
    rows = ny // quarters

    def fetch(c, k):
        span = pl.ds(k * rows if isinstance(k, int) else pl.multiple_of(k * rows, rows), rows)
        return pltpu.make_async_copy(u_hbm.at[c, :, span], u_ref.at[c, :, span], sems.at[c, k])

    for k in range(quarters):
        for c in (0, 1):
            fetch(c, k).start()
    for k in range(quarters):
        fetch(2, k).start()
    for copy in sides:
        copy.start()
    pair = iota((8, nz), 1) // 2

    def pack(members, y, out, first):
        out_rows = pl.ds(out, 8)
        tail = jnp.zeros((8, nz), jnp.float32)
        head = jnp.zeros((8, nz), jnp.float32)
        for c, base in members:
            for x in range(nx):
                place = base // 2 + x
                moved = pltpu.roll(u_ref[c, x, pl.ds(y, 8), :], (base + 2 * x + 2) % nz, 1)
                tail = jnp.where(pair == place, moved, tail)
                head = jnp.where(pair == (place + 1) % (nz // 2), moved, head)
        head = pltpu.roll(head, nz - 2, 1)
        if first:
            tail_ref[out_rows, :] = tail
            head_ref[out_rows, :] = head
        else:
            half = pair < nz // 4
            tail_ref[out_rows, :] = jnp.where(half, tail_ref[out_rows, :], tail)
            head_ref[out_rows, :] = jnp.where(half, head_ref[out_rows, :], head)

    def both(k, carry):
        fetch(0, k).wait()
        fetch(1, k).wait()
        for part in range(rows // 8):
            y = pl.multiple_of(k * rows + part * 8, 8)
            pack(((0, 0), (1, nz // 2)), y, y, True)
        return carry

    lax.fori_loop(0, quarters, both, 0)

    def last(base, offset, first):
        def step(k, carry):
            fetch(2, k).wait()
            for part in range(rows // 8):
                y = pl.multiple_of(k * rows + part * 8, 8)
                pack(((2, base),), y, pl.multiple_of(y + offset, 8), first)
            return carry

        return step

    lax.fori_loop(0, quarters // 2, last(0, ny, True), 0)
    lax.fori_loop(quarters // 2, quarters, last(nz // 2, ny // 2, False), 0)
    for c in range(comps):
        for x in range(nx):
            end = u_ref[c, x, pl.ds(ny - 8, 8), :]
            start = u_ref[c, x, pl.ds(0, 8), :]
            yface_ref[0, c, pl.ds(2 * x, 2), :] = jnp.concatenate([end[6:7] - 8.0 * end[7:8], end[7:8]], axis=0)
            yface_ref[1, c, pl.ds(2 * x, 2), :] = jnp.concatenate([-start[0:1], 8.0 * start[0:1] - start[1:2]], axis=0)
    for copy in sides:
        copy.wait()


def faces(u):
    comps, nx, ny, nz = u.shape

    def shaped(*shape):
        return jax.ShapeDtypeStruct(shape, jnp.float32)

    return pl.pallas_call(
        faces_kernel,
        out_shape=(
            shaped(*u.shape),
            shaped(comps, 2, ny, nz),
            shaped(comps, 2, ny, nz),
            shaped(2, comps, 2 * nx, nz),
            shaped(ny + ny // 2, nz),
            shaped(ny + ny // 2, nz),
        ),
        in_specs=[HBM],
        out_specs=(VMEM,) * 6,
        scratch_shapes=[
            pltpu.SemaphoreType.DMA((comps, 4)),
            pltpu.SemaphoreType.DMA((2,)),
        ],
        compiler_params=pltpu.CompilerParams(vmem_limit_bytes=45 << 20),
        cost_estimate=COST,
    )(u)


def stencil(far):
    one = jnp.where(far == 1, 8.0, 0.0) - jnp.where(far == -1, 8.0, 0.0)
    return (one - jnp.where(far == 2, 1.0, 0.0) + jnp.where(far == -2, 1.0, 0.0)).astype(jnp.bfloat16)


def sides_down(yleft_ref, yright_ref, top_ref, low_ref):
    comps, nx, _, nz = top_ref.shape
    sub = iota((8, nz), 0)
    for c in range(comps):
        for group in range(nx // 4):
            left8 = yleft_ref[c, pl.ds(8 * group, 8), :]
            right8 = yright_ref[c, pl.ds(8 * group, 8), :]
            for k in range(4):
                top = left8 if k == 0 else pltpu.roll(left8, 8 - 2 * k, 0)
                low = right8 if k == 3 else pltpu.roll(right8, 6 - 2 * k, 0)
                top_ref[c, 4 * group + k] = jnp.where(sub < 2, top, 0.0)
                low_ref[c, 4 * group + k] = jnp.where(sub >= 6, low, 0.0)


def shading(occupied_ref, floor, span, scale_ref, offset_ref):
    blocks, ny, nz = scale_ref.shape
    groups = ny // SUB
    mine = iota((ny, groups), 0) // SUB == iota((ny, groups), 1)
    shrink = 1.0 / span
    for block in range(blocks):
        row = occupied_ref[block : block + 1, :].astype(jnp.float32)
        column = jnp.sum(jnp.where(mine, row, 0.0), axis=1, keepdims=True)
        scale_ref[block] = jnp.broadcast_to(column * (shrink * (-1.0 / 144.0)), (ny, nz))
        offset_ref[block] = jnp.broadcast_to(column * (shrink * -floor), (ny, nz))


def lane_shift(x, nz, back):
    if isinstance(x, int):
        return (4 * x + 2 if back else 2 * nz - 2 - 4 * x) % nz
    return lax.rem(4 * x + 2 if back else 2 * nz - 2 - 4 * x, nz)


def slopes(u_ref, x, tables, slope_ref):
    top_ref, low_ref, dz_ref, dy_ref = tables
    comps, ny, nz = slope_ref.shape[1:]
    for c in range(comps):
        high, low = split(u_ref[c, x])
        slope_ref[1, c] = jnp.dot(
            jnp.concatenate([high, low], axis=1), dz_ref[...], preferred_element_type=jnp.float32
        )
        down = jnp.dot(dy_ref[...], jnp.concatenate([high, low], axis=0), preferred_element_type=jnp.float32)
        slope_ref[0, c, pl.ds(0, 8), :] = down[:8] + top_ref[c, x]
        slope_ref[0, c, pl.ds(8, ny - 16), :] = down[8 : ny - 8]
        slope_ref[0, c, pl.ds(ny - 8, 8), :] = down[ny - 8 :] + low_ref[c, x]


def shade(u_ref, x, slope_ref, scale_ref, offset_ref, raw_ref, pack_ref, kept_ref=None, place=None):
    comps, nx, ny, nz = u_ref.shape
    block = x // SUB
    back = lane_shift(x, nz, True)

    def across(c, rows):
        def part(d):
            inside = not isinstance(x, int) or 0 <= x + d < nx
            return u_ref[c, x + d, rows, :] if inside else None

        def difference(high, low):
            if high is None:
                return 0.0 if low is None else -low
            return high if low is None else high - low

        return 8.0 * difference(part(1), part(-1)) - difference(part(2), part(-2))

    for y in range(0, ny, ROWS):
        rows = pl.ds(y, ROWS)
        mine = iota((ROWS, nz), 1) // 4 == x
        side = [across(c, rows) for c in range(comps)]
        down = [slope_ref[0, c, rows, :] for c in range(comps)]
        depth = [slope_ref[1, c, rows, :] for c in range(comps)]
        total = 0.5 * (side[0] * side[0] + down[1] * down[1] + depth[2] * depth[2])
        total = total + side[1] * down[0] + side[2] * depth[0] + down[2] * depth[1]
        raw_ref[x, rows, :] = total * scale_ref[block, rows, :] + offset_ref[block, rows, :]
        for k, values in enumerate((side[2], down[2], depth[2])):
            pack_ref[k, rows, :] = jnp.where(mine, pltpu.roll(values, back, 1), pack_ref[k, rows, :])
        if kept_ref is not None:
            for k, values in enumerate((side[0], down[0], depth[0])):
                kept_ref[place, k, rows, :] = values


def edge_rows(nx):
    return (0, 1, nx - 2, nx - 1)


def shade_kernel(
    u_ref, yleft_ref, yright_ref, occupied_ref, floor_ref, span_ref,
    raw_ref, pack_ref, kept_ref, scale_ref, offset_ref, top_ref, low_ref, dz_ref, dy_ref, slope0_ref, slope1_ref,
):
    comps, nx, ny, nz = u_ref.shape
    dz_ref[...] = stencil(iota((2 * nz, nz), 0) % nz - iota((2 * nz, nz), 1))
    dy_ref[...] = stencil(iota((ny, 2 * ny), 1) % ny - iota((ny, 2 * ny), 0))
    sides_down(yleft_ref, yright_ref, top_ref, low_ref)
    shading(occupied_ref, floor_ref[...].reshape(1, 1), span_ref[...].reshape(1, 1), scale_ref, offset_ref)
    pack_ref[...] = jnp.zeros(pack_ref.shape, jnp.float32)
    tables = (top_ref, low_ref, dz_ref, dy_ref)
    outs = (scale_ref, offset_ref, raw_ref, pack_ref)
    slopes(u_ref, 0, tables, slope0_ref)
    slopes(u_ref, 1, tables, slope1_ref)
    shade(u_ref, 0, slope0_ref, *outs, kept_ref, 0)
    slopes(u_ref, 2, tables, slope0_ref)
    shade(u_ref, 1, slope1_ref, *outs, kept_ref, 1)

    def pair(i, carry):
        x = 2 * i + 2
        slopes(u_ref, x + 1, tables, slope1_ref)
        shade(u_ref, x, slope0_ref, *outs)
        slopes(u_ref, x + 2, tables, slope0_ref)
        shade(u_ref, x + 1, slope1_ref, *outs)
        return carry

    lax.fori_loop(0, (nx - 4) // 2, pair, 0)
    slopes(u_ref, nx - 1, tables, slope1_ref)
    shade(u_ref, nx - 2, slope0_ref, *outs, kept_ref, 2)
    shade(u_ref, nx - 1, slope1_ref, *outs, kept_ref, 3)


def shaded(u, *rest):
    comps, nx, ny, nz = u.shape
    return pl.pallas_call(
        shade_kernel,
        out_shape=(
            jax.ShapeDtypeStruct((nx, ny, nz), jnp.float32),
            jax.ShapeDtypeStruct((comps, ny, nz), jnp.float32),
            jax.ShapeDtypeStruct((4, comps, ny, nz), jnp.float32),
            jax.ShapeDtypeStruct((nx // SUB, ny, nz), jnp.float32),
        ),
        in_specs=[VMEM] * 6,
        out_specs=(VMEM,) * 4,
        scratch_shapes=[
            pltpu.VMEM((nx // SUB, ny, nz), jnp.float32),
            pltpu.VMEM((comps, nx, 8, nz), jnp.float32),
            pltpu.VMEM((comps, nx, 8, nz), jnp.float32),
            pltpu.VMEM((2 * nz, nz), jnp.bfloat16),
            pltpu.VMEM((ny, 2 * ny), jnp.bfloat16),
            pltpu.VMEM((2, comps, ny, nz), jnp.float32),
            pltpu.VMEM((2, comps, ny, nz), jnp.float32),
        ],
        compiler_params=PARAMS,
        cost_estimate=COST,
    )(u, *rest)


def sides_deep(nx, ny, nz, zleft_ref, zright_ref):
    source, target = iota((2 * nz, nz), 0) % nz, iota((2 * nz, nz), 1)
    side, place, layer = source // (2 * nx), source % (2 * nx) // 2, source % 2
    where = jnp.where(place == target // 4, 4 * side + 2 * layer, -1000) + 10 * (target % 4)
    weights = jnp.zeros((2 * nz, nz), jnp.float32)
    for value, (s, l, t) in (
        (1.0, (0, 0, 2)),
        (-8.0, (0, 1, 2)),
        (1.0, (0, 1, 3)),
        (-1.0, (1, 0, 0)),
        (8.0, (1, 0, 1)),
        (-1.0, (1, 1, 1)),
    ):
        weights = jnp.where(where == 4 * s + 2 * l + 10 * t, value, weights)
    weights = weights.astype(jnp.bfloat16)
    first = iota((ny, nz), 1) < nz // 2
    left, right = zleft_ref[:ny], zright_ref[:ny]
    left2, right2 = zleft_ref[ny:], zright_ref[ny:]
    turned_left2, turned_right2 = pltpu.roll(left2, nz // 2, 1), pltpu.roll(right2, nz // 2, 1)
    ghosts = (
        jnp.where(first, left, pltpu.roll(right, nz // 2, 1)),
        jnp.where(first, pltpu.roll(left, nz // 2, 1), right),
        jnp.where(
            first,
            jnp.concatenate([left2, turned_left2], axis=0),
            jnp.concatenate([turned_right2, right2], axis=0),
        ),
    )
    return [
        jnp.dot(jnp.concatenate(split(ghost), axis=1), weights, preferred_element_type=jnp.float32) for ghost in ghosts
    ]


def on_border(packed, x, rows=None):
    ny, nz = packed.shape
    lane = iota((ny, nz), 1)
    return jnp.where((lane >= nz - 2) | (lane < 2), pltpu.roll(packed, lane_shift(x, nz, False), 1), 0.0)


def gather(density, raw, level_ref, sums_ref, sum_ref):
    level = jnp.clip(raw, 0.0, 1.0)
    level_ref[...] = level
    parts = jnp.concatenate(split((density / math.log(2.0)) * level), axis=1)
    sums_ref[...] = jnp.dot(parts, sum_ref[...], preferred_element_type=jnp.float32)


def blend(density, level_ref, sums_ref, store):
    ny, nz = level_ref.shape
    lane_group = iota((8, ny), 1) // 8
    eye = iota((8, ny), 1) % 8 == iota((8, ny), 0)
    totals = [jnp.zeros((8, ny), jnp.float32)] * 3
    for group in range(ny // 8):
        rows = pl.ds(8 * group, 8)
        level = level_ref[rows, :]
        first = (jnp.exp2(sums_ref[rows, pl.ds(0, nz)]) - jnp.exp2(sums_ref[rows, pl.ds(nz, nz)])) * level
        for k, cells in enumerate((first, first * level, level)):
            totals[k] = jnp.where(lane_group == group, jnp.sum(cells, axis=1, keepdims=True), totals[k])
    red, square, whole = [jnp.sum(jnp.where(eye, total, 0.0), axis=0, keepdims=True) for total in totals]
    through = jnp.exp2((-density / math.log(2.0)) * whole)
    store(red, 4.0 * (red - square), 1.0 - through - red, through)


def put(image_ref, x):
    per_view = image_ref.shape[2]
    view, row = (x // per_view, x % per_view) if isinstance(x, int) else (lax.div(x, per_view), lax.rem(x, per_view))

    def store(*channels):
        for k, values in enumerate(channels):
            image_ref[view, k, pl.ds(row, 1), :] = values

    return store


def summing(sum_ref):
    nz = sum_ref.shape[0] // 2
    row = iota((2 * nz, 2 * nz), 0) % nz
    col = iota((2 * nz, 2 * nz), 1)
    sum_ref[...] = jnp.where((row < col) & (col < nz) | (row <= col - nz), -1.0, 0.0).astype(jnp.bfloat16)


def blend_kernel(
    density, raw_ref, pack_ref, scale_ref, zleft_ref, zright_ref,
    image_ref, fix_ref, first_ref, sum_ref, level0_ref, level1_ref, sums0_ref, sums1_ref,
):
    nx, ny, nz = raw_ref.shape
    summing(sum_ref)
    ghosts = sides_deep(nx, ny, nz, zleft_ref, zright_ref)
    first_ref[...] = ghosts[0]
    fix = ghosts[2] * (0.5 * ghosts[2] + pack_ref[2]) + ghosts[0] * pack_ref[0] + ghosts[1] * pack_ref[1]
    per_block = 4 * SUB
    lane_block = iota((ny, nz), 1) // per_block
    scale = scale_ref[0]
    for block in range(1, nx // SUB):
        scale = jnp.where(lane_block == block, scale_ref[block], scale)
    fix_ref[...] = fix * scale
    image_ref[...] = jnp.zeros(image_ref.shape, jnp.float32)

    def load(x, level_ref, sums_ref):
        gather(density, raw_ref[x] + on_border(fix_ref[...], x), level_ref, sums_ref, sum_ref)

    load(2, level0_ref, sums0_ref)

    def pair(i, carry):
        x = 2 * i + 2
        load(x + 1, level1_ref, sums1_ref)
        blend(density, level0_ref, sums0_ref, put(image_ref, x))
        load(x + 2, level0_ref, sums0_ref)
        blend(density, level1_ref, sums1_ref, put(image_ref, x + 1))
        return carry

    lax.fori_loop(0, (nx - 4) // 2, pair, 0)


def row_tables(ny, nz):
    return [
        pltpu.VMEM((2 * nz, 2 * nz), jnp.bfloat16),
        pltpu.VMEM((ny, nz), jnp.float32),
        pltpu.VMEM((ny, nz), jnp.float32),
        pltpu.VMEM((ny, 2 * nz), jnp.float32),
        pltpu.VMEM((ny, 2 * nz), jnp.float32),
    ]


def blended(density, views, raw, *rest):
    nx, ny, nz = raw.shape
    return pl.pallas_call(
        functools.partial(blend_kernel, density),
        out_shape=(
            jax.ShapeDtypeStruct((views, 4, nx // views, ny), jnp.float32),
            jax.ShapeDtypeStruct((ny, nz), jnp.float32),
            jax.ShapeDtypeStruct((ny, nz), jnp.float32),
        ),
        in_specs=[VMEM] * 5,
        out_specs=(VMEM,) * 3,
        scratch_shapes=row_tables(ny, nz),
        compiler_params=PARAMS,
        cost_estimate=COST,
    )(raw, *rest)


def edge_kernel(
    density, middle_ref, raw_ref, kept_ref, scale_ref, fix_ref, first_ref, xleft_ref, xright_ref,
    image_ref, sum_ref, level0_ref, level1_ref, sums0_ref, sums1_ref,
):
    nx, ny, nz = raw_ref.shape
    summing(sum_ref)
    image_ref[...] = middle_ref[...]
    levels, sums = (level0_ref, level1_ref), (sums0_ref, sums1_ref)
    for place, x in enumerate(edge_rows(nx)):
        if place == 0:
            ghost = [xleft_ref[c, 0] - 8.0 * xleft_ref[c, 1] for c in range(3)]
        elif place == 1:
            ghost = [xleft_ref[c, 1] for c in range(3)]
        elif place == 2:
            ghost = [-xright_ref[c, 0] for c in range(3)]
        else:
            ghost = [8.0 * xright_ref[c, 0] - xright_ref[c, 1] for c in range(3)]
        depth = kept_ref[place, 2] + on_border(first_ref[...], x)
        more = ghost[0] * (0.5 * ghost[0] + kept_ref[place, 0]) + ghost[1] * kept_ref[place, 1] + ghost[2] * depth
        raw = raw_ref[x] + on_border(fix_ref[...], x) + more * scale_ref[x // SUB]
        gather(density, raw, levels[place % 2], sums[place % 2], sum_ref)
        blend(density, levels[place % 2], sums[place % 2], put(image_ref, x))


def edged(density, middle, raw, *rest):
    nx, ny, nz = raw.shape
    return pl.pallas_call(
        functools.partial(edge_kernel, density),
        out_shape=jax.ShapeDtypeStruct(middle.shape, jnp.float32),
        in_specs=[VMEM] * 8,
        out_specs=VMEM,
        scratch_shapes=row_tables(ny, nz),
        compiler_params=PARAMS,
        cost_estimate=COST,
    )(middle, raw, *rest)


def turn(block, axis, by):
    count = lax.axis_size(axis)
    return lax.ppermute(block, axis, [(i, (i + by) % count) for i in range(count)])


def both_sides(tail_head, axis):
    if lax.axis_size(axis) == 2:
        other = turn(tail_head, axis, 1)
        return other[0], other[1]
    return turn(tail_head[0], axis, 1), turn(tail_head[1], axis, -1)


def local(velocity, occupied, q_floor, q_span):
    comps, nx, ny, nz = velocity.shape
    views = lax.axis_size("view")
    density = 5.0 / (nz * views)
    u, xtail, xhead, yface, ztail, zhead = faces(velocity)
    xleft = turn(xtail, "gx", 1)
    xright = turn(xhead, "gx", -1)
    zleft = turn(ztail, "view", 1)
    zright = turn(zhead, "view", -1)
    yleft, yright = both_sides(yface, "gy")
    raw, pack, kept, scale = shaded(u, yleft, yright, occupied[:, :, 0], q_floor, q_span)
    middle, fix, first = blended(density, views, raw, pack, scale, zleft, zright)
    blocks = edged(density, middle, raw, kept, scale, fix, first, xleft, xright)
    images = lax.all_to_all(blocks, "view", 0, 0, tiled=True)
    colour, through = images[0, :3], images[0, 3:]
    for view in range(1, views):
        colour = colour + through * images[view, :3]
        through = through * images[view, 3:]
    finished = jnp.concatenate([colour, 1.0 - through], axis=0)
    return finished.reshape(1, 1, 4, nx // views, ny)


def solution(mesh):
    placed = (P(None, "gx", "gy", "view"), P("gx", "gy", "view"), P(), P())
    return jax.shard_map(
        local,
        mesh=mesh,
        in_specs=placed,
        out_specs=P("gx", "gy", None, "view", None),
        check_vma=False,
    )
```

time: 43.7 us -> 38.9 us (0.89)
  blocking collectives: 0 us -> 10.4 us
  waiting for transfers between devices: 7.87 us -> 1.21 us
  local copies, waits for them, and re-layouts: 4.59 us -> 0.02 us
  starting transfers between devices: 11.6 us -> 8.11 us
    all_to_all x0 -> x1, blocking collectives: none -> 10.4 us  [local(): images = lax.all_to_all(blocks, 'view', 0, 0, tiled=True)]
    ppermute x8 -> x5, waiting for transfers between devices: 7.87 us -> 1.21 us  [turn(): lax.ppermute(block, axis, [(i, (i + by) % count) for i in range(count)])]
    ppermute x8 -> x5, starting transfers between devices: 11.6 us -> 8.11 us  [turn(): lax.ppermute(block, axis, [(i, (i + by) % count) for i in range(count)])]
    unnamed x4 -> x2, local copies, waits for them, and re-layouts: 2.79 us -> 0.01 us
    slice x3 -> x0, local copies, waits for them, and re-layouts: 1.19 us -> none  [the longest x1 1.18 us: local(): xright = turn(velocity[:, :2], 'gx', -1)]
    pallas_call x3 -> x4, Pallas kernels: 17.2 us -> 16.9 us  [the longest x1 6.6 us: shaded(): pl.pallas_call(shade_kernel, out_shape=(jax.ShapeDtypeStruct((nx, ny, nz)...]
  transfers between devices with their start and end apart: 8 -> 5, of which waited for: 5 -> 1; matrix products, arithmetic and copies ran while one was open for 1% -> 0% of each run, Pallas kernels for 36% -> 30%
where the time goes in v3:
time: 38.9 us; the launch traced here: 38.7 us
  Pallas kernels  16.9 us (43%)
  blocking collectives  10.4 us (27%)
  starting transfers between devices  8.11 us (21%)
  between operations  1.38 us (4%)
  waiting for transfers between devices  1.21 us (3%)
  other arithmetic  0.63 us (2%)
    all_to_all x1, blocking collectives, local(): images = lax.all_to_all(blocks, 'view', 0, 0, tiled=True)  10.4 us
    ppermute x5, starting transfers between devices, turn(): lax.ppermute(block, axis, [(i, (i + by) % count) for i in range(count)])  8.11 us
    pallas_call x1, Pallas kernels, shaded(): pl.pallas_call(shade_kernel, out_shape=(jax.ShapeDtypeStruct((nx, ny, nz)...  6.6 us
    pallas_call x1, Pallas kernels, blended(): pl.pallas_call(functools.partial(blend_kernel, density), out_shape=(jax.S...  5.14 us
    pallas_call x1, Pallas kernels, faces(): pl.pallas_call(faces_kernel, out_shape=(shaped(*u.shape), shaped(comps, 2...  4.64 us
    ppermute x5, waiting for transfers between devices, turn(): lax.ppermute(block, axis, [(i, (i + by) % count) for i in range(count)])  1.21 us
  transfers between devices with their start and end apart: 5, of which 1 were waited for; matrix products, arithmetic and copies ran while one was open for 0% of the time, Pallas kernels for 30%

profile of v3, /device:TPU:0, one launch (start us, length us, event | category | flops | bytes accessed | tf_op | source)
XLA Modules:
  0.0 38.7 jit_solution(14686474437181206399)
XLA Ops:
  0.0 0.0 copy-start
  0.0 4.6 %shard_map.46 = (f32[3,32,128,128]{3,2,1,0:T(8,128)S(1)}, f32[3,2,128,128]{3,2,1,0:T(8,128)S(1)}, f32[3,2,128,128]{3,2,1,0:T(8,128)S(1)}, f32[2,3,64,128]{3,2,1,...) custom-call(f32[3,32,128,128]{3,2,1,0:T(8,128)} %u_hbm.1), custom_call_target="tpu_custom_call" | custom-call | flops 1048576 | bytes 1048576 | tf_op jit(solution)/shard_map/pallas_call | solution.py:115
  4.6 0.5 %collective-permute-start = (f32[2,3,64,128]{3,2,1,0:T(8,128)S(1)}, f32[2,3,64,128]{3,2,1,0:T(8,128)S(1)}, u32[]{:S(2)}, u32[]{:S(2)}) collective-permute-start(f32[2,3,64,128]{3,2,1,0:T(8,128)S(1)} %get-tuple-element.19), channel_id=1, source_target_pairs={{0,1},{1,0},{2,3},{3,2},{4,5},{5,4},{6,7},{7,6},{8,9},{9,8},{10,11... | collective-permute-start | bytes 589832 | tf_op jit(solution)/shard_map/ppermute | solution.py:461
  5.2 2.6 %collective-permute-start.3 = (f32[3,2,128,128]{3,2,1,0:T(8,128)S(1)}, f32[3,2,128,128]{3,2,1,0:T(8,128)S(1)}, u32[]{:S(2)}, u32[]{:S(2)}) collective-permute-start(f32[3,2,128,128]{3,2,1,0:T(8,128)S(1)} %get-tuple-element.29), channel_id=1, source_target_pairs={{0,2},{2,4},{4,6},{6,0},{1,3},{3,5},{5,7},{7,1},{8,10},{10,12},{12... | collective-permute-start | bytes 1179656 | tf_op jit(solution)/shard_map/ppermute | solution.py:461
  7.7 1.0 %collective-permute-start.4 = (f32[3,2,128,128]{3,2,1,0:T(8,128)S(1)}, f32[3,2,128,128]{3,2,1,0:T(8,128)S(1)}, u32[]{:S(2)}, u32[]{:S(2)}) collective-permute-start(f32[3,2,128,128]{3,2,1,0:T(8,128)S(1)} %get-tuple-element.30), channel_id=1, source_target_pairs={{0,6},{2,0},{4,2},{6,4},{1,7},{3,1},{5,3},{7,5},{8,14},{10,8},{12,... | collective-permute-start | bytes 1179656 | tf_op jit(solution)/shard_map/ppermute | solution.py:461
  8.8 2.0 %collective-permute-start.1 = (f32[192,128]{1,0:T(8,128)S(1)}, f32[192,128]{1,0:T(8,128)S(1)}, u32[]{:S(2)}, u32[]{:S(2)}) collective-permute-start(f32[192,128]{1,0:T(8,128)S(1)} %get-tuple-element.23), channel_id=1, source_target_pairs={{0,8},{8,16},{16,24},{24,0},{1,9},{9,17},{17,25},{25,1},{2,10},{10... | collective-permute-start | bytes 294920 | tf_op jit(solution)/shard_map/ppermute | solution.py:461
  10.7 2.0 %collective-permute-start.2 = (f32[192,128]{1,0:T(8,128)S(1)}, f32[192,128]{1,0:T(8,128)S(1)}, u32[]{:S(2)}, u32[]{:S(2)}) collective-permute-start(f32[192,128]{1,0:T(8,128)S(1)} %get-tuple-element.24), channel_id=1, source_target_pairs={{0,24},{8,0},{16,8},{24,16},{1,25},{9,1},{17,9},{25,17},{2,26},{10... | collective-permute-start | bytes 294920 | tf_op jit(solution)/shard_map/ppermute | solution.py:461
  14.1 0.0 collective-permute-done
  14.1 0.0 copy-done
  14.1 6.6 %shard_map.47 = (f32[32,128,128]{2,1,0:T(8,128)S(1)}, f32[3,128,128]{2,1,0:T(8,128)S(1)}, f32[4,3,128,128]{3,2,1,0:T(8,128)S(1)}, f32[4,128,128]{2,1,0:T(8,128)S(1)}) custom-call(f32[3,32,128,128]{3,2,1,0:T(8,128)S(1)} %get-tuple-element.18.u_ref, f32[3,64,128]{2,1,0:T(8,128)S(1)} %get-tuple-element.34.yleft_ref, ...), custom_call_target="tpu_custom_call" | custom-call | flops 1048576 | bytes 1048576 | tf_op jit(solution)/shard_map/pallas_call | solution.py:258
  20.7 0.0 collective-permute-done.1.zleft_ref
  20.7 0.0 collective-permute-done.2.zright_ref
  20.7 5.1 %shard_map.48 = (f32[4,4,8,128]{3,2,1,0:T(8,128)S(1)}, f32[128,128]{1,0:T(8,128)S(1)}, f32[128,128]{1,0:T(8,128)S(1)}) custom-call(f32[32,128,128]{2,1,0:T(8,128)S(1)} %get-tuple-element.20.raw_ref, f32[3,128,128]{2,1,0:T(8,128)S(1)} %get-tuple-element.21.pack_ref, f32[4,128,128]{2,1,0:T(8,128)S(1)} %get-tuple-element.22.scale_ref, ...), custom_call_target="tpu_custom_call" | custom-call | flops 1048576 | bytes 1048576 | tf_op jit(solution)/shard_map/pallas_call | solution.py:407
  25.9 0.0 collective-permute-done.3.xleft_ref
  25.9 1.2 %collective-permute-done.4.xright_ref = f32[3,2,128,128]{3,2,1,0:T(8,128)S(1)} collective-permute-done((f32[3,2,128,128]{3,2,1,0:T(8,128)S(1)}, f32[3,2,128,128]{3,2,1,0:T(8,128)S(1)}, u32[]{:S(2)}, u32[]{:S(2)}) %collective-permute-start.4) | collective-permute-done | bytes 393248 | tf_op jit(solution)/shard_map/ppermute | solution.py:461
  27.1 0.6 %shard_map.49 = f32[4,4,8,128]{3,2,1,0:T(8,128)S(1)} custom-call(f32[4,4,8,128]{3,2,1,0:T(8,128)S(1)} %get-tuple-element.25.middle_ref, f32[32,128,128]{2,1,0:T(8,128)S(1)} %get-tuple-element.20.raw_ref, f32[4,3,128,128]{3,2,1,0:T(8,128)S(1)} %get-tuple-element.26.kept_ref, f32[4,128,128]{2,1,0:T(8,128)S(1)} %get-tuple-element.22.scale_ref, ...), custom_call_target="tpu_custom_call" | custom-call | flops 1048576 | bytes 1048576 | tf_op jit(solution)/shard_map/pallas_call | solution.py:448
  27.6 10.4 %all_to_all.5 = f32[4,4,8,128]{3,2,1,0:T(8,128)S(1)} all-to-all(f32[4,4,8,128]{3,2,1,0:T(8,128)S(1)} %shard_map.49), channel_id=1, replica_groups=mesh['view'=4,'gx'=4,'gy'=2] {'view'}, dimensions={0} | all-to-all | bytes 131072 | tf_op jit(solution)/shard_map/all_to_all | solution.py:484
  38.1 0.6 %maximum_bitcast_fusion = f32[1,1,4,8,128]{4,3,2,1,0:T(8,128)} fusion(f32[1,8,128]{2,1,0:T(8,128)S(1)} %get-tuple-element.36, f32[3,8,128]{2,1,0:T(8,128)S(1)} %fusion.1), kind=kLoop, calls=%fused_computation.2 | loop fusion | flops 4096 | bytes 32768 | tf_op jit(solution)/shard_map/reshape | solution.py:490
  (4 shorter events, 0.0 us)
Async XLA Ops:
  0.0 14.1 %copy-start = (s32[4,16,1]{1,2,0:T(1,128)S(1)}, s32[4,16,1]{1,2,0:T(1,128)}, u32[]{:S(2)}) copy-start(s32[4,16,1]{1,2,0:T(1,128)} %param.5) | copy-start | bytes 772
  4.6 9.4 %collective-permute-start = (f32[2,3,64,128]{3,2,1,0:T(8,128)S(1)}, f32[2,3,64,128]{3,2,1,0:T(8,128)S(1)}, u32[]{:S(2)}, u32[]{:S(2)}) collective-permute-start(f32[2,3,64,128]{3,2,1,0:T(8,128)S(1)} %get-tuple-element.19), channel_id=1, source_target_pairs={{0,1},{1,0},{2,3},{3,2},{4,5},{5,4},{6,7},{7,6},{8,9},{9,8},{10,11... | collective-permute-start | bytes 589832 | tf_op jit(solution)/shard_map/ppermute | solution.py:461
  5.2 20.7 %collective-permute-start.3 = (f32[3,2,128,128]{3,2,1,0:T(8,128)S(1)}, f32[3,2,128,128]{3,2,1,0:T(8,128)S(1)}, u32[]{:S(2)}, u32[]{:S(2)}) collective-permute-start(f32[3,2,128,128]{3,2,1,0:T(8,128)S(1)} %get-tuple-element.29), channel_id=1, source_target_pairs={{0,2},{2,4},{4,6},{6,0},{1,3},{3,5},{5,7},{7,1},{8,10},{10,12},{12... | collective-permute-start | bytes 1179656 | tf_op jit(solution)/shard_map/ppermute | solution.py:461
  7.7 19.4 %collective-permute-start.4 = (f32[3,2,128,128]{3,2,1,0:T(8,128)S(1)}, f32[3,2,128,128]{3,2,1,0:T(8,128)S(1)}, u32[]{:S(2)}, u32[]{:S(2)}) collective-permute-start(f32[3,2,128,128]{3,2,1,0:T(8,128)S(1)} %get-tuple-element.30), channel_id=1, source_target_pairs={{0,6},{2,0},{4,2},{6,4},{1,7},{3,1},{5,3},{7,5},{8,14},{10,8},{12,... | collective-permute-start | bytes 1179656 | tf_op jit(solution)/shard_map/ppermute | solution.py:461
  8.8 11.9 %collective-permute-start.1 = (f32[192,128]{1,0:T(8,128)S(1)}, f32[192,128]{1,0:T(8,128)S(1)}, u32[]{:S(2)}, u32[]{:S(2)}) collective-permute-start(f32[192,128]{1,0:T(8,128)S(1)} %get-tuple-element.23), channel_id=1, source_target_pairs={{0,8},{8,16},{16,24},{24,0},{1,9},{9,17},{17,25},{25,1},{2,10},{10... | collective-permute-start | bytes 294920 | tf_op jit(solution)/shard_map/ppermute | solution.py:461
  10.7 10.0 %collective-permute-start.2 = (f32[192,128]{1,0:T(8,128)S(1)}, f32[192,128]{1,0:T(8,128)S(1)}, u32[]{:S(2)}, u32[]{:S(2)}) collective-permute-start(f32[192,128]{1,0:T(8,128)S(1)} %get-tuple-element.24), channel_id=1, source_target_pairs={{0,24},{8,0},{16,8},{24,16},{1,25},{9,1},{17,9},{25,17},{2,26},{10... | collective-permute-start | bytes 294920 | tf_op jit(solution)/shard_map/ppermute | solution.py:461

commit v4 on v3

v4 whole, which is shorter than its diff:
```python
import functools
import math

import jax
import jax.numpy as jnp
from jax import lax
from jax.experimental import pallas as pl
from jax.experimental.pallas import tpu as pltpu
from jax.sharding import PartitionSpec as P

SUB = 8
ROWS = 32
VMEM = pl.BlockSpec(memory_space=pltpu.VMEM)
HBM = pl.BlockSpec(memory_space=pltpu.HBM)
COST = pl.CostEstimate(flops=1 << 20, bytes_accessed=1 << 20, transcendentals=0)
PARAMS = pltpu.CompilerParams(vmem_limit_bytes=24 << 20)


def split(values):
    high = values.astype(jnp.bfloat16)
    low = (values - high.astype(jnp.float32)).astype(jnp.bfloat16)
    return high, low


def iota(shape, dim):
    return lax.broadcasted_iota(jnp.int32, shape, dim)


def ends_kernel(u_hbm, xtail_ref, xhead_ref, yface_ref, sems):
    _, nx, ny, _ = u_hbm.shape
    pieces = (
        (u_hbm.at[:, pl.ds(nx - 2, 2)], xtail_ref),
        (u_hbm.at[:, pl.ds(0, 2)], xhead_ref),
        (u_hbm.at[:, :, pl.ds(ny - 8, 8)], yface_ref.at[0]),
        (u_hbm.at[:, :, pl.ds(0, 8)], yface_ref.at[1]),
    )
    copies = [pltpu.make_async_copy(source, target, sems.at[k]) for k, (source, target) in enumerate(pieces)]
    for copy in copies:
        copy.start()
    for copy in copies:
        copy.wait()


def ends(u):
    comps, nx, ny, nz = u.shape
    layers = jax.ShapeDtypeStruct((comps, 2, ny, nz), jnp.float32)
    return pl.pallas_call(
        ends_kernel,
        out_shape=(layers, layers, jax.ShapeDtypeStruct((2, comps, nx, 8, nz), jnp.float32)),
        in_specs=[HBM],
        out_specs=(VMEM,) * 3,
        scratch_shapes=[pltpu.SemaphoreType.DMA((4,))],
        compiler_params=pltpu.CompilerParams(vmem_limit_bytes=50 << 20),
        cost_estimate=COST,
    )(u)


def faces_kernel(u_hbm, u_ref, parts_ref, tail_ref, head_ref, sems):
    comps, nx, ny, nz = u_ref.shape
    quarters = sems.shape[1]
    rows = ny // quarters

    def fetch(c, k):
        span = pl.ds(k * rows if isinstance(k, int) else pl.multiple_of(k * rows, rows), rows)
        return pltpu.make_async_copy(u_hbm.at[c, :, span], u_ref.at[c, :, span], sems.at[c, k])

    for k in range(quarters):
        for c in (0, 1):
            fetch(c, k).start()
    for k in range(quarters):
        fetch(2, k).start()
    pair = iota((8, nz), 1) // 2

    def pack(members, y, out, first):
        out_rows = pl.ds(out, 8)
        tail = jnp.zeros((8, nz), jnp.float32)
        head = jnp.zeros((8, nz), jnp.float32)
        for c, base in members:
            for x in range(nx):
                place = base // 2 + x
                moved = pltpu.roll(u_ref[c, x, pl.ds(y, 8), :], (base + 2 * x + 2) % nz, 1)
                tail = jnp.where(pair == place, moved, tail)
                head = jnp.where(pair == (place + 1) % (nz // 2), moved, head)
        head = pltpu.roll(head, nz - 2, 1)
        if first:
            tail_ref[out_rows, :] = tail
            head_ref[out_rows, :] = head
        else:
            half = pair < nz // 4
            tail_ref[out_rows, :] = jnp.where(half, tail_ref[out_rows, :], tail)
            head_ref[out_rows, :] = jnp.where(half, head_ref[out_rows, :], head)

    def parted(c, k):
        span = pl.ds(pl.multiple_of(k * rows, rows), rows)
        for x in range(nx):
            high, low = split(u_ref[c, x, span, :])
            parts_ref[c, x, span, pl.ds(0, nz)] = high
            parts_ref[c, x, span, pl.ds(nz, nz)] = low

    def both(k, carry):
        fetch(0, k).wait()
        fetch(1, k).wait()
        parted(0, k)
        parted(1, k)
        for part in range(rows // 8):
            y = pl.multiple_of(k * rows + part * 8, 8)
            pack(((0, 0), (1, nz // 2)), y, y, True)
        return carry

    lax.fori_loop(0, quarters, both, 0)

    def last(base, offset, first):
        def step(k, carry):
            fetch(2, k).wait()
            parted(2, k)
            for part in range(rows // 8):
                y = pl.multiple_of(k * rows + part * 8, 8)
                pack(((2, base),), y, pl.multiple_of(y + offset, 8), first)
            return carry

        return step

    lax.fori_loop(0, quarters // 2, last(0, ny, True), 0)
    lax.fori_loop(quarters // 2, quarters, last(nz // 2, ny // 2, False), 0)


def faces(u):
    comps, nx, ny, nz = u.shape

    def shaped(*shape):
        return jax.ShapeDtypeStruct(shape, jnp.float32)

    return pl.pallas_call(
        faces_kernel,
        out_shape=(
            shaped(*u.shape),
            jax.ShapeDtypeStruct((comps, nx, ny, 2 * nz), jnp.bfloat16),
            shaped(ny + ny // 2, nz),
            shaped(ny + ny // 2, nz),
        ),
        in_specs=[HBM],
        out_specs=(VMEM,) * 4,
        scratch_shapes=[
            pltpu.SemaphoreType.DMA((comps, 4)),
        ],
        compiler_params=pltpu.CompilerParams(vmem_limit_bytes=37 << 20),
        cost_estimate=COST,
    )(u)


def stencil(far):
    one = jnp.where(far == 1, 8.0, 0.0) - jnp.where(far == -1, 8.0, 0.0)
    return (one - jnp.where(far == 2, 1.0, 0.0) + jnp.where(far == -2, 1.0, 0.0)).astype(jnp.bfloat16)


def shading(occupied_ref, floor, span, scale_ref, offset_ref):
    blocks, ny, nz = scale_ref.shape
    groups = ny // SUB
    mine = iota((ny, groups), 0) // SUB == iota((ny, groups), 1)
    shrink = 1.0 / span
    for block in range(blocks):
        row = occupied_ref[block : block + 1, :].astype(jnp.float32)
        column = jnp.sum(jnp.where(mine, row, 0.0), axis=1, keepdims=True)
        scale_ref[block] = jnp.broadcast_to(column * (shrink * (-1.0 / 144.0)), (ny, nz))
        offset_ref[block] = jnp.broadcast_to(column * (shrink * -floor), (ny, nz))


def lane_shift(x, nz, back):
    if isinstance(x, int):
        return (4 * x + 2 if back else 2 * nz - 2 - 4 * x) % nz
    return lax.rem(4 * x + 2 if back else 2 * nz - 2 - 4 * x, nz)


def slopes(parts_ref, x, tables, slope_ref):
    yleft_ref, yright_ref, dz_ref, dy_ref = tables
    comps, ny, nz = slope_ref.shape[2:]
    sub = iota((8, nz), 0)

    def top(left):
        return jnp.where(sub < 2, pltpu.roll(left, 2, 0) - jnp.where(sub == 0, 8.0 * pltpu.roll(left, 1, 0), 0.0), 0.0)

    def low(right):
        far = pltpu.roll(right, 6, 0)
        return jnp.where(sub >= 6, jnp.where(sub == 7, 8.0 * pltpu.roll(right, 7, 0), 0.0) - far, 0.0)

    parts = [[parts_ref[c, x + k] for k in range(2)] for c in range(comps)]
    depth = jnp.dot(
        jnp.concatenate([part for pair in parts for part in pair], axis=0),
        dz_ref[...],
        preferred_element_type=jnp.float32,
    )
    for c in range(comps):
        both = jnp.concatenate(
            [jnp.concatenate([part[:, half : half + nz] for part in parts[c]], axis=1) for half in (0, nz)], axis=0
        )
        down = jnp.dot(dy_ref[...], both, preferred_element_type=jnp.float32)
        for k in range(2):
            slope_ref[1, k, c] = depth[(2 * c + k) * ny : (2 * c + k + 1) * ny]
            mine = down[:, k * nz : (k + 1) * nz]
            slope_ref[0, k, c, pl.ds(0, 8), :] = mine[:8] + top(yleft_ref[c, x + k])
            slope_ref[0, k, c, pl.ds(8, ny - 16), :] = mine[8 : ny - 8]
            slope_ref[0, k, c, pl.ds(ny - 8, 8), :] = mine[ny - 8 :] + low(yright_ref[c, x + k])


def shade(u_ref, x, slope_ref, scale_ref, offset_ref, raw_ref, pack_ref, kept_ref=None, place=None):
    comps, nx, ny, nz = u_ref.shape
    block = x // SUB

    def difference(high, low):
        if high is None:
            return 0.0 if low is None else -low
        return high if low is None else high - low

    for y in range(0, ny, ROWS):
        rows = pl.ds(y, ROWS)
        slots = iota((ROWS, nz), 1) // 4
        across = []
        for c in range(comps):
            near = [
                u_ref[c, x + d, rows, :] if not isinstance(x, int) or 0 <= x + d < nx else None for d in range(-2, 4)
            ]
            across.append(
                [8.0 * difference(near[k + 3], near[k + 1]) - difference(near[k + 4], near[k]) for k in range(2)]
            )
        packs = [pack_ref[k, rows, :] for k in range(3)]
        for k in range(2):
            side = [across[c][k] for c in range(comps)]
            down = [slope_ref[0, k, c, rows, :] for c in range(comps)]
            depth = [slope_ref[1, k, c, rows, :] for c in range(comps)]
            total = 0.5 * (side[0] * side[0] + down[1] * down[1] + depth[2] * depth[2])
            total = total + side[1] * down[0] + side[2] * depth[0] + down[2] * depth[1]
            raw_ref[x + k, rows, :] = total * scale_ref[block, rows, :] + offset_ref[block, rows, :]
            back = lane_shift(x + k, nz, True)
            packs = [
                jnp.where(slots == x + k, pltpu.roll(values, back, 1), pack)
                for values, pack in zip((side[2], down[2], depth[2]), packs)
            ]
            if kept_ref is not None:
                for n, values in enumerate((side[0], down[0], depth[0])):
                    kept_ref[place + k, n, rows, :] = values
        for k in range(3):
            pack_ref[k, rows, :] = packs[k]


def edge_rows(nx):
    return (0, 1, nx - 2, nx - 1)


def shade_kernel(
    u_ref, parts_ref, yleft_ref, yright_ref, occupied_ref, floor_ref, span_ref,
    raw_ref, pack_ref, kept_ref, scale_ref, offset_ref, dz_ref, dy_ref, slope0_ref, slope1_ref,
):
    comps, nx, ny, nz = u_ref.shape
    dz_ref[...] = stencil(iota((2 * nz, nz), 0) % nz - iota((2 * nz, nz), 1))
    dy_ref[...] = stencil(iota((ny, 2 * ny), 1) % ny - iota((ny, 2 * ny), 0))
    shading(occupied_ref, floor_ref[...].reshape(1, 1), span_ref[...].reshape(1, 1), scale_ref, offset_ref)
    pack_ref[...] = jnp.zeros(pack_ref.shape, jnp.float32)
    tables = (yleft_ref, yright_ref, dz_ref, dy_ref)
    outs = (scale_ref, offset_ref, raw_ref, pack_ref)
    slopes(parts_ref, 0, tables, slope0_ref)
    slopes(parts_ref, 2, tables, slope1_ref)
    shade(u_ref, 0, slope0_ref, *outs, kept_ref, 0)

    def pairs(i, carry):
        x = 4 * i + 2
        slopes(parts_ref, x + 2, tables, slope0_ref)
        shade(u_ref, x, slope1_ref, *outs)
        slopes(parts_ref, x + 4, tables, slope1_ref)
        shade(u_ref, x + 2, slope0_ref, *outs)
        return carry

    lax.fori_loop(0, (nx - 4) // 4, pairs, 0)
    shade(u_ref, nx - 2, slope1_ref, *outs, kept_ref, 2)


def shaded(u, *rest):
    comps, nx, ny, nz = u.shape
    return pl.pallas_call(
        shade_kernel,
        out_shape=(
            jax.ShapeDtypeStruct((nx, ny, nz), jnp.float32),
            jax.ShapeDtypeStruct((comps, ny, nz), jnp.float32),
            jax.ShapeDtypeStruct((4, comps, ny, nz), jnp.float32),
            jax.ShapeDtypeStruct((nx // SUB, ny, nz), jnp.float32),
        ),
        in_specs=[VMEM] * 7,
        out_specs=(VMEM,) * 4,
        scratch_shapes=[
            pltpu.VMEM((nx // SUB, ny, nz), jnp.float32),
            pltpu.VMEM((2 * nz, nz), jnp.bfloat16),
            pltpu.VMEM((ny, 2 * ny), jnp.bfloat16),
            pltpu.VMEM((2, 2, comps, ny, nz), jnp.float32),
            pltpu.VMEM((2, 2, comps, ny, nz), jnp.float32),
        ],
        compiler_params=PARAMS,
        cost_estimate=COST,
    )(u, *rest)


def sides_deep(nx, ny, nz, zleft_ref, zright_ref):
    source, target = iota((2 * nz, nz), 0) % nz, iota((2 * nz, nz), 1)
    side, place, layer = source // (2 * nx), source % (2 * nx) // 2, source % 2
    where = jnp.where(place == target // 4, 4 * side + 2 * layer, -1000) + 10 * (target % 4)
    weights = jnp.zeros((2 * nz, nz), jnp.float32)
    for value, (s, l, t) in (
        (1.0, (0, 0, 2)),
        (-8.0, (0, 1, 2)),
        (1.0, (0, 1, 3)),
        (-1.0, (1, 0, 0)),
        (8.0, (1, 0, 1)),
        (-1.0, (1, 1, 1)),
    ):
        weights = jnp.where(where == 4 * s + 2 * l + 10 * t, value, weights)
    weights = weights.astype(jnp.bfloat16)
    first = iota((ny, nz), 1) < nz // 2
    left, right = zleft_ref[:ny], zright_ref[:ny]
    left2, right2 = zleft_ref[ny:], zright_ref[ny:]
    turned_left2, turned_right2 = pltpu.roll(left2, nz // 2, 1), pltpu.roll(right2, nz // 2, 1)
    ghosts = (
        jnp.where(first, left, pltpu.roll(right, nz // 2, 1)),
        jnp.where(first, pltpu.roll(left, nz // 2, 1), right),
        jnp.where(
            first,
            jnp.concatenate([left2, turned_left2], axis=0),
            jnp.concatenate([turned_right2, right2], axis=0),
        ),
    )
    return [
        jnp.dot(jnp.concatenate(split(ghost), axis=1), weights, preferred_element_type=jnp.float32) for ghost in ghosts
    ]


def on_border(packed, x, rows=None):
    ny, nz = packed.shape
    lane = iota((ny, nz), 1)
    return jnp.where((lane >= nz - 2) | (lane < 2), pltpu.roll(packed, lane_shift(x, nz, False), 1), 0.0)


def gather(density, raws, level_ref, sums_ref, sum_ref):
    parts = []
    for k, raw in enumerate(raws):
        level = jnp.clip(raw, 0.0, 1.0)
        level_ref[k] = level
        parts.append(jnp.concatenate(split((density / math.log(2.0)) * level), axis=1))
    ny, nz = level_ref.shape[1:]
    sums = jnp.dot(jnp.concatenate(parts, axis=0), sum_ref[...], preferred_element_type=jnp.float32)
    for k in range(len(raws)):
        sums_ref[k] = sums[k * ny : (k + 1) * ny]


def blend(level_ref, sums_ref, k, store):
    ny, nz = level_ref.shape[1:]
    lane_group = iota((8, ny), 1) // 8
    eye = iota((8, ny), 1) % 8 == iota((8, ny), 0)
    totals = [jnp.zeros((8, ny), jnp.float32)] * 3
    for group in range(ny // 8):
        rows = pl.ds(8 * group, 8)
        level = level_ref[k, rows, :]
        passing = jnp.exp2(sums_ref[k, rows, pl.ds(0, nz)])
        first = (passing - jnp.exp2(sums_ref[k, rows, pl.ds(nz, nz)])) * level
        red = jnp.sum(first, axis=1, keepdims=True)
        square = jnp.sum(first * level, axis=1, keepdims=True)
        whole = sums_ref[k, rows, pl.ds(2 * nz, ny)]
        totals = [jnp.where(lane_group == group, part, total) for part, total in zip((red, square, whole), totals)]
    red, square, whole = [jnp.sum(jnp.where(eye, total, 0.0), axis=0, keepdims=True) for total in totals]
    through = jnp.exp2(whole)
    store(red, 4.0 * (red - square), 1.0 - through - red, through)


def put(image_ref, x):
    per_view = image_ref.shape[2]
    view, row = (x // per_view, x % per_view) if isinstance(x, int) else (lax.div(x, per_view), lax.rem(x, per_view))

    def store(*channels):
        for k, values in enumerate(channels):
            image_ref[view, k, pl.ds(row, 1), :] = values

    return store


def summing(sum_ref):
    nz = sum_ref.shape[0] // 2
    row = iota(sum_ref.shape, 0) % nz
    col = iota(sum_ref.shape, 1)
    sum_ref[...] = jnp.where((row < col) & (col < nz) | (row <= col - nz), -1.0, 0.0).astype(jnp.bfloat16)


def blend_kernel(
    density, raw_ref, pack_ref, scale_ref, zleft_ref, zright_ref,
    image_ref, fix_ref, first_ref, sum_ref, level0_ref, level1_ref, sums0_ref, sums1_ref,
):
    nx, ny, nz = raw_ref.shape
    summing(sum_ref)
    ghosts = sides_deep(nx, ny, nz, zleft_ref, zright_ref)
    first_ref[...] = ghosts[0]
    fix = ghosts[2] * (0.5 * ghosts[2] + pack_ref[2]) + ghosts[0] * pack_ref[0] + ghosts[1] * pack_ref[1]
    per_block = 4 * SUB
    lane_block = iota((ny, nz), 1) // per_block
    scale = scale_ref[0]
    for block in range(1, nx // SUB):
        scale = jnp.where(lane_block == block, scale_ref[block], scale)
    fix_ref[...] = fix * scale
    image_ref[...] = jnp.zeros(image_ref.shape, jnp.float32)
    batch = level0_ref.shape[0]

    def load(x, level_ref, sums_ref):
        raws = [raw_ref[x + k] + on_border(fix_ref[...], x + k) for k in range(batch)]
        gather(density, raws, level_ref, sums_ref, sum_ref)

    def mix(x, level_ref, sums_ref):
        for k in range(batch):
            blend(level_ref, sums_ref, k, put(image_ref, x + k))

    load(2, level0_ref, sums0_ref)

    def batches(i, carry):
        x = 2 * batch * i + 2
        load(x + batch, level1_ref, sums1_ref)
        mix(x, level0_ref, sums0_ref)
        load(x + 2 * batch, level0_ref, sums0_ref)
        mix(x + batch, level1_ref, sums1_ref)
        return carry

    count = (nx - 4) // batch
    lax.fori_loop(0, (count - 1) // 2, batches, 0)
    if count % 2 == 0:
        load(nx - 2 - batch, level1_ref, sums1_ref)
        mix(nx - 2 - 2 * batch, level0_ref, sums0_ref)
        mix(nx - 2 - batch, level1_ref, sums1_ref)
    else:
        mix(nx - 2 - batch, level0_ref, sums0_ref)


def row_tables(batch, ny, nz, buffers):
    return (
        [pltpu.VMEM((2 * nz, 2 * nz + ny), jnp.bfloat16)]
        + [pltpu.VMEM((batch, ny, nz), jnp.float32)] * buffers
        + [pltpu.VMEM((batch, ny, 2 * nz + ny), jnp.float32)] * buffers
    )


def blended(density, views, raw, *rest):
    nx, ny, nz = raw.shape
    return pl.pallas_call(
        functools.partial(blend_kernel, density),
        out_shape=(
            jax.ShapeDtypeStruct((views, 4, nx // views, ny), jnp.float32),
            jax.ShapeDtypeStruct((ny, nz), jnp.float32),
            jax.ShapeDtypeStruct((ny, nz), jnp.float32),
        ),
        in_specs=[VMEM] * 5,
        out_specs=(VMEM,) * 3,
        scratch_shapes=row_tables(4, ny, nz, 2),
        compiler_params=PARAMS,
        cost_estimate=COST,
    )(raw, *rest)


def edge_kernel(
    density, middle_ref, raw_ref, kept_ref, scale_ref, fix_ref, first_ref, xleft_ref, xright_ref,
    image_ref, sum_ref, level_ref, sums_ref,
):
    nx, ny, nz = raw_ref.shape
    summing(sum_ref)
    image_ref[...] = middle_ref[...]
    raws = []
    for place, x in enumerate(edge_rows(nx)):
        if place == 0:
            ghost = [xleft_ref[c, 0] - 8.0 * xleft_ref[c, 1] for c in range(3)]
        elif place == 1:
            ghost = [xleft_ref[c, 1] for c in range(3)]
        elif place == 2:
            ghost = [-xright_ref[c, 0] for c in range(3)]
        else:
            ghost = [8.0 * xright_ref[c, 0] - xright_ref[c, 1] for c in range(3)]
        depth = kept_ref[place, 2] + on_border(first_ref[...], x)
        more = ghost[0] * (0.5 * ghost[0] + kept_ref[place, 0]) + ghost[1] * kept_ref[place, 1] + ghost[2] * depth
        raws.append(raw_ref[x] + on_border(fix_ref[...], x) + more * scale_ref[x // SUB])
    gather(density, raws, level_ref, sums_ref, sum_ref)
    for place, x in enumerate(edge_rows(nx)):
        blend(level_ref, sums_ref, place, put(image_ref, x))


def edged(density, middle, raw, *rest):
    nx, ny, nz = raw.shape
    return pl.pallas_call(
        functools.partial(edge_kernel, density),
        out_shape=jax.ShapeDtypeStruct(middle.shape, jnp.float32),
        in_specs=[VMEM] * 8,
        out_specs=VMEM,
        scratch_shapes=row_tables(4, ny, nz, 1),
        compiler_params=PARAMS,
        cost_estimate=COST,
    )(middle, raw, *rest)


def turn(block, axis, by):
    count = lax.axis_size(axis)
    return lax.ppermute(block, axis, [(i, (i + by) % count) for i in range(count)])


def both_sides(tail_head, axis):
    if lax.axis_size(axis) == 2:
        other = turn(tail_head, axis, 1)
        return other[0], other[1]
    return turn(tail_head[0], axis, 1), turn(tail_head[1], axis, -1)


def exchanged(blocks, axis):
    count = lax.axis_size(axis)
    me = lax.axis_index(axis)
    paired = count & (count - 1) == 0
    found = [(me, lax.dynamic_index_in_dim(blocks, me, 0, keepdims=False))]
    for step in range(count - 1, 0, -1):
        if paired:
            to = source = me ^ step
            route = [(i, i ^ step) for i in range(count)]
        else:
            to, source = (me + step) % count, (me - step) % count
            route = [(i, (i + step) % count) for i in range(count)]
        sent = lax.dynamic_index_in_dim(blocks, to, 0, keepdims=False)
        found.append((source, lax.ppermute(sent, axis, route)))
    return found


def local(velocity, occupied, q_floor, q_span):
    comps, nx, ny, nz = velocity.shape
    views = lax.axis_size("view")
    density = 5.0 / (nz * views)
    xtail, xhead, yface = ends(velocity)
    xleft = turn(xtail, "gx", 1)
    xright = turn(xhead, "gx", -1)
    u, parts, ztail, zhead = faces(velocity)
    zleft = turn(ztail, "view", 1)
    zright = turn(zhead, "view", -1)
    yleft, yright = both_sides(yface, "gy")
    raw, pack, kept, scale = shaded(u, parts, yleft, yright, occupied[:, :, 0], q_floor, q_span)
    middle, fix, first = blended(density, views, raw, pack, scale, zleft, zright)
    blocks = edged(density, middle, raw, kept, scale, fix, first, xleft, xright)
    images = exchanged(blocks, "view")
    colour = jnp.zeros((3, nx // views, ny), jnp.float32)
    through = jnp.ones((nx // views, ny), jnp.float32)
    for source, image in images:
        passing = jnp.ones((nx // views, ny), jnp.float32)
        for other, front in images:
            passing = passing * jnp.where(other < source, front[3], 1.0)
        colour = colour + passing * image[:3]
        through = through * image[3]
    finished = jnp.concatenate([colour, 1.0 - through[None]], axis=0)
    return finished.reshape(1, 1, 4, nx // views, ny)


def solution(mesh):
    placed = (P(None, "gx", "gy", "view"), P("gx", "gy", "view"), P(), P())
    return jax.shard_map(
        local,
        mesh=mesh,
        in_specs=placed,
        out_specs=P("gx", "gy", None, "view", None),
        check_vma=False,
    )
```

time: 38.9 us -> 42.5 us (1.093)
  local copies, waits for them, and re-layouts: 0.02 us -> 10.9 us
  blocking collectives: 10.4 us -> 0 us
  starting transfers between devices: 8.11 us -> 12.6 us
  Pallas kernels: 16.9 us -> 14.5 us
  waiting for transfers between devices: 1.21 us -> 2.24 us
    unnamed x2 -> x10, local copies, waits for them, and re-layouts: 0.01 us -> 10.8 us
    all_to_all x1 -> x0, blocking collectives: 10.4 us -> none  [local(): images = lax.all_to_all(blocks, 'view', 0, 0, tiled=True)]
    ppermute x0 -> x3, starting transfers between devices: none -> 4.45 us  [exchanged(): found.append((source, lax.ppermute(sent, axis, route)))]
    pallas_call x1, Pallas kernels: 5.14 us -> 2.85 us  [blended(): pl.pallas_call(functools.partial(blend_kernel, density), out_shape=(jax.S...]
    ppermute x0 -> x3, waiting for transfers between devices: none -> 2.23 us  [exchanged(): found.append((source, lax.ppermute(sent, axis, route)))]
    pallas_call x1, Pallas kernels: 6.6 us -> 4.87 us  [shaded(): pl.pallas_call(shade_kernel, out_shape=(jax.ShapeDtypeStruct((nx, ny, nz)...]
    pallas_call x1 -> x2, Pallas kernels: 4.64 us -> 6.25 us  [the longest x1 4.85 us: faces(): pl.pallas_call(faces_kernel, out_shape=(shaped(*u.shape), jax.ShapeDtypeS...]
    ppermute x5, waiting for transfers between devices: 1.21 us -> 0.01 us  [turn(): lax.ppermute(block, axis, [(i, (i + by) % count) for i in range(count)])]
  transfers between devices with their start and end apart: 5 -> 8, of which waited for: 1 -> 2; matrix products, arithmetic and copies ran while one was open for 0% -> 0% of each run, Pallas kernels for 30% -> 30%
where the time goes in v4:
time: 42.5 us; the launch traced here: 42.3 us
  Pallas kernels  14.5 us (34%)
  starting transfers between devices  12.6 us (30%)
  local copies, waits for them, and re-layouts  10.9 us (26%)
  waiting for transfers between devices  2.24 us (5%)
  between operations  1.45 us (3%)
  other arithmetic  0.65 us (2%)
    unnamed x10, local copies, waits for them, and re-layouts  10.8 us
    ppermute x5, starting transfers between devices, turn(): lax.ppermute(block, axis, [(i, (i + by) % count) for i in range(count)])  8.11 us
    pallas_call x1, Pallas kernels, shaded(): pl.pallas_call(shade_kernel, out_shape=(jax.ShapeDtypeStruct((nx, ny, nz)...  4.87 us
    pallas_call x1, Pallas kernels, faces(): pl.pallas_call(faces_kernel, out_shape=(shaped(*u.shape), jax.ShapeDtypeS...  4.85 us
    ppermute x3, starting transfers between devices, exchanged(): found.append((source, lax.ppermute(sent, axis, route)))  4.45 us
    pallas_call x1, Pallas kernels, blended(): pl.pallas_call(functools.partial(blend_kernel, density), out_shape=(jax.S...  2.85 us
    ppermute x3, waiting for transfers between devices, exchanged(): found.append((source, lax.ppermute(sent, axis, route)))  2.23 us
    pallas_call x1, Pallas kernels, ends(): pl.pallas_call(ends_kernel, out_shape=(layers, layers, jax.ShapeDtypeStru...  1.4 us
  transfers between devices with their start and end apart: 8, of which 2 were waited for; matrix products, arithmetic and copies ran while one was open for 0% of the time, Pallas kernels for 30%

profile of v4, /device:TPU:0, one launch (start us, length us, event | category | flops | bytes accessed | tf_op | source)
XLA Modules:
  0.0 42.3 jit_solution(8649108434533903626)
XLA Ops:
  0.0 0.0 copy-start.4
  0.0 1.4 %shard_map.47 = (f32[3,2,128,128]{3,2,1,0:T(8,128)S(1)}, f32[3,2,128,128]{3,2,1,0:T(8,128)S(1)}, f32[2,3,32,8,128]{4,3,2,1,0:T(8,128)S(1)}) custom-call(f32[3,32,128,128]{3,2,1,0:T(8,128)} %u_hbm.3), custom_call_target="tpu_custom_call" | custom-call | flops 1048576 | bytes 1048576 | tf_op jit(solution)/shard_map/pallas_call | solution.py:47
  1.4 0.5 %collective-permute-start = (f32[2,3,32,8,128]{4,3,2,1,0:T(8,128)S(1)}, f32[2,3,32,8,128]{4,3,2,1,0:T(8,128)S(1)}, u32[]{:S(2)}, u32[]{:S(2)}) collective-permute-start(f32[2,3,32,8,128]{4,3,2,1,0:T(8,128)S(1)} %get-tuple-element.21), channel_id=1, source_target_pairs={{0,1},{1,0},{2,3},{3,2},{4,5},{5,4},{6,7},{7,6},{8,9},{9,8},{10,11... | collective-permute-start | bytes 2359304 | tf_op jit(solution)/shard_map/ppermute | solution.py:499
  1.9 2.6 %collective-permute-start.3 = (f32[3,2,128,128]{3,2,1,0:T(8,128)S(1)}, f32[3,2,128,128]{3,2,1,0:T(8,128)S(1)}, u32[]{:S(2)}, u32[]{:S(2)}) collective-permute-start(f32[3,2,128,128]{3,2,1,0:T(8,128)S(1)} %get-tuple-element.31), channel_id=1, source_target_pairs={{0,2},{2,4},{4,6},{6,0},{1,3},{3,5},{5,7},{7,1},{8,10},{10,12},{12... | collective-permute-start | bytes 1179656 | tf_op jit(solution)/shard_map/ppermute | solution.py:499
  4.5 1.0 %collective-permute-start.4 = (f32[3,2,128,128]{3,2,1,0:T(8,128)S(1)}, f32[3,2,128,128]{3,2,1,0:T(8,128)S(1)}, u32[]{:S(2)}, u32[]{:S(2)}) collective-permute-start(f32[3,2,128,128]{3,2,1,0:T(8,128)S(1)} %get-tuple-element.32), channel_id=1, source_target_pairs={{0,6},{2,0},{4,2},{6,4},{1,7},{3,1},{5,3},{7,5},{8,14},{10,8},{12,... | collective-permute-start | bytes 1179656 | tf_op jit(solution)/shard_map/ppermute | solution.py:499
  5.5 4.8 %shard_map.46 = (f32[3,32,128,128]{3,2,1,0:T(8,128)S(1)}, bf16[3,32,128,256]{3,2,1,0:T(8,128)(2,1)S(1)}, f32[192,128]{1,0:T(8,128)S(1)}, f32[192,128]{1,0:T(8,128)S(1)}) custom-call(f32[3,32,128,128]{3,2,1,0:T(8,128)} %u_hbm.3), custom_call_target="tpu_custom_call" | custom-call | flops 1048576 | bytes 1048576 | tf_op jit(solution)/shard_map/pallas_call | solution.py:133
  10.4 0.0 copy-start
  10.4 2.7 %copy-done = f32[3,32,128,128]{3,2,1,0:T(8,128)} copy-done((f32[3,32,128,128]{3,2,1,0:T(8,128)}, f32[3,32,128,128]{3,2,1,0:T(8,128)S(1)}, u32[]{:S(2)}) %copy-start) | copy-done | bytes 6291480
  13.1 0.0 copy-start.2
  13.1 2.6 %copy-done.2 = bf16[3,32,128,256]{3,2,1,0:T(8,128)(2,1)} copy-done((bf16[3,32,128,256]{3,2,1,0:T(8,128)(2,1)}, bf16[3,32,128,256]{3,2,1,0:T(8,128)(2,1)S(1)}, u32[]{:S(2)}) %copy-start.2) | copy-done | bytes 6291480
  15.7 2.0 %collective-permute-start.1 = (f32[192,128]{1,0:T(8,128)S(1)}, f32[192,128]{1,0:T(8,128)S(1)}, u32[]{:S(2)}, u32[]{:S(2)}) collective-permute-start(f32[192,128]{1,0:T(8,128)S(1)} %get-tuple-element.25), channel_id=1, source_target_pairs={{0,8},{8,16},{16,24},{24,0},{1,9},{9,17},{17,25},{25,1},{2,10},{10... | collective-permute-start | bytes 294920 | tf_op jit(solution)/shard_map/ppermute | solution.py:499
  17.6 2.0 %collective-permute-start.2 = (f32[192,128]{1,0:T(8,128)S(1)}, f32[192,128]{1,0:T(8,128)S(1)}, u32[]{:S(2)}, u32[]{:S(2)}) collective-permute-start(f32[192,128]{1,0:T(8,128)S(1)} %get-tuple-element.26), channel_id=1, source_target_pairs={{0,24},{8,0},{16,8},{24,16},{1,25},{9,1},{17,9},{25,17},{2,26},{10... | collective-permute-start | bytes 294920 | tf_op jit(solution)/shard_map/ppermute | solution.py:499
  21.0 0.0 collective-permute-done
  21.0 0.1 slice_bitcast_fusion
  21.0 0.0 copy-done.4
  21.1 0.0 copy-start.1
  21.1 2.8 %copy-done.1 = f32[3,32,128,128]{3,2,1,0:T(8,128)S(1)} copy-done((f32[3,32,128,128]{3,2,1,0:T(8,128)S(1)}, f32[3,32,128,128]{3,2,1,0:T(8,128)}, u32[]{:S(2)}) %copy-start.1) | copy-done | bytes 6291480
  23.8 0.0 copy-start.3
  23.8 2.8 %copy-done.3 = bf16[3,32,128,256]{3,2,1,0:T(8,128)(2,1)S(1)} copy-done((bf16[3,32,128,256]{3,2,1,0:T(8,128)(2,1)S(1)}, bf16[3,32,128,256]{3,2,1,0:T(8,128)(2,1)}, u32[]{:S(2)}) %copy-start.3) | copy-done | bytes 6291480
  26.6 4.9 %shard_map.48 = (f32[32,128,128]{2,1,0:T(8,128)S(1)}, f32[3,128,128]{2,1,0:T(8,128)S(1)}, f32[4,3,128,128]{3,2,1,0:T(8,128)S(1)}, f32[4,128,128]{2,1,0:T(8,128)S(1)}) custom-call(f32[3,32,128,128]{3,2,1,0:T(8,128)S(1)} %copy-done.1, bf16[3,32,128,256]{3,2,1,0:T(8,128)(2,1)S(1)} %copy-done.3, f32[3,32,8,128]{3,2,1,0:T(8,128)S(1)} %get-tuple-element.34.yleft_ref, ...), custom_call_target="tpu_custom_call" | custom-call | flops 1048576 | bytes 1048576 | tf_op jit(solution)/shard_map/pallas_call | solution.py:278
  31.5 0.0 collective-permute-done.1.zleft_ref
  31.5 0.0 collective-permute-done.2.zright_ref
  31.5 2.8 %shard_map.49 = (f32[4,4,8,128]{3,2,1,0:T(8,128)S(1)}, f32[128,128]{1,0:T(8,128)S(1)}, f32[128,128]{1,0:T(8,128)S(1)}) custom-call(f32[32,128,128]{2,1,0:T(8,128)S(1)} %get-tuple-element.22.raw_ref, f32[3,128,128]{2,1,0:T(8,128)S(1)} %get-tuple-element.23.pack_ref, f32[4,128,128]{2,1,0:T(8,128)S(1)} %get-tuple-element.24.scale_ref, ...), custom_call_target="tpu_custom_call" | custom-call | flops 1048576 | bytes 1048576 | tf_op jit(solution)/shard_map/pallas_call | solution.py:444
  34.4 0.0 collective-permute-done.3.xleft_ref
  34.4 0.0 collective-permute-done.4.xright_ref
  34.4 0.5 %shard_map.50 = f32[4,4,8,128]{3,2,1,0:T(8,128)S(1)} custom-call(f32[4,4,8,128]{3,2,1,0:T(8,128)S(1)} %get-tuple-element.27.middle_ref, f32[32,128,128]{2,1,0:T(8,128)S(1)} %get-tuple-element.22.raw_ref, f32[4,3,128,128]{3,2,1,0:T(8,128)S(1)} %get-tuple-element.28.kept_ref, f32[4,128,128]{2,1,0:T(8,128)S(1)} %get-tuple-element.24.scale_ref, ...), custom_call_target="tpu_custom_call" | custom-call | flops 1048576 | bytes 1048576 | tf_op jit(solution)/shard_map/pallas_call | solution.py:486
  34.9 2.0 %collective-permute-start.5 = (f32[4,8,128]{2,1,0:T(8,128)S(1)}, f32[4,8,128]{2,1,0:T(8,128)S(1)}, u32[]{:S(2)}, u32[]{:S(2)}) collective-permute-start(f32[4,8,128]{2,1,0:T(8,128)S(1)} %get-tuple-element.38), channel_id=1, source_target_pairs={{0,24},{8,16},{16,8},{24,0},{1,25},{9,17},{17,9},{25,1},{2,26},{10... | collective-permute-start | bytes 49160 | tf_op jit(solution)/shard_map/ppermute | solution.py:522
  37.0 0.0 collective-permute-start.6
  37.0 2.4 %collective-permute-start.7 = (f32[4,8,128]{2,1,0:T(8,128)S(1)}, f32[4,8,128]{2,1,0:T(8,128)S(1)}, u32[]{:S(2)}, u32[]{:S(2)}) collective-permute-start(f32[4,8,128]{2,1,0:T(8,128)S(1)} %get-tuple-element.39), channel_id=1, source_target_pairs={{0,8},{8,0},{16,24},{24,16},{1,9},{9,1},{17,25},{25,17},{2,10},{10... | collective-permute-start | bytes 49160 | tf_op jit(solution)/shard_map/ppermute | solution.py:522
  39.4 1.1 %collective-permute-done.5 = f32[4,8,128]{2,1,0:T(8,128)S(1)} collective-permute-done((f32[4,8,128]{2,1,0:T(8,128)S(1)}, f32[4,8,128]{2,1,0:T(8,128)S(1)}, u32[]{:S(2)}, u32[]{:S(2)}) %collective-permute-start.5) | collective-permute-done | bytes 16416 | tf_op jit(solution)/shard_map/ppermute | solution.py:522
  40.5 1.1 %collective-permute-done.6 = f32[4,8,128]{2,1,0:T(8,128)S(1)} collective-permute-done((f32[4,8,128]{2,1,0:T(8,128)S(1)}, f32[4,8,128]{2,1,0:T(8,128)S(1)}, u32[]{:S(2)}, u32[]{:S(2)}) %collective-permute-start.6) | collective-permute-done | bytes 16416 | tf_op jit(solution)/shard_map/ppermute | solution.py:522
  41.6 0.0 collective-permute-done.7
  41.7 0.6 %maximum_bitcast_fusion = f32[1,1,4,8,128]{4,3,2,1,0:T(8,128)} fusion(f32[1,8,128]{2,1,0:T(8,128)S(1)} %get-tuple-element.36, f32[3,8,128]{2,1,0:T(8,128)S(1)} %fusion), kind=kLoop, calls=%fused_computation.2 | loop fusion | flops 4096 | bytes 32768 | tf_op jit(solution)/shard_map/reshape | solution.py:550
  (4 shorter events, 0.1 us)
Async XLA Ops:
  0.0 21.0 %copy-start.4 = (s32[4,16,1]{1,2,0:T(1,128)S(1)}, s32[4,16,1]{1,2,0:T(1,128)}, u32[]{:S(2)}) copy-start(s32[4,16,1]{1,2,0:T(1,128)} %param.5) | copy-start | bytes 772
  1.4 19.6 %collective-permute-start = (f32[2,3,32,8,128]{4,3,2,1,0:T(8,128)S(1)}, f32[2,3,32,8,128]{4,3,2,1,0:T(8,128)S(1)}, u32[]{:S(2)}, u32[]{:S(2)}) collective-permute-start(f32[2,3,32,8,128]{4,3,2,1,0:T(8,128)S(1)} %get-tuple-element.21), channel_id=1, source_target_pairs={{0,1},{1,0},{2,3},{3,2},{4,5},{5,4},{6,7},{7,6},{8,9},{9,8},{10,11... | collective-permute-start | bytes 2359304 | tf_op jit(solution)/shard_map/ppermute | solution.py:499
  1.9 32.4 %collective-permute-start.3 = (f32[3,2,128,128]{3,2,1,0:T(8,128)S(1)}, f32[3,2,128,128]{3,2,1,0:T(8,128)S(1)}, u32[]{:S(2)}, u32[]{:S(2)}) collective-permute-start(f32[3,2,128,128]{3,2,1,0:T(8,128)S(1)} %get-tuple-element.31), channel_id=1, source_target_pairs={{0,2},{2,4},{4,6},{6,0},{1,3},{3,5},{5,7},{7,1},{8,10},{10,12},{12... | collective-permute-start | bytes 1179656 | tf_op jit(solution)/shard_map/ppermute | solution.py:499
  4.5 29.9 %collective-permute-start.4 = (f32[3,2,128,128]{3,2,1,0:T(8,128)S(1)}, f32[3,2,128,128]{3,2,1,0:T(8,128)S(1)}, u32[]{:S(2)}, u32[]{:S(2)}) collective-permute-start(f32[3,2,128,128]{3,2,1,0:T(8,128)S(1)} %get-tuple-element.32), channel_id=1, source_target_pairs={{0,6},{2,0},{4,2},{6,4},{1,7},{3,1},{5,3},{7,5},{8,14},{10,8},{12,... | collective-permute-start | bytes 1179656 | tf_op jit(solution)/shard_map/ppermute | solution.py:499
  10.4 2.7 %copy-start = (f32[3,32,128,128]{3,2,1,0:T(8,128)}, f32[3,32,128,128]{3,2,1,0:T(8,128)S(1)}, u32[]{:S(2)}) copy-start(f32[3,32,128,128]{3,2,1,0:T(8,128)S(1)} %get-tuple-element.19.u_ref) | copy-start | bytes 18874372
  13.1 2.6 %copy-start.2 = (bf16[3,32,128,256]{3,2,1,0:T(8,128)(2,1)}, bf16[3,32,128,256]{3,2,1,0:T(8,128)(2,1)S(1)}, u32[]{:S(2)}) copy-start(bf16[3,32,128,256]{3,2,1,0:T(8,128)(2,1)S(1)} %get-tuple-element.20.parts_ref) | copy-start | bytes 18874372
  15.7 15.8 %collective-permute-start.1 = (f32[192,128]{1,0:T(8,128)S(1)}, f32[192,128]{1,0:T(8,128)S(1)}, u32[]{:S(2)}, u32[]{:S(2)}) collective-permute-start(f32[192,128]{1,0:T(8,128)S(1)} %get-tuple-element.25), channel_id=1, source_target_pairs={{0,8},{8,16},{16,24},{24,0},{1,9},{9,17},{17,25},{25,1},{2,10},{10... | collective-permute-start | bytes 294920 | tf_op jit(solution)/shard_map/ppermute | solution.py:499
  17.6 13.9 %collective-permute-start.2 = (f32[192,128]{1,0:T(8,128)S(1)}, f32[192,128]{1,0:T(8,128)S(1)}, u32[]{:S(2)}, u32[]{:S(2)}) collective-permute-start(f32[192,128]{1,0:T(8,128)S(1)} %get-tuple-element.26), channel_id=1, source_target_pairs={{0,24},{8,0},{16,8},{24,16},{1,25},{9,1},{17,9},{25,17},{2,26},{10... | collective-permute-start | bytes 294920 | tf_op jit(solution)/shard_map/ppermute | solution.py:499
  21.1 2.8 %copy-start.1 = (f32[3,32,128,128]{3,2,1,0:T(8,128)S(1)}, f32[3,32,128,128]{3,2,1,0:T(8,128)}, u32[]{:S(2)}) copy-start(f32[3,32,128,128]{3,2,1,0:T(8,128)} %copy-done) | copy-start | bytes 18874372
  23.8 2.8 %copy-start.3 = (bf16[3,32,128,256]{3,2,1,0:T(8,128)(2,1)S(1)}, bf16[3,32,128,256]{3,2,1,0:T(8,128)(2,1)}, u32[]{:S(2)}) copy-start(bf16[3,32,128,256]{3,2,1,0:T(8,128)(2,1)} %copy-done.2) | copy-start | bytes 18874372
  34.9 5.6 %collective-permute-start.5 = (f32[4,8,128]{2,1,0:T(8,128)S(1)}, f32[4,8,128]{2,1,0:T(8,128)S(1)}, u32[]{:S(2)}, u32[]{:S(2)}) collective-permute-start(f32[4,8,128]{2,1,0:T(8,128)S(1)} %get-tuple-element.38), channel_id=1, source_target_pairs={{0,24},{8,16},{16,8},{24,0},{1,25},{9,17},{17,9},{25,1},{2,26},{10... | collective-permute-start | bytes 49160 | tf_op jit(solution)/shard_map/ppermute | solution.py:522
  37.0 4.6 %collective-permute-start.6 = (f32[4,8,128]{2,1,0:T(8,128)S(1)}, f32[4,8,128]{2,1,0:T(8,128)S(1)}, u32[]{:S(2)}, u32[]{:S(2)}) collective-permute-start(f32[4,8,128]{2,1,0:T(8,128)S(1)} %get-tuple-element.40), channel_id=1, source_target_pairs={{0,16},{8,24},{16,0},{24,8},{1,17},{9,25},{17,1},{25,9},{2,18},{10... | collective-permute-start | bytes 49160 | tf_op jit(solution)/shard_map/ppermute | solution.py:522
  37.0 4.6 %collective-permute-start.7 = (f32[4,8,128]{2,1,0:T(8,128)S(1)}, f32[4,8,128]{2,1,0:T(8,128)S(1)}, u32[]{:S(2)}, u32[]{:S(2)}) collective-permute-start(f32[4,8,128]{2,1,0:T(8,128)S(1)} %get-tuple-element.39), channel_id=1, source_target_pairs={{0,8},{8,0},{16,24},{24,16},{1,9},{9,1},{17,25},{25,17},{2,10},{10... | collective-permute-start | bytes 49160 | tf_op jit(solution)/shard_map/ppermute | solution.py:522

commit v5 on v4

--- a/solution.py
+++ b/solution.py
@@ -13,7 +13,7 @@
 VMEM = pl.BlockSpec(memory_space=pltpu.VMEM)
 HBM = pl.BlockSpec(memory_space=pltpu.HBM)
 COST = pl.CostEstimate(flops=1 << 20, bytes_accessed=1 << 20, transcendentals=0)
-PARAMS = pltpu.CompilerParams(vmem_limit_bytes=24 << 20)
+PARAMS = pltpu.CompilerParams(vmem_limit_bytes=16 << 20)
 
 
 def split(values):
@@ -55,7 +55,7 @@
     )(u)
 
 
-def faces_kernel(u_hbm, u_ref, parts_ref, tail_ref, head_ref, sems):
+def faces_kernel(u_hbm, u_ref, parts_ref, tail_ref, head_ref, packed_ref, sems):
     comps, nx, ny, nz = u_ref.shape
     quarters = sems.shape[1]
     rows = ny // quarters
@@ -64,85 +64,71 @@
         span = pl.ds(k * rows if isinstance(k, int) else pl.multiple_of(k * rows, rows), rows)
         return pltpu.make_async_copy(u_hbm.at[c, :, span], u_ref.at[c, :, span], sems.at[c, k])
 
-    for k in range(quarters):
-        for c in (0, 1):
+    for c in range(comps):
+        for k in range(quarters):
             fetch(c, k).start()
-    for k in range(quarters):
-        fetch(2, k).start()
-    pair = iota((8, nz), 1) // 2
-
-    def pack(members, y, out, first):
-        out_rows = pl.ds(out, 8)
-        tail = jnp.zeros((8, nz), jnp.float32)
-        head = jnp.zeros((8, nz), jnp.float32)
-        for c, base in members:
+    slot = iota((8, nz), 1) // 4
+    for c in range(comps):
+
+        def quarter(k, carry):
+            fetch(c, k).wait()
+            start = pl.multiple_of(k * rows, rows)
+            packed = [jnp.zeros((8, nz), jnp.float32)] * (rows // 8)
             for x in range(nx):
-                place = base // 2 + x
-                moved = pltpu.roll(u_ref[c, x, pl.ds(y, 8), :], (base + 2 * x + 2) % nz, 1)
-                tail = jnp.where(pair == place, moved, tail)
-                head = jnp.where(pair == (place + 1) % (nz // 2), moved, head)
-        head = pltpu.roll(head, nz - 2, 1)
-        if first:
-            tail_ref[out_rows, :] = tail
-            head_ref[out_rows, :] = head
-        else:
-            half = pair < nz // 4
-            tail_ref[out_rows, :] = jnp.where(half, tail_ref[out_rows, :], tail)
-            head_ref[out_rows, :] = jnp.where(half, head_ref[out_rows, :], head)
-
-    def parted(c, k):
-        span = pl.ds(pl.multiple_of(k * rows, rows), rows)
-        for x in range(nx):
-            high, low = split(u_ref[c, x, span, :])
-            parts_ref[c, x, span, pl.ds(0, nz)] = high
-            parts_ref[c, x, span, pl.ds(nz, nz)] = low
-
-    def both(k, carry):
-        fetch(0, k).wait()
-        fetch(1, k).wait()
-        parted(0, k)
-        parted(1, k)
-        for part in range(rows // 8):
-            y = pl.multiple_of(k * rows + part * 8, 8)
-            pack(((0, 0), (1, nz // 2)), y, y, True)
-        return carry
-
-    lax.fori_loop(0, quarters, both, 0)
-
-    def last(base, offset, first):
-        def step(k, carry):
-            fetch(2, k).wait()
-            parted(2, k)
-            for part in range(rows // 8):
-                y = pl.multiple_of(k * rows + part * 8, 8)
-                pack(((2, base),), y, pl.multiple_of(y + offset, 8), first)
+                cells = u_ref[c, x, pl.ds(start, rows), :]
+                high, low = split(cells)
+                parts_ref[c, x, pl.ds(start, rows), pl.ds(0, nz)] = high
+                parts_ref[c, x, pl.ds(start, rows), pl.ds(nz, nz)] = low
+                mine = slot == x
+                for n in range(rows // 8):
+                    packed[n] = jnp.where(mine, pltpu.roll(cells[8 * n : 8 * n + 8], (4 * x + 2) % nz, 1), packed[n])
+            for n in range(rows // 8):
+                packed_ref[c, pl.ds(pl.multiple_of(start + 8 * n, 8), 8), :] = packed[n]
             return carry
 
-        return step
-
-    lax.fori_loop(0, quarters // 2, last(0, ny, True), 0)
-    lax.fori_loop(quarters // 2, quarters, last(nz // 2, ny // 2, False), 0)
+        lax.fori_loop(0, quarters, quarter, 0)
+    tails, heads = fold([packed_ref[c] for c in range(comps)], ny, nz)
+    tail_ref[...] = tails
+    head_ref[...] = heads
+
+
+def fold(packed, ny, nz):
+    early = iota((ny, nz), 1) % 4 < 2
+    early2 = early[: ny // 2]
+    third, fourth = packed[2][: ny // 2], packed[2][ny // 2 :]
+    tails = jnp.where(early, packed[0], pltpu.roll(packed[1], 2, 1))
+    tails2 = jnp.where(early2, third, pltpu.roll(fourth, 2, 1))
+    heads = jnp.where(early, pltpu.roll(packed[0], nz - 2, 1), packed[1])
+    heads2 = jnp.where(early2, pltpu.roll(third, nz - 2, 1), fourth)
+    return jnp.concatenate([tails, tails2], axis=0), jnp.concatenate([heads, heads2], axis=0)
+
+
+def unfold(left, right, ny, nz):
+    early = iota((ny, nz), 1) % 4 < 2
+    early2 = early[: ny // 2]
+    left2, right2 = left[ny:], right[ny:]
+    left, right = left[:ny], right[:ny]
+    first = jnp.where(early, left, pltpu.roll(right, 2, 1))
+    second = jnp.where(early, pltpu.roll(left, nz - 2, 1), right)
+    third = jnp.where(early2, left2, pltpu.roll(right2, 2, 1))
+    fourth = jnp.where(early2, pltpu.roll(left2, nz - 2, 1), right2)
+    return first, second, jnp.concatenate([third, fourth], axis=0)
 
 
 def faces(u):
     comps, nx, ny, nz = u.shape
-
-    def shaped(*shape):
-        return jax.ShapeDtypeStruct(shape, jnp.float32)
-
+    message = jax.ShapeDtypeStruct((ny + ny // 2, nz), jnp.float32)
     return pl.pallas_call(
         faces_kernel,
         out_shape=(
-            shaped(*u.shape),
+            jax.ShapeDtypeStruct(u.shape, jnp.float32),
             jax.ShapeDtypeStruct((comps, nx, ny, 2 * nz), jnp.bfloat16),
-            shaped(ny + ny // 2, nz),
-            shaped(ny + ny // 2, nz),
+            message,
+            message,
         ),
         in_specs=[HBM],
         out_specs=(VMEM,) * 4,
-        scratch_shapes=[
-            pltpu.SemaphoreType.DMA((comps, 4)),
-        ],
+        scratch_shapes=[pltpu.VMEM((comps, ny, nz), jnp.float32), pltpu.SemaphoreType.DMA((comps, 4))],
         compiler_params=pltpu.CompilerParams(vmem_limit_bytes=37 << 20),
         cost_estimate=COST,
     )(u)
@@ -299,34 +285,14 @@
 
 def sides_deep(nx, ny, nz, zleft_ref, zright_ref):
     source, target = iota((2 * nz, nz), 0) % nz, iota((2 * nz, nz), 1)
-    side, place, layer = source // (2 * nx), source % (2 * nx) // 2, source % 2
-    where = jnp.where(place == target // 4, 4 * side + 2 * layer, -1000) + 10 * (target % 4)
+    where = jnp.where(source // 4 == target // 4, source % 4 + 10 * (target % 4), -1)
     weights = jnp.zeros((2 * nz, nz), jnp.float32)
-    for value, (s, l, t) in (
-        (1.0, (0, 0, 2)),
-        (-8.0, (0, 1, 2)),
-        (1.0, (0, 1, 3)),
-        (-1.0, (1, 0, 0)),
-        (8.0, (1, 0, 1)),
-        (-1.0, (1, 1, 1)),
-    ):
-        weights = jnp.where(where == 4 * s + 2 * l + 10 * t, value, weights)
+    for value, m, t in ((1.0, 0, 2), (-8.0, 1, 2), (1.0, 1, 3), (-1.0, 2, 0), (8.0, 2, 1), (-1.0, 3, 1)):
+        weights = jnp.where(where == m + 10 * t, value, weights)
     weights = weights.astype(jnp.bfloat16)
-    first = iota((ny, nz), 1) < nz // 2
-    left, right = zleft_ref[:ny], zright_ref[:ny]
-    left2, right2 = zleft_ref[ny:], zright_ref[ny:]
-    turned_left2, turned_right2 = pltpu.roll(left2, nz // 2, 1), pltpu.roll(right2, nz // 2, 1)
-    ghosts = (
-        jnp.where(first, left, pltpu.roll(right, nz // 2, 1)),
-        jnp.where(first, pltpu.roll(left, nz // 2, 1), right),
-        jnp.where(
-            first,
-            jnp.concatenate([left2, turned_left2], axis=0),
-            jnp.concatenate([turned_right2, right2], axis=0),
-        ),
-    )
     return [
-        jnp.dot(jnp.concatenate(split(ghost), axis=1), weights, preferred_element_type=jnp.float32) for ghost in ghosts
+        jnp.dot(jnp.concatenate(split(ghost), axis=1), weights, preferred_element_type=jnp.float32)
+        for ghost in unfold(zleft_ref[...], zright_ref[...], ny, nz)
     ]
 
 
@@ -367,13 +333,13 @@
     store(red, 4.0 * (red - square), 1.0 - through - red, through)
 
 
-def put(image_ref, x):
+def put(image_ref, x, slot=lambda view: view):
     per_view = image_ref.shape[2]
     view, row = (x // per_view, x % per_view) if isinstance(x, int) else (lax.div(x, per_view), lax.rem(x, per_view))
 
     def store(*channels):
         for k, values in enumerate(channels):
-            image_ref[view, k, pl.ds(row, 1), :] = values
+            image_ref[slot(view), k, pl.ds(row, 1), :] = values
 
     return store
 
@@ -462,7 +428,14 @@
 ):
     nx, ny, nz = raw_ref.shape
     summing(sum_ref)
-    image_ref[...] = middle_ref[...]
+    views = image_ref.shape[0]
+    me = lax.axis_index("view")
+
+    def slot(view):
+        return step_to(me, view, views)
+
+    for view in range(views):
+        image_ref[slot(view)] = middle_ref[view]
     raws = []
     for place, x in enumerate(edge_rows(nx)):
         if place == 0:
@@ -478,7 +451,7 @@
         raws.append(raw_ref[x] + on_border(fix_ref[...], x) + more * scale_ref[x // SUB])
     gather(density, raws, level_ref, sums_ref, sum_ref)
     for place, x in enumerate(edge_rows(nx)):
-        blend(level_ref, sums_ref, place, put(image_ref, x))
+        blend(level_ref, sums_ref, place, put(image_ref, x, slot))
 
 
 def edged(density, middle, raw, *rest):
@@ -506,21 +479,50 @@
     return turn(tail_head[0], axis, 1), turn(tail_head[1], axis, -1)
 
 
+def step_to(me, other, count):
+    return me ^ other if count & (count - 1) == 0 else lax.rem(other - me + count, count)
+
+
 def exchanged(blocks, axis):
     count = lax.axis_size(axis)
-    me = lax.axis_index(axis)
     paired = count & (count - 1) == 0
-    found = [(me, lax.dynamic_index_in_dim(blocks, me, 0, keepdims=False))]
+    found = [blocks[0]]
     for step in range(count - 1, 0, -1):
-        if paired:
-            to = source = me ^ step
-            route = [(i, i ^ step) for i in range(count)]
-        else:
-            to, source = (me + step) % count, (me - step) % count
-            route = [(i, (i + step) % count) for i in range(count)]
-        sent = lax.dynamic_index_in_dim(blocks, to, 0, keepdims=False)
-        found.append((source, lax.ppermute(sent, axis, route)))
+        route = [(i, i ^ step if paired else (i + step) % count) for i in range(count)]
+        found.insert(1, lax.ppermute(blocks[step], axis, route))
     return found
+
+
+def composite_kernel(*refs):
+    *image_refs, out_ref = refs
+    count = len(image_refs)
+    me = lax.axis_index("view")
+    if count & (count - 1) == 0:
+        sources = [me ^ step for step in range(count)]
+    else:
+        sources = [lax.rem(me - step + count, count) for step in range(count)]
+    colour = [0.0] * 3
+    through = 1.0
+    for source, image_ref in zip(sources, image_refs):
+        passing = 1.0
+        for other, front_ref in zip(sources, image_refs):
+            passing = passing * jnp.where(other < source, front_ref[3], 1.0)
+        colour = [total + passing * image_ref[k] for k, total in enumerate(colour)]
+        through = through * image_ref[3]
+    for k in range(3):
+        out_ref[0, 0, k] = colour[k]
+    out_ref[0, 0, 3] = 1.0 - through
+
+
+def composited(images):
+    return pl.pallas_call(
+        composite_kernel,
+        out_shape=jax.ShapeDtypeStruct((1, 1) + images[0].shape, jnp.float32),
+        in_specs=[VMEM] * len(images),
+        out_specs=VMEM,
+        compiler_params=PARAMS,
+        cost_estimate=COST,
+    )(*images)
 
 
 def local(velocity, occupied, q_floor, q_span):
@@ -537,17 +539,7 @@
     raw, pack, kept, scale = shaded(u, parts, yleft, yright, occupied[:, :, 0], q_floor, q_span)
     middle, fix, first = blended(density, views, raw, pack, scale, zleft, zright)
     blocks = edged(density, middle, raw, kept, scale, fix, first, xleft, xright)
-    images = exchanged(blocks, "view")
-    colour = jnp.zeros((3, nx // views, ny), jnp.float32)
-    through = jnp.ones((nx // views, ny), jnp.float32)
-    for source, image in images:
-        passing = jnp.ones((nx // views, ny), jnp.float32)
-        for other, front in images:
-            passing = passing * jnp.where(other < source, front[3], 1.0)
-        colour = colour + passing * image[:3]
-        through = through * image[3]
-    finished = jnp.concatenate([colour, 1.0 - through[None]], axis=0)
-    return finished.reshape(1, 1, 4, nx // views, ny)
+    return composited(exchanged(blocks, "view"))
 
 
 def solution(mesh):

time: 42.5 us -> 33.5 us (0.79)
  local copies, waits for them, and re-layouts: 10.9 us -> 0.06 us
  waiting for transfers between devices: 2.24 us -> 5.13 us
  other arithmetic: 0.65 us -> 0 us
    unnamed x10 -> x2, local copies, waits for them, and re-layouts: 10.8 us -> 0.01 us
    ppermute x3, waiting for transfers between devices: 2.23 us -> 3.85 us  [exchanged(): found.insert(1, lax.ppermute(blocks[step], axis, route))]
    ppermute x5, waiting for transfers between devices: 0.01 us -> 1.28 us  [turn(): lax.ppermute(block, axis, [(i, (i + by) % count) for i in range(count)])]
    reshape x1 -> x0, other arithmetic: 0.61 us -> none  [local(): return finished.reshape(1, 1, 4, nx // views, ny)]
    pallas_call x1 -> x2, Pallas kernels: 4.85 us -> 4.41 us  [the longest x1 3.78 us: faces(): pl.pallas_call(faces_kernel, out_shape=(jax.ShapeDtypeStruct(u.shape, jnp...]
  transfers between devices with their start and end apart: 8 -> 8, of which waited for: 2 -> 3; matrix products, arithmetic and copies ran while one was open for 0% -> 0% of each run, Pallas kernels for 30% -> 35%
where the time goes in v5:
time: 33.5 us; the launch traced here: 33.3 us
  Pallas kernels  14.1 us (42%)
  starting transfers between devices  12.7 us (38%)
  waiting for transfers between devices  5.13 us (15%)
  between operations  1.4 us (4%)
    ppermute x5, starting transfers between devices, turn(): lax.ppermute(block, axis, [(i, (i + by) % count) for i in range(count)])  8.22 us
    pallas_call x1, Pallas kernels, shaded(): pl.pallas_call(shade_kernel, out_shape=(jax.ShapeDtypeStruct((nx, ny, nz)...  4.89 us
    ppermute x3, starting transfers between devices, exchanged(): found.insert(1, lax.ppermute(blocks[step], axis, route))  4.45 us
    ppermute x3, waiting for transfers between devices, exchanged(): found.insert(1, lax.ppermute(blocks[step], axis, route))  3.85 us
    pallas_call x1, Pallas kernels, faces(): pl.pallas_call(faces_kernel, out_shape=(jax.ShapeDtypeStruct(u.shape, jnp...  3.78 us
    pallas_call x1, Pallas kernels, blended(): pl.pallas_call(functools.partial(blend_kernel, density), out_shape=(jax.S...  2.83 us
    pallas_call x1, Pallas kernels, ends(): pl.pallas_call(ends_kernel, out_shape=(layers, layers, jax.ShapeDtypeStru...  1.4 us
    ppermute x5, waiting for transfers between devices, turn(): lax.ppermute(block, axis, [(i, (i + by) % count) for i in range(count)])  1.28 us
  transfers between devices with their start and end apart: 8, of which 3 were waited for; matrix products, arithmetic and copies ran while one was open for 0% of the time, Pallas kernels for 35%

profile of v5, /device:TPU:0, one launch (start us, length us, event | category | flops | bytes accessed | tf_op | source)
XLA Modules:
  0.0 33.3 jit_solution(6660409637500186782)
XLA Ops:
  0.0 0.0 copy-start
  0.0 1.4 %shard_map.47 = (f32[3,2,128,128]{3,2,1,0:T(8,128)S(1)}, f32[3,2,128,128]{3,2,1,0:T(8,128)S(1)}, f32[2,3,32,8,128]{4,3,2,1,0:T(8,128)S(1)}) custom-call(f32[3,32,128,128]{3,2,1,0:T(8,128)} %u_hbm.3), custom_call_target="tpu_custom_call" | custom-call | flops 1048576 | bytes 1048576 | tf_op jit(solution)/shard_map/pallas_call | solution.py:47
  1.4 0.5 %collective-permute-start = (f32[2,3,32,8,128]{4,3,2,1,0:T(8,128)S(1)}, f32[2,3,32,8,128]{4,3,2,1,0:T(8,128)S(1)}, u32[]{:S(2)}, u32[]{:S(2)}) collective-permute-start(f32[2,3,32,8,128]{4,3,2,1,0:T(8,128)S(1)} %get-tuple-element.21), channel_id=1, source_target_pairs={{0,1},{1,0},{2,3},{3,2},{4,5},{5,4},{6,7},{7,6},{8,9},{9,8},{10,11... | collective-permute-start | bytes 2359304 | tf_op jit(solution)/shard_map/ppermute | solution.py:472
  1.9 2.6 %collective-permute-start.3 = (f32[3,2,128,128]{3,2,1,0:T(8,128)S(1)}, f32[3,2,128,128]{3,2,1,0:T(8,128)S(1)}, u32[]{:S(2)}, u32[]{:S(2)}) collective-permute-start(f32[3,2,128,128]{3,2,1,0:T(8,128)S(1)} %get-tuple-element.31), channel_id=1, source_target_pairs={{0,2},{2,4},{4,6},{6,0},{1,3},{3,5},{5,7},{7,1},{8,10},{10,12},{12... | collective-permute-start | bytes 1179656 | tf_op jit(solution)/shard_map/ppermute | solution.py:472
  4.5 1.0 %collective-permute-start.4 = (f32[3,2,128,128]{3,2,1,0:T(8,128)S(1)}, f32[3,2,128,128]{3,2,1,0:T(8,128)S(1)}, u32[]{:S(2)}, u32[]{:S(2)}) collective-permute-start(f32[3,2,128,128]{3,2,1,0:T(8,128)S(1)} %get-tuple-element.32), channel_id=1, source_target_pairs={{0,6},{2,0},{4,2},{6,4},{1,7},{3,1},{5,3},{7,5},{8,14},{10,8},{12,... | collective-permute-start | bytes 1179656 | tf_op jit(solution)/shard_map/ppermute | solution.py:472
  5.5 3.8 %shard_map.46 = (f32[3,32,128,128]{3,2,1,0:T(8,128)S(1)}, bf16[3,32,128,256]{3,2,1,0:T(8,128)(2,1)S(1)}, f32[192,128]{1,0:T(8,128)S(1)}, f32[192,128]{1,0:T(8,128)S(1)}) custom-call(f32[3,32,128,128]{3,2,1,0:T(8,128)} %u_hbm.3), custom_call_target="tpu_custom_call" | custom-call | flops 1048576 | bytes 1048576 | tf_op jit(solution)/shard_map/pallas_call | solution.py:121
  9.3 2.0 %collective-permute-start.1 = (f32[192,128]{1,0:T(8,128)S(1)}, f32[192,128]{1,0:T(8,128)S(1)}, u32[]{:S(2)}, u32[]{:S(2)}) collective-permute-start(f32[192,128]{1,0:T(8,128)S(1)} %get-tuple-element.25), channel_id=1, source_target_pairs={{0,8},{8,16},{16,24},{24,0},{1,9},{9,17},{17,25},{25,1},{2,10},{10... | collective-permute-start | bytes 294920 | tf_op jit(solution)/shard_map/ppermute | solution.py:472
  11.3 2.1 %collective-permute-start.2 = (f32[192,128]{1,0:T(8,128)S(1)}, f32[192,128]{1,0:T(8,128)S(1)}, u32[]{:S(2)}, u32[]{:S(2)}) collective-permute-start(f32[192,128]{1,0:T(8,128)S(1)} %get-tuple-element.26), channel_id=1, source_target_pairs={{0,24},{8,0},{16,8},{24,16},{1,25},{9,1},{17,9},{25,17},{2,26},{10... | collective-permute-start | bytes 294920 | tf_op jit(solution)/shard_map/ppermute | solution.py:472
  14.7 0.0 collective-permute-done
  14.7 0.1 slice_bitcast_fusion
  14.8 0.0 copy-done
  14.8 4.9 %shard_map.48 = (f32[32,128,128]{2,1,0:T(8,128)S(1)}, f32[3,128,128]{2,1,0:T(8,128)S(1)}, f32[4,3,128,128]{3,2,1,0:T(8,128)S(1)}, f32[4,128,128]{2,1,0:T(8,128)S(1)}) custom-call(f32[3,32,128,128]{3,2,1,0:T(8,128)S(1)} %get-tuple-element.19.u_ref, bf16[3,32,128,256]{3,2,1,0:T(8,128)(2,1)S(1)} %get-tuple-element.20.parts_ref, ...), custom_call_target="tpu_custom_call" | custom-call | flops 1048576 | bytes 1048576 | tf_op jit(solution)/shard_map/pallas_call | solution.py:264
  19.7 0.0 collective-permute-done.1.zleft_ref
  19.7 0.0 collective-permute-done.2.zright_ref
  19.7 2.8 %shard_map.49 = (f32[4,4,8,128]{3,2,1,0:T(8,128)S(1)}, f32[128,128]{1,0:T(8,128)S(1)}, f32[128,128]{1,0:T(8,128)S(1)}) custom-call(f32[32,128,128]{2,1,0:T(8,128)S(1)} %get-tuple-element.22.raw_ref, f32[3,128,128]{2,1,0:T(8,128)S(1)} %get-tuple-element.23.pack_ref, f32[4,128,128]{2,1,0:T(8,128)S(1)} %get-tuple-element.24.scale_ref, ...), custom_call_target="tpu_custom_call" | custom-call | flops 1048576 | bytes 1048576 | tf_op jit(solution)/shard_map/pallas_call | solution.py:410
  22.6 0.0 collective-permute-done.3.xleft_ref
  22.6 1.3 %collective-permute-done.4.xright_ref = f32[3,2,128,128]{3,2,1,0:T(8,128)S(1)} collective-permute-done((f32[3,2,128,128]{3,2,1,0:T(8,128)S(1)}, f32[3,2,128,128]{3,2,1,0:T(8,128)S(1)}, u32[]{:S(2)}, u32[]{:S(2)}) %collective-permute-start.4) | collective-permute-done | bytes 393248 | tf_op jit(solution)/shard_map/ppermute | solution.py:472
  23.8 0.5 %shard_map.50 = f32[4,4,8,128]{3,2,1,0:T(8,128)S(1)} custom-call(f32[4,4,8,128]{3,2,1,0:T(8,128)S(1)} %get-tuple-element.27.middle_ref, f32[32,128,128]{2,1,0:T(8,128)S(1)} %get-tuple-element.22.raw_ref, f32[4,3,128,128]{3,2,1,0:T(8,128)S(1)} %get-tuple-element.28.kept_ref, f32[4,128,128]{2,1,0:T(8,128)S(1)} %get-tuple-element.24.scale_ref, ...), custom_call_target="tpu_custom_call" | custom-call | flops 1048576 | bytes 1048576 | tf_op jit(solution)/shard_map/pallas_call | solution.py:459
  24.4 3.7 %collective-permute-start.7 = (f32[4,8,128]{2,1,0:T(8,128)S(1)}, f32[4,8,128]{2,1,0:T(8,128)S(1)}, u32[]{:S(2)}, u32[]{:S(2)}) collective-permute-start(f32[4,8,128]{2,1,0:T(8,128)S(1)} %get-tuple-element.35), channel_id=1, source_target_pairs={{0,24},{8,16},{16,8},{24,0},{1,25},{9,17},{17,9},{25,1},{2,26},{10... | collective-permute-start | bytes 49160 | tf_op jit(solution)/shard_map/ppermute | solution.py:492
  28.0 0.0 collective-permute-start.6
  28.1 0.8 %collective-permute-start.5 = (f32[4,8,128]{2,1,0:T(8,128)S(1)}, f32[4,8,128]{2,1,0:T(8,128)S(1)}, u32[]{:S(2)}, u32[]{:S(2)}) collective-permute-start(f32[4,8,128]{2,1,0:T(8,128)S(1)} %get-tuple-element.37), channel_id=1, source_target_pairs={{0,8},{8,0},{16,24},{24,16},{1,9},{9,1},{17,25},{25,17},{2,10},{10... | collective-permute-start | bytes 49160 | tf_op jit(solution)/shard_map/ppermute | solution.py:492
  28.8 1.2 %collective-permute-done.7.refs_3_ = f32[4,8,128]{2,1,0:T(8,128)S(1)} collective-permute-done((f32[4,8,128]{2,1,0:T(8,128)S(1)}, f32[4,8,128]{2,1,0:T(8,128)S(1)}, u32[]{:S(2)}, u32[]{:S(2)}) %collective-permute-start.7) | collective-permute-done | bytes 16416 | tf_op jit(solution)/shard_map/ppermute | solution.py:492
  30.1 2.6 %collective-permute-done.6.refs_2_ = f32[4,8,128]{2,1,0:T(8,128)S(1)} collective-permute-done((f32[4,8,128]{2,1,0:T(8,128)S(1)}, f32[4,8,128]{2,1,0:T(8,128)S(1)}, u32[]{:S(2)}, u32[]{:S(2)}) %collective-permute-start.6) | collective-permute-done | bytes 16416 | tf_op jit(solution)/shard_map/ppermute | solution.py:492
  32.7 0.0 collective-permute-done.5.refs_1_
  32.7 0.6 %shard_map.51 = f32[1,1,4,8,128]{4,3,2,1,0:T(8,128)} custom-call(f32[4,8,128]{2,1,0:T(8,128)S(1)} %get-tuple-element.38.refs_0_, f32[4,8,128]{2,1,0:T(8,128)S(1)} %collective-permute-done.5.refs_1_, f32[4,8,128]{2,1,0:T(8,128)S(1)} %collective-permute-done.6.refs_2_, f32[4,8,128]{2,1,0:T(8,128)S(1)} %collective-permute-done.7.refs_3_), custom_call_target="tpu_custom_call" | custom-call | flops 1048576 | bytes 1048576 | tf_op jit(solution)/shard_map/pallas_call | solution.py:518
  (1 shorter events, 0.0 us)
Async XLA Ops:
  0.0 14.8 %copy-start = (s32[4,16,1]{1,2,0:T(1,128)S(1)}, s32[4,16,1]{1,2,0:T(1,128)}, u32[]{:S(2)}) copy-start(s32[4,16,1]{1,2,0:T(1,128)} %param.5) | copy-start | bytes 772
  1.4 13.3 %collective-permute-start = (f32[2,3,32,8,128]{4,3,2,1,0:T(8,128)S(1)}, f32[2,3,32,8,128]{4,3,2,1,0:T(8,128)S(1)}, u32[]{:S(2)}, u32[]{:S(2)}) collective-permute-start(f32[2,3,32,8,128]{4,3,2,1,0:T(8,128)S(1)} %get-tuple-element.21), channel_id=1, source_target_pairs={{0,1},{1,0},{2,3},{3,2},{4,5},{5,4},{6,7},{7,6},{8,9},{9,8},{10,11... | collective-permute-start | bytes 2359304 | tf_op jit(solution)/shard_map/ppermute | solution.py:472
  1.9 20.6 %collective-permute-start.3 = (f32[3,2,128,128]{3,2,1,0:T(8,128)S(1)}, f32[3,2,128,128]{3,2,1,0:T(8,128)S(1)}, u32[]{:S(2)}, u32[]{:S(2)}) collective-permute-start(f32[3,2,128,128]{3,2,1,0:T(8,128)S(1)} %get-tuple-element.31), channel_id=1, source_target_pairs={{0,2},{2,4},{4,6},{6,0},{1,3},{3,5},{5,7},{7,1},{8,10},{10,12},{12... | collective-permute-start | bytes 1179656 | tf_op jit(solution)/shard_map/ppermute | solution.py:472
  4.5 19.4 %collective-permute-start.4 = (f32[3,2,128,128]{3,2,1,0:T(8,128)S(1)}, f32[3,2,128,128]{3,2,1,0:T(8,128)S(1)}, u32[]{:S(2)}, u32[]{:S(2)}) collective-permute-start(f32[3,2,128,128]{3,2,1,0:T(8,128)S(1)} %get-tuple-element.32), channel_id=1, source_target_pairs={{0,6},{2,0},{4,2},{6,4},{1,7},{3,1},{5,3},{7,5},{8,14},{10,8},{12,... | collective-permute-start | bytes 1179656 | tf_op jit(solution)/shard_map/ppermute | solution.py:472
  9.3 10.4 %collective-permute-start.1 = (f32[192,128]{1,0:T(8,128)S(1)}, f32[192,128]{1,0:T(8,128)S(1)}, u32[]{:S(2)}, u32[]{:S(2)}) collective-permute-start(f32[192,128]{1,0:T(8,128)S(1)} %get-tuple-element.25), channel_id=1, source_target_pairs={{0,8},{8,16},{16,24},{24,0},{1,9},{9,17},{17,25},{25,1},{2,10},{10... | collective-permute-start | bytes 294920 | tf_op jit(solution)/shard_map/ppermute | solution.py:472
  11.3 8.4 %collective-permute-start.2 = (f32[192,128]{1,0:T(8,128)S(1)}, f32[192,128]{1,0:T(8,128)S(1)}, u32[]{:S(2)}, u32[]{:S(2)}) collective-permute-start(f32[192,128]{1,0:T(8,128)S(1)} %get-tuple-element.26), channel_id=1, source_target_pairs={{0,24},{8,0},{16,8},{24,16},{1,25},{9,1},{17,9},{25,17},{2,26},{10... | collective-permute-start | bytes 294920 | tf_op jit(solution)/shard_map/ppermute | solution.py:472
  24.4 5.7 %collective-permute-start.7 = (f32[4,8,128]{2,1,0:T(8,128)S(1)}, f32[4,8,128]{2,1,0:T(8,128)S(1)}, u32[]{:S(2)}, u32[]{:S(2)}) collective-permute-start(f32[4,8,128]{2,1,0:T(8,128)S(1)} %get-tuple-element.35), channel_id=1, source_target_pairs={{0,24},{8,16},{16,8},{24,0},{1,25},{9,17},{17,9},{25,1},{2,26},{10... | collective-permute-start | bytes 49160 | tf_op jit(solution)/shard_map/ppermute | solution.py:492
  28.0 4.6 %collective-permute-start.6 = (f32[4,8,128]{2,1,0:T(8,128)S(1)}, f32[4,8,128]{2,1,0:T(8,128)S(1)}, u32[]{:S(2)}, u32[]{:S(2)}) collective-permute-start(f32[4,8,128]{2,1,0:T(8,128)S(1)} %get-tuple-element.36), channel_id=1, source_target_pairs={{0,16},{8,24},{16,0},{24,8},{1,17},{9,25},{17,1},{25,9},{2,18},{10... | collective-permute-start | bytes 49160 | tf_op jit(solution)/shard_map/ppermute | solution.py:492
  28.1 4.6 %collective-permute-start.5 = (f32[4,8,128]{2,1,0:T(8,128)S(1)}, f32[4,8,128]{2,1,0:T(8,128)S(1)}, u32[]{:S(2)}, u32[]{:S(2)}) collective-permute-start(f32[4,8,128]{2,1,0:T(8,128)S(1)} %get-tuple-element.37), channel_id=1, source_target_pairs={{0,8},{8,0},{16,24},{24,16},{1,9},{9,1},{17,25},{25,17},{2,10},{10... | collective-permute-start | bytes 49160 | tf_op jit(solution)/shard_map/ppermute | solution.py:492

commit v6 on v5

--- a/solution.py
+++ b/solution.py
@@ -423,19 +423,12 @@
 
 
 def edge_kernel(
-    density, middle_ref, raw_ref, kept_ref, scale_ref, fix_ref, first_ref, xleft_ref, xright_ref,
-    image_ref, sum_ref, level_ref, sums_ref,
+    density, raw_ref, kept_ref, scale_ref, fix_ref, first_ref, xleft_ref, xright_ref,
+    own_ref, *refs,
 ):
+    *sent_refs, sum_ref, level_ref, sums_ref = refs
     nx, ny, nz = raw_ref.shape
     summing(sum_ref)
-    views = image_ref.shape[0]
-    me = lax.axis_index("view")
-
-    def slot(view):
-        return step_to(me, view, views)
-
-    for view in range(views):
-        image_ref[slot(view)] = middle_ref[view]
     raws = []
     for place, x in enumerate(edge_rows(nx)):
         if place == 0:
@@ -450,21 +443,33 @@
         more = ghost[0] * (0.5 * ghost[0] + kept_ref[place, 0]) + ghost[1] * kept_ref[place, 1] + ghost[2] * depth
         raws.append(raw_ref[x] + on_border(fix_ref[...], x) + more * scale_ref[x // SUB])
     gather(density, raws, level_ref, sums_ref, sum_ref)
-    for place, x in enumerate(edge_rows(nx)):
-        blend(level_ref, sums_ref, place, put(image_ref, x, slot))
-
-
-def edged(density, middle, raw, *rest):
+
+    def put_edge(place):
+        def store(*channels):
+            for k, values in enumerate(channels):
+                own_ref[place // 2, pl.ds(2 * k + place % 2, 1), :] = values
+
+        return store
+
+    for place in range(4):
+        blend(level_ref, sums_ref, place, put_edge(place))
+    me = lax.axis_index("view")
+    for step, sent_ref in enumerate(sent_refs, 1):
+        sent_ref[...] = jnp.where(me == step, own_ref[0], own_ref[1])
+
+
+def edged(density, raw, *rest, views):
     nx, ny, nz = raw.shape
+    rows = jax.ShapeDtypeStruct((8, ny), jnp.float32)
     return pl.pallas_call(
         functools.partial(edge_kernel, density),
-        out_shape=jax.ShapeDtypeStruct(middle.shape, jnp.float32),
-        in_specs=[VMEM] * 8,
-        out_specs=VMEM,
+        out_shape=(jax.ShapeDtypeStruct((2, 8, ny), jnp.float32),) + (rows,) * (views - 1),
+        in_specs=[VMEM] * 7,
+        out_specs=(VMEM,) * views,
         scratch_shapes=row_tables(4, ny, nz, 1),
         compiler_params=PARAMS,
         cost_estimate=COST,
-    )(middle, raw, *rest)
+    )(raw, *rest)
 
 
 def turn(block, axis, by):
@@ -479,50 +484,78 @@
     return turn(tail_head[0], axis, 1), turn(tail_head[1], axis, -1)
 
 
-def step_to(me, other, count):
-    return me ^ other if count & (count - 1) == 0 else lax.rem(other - me + count, count)
-
-
-def exchanged(blocks, axis):
-    count = lax.axis_size(axis)
-    paired = count & (count - 1) == 0
-    found = [blocks[0]]
-    for step in range(count - 1, 0, -1):
-        route = [(i, i ^ step if paired else (i + step) % count) for i in range(count)]
-        found.insert(1, lax.ppermute(blocks[step], axis, route))
+def owners_edges(sent, views):
+    found = []
+    for step, rows in enumerate(sent, 1):
+        mirror = views - 1 - step
+        if mirror == step:
+            received = [lax.ppermute(rows, "view", [(step, owner)]) for owner in (0, views - 1)]
+            found.append(jnp.where(lax.axis_index("view") == 0, *received))
+        else:
+            found.append(lax.ppermute(rows, "view", [(step, 0), (mirror, views - 1)]))
     return found
 
 
-def composite_kernel(*refs):
-    *image_refs, out_ref = refs
-    count = len(image_refs)
+def composite(images):
+    colour, through = images[0][:3], images[0][3]
+    for image in images[1:]:
+        colour = [front + through * behind for front, behind in zip(colour, image[:3])]
+        through = through * image[3]
+    return [*colour, 1.0 - through]
+
+
+def inside_kernel(gathered_hbm, out_ref, images_ref, sem):
+    copy = pltpu.make_async_copy(gathered_hbm.at[:, lax.axis_index("view")], images_ref, sem)
+    copy.start()
+    copy.wait()
+    block = composite([[images_ref[view, k] for k in range(4)] for view in range(images_ref.shape[0])])
+    for k in range(4):
+        out_ref[k] = block[k]
+
+
+def inside(gathered):
+    views, _, channels, rows, ny = gathered.shape
+    return pl.pallas_call(
+        inside_kernel,
+        out_shape=jax.ShapeDtypeStruct((channels, rows, ny), jnp.float32),
+        in_specs=[HBM],
+        out_specs=VMEM,
+        scratch_shapes=[pltpu.VMEM((views, channels, rows, ny), jnp.float32), pltpu.SemaphoreType.DMA],
+        compiler_params=pltpu.CompilerParams(vmem_limit_bytes=54 << 20),
+        cost_estimate=COST,
+    )(gathered)
+
+
+def finish_kernel(block_ref, own_ref, *refs):
+    *edge_refs, out_ref = refs
+    _, rows, ny = block_ref.shape
+    views = len(edge_refs) + 1
     me = lax.axis_index("view")
-    if count & (count - 1) == 0:
-        sources = [me ^ step for step in range(count)]
-    else:
-        sources = [lax.rem(me - step + count, count) for step in range(count)]
-    colour = [0.0] * 3
-    through = 1.0
-    for source, image_ref in zip(sources, image_refs):
-        passing = 1.0
-        for other, front_ref in zip(sources, image_refs):
-            passing = passing * jnp.where(other < source, front_ref[3], 1.0)
-        colour = [total + passing * image_ref[k] for k, total in enumerate(colour)]
-        through = through * image_ref[3]
-    for k in range(3):
-        out_ref[0, 0, k] = colour[k]
-    out_ref[0, 0, 3] = 1.0 - through
-
-
-def composited(images):
-    return pl.pallas_call(
-        composite_kernel,
-        out_shape=jax.ShapeDtypeStruct((1, 1) + images[0].shape, jnp.float32),
-        in_specs=[VMEM] * len(images),
+    out_ref[0, 0] = block_ref[...]
+
+    def channels(values):
+        return [values[2 * k : 2 * k + 2] for k in range(4)]
+
+    for owner, order, place in (
+        (0, [own_ref[0]] + [ref[...] for ref in edge_refs], 0),
+        (views - 1, [ref[...] for ref in edge_refs[::-1]] + [own_ref[1]], rows - 2),
+    ):
+
+        @pl.when(me == owner)
+        def _():
+            for k, values in enumerate(composite([channels(values) for values in order])):
+                out_ref[0, 0, k, pl.ds(place, 2), :] = values
+
+
+def finished(block, own, edges):
+    return pl.pallas_call(
+        finish_kernel,
+        out_shape=jax.ShapeDtypeStruct((1, 1) + block.shape, jnp.float32),
+        in_specs=[VMEM] * (2 + len(edges)),
         out_specs=VMEM,
         compiler_params=PARAMS,
         cost_estimate=COST,
-    )(*images)
+    )(block, own, *edges)
 
 
 def local(velocity, occupied, q_floor, q_span):
@@ -538,8 +571,9 @@
     yleft, yright = both_sides(yface, "gy")
     raw, pack, kept, scale = shaded(u, parts, yleft, yright, occupied[:, :, 0], q_floor, q_span)
     middle, fix, first = blended(density, views, raw, pack, scale, zleft, zright)
-    blocks = edged(density, middle, raw, kept, scale, fix, first, xleft, xright)
-    return composited(exchanged(blocks, "view"))
+    gathered = lax.all_gather(middle, "view")
+    own, *sent = edged(density, raw, kept, scale, fix, first, xleft, xright, views=views)
+    return finished(inside(gathered), own, owners_edges(sent, views))
 
 
 def solution(mesh):

time: 33.5 us -> 50.7 us (1.51)
  blocking collectives: 0 us -> 15.1 us
  waiting for transfers between devices: 5.13 us -> 1.28 us
  starting transfers between devices: 12.7 us -> 16.3 us
  Pallas kernels: 14.1 us -> 15.5 us
  local copies, waits for them, and re-layouts: 0.06 us -> 0.77 us
    all_gather x0 -> x1, blocking collectives: none -> 15.1 us  [local(): gathered = lax.all_gather(middle, 'view')]
    ppermute x3, waiting for transfers between devices: 3.85 us -> 0.01 us  [owners_edges(): found.append(lax.ppermute(rows, 'view', [(step, 0), (mirror, views - 1)]))]
    ppermute x3, starting transfers between devices: 4.45 us -> 8.1 us  [owners_edges(): found.append(lax.ppermute(rows, 'view', [(step, 0), (mirror, views - 1)]))]
    pallas_call x2 -> x3, Pallas kernels: 1.14 us -> 2.59 us  [the longest x1 1.46 us: inside(): pl.pallas_call(inside_kernel, out_shape=jax.ShapeDtypeStruct((channels, r...]
    unnamed x2 -> x4, local copies, waits for them, and re-layouts: 0.01 us -> 0.72 us
  transfers between devices with their start and end apart: 8 -> 8, of which waited for: 3 -> 1; matrix products, arithmetic and copies ran while one was open for 0% -> 0% of each run, Pallas kernels for 35% -> 26%
where the time goes in v6:
time: 50.7 us; the launch traced here: 50.4 us
  starting transfers between devices  16.3 us (32%)
  Pallas kernels  15.5 us (31%)
  blocking collectives  15.1 us (30%)
  between operations  1.44 us (3%)
  waiting for transfers between devices  1.28 us (3%)
  local copies, waits for them, and re-layouts  0.77 us (2%)
    all_gather x1, blocking collectives, local(): gathered = lax.all_gather(middle, 'view')  15.1 us
    ppermute x5, starting transfers between devices, turn(): lax.ppermute(block, axis, [(i, (i + by) % count) for i in range(count)])  8.22 us
    ppermute x3, starting transfers between devices, owners_edges(): found.append(lax.ppermute(rows, 'view', [(step, 0), (mirror, views - 1)]))  8.1 us
    pallas_call x1, Pallas kernels, shaded(): pl.pallas_call(shade_kernel, out_shape=(jax.ShapeDtypeStruct((nx, ny, nz)...  4.89 us
    pallas_call x1, Pallas kernels, faces(): pl.pallas_call(faces_kernel, out_shape=(jax.ShapeDtypeStruct(u.shape, jnp...  3.78 us
    pallas_call x1, Pallas kernels, blended(): pl.pallas_call(functools.partial(blend_kernel, density), out_shape=(jax.S...  2.83 us
    pallas_call x1, Pallas kernels, inside(): pl.pallas_call(inside_kernel, out_shape=jax.ShapeDtypeStruct((channels, r...  1.46 us
    pallas_call x1, Pallas kernels, ends(): pl.pallas_call(ends_kernel, out_shape=(layers, layers, jax.ShapeDtypeStru...  1.4 us
  transfers between devices with their start and end apart: 8, of which 1 were waited for; matrix products, arithmetic and copies ran while one was open for 0% of the time, Pallas kernels for 26%

profile of v6, /device:TPU:0, one launch (start us, length us, event | category | flops | bytes accessed | tf_op | source)
XLA Modules:
  0.0 50.4 jit_solution(12878973286813817119)
XLA Ops:
  0.0 0.0 copy-start.1
  0.0 1.4 %shard_map.47 = (f32[3,2,128,128]{3,2,1,0:T(8,128)S(1)}, f32[3,2,128,128]{3,2,1,0:T(8,128)S(1)}, f32[2,3,32,8,128]{4,3,2,1,0:T(8,128)S(1)}) custom-call(f32[3,32,128,128]{3,2,1,0:T(8,128)} %u_hbm.3), custom_call_target="tpu_custom_call" | custom-call | flops 1048576 | bytes 1048576 | tf_op jit(solution)/shard_map/pallas_call | solution.py:47
  1.4 0.5 %collective-permute-start = (f32[2,3,32,8,128]{4,3,2,1,0:T(8,128)S(1)}, f32[2,3,32,8,128]{4,3,2,1,0:T(8,128)S(1)}, u32[]{:S(2)}, u32[]{:S(2)}) collective-permute-start(f32[2,3,32,8,128]{4,3,2,1,0:T(8,128)S(1)} %get-tuple-element.25), channel_id=1, source_target_pairs={{0,1},{1,0},{2,3},{3,2},{4,5},{5,4},{6,7},{7,6},{8,9},{9,8},{10,11... | collective-permute-start | bytes 2359304 | tf_op jit(solution)/shard_map/ppermute | solution.py:477
  1.9 2.6 %collective-permute-start.3 = (f32[3,2,128,128]{3,2,1,0:T(8,128)S(1)}, f32[3,2,128,128]{3,2,1,0:T(8,128)S(1)}, u32[]{:S(2)}, u32[]{:S(2)}) collective-permute-start(f32[3,2,128,128]{3,2,1,0:T(8,128)S(1)} %get-tuple-element.35), channel_id=1, source_target_pairs={{0,2},{2,4},{4,6},{6,0},{1,3},{3,5},{5,7},{7,1},{8,10},{10,12},{12... | collective-permute-start | bytes 1179656 | tf_op jit(solution)/shard_map/ppermute | solution.py:477
  4.5 1.0 %collective-permute-start.4 = (f32[3,2,128,128]{3,2,1,0:T(8,128)S(1)}, f32[3,2,128,128]{3,2,1,0:T(8,128)S(1)}, u32[]{:S(2)}, u32[]{:S(2)}) collective-permute-start(f32[3,2,128,128]{3,2,1,0:T(8,128)S(1)} %get-tuple-element.36), channel_id=1, source_target_pairs={{0,6},{2,0},{4,2},{6,4},{1,7},{3,1},{5,3},{7,5},{8,14},{10,8},{12,... | collective-permute-start | bytes 1179656 | tf_op jit(solution)/shard_map/ppermute | solution.py:477
  5.5 3.8 %shard_map.46 = (f32[3,32,128,128]{3,2,1,0:T(8,128)S(1)}, bf16[3,32,128,256]{3,2,1,0:T(8,128)(2,1)S(1)}, f32[192,128]{1,0:T(8,128)S(1)}, f32[192,128]{1,0:T(8,128)S(1)}) custom-call(f32[3,32,128,128]{3,2,1,0:T(8,128)} %u_hbm.3), custom_call_target="tpu_custom_call" | custom-call | flops 1048576 | bytes 1048576 | tf_op jit(solution)/shard_map/pallas_call | solution.py:121
  9.3 2.0 %collective-permute-start.1 = (f32[192,128]{1,0:T(8,128)S(1)}, f32[192,128]{1,0:T(8,128)S(1)}, u32[]{:S(2)}, u32[]{:S(2)}) collective-permute-start(f32[192,128]{1,0:T(8,128)S(1)} %get-tuple-element.29), channel_id=1, source_target_pairs={{0,8},{8,16},{16,24},{24,0},{1,9},{9,17},{17,25},{25,1},{2,10},{10... | collective-permute-start | bytes 294920 | tf_op jit(solution)/shard_map/ppermute | solution.py:477
  11.3 2.1 %collective-permute-start.2 = (f32[192,128]{1,0:T(8,128)S(1)}, f32[192,128]{1,0:T(8,128)S(1)}, u32[]{:S(2)}, u32[]{:S(2)}) collective-permute-start(f32[192,128]{1,0:T(8,128)S(1)} %get-tuple-element.30), channel_id=1, source_target_pairs={{0,24},{8,0},{16,8},{24,16},{1,25},{9,1},{17,9},{25,17},{2,26},{10... | collective-permute-start | bytes 294920 | tf_op jit(solution)/shard_map/ppermute | solution.py:477
  14.7 0.0 collective-permute-done
  14.7 0.1 slice_bitcast_fusion
  14.8 0.0 copy-done.1
  14.8 4.9 %shard_map.48 = (f32[32,128,128]{2,1,0:T(8,128)S(1)}, f32[3,128,128]{2,1,0:T(8,128)S(1)}, f32[4,3,128,128]{3,2,1,0:T(8,128)S(1)}, f32[4,128,128]{2,1,0:T(8,128)S(1)}) custom-call(f32[3,32,128,128]{3,2,1,0:T(8,128)S(1)} %get-tuple-element.23.u_ref, bf16[3,32,128,256]{3,2,1,0:T(8,128)(2,1)S(1)} %get-tuple-element.24.parts_ref, ...), custom_call_target="tpu_custom_call" | custom-call | flops 1048576 | bytes 1048576 | tf_op jit(solution)/shard_map/pallas_call | solution.py:264
  19.7 0.0 collective-permute-done.1.zleft_ref
  19.7 0.0 collective-permute-done.2.zright_ref
  19.7 2.8 %shard_map.49 = (f32[4,4,8,128]{3,2,1,0:T(8,128)S(1)}, f32[128,128]{1,0:T(8,128)S(1)}, f32[128,128]{1,0:T(8,128)S(1)}) custom-call(f32[32,128,128]{2,1,0:T(8,128)S(1)} %get-tuple-element.26.raw_ref, f32[3,128,128]{2,1,0:T(8,128)S(1)} %get-tuple-element.27.pack_ref, f32[4,128,128]{2,1,0:T(8,128)S(1)} %get-tuple-element.28.scale_ref, ...), custom_call_target="tpu_custom_call" | custom-call | flops 1048576 | bytes 1048576 | tf_op jit(solution)/shard_map/pallas_call | solution.py:410
  22.6 0.0 collective-permute-done.3.xleft_ref
  22.6 1.3 %collective-permute-done.4.xright_ref = f32[3,2,128,128]{3,2,1,0:T(8,128)S(1)} collective-permute-done((f32[3,2,128,128]{3,2,1,0:T(8,128)S(1)}, f32[3,2,128,128]{3,2,1,0:T(8,128)S(1)}, u32[]{:S(2)}, u32[]{:S(2)}) %collective-permute-start.4) | collective-permute-done | bytes 393248 | tf_op jit(solution)/shard_map/ppermute | solution.py:477
  23.8 0.5 %shard_map.51 = (f32[2,8,128]{2,1,0:T(8,128)S(1)}, f32[8,128]{1,0:T(8,128)S(1)}, f32[8,128]{1,0:T(8,128)S(1)}, f32[8,128]{1,0:T(8,128)S(1)}) custom-call(f32[32,128,128]{2,1,0:T(8,128)S(1)} %get-tuple-element.26.raw_ref, f32[4,3,128,128]{3,2,1,0:T(8,128)S(1)} %get-tuple-element.32.kept_ref, f32[4,128,128]{2,1,0:T(8,128)S(1)} %get-tuple-element.28.scale_ref, ...), custom_call_target="tpu_custom_call" | custom-call | flops 1048576 | bytes 1048576 | tf_op jit(solution)/shard_map/pallas_call | solution.py:464
  24.4 1.3 %collective-permute-start.5 = (f32[8,128]{1,0:T(8,128)S(1)}, f32[8,128]{1,0:T(8,128)S(1)}, u32[]{:S(2)}, u32[]{:S(2)}) collective-permute-start(f32[8,128]{1,0:T(8,128)S(1)} %get-tuple-element.38), channel_id=1, source_target_pairs={{8,0},{16,24},{9,1},{17,25},{10,2},{18,26},{11,3},{19,27},{12,4},{... | collective-permute-start | bytes 12296 | tf_op jit(solution)/shard_map/ppermute | solution.py:495
  25.7 1.3 %collective-permute-start.6 = (f32[8,128]{1,0:T(8,128)S(1)}, f32[8,128]{1,0:T(8,128)S(1)}, u32[]{:S(2)}, u32[]{:S(2)}) collective-permute-start(f32[8,128]{1,0:T(8,128)S(1)} %get-tuple-element.39), channel_id=1, source_target_pairs={{16,0},{8,24},{17,1},{9,25},{18,2},{10,26},{19,3},{11,27},{20,4},{... | collective-permute-start | bytes 12296 | tf_op jit(solution)/shard_map/ppermute | solution.py:495
  27.0 5.5 %collective-permute-start.7 = (f32[8,128]{1,0:T(8,128)S(1)}, f32[8,128]{1,0:T(8,128)S(1)}, u32[]{:S(2)}, u32[]{:S(2)}) collective-permute-start(f32[8,128]{1,0:T(8,128)S(1)} %get-tuple-element.40), channel_id=1, source_target_pairs={{24,0},{0,24},{25,1},{1,25},{26,2},{2,26},{27,3},{3,27},{28,4},{4,... | collective-permute-start | bytes 12296 | tf_op jit(solution)/shard_map/ppermute | solution.py:495
  32.5 15.1 %all-gather = f32[16,4,8,128]{3,2,1,0:T(8,128)} all-gather(f32[4,4,8,128]{3,2,1,0:T(8,128)S(1)} %get-tuple-element.31), channel_id=2, replica_groups=mesh['view'=4,'gx'=4,'gy'=2] {'view'}, dimensions={0}, use_global_device_ids=true | all-gather | bytes 327680 | tf_op jit(solution)/shard_map/all_gather | solution.py:574
  47.5 1.5 %shard_map.50.block_ref = f32[4,8,128]{2,1,0:T(8,128)} custom-call(f32[4,4,4,8,128]{4,3,2,1,0:T(8,128)} %bitcast.7), custom_call_target="tpu_custom_call" | custom-call | flops 1048576 | bytes 1048576 | tf_op jit(solution)/shard_map/pallas_call | solution.py:518
  49.0 0.0 collective-permute-done.5.refs_0_
  49.0 0.0 collective-permute-done.6.refs_1_
  49.0 0.0 collective-permute-done.7.refs_2_
  49.0 0.0 copy-start
  49.1 0.7 %copy-done = f32[4,8,128]{2,1,0:T(8,128)S(1)} copy-done((f32[4,8,128]{2,1,0:T(8,128)S(1)}, f32[4,8,128]{2,1,0:T(8,128)}, u32[]{:S(2)}) %copy-start) | copy-done | bytes 16408
  49.8 0.6 %shard_map.52 = f32[1,1,4,8,128]{4,3,2,1,0:T(8,128)} custom-call(f32[4,8,128]{2,1,0:T(8,128)S(1)} %copy-done, f32[2,8,128]{2,1,0:T(8,128)S(1)} %get-tuple-element.37.own_ref, f32[8,128]{1,0:T(8,128)S(1)} %collective-permute-done.5.refs_0_, f32[8,128]{1,0:T(8,128)S(1)} %collective-permute-done.6.refs_1_, f32[8,128]{1,0:T(8,128)S(1)} %collective-permute-done.7.refs_2_), custom_call_target="tpu_custom_call" | custom-call | flops 1048576 | bytes 1048576 | tf_op jit(solution)/shard_map/pallas_call | solution.py:551
Async XLA Ops:
  0.0 14.8 %copy-start.1 = (s32[4,16,1]{1,2,0:T(1,128)S(1)}, s32[4,16,1]{1,2,0:T(1,128)}, u32[]{:S(2)}) copy-start(s32[4,16,1]{1,2,0:T(1,128)} %param.5) | copy-start | bytes 772
  1.4 13.3 %collective-permute-start = (f32[2,3,32,8,128]{4,3,2,1,0:T(8,128)S(1)}, f32[2,3,32,8,128]{4,3,2,1,0:T(8,128)S(1)}, u32[]{:S(2)}, u32[]{:S(2)}) collective-permute-start(f32[2,3,32,8,128]{4,3,2,1,0:T(8,128)S(1)} %get-tuple-element.25), channel_id=1, source_target_pairs={{0,1},{1,0},{2,3},{3,2},{4,5},{5,4},{6,7},{7,6},{8,9},{9,8},{10,11... | collective-permute-start | bytes 2359304 | tf_op jit(solution)/shard_map/ppermute | solution.py:477
  1.9 20.6 %collective-permute-start.3 = (f32[3,2,128,128]{3,2,1,0:T(8,128)S(1)}, f32[3,2,128,128]{3,2,1,0:T(8,128)S(1)}, u32[]{:S(2)}, u32[]{:S(2)}) collective-permute-start(f32[3,2,128,128]{3,2,1,0:T(8,128)S(1)} %get-tuple-element.35), channel_id=1, source_target_pairs={{0,2},{2,4},{4,6},{6,0},{1,3},{3,5},{5,7},{7,1},{8,10},{10,12},{12... | collective-permute-start | bytes 1179656 | tf_op jit(solution)/shard_map/ppermute | solution.py:477
  4.5 19.4 %collective-permute-start.4 = (f32[3,2,128,128]{3,2,1,0:T(8,128)S(1)}, f32[3,2,128,128]{3,2,1,0:T(8,128)S(1)}, u32[]{:S(2)}, u32[]{:S(2)}) collective-permute-start(f32[3,2,128,128]{3,2,1,0:T(8,128)S(1)} %get-tuple-element.36), channel_id=1, source_target_pairs={{0,6},{2,0},{4,2},{6,4},{1,7},{3,1},{5,3},{7,5},{8,14},{10,8},{12,... | collective-permute-start | bytes 1179656 | tf_op jit(solution)/shard_map/ppermute | solution.py:477
  9.3 10.4 %collective-permute-start.1 = (f32[192,128]{1,0:T(8,128)S(1)}, f32[192,128]{1,0:T(8,128)S(1)}, u32[]{:S(2)}, u32[]{:S(2)}) collective-permute-start(f32[192,128]{1,0:T(8,128)S(1)} %get-tuple-element.29), channel_id=1, source_target_pairs={{0,8},{8,16},{16,24},{24,0},{1,9},{9,17},{17,25},{25,1},{2,10},{10... | collective-permute-start | bytes 294920 | tf_op jit(solution)/shard_map/ppermute | solution.py:477
  11.3 8.4 %collective-permute-start.2 = (f32[192,128]{1,0:T(8,128)S(1)}, f32[192,128]{1,0:T(8,128)S(1)}, u32[]{:S(2)}, u32[]{:S(2)}) collective-permute-start(f32[192,128]{1,0:T(8,128)S(1)} %get-tuple-element.30), channel_id=1, source_target_pairs={{0,24},{8,0},{16,8},{24,16},{1,25},{9,1},{17,9},{25,17},{2,26},{10... | collective-permute-start | bytes 294920 | tf_op jit(solution)/shard_map/ppermute | solution.py:477
  24.4 24.7 %collective-permute-start.5 = (f32[8,128]{1,0:T(8,128)S(1)}, f32[8,128]{1,0:T(8,128)S(1)}, u32[]{:S(2)}, u32[]{:S(2)}) collective-permute-start(f32[8,128]{1,0:T(8,128)S(1)} %get-tuple-element.38), channel_id=1, source_target_pairs={{8,0},{16,24},{9,1},{17,25},{10,2},{18,26},{11,3},{19,27},{12,4},{... | collective-permute-start | bytes 12296 | tf_op jit(solution)/shard_map/ppermute | solution.py:495
  25.7 23.4 %collective-permute-start.6 = (f32[8,128]{1,0:T(8,128)S(1)}, f32[8,128]{1,0:T(8,128)S(1)}, u32[]{:S(2)}, u32[]{:S(2)}) collective-permute-start(f32[8,128]{1,0:T(8,128)S(1)} %get-tuple-element.39), channel_id=1, source_target_pairs={{16,0},{8,24},{17,1},{9,25},{18,2},{10,26},{19,3},{11,27},{20,4},{... | collective-permute-start | bytes 12296 | tf_op jit(solution)/shard_map/ppermute | solution.py:495
  27.0 22.1 %collective-permute-start.7 = (f32[8,128]{1,0:T(8,128)S(1)}, f32[8,128]{1,0:T(8,128)S(1)}, u32[]{:S(2)}, u32[]{:S(2)}) collective-permute-start(f32[8,128]{1,0:T(8,128)S(1)} %get-tuple-element.40), channel_id=1, source_target_pairs={{24,0},{0,24},{25,1},{1,25},{26,2},{2,26},{27,3},{3,27},{28,4},{4,... | collective-permute-start | bytes 12296 | tf_op jit(solution)/shard_map/ppermute | solution.py:495
  49.0 0.7 %copy-start = (f32[4,8,128]{2,1,0:T(8,128)S(1)}, f32[4,8,128]{2,1,0:T(8,128)}, u32[]{:S(2)}) copy-start(f32[4,8,128]{2,1,0:T(8,128)} %shard_map.50.block_ref) | copy-start | bytes 49156

commit v7 on v5

--- a/solution.py
+++ b/solution.py
@@ -31,8 +31,8 @@
     pieces = (
         (u_hbm.at[:, pl.ds(nx - 2, 2)], xtail_ref),
         (u_hbm.at[:, pl.ds(0, 2)], xhead_ref),
-        (u_hbm.at[:, :, pl.ds(ny - 8, 8)], yface_ref.at[0]),
-        (u_hbm.at[:, :, pl.ds(0, 8)], yface_ref.at[1]),
+        (u_hbm.at[:, :, pl.ds(ny - 2, 2)], yface_ref.at[:, :, pl.ds(6, 2)]),
+        (u_hbm.at[:, :, pl.ds(0, 2)], yface_ref.at[:, :, pl.ds(0, 2)]),
     )
     copies = [pltpu.make_async_copy(source, target, sems.at[k]) for k, (source, target) in enumerate(pieces)]
     for copy in copies:
@@ -46,7 +46,7 @@
     layers = jax.ShapeDtypeStruct((comps, 2, ny, nz), jnp.float32)
     return pl.pallas_call(
         ends_kernel,
-        out_shape=(layers, layers, jax.ShapeDtypeStruct((2, comps, nx, 8, nz), jnp.float32)),
+        out_shape=(layers, layers, jax.ShapeDtypeStruct((comps, nx, 8, nz), jnp.float32)),
         in_specs=[HBM],
         out_specs=(VMEM,) * 3,
         scratch_shapes=[pltpu.SemaphoreType.DMA((4,))],
@@ -228,10 +228,6 @@
             pack_ref[k, rows, :] = packs[k]
 
 
-def edge_rows(nx):
-    return (0, 1, nx - 2, nx - 1)
-
-
 def shade_kernel(
     u_ref, parts_ref, yleft_ref, yright_ref, occupied_ref, floor_ref, span_ref,
     raw_ref, pack_ref, kept_ref, scale_ref, offset_ref, dz_ref, dy_ref, slope0_ref, slope1_ref,
@@ -399,8 +395,7 @@
 
 def row_tables(batch, ny, nz, buffers):
     return (
-        [pltpu.VMEM((2 * nz, 2 * nz + ny), jnp.bfloat16)]
-        + [pltpu.VMEM((batch, ny, nz), jnp.float32)] * buffers
+        [pltpu.VMEM((batch, ny, nz), jnp.float32)] * buffers
         + [pltpu.VMEM((batch, ny, 2 * nz + ny), jnp.float32)] * buffers
     )
 
@@ -413,21 +408,40 @@
             jax.ShapeDtypeStruct((views, 4, nx // views, ny), jnp.float32),
             jax.ShapeDtypeStruct((ny, nz), jnp.float32),
             jax.ShapeDtypeStruct((ny, nz), jnp.float32),
+            jax.ShapeDtypeStruct((2 * nz, 2 * nz + ny), jnp.bfloat16),
         ),
         in_specs=[VMEM] * 5,
-        out_specs=(VMEM,) * 3,
+        out_specs=(VMEM,) * 4,
         scratch_shapes=row_tables(4, ny, nz, 2),
         compiler_params=PARAMS,
         cost_estimate=COST,
     )(raw, *rest)
 
 
-def edge_kernel(
-    density, middle_ref, raw_ref, kept_ref, scale_ref, fix_ref, first_ref, xleft_ref, xright_ref,
-    image_ref, sum_ref, level_ref, sums_ref,
+def edge_raw(x, place, ghost, raw_ref, kept_ref, scale_ref, fix_ref, first_ref):
+    depth = kept_ref[place, 2] + on_border(first_ref[...], x)
+    more = ghost[0] * (0.5 * ghost[0] + kept_ref[place, 0]) + ghost[1] * kept_ref[place, 1] + ghost[2] * depth
+    return raw_ref[x] + on_border(fix_ref[...], x) + more * scale_ref[x // SUB]
+
+
+def first_kernel(
+    density, image_in_ref, raw_ref, kept_ref, scale_ref, fix_ref, first_ref, sum_ref, xleft_ref,
+    image_ref, level_ref, sums_ref,
 ):
-    nx, ny, nz = raw_ref.shape
-    summing(sum_ref)
+    image_ref[...] = image_in_ref[...]
+    near = [xleft_ref[c, 1] for c in range(3)]
+    far = [xleft_ref[c, 0] - 8.0 * cells for c, cells in enumerate(near)]
+    edge_refs = (raw_ref, kept_ref, scale_ref, fix_ref, first_ref)
+    gather(density, [edge_raw(0, 0, far, *edge_refs), edge_raw(1, 1, near, *edge_refs)], level_ref, sums_ref, sum_ref)
+    for x in range(2):
+        blend(level_ref, sums_ref, x, put(image_ref, x))
+
+
+def last_kernel(
+    density, image_in_ref, raw_ref, kept_ref, scale_ref, fix_ref, first_ref, sum_ref, xright_ref,
+    image_ref, level_ref, sums_ref,
+):
+    nx = raw_ref.shape[0]
     views = image_ref.shape[0]
     me = lax.axis_index("view")
 
@@ -435,36 +449,27 @@
         return step_to(me, view, views)
 
     for view in range(views):
-        image_ref[slot(view)] = middle_ref[view]
-    raws = []
-    for place, x in enumerate(edge_rows(nx)):
-        if place == 0:
-            ghost = [xleft_ref[c, 0] - 8.0 * xleft_ref[c, 1] for c in range(3)]
-        elif place == 1:
-            ghost = [xleft_ref[c, 1] for c in range(3)]
-        elif place == 2:
-            ghost = [-xright_ref[c, 0] for c in range(3)]
-        else:
-            ghost = [8.0 * xright_ref[c, 0] - xright_ref[c, 1] for c in range(3)]
-        depth = kept_ref[place, 2] + on_border(first_ref[...], x)
-        more = ghost[0] * (0.5 * ghost[0] + kept_ref[place, 0]) + ghost[1] * kept_ref[place, 1] + ghost[2] * depth
-        raws.append(raw_ref[x] + on_border(fix_ref[...], x) + more * scale_ref[x // SUB])
+        image_ref[slot(view)] = image_in_ref[view]
+    near = [-xright_ref[c, 0] for c in range(3)]
+    far = [-8.0 * cells - xright_ref[c, 1] for c, cells in enumerate(near)]
+    edge_refs = (raw_ref, kept_ref, scale_ref, fix_ref, first_ref)
+    raws = [edge_raw(nx - 2, 2, near, *edge_refs), edge_raw(nx - 1, 3, far, *edge_refs)]
     gather(density, raws, level_ref, sums_ref, sum_ref)
-    for place, x in enumerate(edge_rows(nx)):
-        blend(level_ref, sums_ref, place, put(image_ref, x, slot))
-
-
-def edged(density, middle, raw, *rest):
+    for k in range(2):
+        blend(level_ref, sums_ref, k, put(image_ref, nx - 2 + k, slot))
+
+
+def edged(kernel, density, image, raw, *rest):
     nx, ny, nz = raw.shape
     return pl.pallas_call(
-        functools.partial(edge_kernel, density),
-        out_shape=jax.ShapeDtypeStruct(middle.shape, jnp.float32),
+        functools.partial(kernel, density),
+        out_shape=jax.ShapeDtypeStruct(image.shape, jnp.float32),
         in_specs=[VMEM] * 8,
         out_specs=VMEM,
-        scratch_shapes=row_tables(4, ny, nz, 1),
+        scratch_shapes=row_tables(2, ny, nz, 1),
         compiler_params=PARAMS,
         cost_estimate=COST,
-    )(middle, raw, *rest)
+    )(image, raw, *rest)
 
 
 def turn(block, axis, by):
@@ -472,11 +477,9 @@
     return lax.ppermute(block, axis, [(i, (i + by) % count) for i in range(count)])
 
 
-def both_sides(tail_head, axis):
-    if lax.axis_size(axis) == 2:
-        other = turn(tail_head, axis, 1)
-        return other[0], other[1]
-    return turn(tail_head[0], axis, 1), turn(tail_head[1], axis, -1)
+def both_sides(block, axis):
+    before = turn(block, axis, 1)
+    return before, before if lax.axis_size(axis) == 2 else turn(block, axis, -1)
 
 
 def step_to(me, other, count):
@@ -537,8 +540,10 @@
     zright = turn(zhead, "view", -1)
     yleft, yright = both_sides(yface, "gy")
     raw, pack, kept, scale = shaded(u, parts, yleft, yright, occupied[:, :, 0], q_floor, q_span)
-    middle, fix, first = blended(density, views, raw, pack, scale, zleft, zright)
-    blocks = edged(density, middle, raw, kept, scale, fix, first, xleft, xright)
+    image, fix, first, summer = blended(density, views, raw, pack, scale, zleft, zright)
+    shared = (raw, kept, scale, fix, first, summer)
+    image = edged(first_kernel, density, image, *shared, xleft)
+    blocks = edged(last_kernel, density, image, *shared, xright)
     return composited(exchanged(blocks, "view"))
 
 

time: 33.5 us -> 33.2 us (level)
    pallas_call x1 -> x2, Pallas kernels: 0.52 us -> 0.79 us  [edged(): pl.pallas_call(functools.partial(kernel, density), out_shape=jax.ShapeDty...]
  transfers between devices with their start and end apart: 8 -> 8, of which waited for: 3 -> 3; matrix products, arithmetic and copies ran while one was open for 0% -> 0% of each run, Pallas kernels for 35% -> 36%
where the time goes in v7:
time: 33.2 us; the launch traced here: 33 us
  Pallas kernels  14 us (42%)
  starting transfers between devices  12.7 us (38%)
  waiting for transfers between devices  4.91 us (15%)
  between operations  1.39 us (4%)
    ppermute x5, starting transfers between devices, turn(): lax.ppermute(block, axis, [(i, (i + by) % count) for i in range(count)])  8.22 us
    pallas_call x1, Pallas kernels, shaded(): pl.pallas_call(shade_kernel, out_shape=(jax.ShapeDtypeStruct((nx, ny, nz)...  4.77 us
    ppermute x3, starting transfers between devices, exchanged(): found.insert(1, lax.ppermute(blocks[step], axis, route))  4.45 us
    ppermute x3, waiting for transfers between devices, exchanged(): found.insert(1, lax.ppermute(blocks[step], axis, route))  3.85 us
    pallas_call x1, Pallas kernels, faces(): pl.pallas_call(faces_kernel, out_shape=(jax.ShapeDtypeStruct(u.shape, jnp...  3.78 us
    pallas_call x1, Pallas kernels, blended(): pl.pallas_call(functools.partial(blend_kernel, density), out_shape=(jax.S...  2.84 us
    pallas_call x1, Pallas kernels, ends(): pl.pallas_call(ends_kernel, out_shape=(layers, layers, jax.ShapeDtypeStru...  1.21 us
    ppermute x5, waiting for transfers between devices, turn(): lax.ppermute(block, axis, [(i, (i + by) % count) for i in range(count)])  1.06 us
  transfers between devices with their start and end apart: 8, of which 3 were waited for; matrix products, arithmetic and copies ran while one was open for 0% of the time, Pallas kernels for 36%

profile of v7, /device:TPU:0, one launch (start us, length us, event | category | flops | bytes accessed | tf_op | source)
XLA Modules:
  0.0 33.0 jit_solution(2556525099340737528)
XLA Ops:
  0.0 0.0 copy-start
  0.0 1.2 %shard_map.47 = (f32[3,2,128,128]{3,2,1,0:T(8,128)S(1)}, f32[3,2,128,128]{3,2,1,0:T(8,128)S(1)}, f32[3,32,8,128]{3,2,1,0:T(8,128)S(1)}) custom-call(f32[3,32,128,128]{3,2,1,0:T(8,128)} %u_hbm.3), custom_call_target="tpu_custom_call" | custom-call | flops 1048576 | bytes 1048576 | tf_op jit(solution)/shard_map/pallas_call | solution.py:47
  1.2 0.5 %collective-permute-start = (f32[3,32,8,128]{3,2,1,0:T(8,128)S(1)}, f32[3,32,8,128]{3,2,1,0:T(8,128)S(1)}, u32[]{:S(2)}, u32[]{:S(2)}) collective-permute-start(f32[3,32,8,128]{3,2,1,0:T(8,128)S(1)} %get-tuple-element.22), channel_id=1, source_target_pairs={{0,1},{1,0},{2,3},{3,2},{4,5},{5,4},{6,7},{7,6},{8,9},{9,8},{10,11... | collective-permute-start | bytes 1179656 | tf_op jit(solution)/shard_map/ppermute | solution.py:477
  1.7 2.6 %collective-permute-start.3 = (f32[3,2,128,128]{3,2,1,0:T(8,128)S(1)}, f32[3,2,128,128]{3,2,1,0:T(8,128)S(1)}, u32[]{:S(2)}, u32[]{:S(2)}) collective-permute-start(f32[3,2,128,128]{3,2,1,0:T(8,128)S(1)} %get-tuple-element.33), channel_id=1, source_target_pairs={{0,2},{2,4},{4,6},{6,0},{1,3},{3,5},{5,7},{7,1},{8,10},{10,12},{12... | collective-permute-start | bytes 1179656 | tf_op jit(solution)/shard_map/ppermute | solution.py:477
  4.3 1.0 %collective-permute-start.4 = (f32[3,2,128,128]{3,2,1,0:T(8,128)S(1)}, f32[3,2,128,128]{3,2,1,0:T(8,128)S(1)}, u32[]{:S(2)}, u32[]{:S(2)}) collective-permute-start(f32[3,2,128,128]{3,2,1,0:T(8,128)S(1)} %get-tuple-element.34), channel_id=1, source_target_pairs={{0,6},{2,0},{4,2},{6,4},{1,7},{3,1},{5,3},{7,5},{8,14},{10,8},{12,... | collective-permute-start | bytes 1179656 | tf_op jit(solution)/shard_map/ppermute | solution.py:477
  5.3 3.8 %shard_map.46 = (f32[3,32,128,128]{3,2,1,0:T(8,128)S(1)}, bf16[3,32,128,256]{3,2,1,0:T(8,128)(2,1)S(1)}, f32[192,128]{1,0:T(8,128)S(1)}, f32[192,128]{1,0:T(8,128)S(1)}) custom-call(f32[3,32,128,128]{3,2,1,0:T(8,128)} %u_hbm.3), custom_call_target="tpu_custom_call" | custom-call | flops 1048576 | bytes 1048576 | tf_op jit(solution)/shard_map/pallas_call | solution.py:121
  9.1 2.0 %collective-permute-start.1 = (f32[192,128]{1,0:T(8,128)S(1)}, f32[192,128]{1,0:T(8,128)S(1)}, u32[]{:S(2)}, u32[]{:S(2)}) collective-permute-start(f32[192,128]{1,0:T(8,128)S(1)} %get-tuple-element.26), channel_id=1, source_target_pairs={{0,8},{8,16},{16,24},{24,0},{1,9},{9,17},{17,25},{25,1},{2,10},{10... | collective-permute-start | bytes 294920 | tf_op jit(solution)/shard_map/ppermute | solution.py:477
  11.1 2.1 %collective-permute-start.2 = (f32[192,128]{1,0:T(8,128)S(1)}, f32[192,128]{1,0:T(8,128)S(1)}, u32[]{:S(2)}, u32[]{:S(2)}) collective-permute-start(f32[192,128]{1,0:T(8,128)S(1)} %get-tuple-element.27), channel_id=1, source_target_pairs={{0,24},{8,0},{16,8},{24,16},{1,25},{9,1},{17,9},{25,17},{2,26},{10... | collective-permute-start | bytes 294920 | tf_op jit(solution)/shard_map/ppermute | solution.py:477
  14.5 0.0 collective-permute-done.yleft_ref.yright_ref
  14.5 0.0 copy-done
  14.6 4.8 %shard_map.48 = (f32[32,128,128]{2,1,0:T(8,128)S(1)}, f32[3,128,128]{2,1,0:T(8,128)S(1)}, f32[4,3,128,128]{3,2,1,0:T(8,128)S(1)}, f32[4,128,128]{2,1,0:T(8,128)S(1)}) custom-call(f32[3,32,128,128]{3,2,1,0:T(8,128)S(1)} %get-tuple-element.20.u_ref, bf16[3,32,128,256]{3,2,1,0:T(8,128)(2,1)S(1)} %get-tuple-element.21.parts_ref, ...), custom_call_target="tpu_custom_call" | custom-call | flops 1048576 | bytes 1048576 | tf_op jit(solution)/shard_map/pallas_call | solution.py:260
  19.3 0.0 collective-permute-done.1.zleft_ref
  19.3 0.0 collective-permute-done.2.zright_ref
  19.4 2.8 %shard_map.49 = (f32[4,4,8,128]{3,2,1,0:T(8,128)S(1)}, f32[128,128]{1,0:T(8,128)S(1)}, f32[128,128]{1,0:T(8,128)S(1)}, bf16[256,384]{1,0:T(8,128)(2,1)S(1)}) custom-call(f32[32,128,128]{2,1,0:T(8,128)S(1)} %get-tuple-element.23.raw_ref, f32[3,128,128]{2,1,0:T(8,128)S(1)} %get-tuple-element.24.pack_ref, f32[4,128,128]{2,1,0:T(8,128)S(1)} %get-tuple-element.25.scale_ref, ...), custom_call_target="tpu_custom_call" | custom-call | flops 1048576 | bytes 1048576 | tf_op jit(solution)/shard_map/pallas_call | solution.py:405
  22.2 0.0 collective-permute-done.3.xleft_ref
  22.2 0.4 %shard_map.50.image_in_ref = f32[4,4,8,128]{3,2,1,0:T(8,128)S(1)} custom-call(f32[4,4,8,128]{3,2,1,0:T(8,128)S(1)} %get-tuple-element.28.image_in_ref, f32[32,128,128]{2,1,0:T(8,128)S(1)} %get-tuple-element.23.raw_ref, f32[4,3,128,128]{3,2,1,0:T(8,128)S(1)} %get-tuple-element.29.kept_ref, f32[4,128,128]{2,1,0:T(8,128)S(1)} %get-tuple-element.25.scale_ref, ...), custom_call_target="tpu_custom_call" | custom-call | flops 1048576 | bytes 1048576 | tf_op jit(solution)/shard_map/pallas_call | solution.py:464
  22.6 1.0 %collective-permute-done.4.xright_ref = f32[3,2,128,128]{3,2,1,0:T(8,128)S(1)} collective-permute-done((f32[3,2,128,128]{3,2,1,0:T(8,128)S(1)}, f32[3,2,128,128]{3,2,1,0:T(8,128)S(1)}, u32[]{:S(2)}, u32[]{:S(2)}) %collective-permute-start.4) | collective-permute-done | bytes 393248 | tf_op jit(solution)/shard_map/ppermute | solution.py:477
  23.6 0.4 %shard_map.51 = f32[4,4,8,128]{3,2,1,0:T(8,128)S(1)} custom-call(f32[4,4,8,128]{3,2,1,0:T(8,128)S(1)} %shard_map.50.image_in_ref, f32[32,128,128]{2,1,0:T(8,128)S(1)} %get-tuple-element.23.raw_ref, f32[4,3,128,128]{3,2,1,0:T(8,128)S(1)} %get-tuple-element.29.kept_ref, f32[4,128,128]{2,1,0:T(8,128)S(1)} %get-tuple-element.25.scale_ref, ...), custom_call_target="tpu_custom_call" | custom-call | flops 1048576 | bytes 1048576 | tf_op jit(solution)/shard_map/pallas_call | solution.py:464
  24.1 3.7 %collective-permute-start.7 = (f32[4,8,128]{2,1,0:T(8,128)S(1)}, f32[4,8,128]{2,1,0:T(8,128)S(1)}, u32[]{:S(2)}, u32[]{:S(2)}) collective-permute-start(f32[4,8,128]{2,1,0:T(8,128)S(1)} %get-tuple-element.35), channel_id=1, source_target_pairs={{0,24},{8,16},{16,8},{24,0},{1,25},{9,17},{17,9},{25,1},{2,26},{10... | collective-permute-start | bytes 49160 | tf_op jit(solution)/shard_map/ppermute | solution.py:495
  27.7 0.0 collective-permute-start.6
  27.7 0.8 %collective-permute-start.5 = (f32[4,8,128]{2,1,0:T(8,128)S(1)}, f32[4,8,128]{2,1,0:T(8,128)S(1)}, u32[]{:S(2)}, u32[]{:S(2)}) collective-permute-start(f32[4,8,128]{2,1,0:T(8,128)S(1)} %get-tuple-element.37), channel_id=1, source_target_pairs={{0,8},{8,0},{16,24},{24,16},{1,9},{9,1},{17,25},{25,17},{2,10},{10... | collective-permute-start | bytes 49160 | tf_op jit(solution)/shard_map/ppermute | solution.py:495
  28.5 1.2 %collective-permute-done.7.refs_3_ = f32[4,8,128]{2,1,0:T(8,128)S(1)} collective-permute-done((f32[4,8,128]{2,1,0:T(8,128)S(1)}, f32[4,8,128]{2,1,0:T(8,128)S(1)}, u32[]{:S(2)}, u32[]{:S(2)}) %collective-permute-start.7) | collective-permute-done | bytes 16416 | tf_op jit(solution)/shard_map/ppermute | solution.py:495
  29.7 2.6 %collective-permute-done.6.refs_2_ = f32[4,8,128]{2,1,0:T(8,128)S(1)} collective-permute-done((f32[4,8,128]{2,1,0:T(8,128)S(1)}, f32[4,8,128]{2,1,0:T(8,128)S(1)}, u32[]{:S(2)}, u32[]{:S(2)}) %collective-permute-start.6) | collective-permute-done | bytes 16416 | tf_op jit(solution)/shard_map/ppermute | solution.py:495
  32.4 0.0 collective-permute-done.5.refs_1_
  32.4 0.6 %shard_map.52 = f32[1,1,4,8,128]{4,3,2,1,0:T(8,128)} custom-call(f32[4,8,128]{2,1,0:T(8,128)S(1)} %get-tuple-element.38.refs_0_, f32[4,8,128]{2,1,0:T(8,128)S(1)} %collective-permute-done.5.refs_1_, f32[4,8,128]{2,1,0:T(8,128)S(1)} %collective-permute-done.6.refs_2_, f32[4,8,128]{2,1,0:T(8,128)S(1)} %collective-permute-done.7.refs_3_), custom_call_target="tpu_custom_call" | custom-call | flops 1048576 | bytes 1048576 | tf_op jit(solution)/shard_map/pallas_call | solution.py:521
  (1 shorter events, 0.0 us)
Async XLA Ops:
  0.0 14.5 %copy-start = (s32[4,16,1]{1,2,0:T(1,128)S(1)}, s32[4,16,1]{1,2,0:T(1,128)}, u32[]{:S(2)}) copy-start(s32[4,16,1]{1,2,0:T(1,128)} %param.5) | copy-start | bytes 772
  1.2 13.3 %collective-permute-start = (f32[3,32,8,128]{3,2,1,0:T(8,128)S(1)}, f32[3,32,8,128]{3,2,1,0:T(8,128)S(1)}, u32[]{:S(2)}, u32[]{:S(2)}) collective-permute-start(f32[3,32,8,128]{3,2,1,0:T(8,128)S(1)} %get-tuple-element.22), channel_id=1, source_target_pairs={{0,1},{1,0},{2,3},{3,2},{4,5},{5,4},{6,7},{7,6},{8,9},{9,8},{10,11... | collective-permute-start | bytes 1179656 | tf_op jit(solution)/shard_map/ppermute | solution.py:477
  1.7 20.5 %collective-permute-start.3 = (f32[3,2,128,128]{3,2,1,0:T(8,128)S(1)}, f32[3,2,128,128]{3,2,1,0:T(8,128)S(1)}, u32[]{:S(2)}, u32[]{:S(2)}) collective-permute-start(f32[3,2,128,128]{3,2,1,0:T(8,128)S(1)} %get-tuple-element.33), channel_id=1, source_target_pairs={{0,2},{2,4},{4,6},{6,0},{1,3},{3,5},{5,7},{7,1},{8,10},{10,12},{12... | collective-permute-start | bytes 1179656 | tf_op jit(solution)/shard_map/ppermute | solution.py:477
  4.3 19.4 %collective-permute-start.4 = (f32[3,2,128,128]{3,2,1,0:T(8,128)S(1)}, f32[3,2,128,128]{3,2,1,0:T(8,128)S(1)}, u32[]{:S(2)}, u32[]{:S(2)}) collective-permute-start(f32[3,2,128,128]{3,2,1,0:T(8,128)S(1)} %get-tuple-element.34), channel_id=1, source_target_pairs={{0,6},{2,0},{4,2},{6,4},{1,7},{3,1},{5,3},{7,5},{8,14},{10,8},{12,... | collective-permute-start | bytes 1179656 | tf_op jit(solution)/shard_map/ppermute | solution.py:477
  9.1 10.2 %collective-permute-start.1 = (f32[192,128]{1,0:T(8,128)S(1)}, f32[192,128]{1,0:T(8,128)S(1)}, u32[]{:S(2)}, u32[]{:S(2)}) collective-permute-start(f32[192,128]{1,0:T(8,128)S(1)} %get-tuple-element.26), channel_id=1, source_target_pairs={{0,8},{8,16},{16,24},{24,0},{1,9},{9,17},{17,25},{25,1},{2,10},{10... | collective-permute-start | bytes 294920 | tf_op jit(solution)/shard_map/ppermute | solution.py:477
  11.1 8.2 %collective-permute-start.2 = (f32[192,128]{1,0:T(8,128)S(1)}, f32[192,128]{1,0:T(8,128)S(1)}, u32[]{:S(2)}, u32[]{:S(2)}) collective-permute-start(f32[192,128]{1,0:T(8,128)S(1)} %get-tuple-element.27), channel_id=1, source_target_pairs={{0,24},{8,0},{16,8},{24,16},{1,25},{9,1},{17,9},{25,17},{2,26},{10... | collective-permute-start | bytes 294920 | tf_op jit(solution)/shard_map/ppermute | solution.py:477
  24.1 5.7 %collective-permute-start.7 = (f32[4,8,128]{2,1,0:T(8,128)S(1)}, f32[4,8,128]{2,1,0:T(8,128)S(1)}, u32[]{:S(2)}, u32[]{:S(2)}) collective-permute-start(f32[4,8,128]{2,1,0:T(8,128)S(1)} %get-tuple-element.35), channel_id=1, source_target_pairs={{0,24},{8,16},{16,8},{24,0},{1,25},{9,17},{17,9},{25,1},{2,26},{10... | collective-permute-start | bytes 49160 | tf_op jit(solution)/shard_map/ppermute | solution.py:495
  27.7 4.6 %collective-permute-start.6 = (f32[4,8,128]{2,1,0:T(8,128)S(1)}, f32[4,8,128]{2,1,0:T(8,128)S(1)}, u32[]{:S(2)}, u32[]{:S(2)}) collective-permute-start(f32[4,8,128]{2,1,0:T(8,128)S(1)} %get-tuple-element.36), channel_id=1, source_target_pairs={{0,16},{8,24},{16,0},{24,8},{1,17},{9,25},{17,1},{25,9},{2,18},{10... | collective-permute-start | bytes 49160 | tf_op jit(solution)/shard_map/ppermute | solution.py:495
  27.7 4.6 %collective-permute-start.5 = (f32[4,8,128]{2,1,0:T(8,128)S(1)}, f32[4,8,128]{2,1,0:T(8,128)S(1)}, u32[]{:S(2)}, u32[]{:S(2)}) collective-permute-start(f32[4,8,128]{2,1,0:T(8,128)S(1)} %get-tuple-element.37), channel_id=1, source_target_pairs={{0,8},{8,0},{16,24},{24,16},{1,9},{9,1},{17,25},{25,17},{2,10},{10... | collective-permute-start | bytes 49160 | tf_op jit(solution)/shard_map/ppermute | solution.py:495

commit v8 on v7

--- a/solution.py
+++ b/solution.py
@@ -26,36 +26,26 @@
     return lax.broadcasted_iota(jnp.int32, shape, dim)
 
 
-def ends_kernel(u_hbm, xtail_ref, xhead_ref, yface_ref, sems):
-    _, nx, ny, _ = u_hbm.shape
-    pieces = (
-        (u_hbm.at[:, pl.ds(nx - 2, 2)], xtail_ref),
-        (u_hbm.at[:, pl.ds(0, 2)], xhead_ref),
-        (u_hbm.at[:, :, pl.ds(ny - 2, 2)], yface_ref.at[:, :, pl.ds(6, 2)]),
-        (u_hbm.at[:, :, pl.ds(0, 2)], yface_ref.at[:, :, pl.ds(0, 2)]),
-    )
-    copies = [pltpu.make_async_copy(source, target, sems.at[k]) for k, (source, target) in enumerate(pieces)]
-    for copy in copies:
-        copy.start()
-    for copy in copies:
-        copy.wait()
-
-
-def ends(u):
-    comps, nx, ny, nz = u.shape
-    layers = jax.ShapeDtypeStruct((comps, 2, ny, nz), jnp.float32)
+def layers_kernel(start, u_hbm, out_ref, sem):
+    copy = pltpu.make_async_copy(u_hbm.at[:, pl.ds(start, 2)], out_ref, sem)
+    copy.start()
+    copy.wait()
+
+
+def layers(u, start):
+    comps, _, ny, nz = u.shape
     return pl.pallas_call(
-        ends_kernel,
-        out_shape=(layers, layers, jax.ShapeDtypeStruct((comps, nx, 8, nz), jnp.float32)),
+        functools.partial(layers_kernel, start),
+        out_shape=jax.ShapeDtypeStruct((comps, 2, ny, nz), jnp.float32),
         in_specs=[HBM],
-        out_specs=(VMEM,) * 3,
-        scratch_shapes=[pltpu.SemaphoreType.DMA((4,))],
+        out_specs=VMEM,
+        scratch_shapes=[pltpu.SemaphoreType.DMA],
         compiler_params=pltpu.CompilerParams(vmem_limit_bytes=50 << 20),
         cost_estimate=COST,
     )(u)
 
 
-def faces_kernel(u_hbm, u_ref, parts_ref, tail_ref, head_ref, packed_ref, sems):
+def faces_kernel(u_hbm, u_ref, parts_ref, yface_ref, tail_ref, head_ref, packed_ref, sems):
     comps, nx, ny, nz = u_ref.shape
     quarters = sems.shape[1]
     rows = ny // quarters
@@ -87,6 +77,11 @@
             return carry
 
         lax.fori_loop(0, quarters, quarter, 0)
+    sub = iota((8, nz), 0)
+    for c in range(comps):
+        for x in range(nx):
+            lines = jnp.where(sub >= 6, u_ref[c, x, pl.ds(ny - 8, 8), :], u_ref[c, x, pl.ds(0, 8), :])
+            yface_ref[c, x] = pltpu.roll(lines, 2, 0)[:4]
     tails, heads = fold([packed_ref[c] for c in range(comps)], ny, nz)
     tail_ref[...] = tails
     head_ref[...] = heads
@@ -123,11 +118,12 @@
         out_shape=(
             jax.ShapeDtypeStruct(u.shape, jnp.float32),
             jax.ShapeDtypeStruct((comps, nx, ny, 2 * nz), jnp.bfloat16),
+            jax.ShapeDtypeStruct((comps, nx, 4, nz), jnp.float32),
             message,
             message,
         ),
         in_specs=[HBM],
-        out_specs=(VMEM,) * 4,
+        out_specs=(VMEM,) * 5,
         scratch_shapes=[pltpu.VMEM((comps, ny, nz), jnp.float32), pltpu.SemaphoreType.DMA((comps, 4))],
         compiler_params=pltpu.CompilerParams(vmem_limit_bytes=37 << 20),
         cost_estimate=COST,
@@ -163,11 +159,12 @@
     sub = iota((8, nz), 0)
 
     def top(left):
-        return jnp.where(sub < 2, pltpu.roll(left, 2, 0) - jnp.where(sub == 0, 8.0 * pltpu.roll(left, 1, 0), 0.0), 0.0)
+        lines = jnp.concatenate([left, left], axis=0)
+        return jnp.where(sub < 2, lines - jnp.where(sub == 0, 8.0 * pltpu.roll(lines, 7, 0), 0.0), 0.0)
 
     def low(right):
-        far = pltpu.roll(right, 6, 0)
-        return jnp.where(sub >= 6, jnp.where(sub == 7, 8.0 * pltpu.roll(right, 7, 0), 0.0) - far, 0.0)
+        lines = jnp.concatenate([right, right], axis=0)
+        return jnp.where(sub >= 6, jnp.where(sub == 7, 8.0 * pltpu.roll(lines, 1, 0), 0.0) - lines, 0.0)
 
     parts = [[parts_ref[c, x + k] for k in range(2)] for c in range(comps)]
     depth = jnp.dot(
@@ -482,28 +479,36 @@
     return before, before if lax.axis_size(axis) == 2 else turn(block, axis, -1)
 
 
+def exchange(count):
+    if count == 4:
+        return [(1, 0, 3, 2), (3, 2, 0, 1), (2, 3, 1, 0)]
+    if count & (count - 1) == 0:
+        return [tuple(i ^ step for i in range(count)) for step in range(1, count)]
+    return [tuple((i + step) % count for i in range(count)) for step in range(1, count)]
+
+
+def looked_up(index, table):
+    found = jnp.int32(table[0])
+    for place, entry in enumerate(table[1:], 1):
+        found = jnp.where(index == place, entry, found)
+    return found
+
+
 def step_to(me, other, count):
-    return me ^ other if count & (count - 1) == 0 else lax.rem(other - me + count, count)
+    steps = [(i,) + targets for i, targets in enumerate(zip(*exchange(count)))]
+    return looked_up(me, [targets.index(other) for targets in steps])
 
 
 def exchanged(blocks, axis):
-    count = lax.axis_size(axis)
-    paired = count & (count - 1) == 0
-    found = [blocks[0]]
-    for step in range(count - 1, 0, -1):
-        route = [(i, i ^ step if paired else (i + step) % count) for i in range(count)]
-        found.insert(1, lax.ppermute(blocks[step], axis, route))
-    return found
+    routes = exchange(lax.axis_size(axis))
+    return [blocks[0]] + [lax.ppermute(blocks[k], axis, list(enumerate(route))) for k, route in enumerate(routes, 1)]
 
 
 def composite_kernel(*refs):
     *image_refs, out_ref = refs
     count = len(image_refs)
     me = lax.axis_index("view")
-    if count & (count - 1) == 0:
-        sources = [me ^ step for step in range(count)]
-    else:
-        sources = [lax.rem(me - step + count, count) for step in range(count)]
+    sources = [me] + [looked_up(me, [route.index(i) for i in range(count)]) for route in exchange(count)]
     colour = [0.0] * 3
     through = 1.0
     for source, image_ref in zip(sources, image_refs):
@@ -532,10 +537,9 @@
     comps, nx, ny, nz = velocity.shape
     views = lax.axis_size("view")
     density = 5.0 / (nz * views)
-    xtail, xhead, yface = ends(velocity)
-    xleft = turn(xtail, "gx", 1)
-    xright = turn(xhead, "gx", -1)
-    u, parts, ztail, zhead = faces(velocity)
+    xleft = turn(layers(velocity, nx - 2), "gx", 1)
+    xright = turn(layers(velocity, 0), "gx", -1)
+    u, parts, yface, ztail, zhead = faces(velocity)
     zleft = turn(ztail, "view", 1)
     zright = turn(zhead, "view", -1)
     yleft, yright = both_sides(yface, "gy")

time: 33.2 us -> 33.7 us (1.015)
  Pallas kernels: 14 us -> 14.8 us
  starting transfers between devices: 12.7 us -> 12.1 us
    ppermute x3, waiting for transfers between devices: 3.85 us -> 5.09 us  [exchanged(): lax.ppermute(blocks[k], axis, list(enumerate(route)))]
    ppermute x5, waiting for transfers between devices: 1.06 us -> 0.01 us  [turn(): lax.ppermute(block, axis, [(i, (i + by) % count) for i in range(count)])]
    pallas_call x1 -> x2, Pallas kernels: 1.21 us -> 2.01 us  [layers(): pl.pallas_call(functools.partial(layers_kernel, start), out_shape=jax.Sha...]
    ppermute x3, starting transfers between devices: 4.45 us -> 3.84 us  [exchanged(): lax.ppermute(blocks[k], axis, list(enumerate(route)))]
  transfers between devices with their start and end apart: 8 -> 8, of which waited for: 3 -> 2; matrix products, arithmetic and copies ran while one was open for 0% -> 0% of each run, Pallas kernels for 36% -> 38%
where the time goes in v8:
time: 33.7 us; the launch traced here: 33.5 us
  Pallas kernels  14.8 us (44%)
  starting transfers between devices  12.1 us (36%)
  waiting for transfers between devices  5.1 us (15%)
  between operations  1.42 us (4%)
    ppermute x5, starting transfers between devices, turn(): lax.ppermute(block, axis, [(i, (i + by) % count) for i in range(count)])  8.29 us
    ppermute x3, waiting for transfers between devices, exchanged(): lax.ppermute(blocks[k], axis, list(enumerate(route)))  5.09 us
    pallas_call x1, Pallas kernels, shaded(): pl.pallas_call(shade_kernel, out_shape=(jax.ShapeDtypeStruct((nx, ny, nz)...  4.76 us
    ppermute x3, starting transfers between devices, exchanged(): lax.ppermute(blocks[k], axis, list(enumerate(route)))  3.84 us
    pallas_call x1, Pallas kernels, faces(): pl.pallas_call(faces_kernel, out_shape=(jax.ShapeDtypeStruct(u.shape, jnp...  3.78 us
    pallas_call x1, Pallas kernels, blended(): pl.pallas_call(functools.partial(blend_kernel, density), out_shape=(jax.S...  2.84 us
    pallas_call x2, Pallas kernels, layers(): pl.pallas_call(functools.partial(layers_kernel, start), out_shape=jax.Sha...  2.01 us
    pallas_call x2, Pallas kernels, edged(): pl.pallas_call(functools.partial(kernel, density), out_shape=jax.ShapeDty...  0.79 us
  transfers between devices with their start and end apart: 8, of which 2 were waited for; matrix products, arithmetic and copies ran while one was open for 0% of the time, Pallas kernels for 38%

profile of v8, /device:TPU:0, one launch (start us, length us, event | category | flops | bytes accessed | tf_op | source)
XLA Modules:
  0.0 33.5 jit_solution(4389036236772607871)
XLA Ops:
  0.0 1.0 %shard_map.49 = f32[3,2,128,128]{3,2,1,0:T(8,128)S(1)} custom-call(f32[3,32,128,128]{3,2,1,0:T(8,128)} %u_hbm.5), custom_call_target="tpu_custom_call" | custom-call | flops 1048576 | bytes 1048576 | tf_op jit(solution)/shard_map/pallas_call | solution.py:37
  1.0 0.0 copy-start
  1.0 3.0 %collective-permute-start.3 = (f32[3,2,128,128]{3,2,1,0:T(8,128)S(1)}, f32[3,2,128,128]{3,2,1,0:T(8,128)S(1)}, u32[]{:S(2)}, u32[]{:S(2)}) collective-permute-start(f32[3,2,128,128]{3,2,1,0:T(8,128)S(1)} %shard_map.49), channel_id=1, source_target_pairs={{0,2},{2,4},{4,6},{6,0},{1,3},{3,5},{5,7},{7,1},{8,10},{10,12},{12... | collective-permute-start | bytes 1179656 | tf_op jit(solution)/shard_map/ppermute | solution.py:474
  4.0 1.0 %shard_map.51 = f32[3,2,128,128]{3,2,1,0:T(8,128)S(1)} custom-call(f32[3,32,128,128]{3,2,1,0:T(8,128)} %u_hbm.5), custom_call_target="tpu_custom_call" | custom-call | flops 1048576 | bytes 1048576 | tf_op jit(solution)/shard_map/pallas_call | solution.py:37
  5.0 1.0 %collective-permute-start.4 = (f32[3,2,128,128]{3,2,1,0:T(8,128)S(1)}, f32[3,2,128,128]{3,2,1,0:T(8,128)S(1)}, u32[]{:S(2)}, u32[]{:S(2)}) collective-permute-start(f32[3,2,128,128]{3,2,1,0:T(8,128)S(1)} %shard_map.51), channel_id=1, source_target_pairs={{0,6},{2,0},{4,2},{6,4},{1,7},{3,1},{5,3},{7,5},{8,14},{10,8},{12,... | collective-permute-start | bytes 1179656 | tf_op jit(solution)/shard_map/ppermute | solution.py:474
  6.1 3.8 %shard_map.46 = (f32[3,32,128,128]{3,2,1,0:T(8,128)S(1)}, bf16[3,32,128,256]{3,2,1,0:T(8,128)(2,1)S(1)}, f32[3,32,4,128]{3,2,1,0:T(4,128)S(1)}, f32[192,128]{1,0:T(8,128)S(1)}, f32[192,128]{1,0:T(8,128)S(1)}) custom-call(f32[3,32,128,128]{3,2,1,0:T(8,128)} %u_hbm.5), custom_call_target="tpu_custom_call" | custom-call | flops 1048576 | bytes 1048576 | tf_op jit(solution)/shard_map/pallas_call | solution.py:116
  9.8 0.1 collective-permute-start
  9.9 2.1 %collective-permute-start.1 = (f32[192,128]{1,0:T(8,128)S(1)}, f32[192,128]{1,0:T(8,128)S(1)}, u32[]{:S(2)}, u32[]{:S(2)}) collective-permute-start(f32[192,128]{1,0:T(8,128)S(1)} %get-tuple-element.24), channel_id=1, source_target_pairs={{0,8},{8,16},{16,24},{24,0},{1,9},{9,17},{17,25},{25,1},{2,10},{10... | collective-permute-start | bytes 294920 | tf_op jit(solution)/shard_map/ppermute | solution.py:474
  12.0 2.1 %collective-permute-start.2 = (f32[192,128]{1,0:T(8,128)S(1)}, f32[192,128]{1,0:T(8,128)S(1)}, u32[]{:S(2)}, u32[]{:S(2)}) collective-permute-start(f32[192,128]{1,0:T(8,128)S(1)} %get-tuple-element.25), channel_id=1, source_target_pairs={{0,24},{8,0},{16,8},{24,16},{1,25},{9,1},{17,9},{25,17},{2,26},{10... | collective-permute-start | bytes 294920 | tf_op jit(solution)/shard_map/ppermute | solution.py:474
  15.4 0.0 collective-permute-done.yleft_ref.yright_ref
  15.4 0.0 copy-done
  15.4 4.8 %shard_map.47 = (f32[32,128,128]{2,1,0:T(8,128)S(1)}, f32[3,128,128]{2,1,0:T(8,128)S(1)}, f32[4,3,128,128]{3,2,1,0:T(8,128)S(1)}, f32[4,128,128]{2,1,0:T(8,128)S(1)}) custom-call(f32[3,32,128,128]{3,2,1,0:T(8,128)S(1)} %get-tuple-element.18.u_ref, bf16[3,32,128,256]{3,2,1,0:T(8,128)(2,1)S(1)} %get-tuple-element.19.parts_ref, ...), custom_call_target="tpu_custom_call" | custom-call | flops 1048576 | bytes 1048576 | tf_op jit(solution)/shard_map/pallas_call | solution.py:257
  20.2 0.0 collective-permute-done.1.zleft_ref
  20.2 0.0 collective-permute-done.2.zright_ref
  20.2 2.8 %shard_map.48 = (f32[4,4,8,128]{3,2,1,0:T(8,128)S(1)}, f32[128,128]{1,0:T(8,128)S(1)}, f32[128,128]{1,0:T(8,128)S(1)}, bf16[256,384]{1,0:T(8,128)(2,1)S(1)}) custom-call(f32[32,128,128]{2,1,0:T(8,128)S(1)} %get-tuple-element.21.raw_ref, f32[3,128,128]{2,1,0:T(8,128)S(1)} %get-tuple-element.22.pack_ref, f32[4,128,128]{2,1,0:T(8,128)S(1)} %get-tuple-element.23.scale_ref, ...), custom_call_target="tpu_custom_call" | custom-call | flops 1048576 | bytes 1048576 | tf_op jit(solution)/shard_map/pallas_call | solution.py:402
  23.1 0.0 collective-permute-done.3.xleft_ref
  23.1 0.4 %shard_map.50.image_in_ref = f32[4,4,8,128]{3,2,1,0:T(8,128)S(1)} custom-call(f32[4,4,8,128]{3,2,1,0:T(8,128)S(1)} %get-tuple-element.26.image_in_ref, f32[32,128,128]{2,1,0:T(8,128)S(1)} %get-tuple-element.21.raw_ref, f32[4,3,128,128]{3,2,1,0:T(8,128)S(1)} %get-tuple-element.27.kept_ref, f32[4,128,128]{2,1,0:T(8,128)S(1)} %get-tuple-element.23.scale_ref, ...), custom_call_target="tpu_custom_call" | custom-call | flops 1048576 | bytes 1048576 | tf_op jit(solution)/shard_map/pallas_call | solution.py:461
  23.5 0.0 collective-permute-done.4.xright_ref
  23.5 0.4 %shard_map.52 = f32[4,4,8,128]{3,2,1,0:T(8,128)S(1)} custom-call(f32[4,4,8,128]{3,2,1,0:T(8,128)S(1)} %shard_map.50.image_in_ref, f32[32,128,128]{2,1,0:T(8,128)S(1)} %get-tuple-element.21.raw_ref, f32[4,3,128,128]{3,2,1,0:T(8,128)S(1)} %get-tuple-element.27.kept_ref, f32[4,128,128]{2,1,0:T(8,128)S(1)} %get-tuple-element.23.scale_ref, ...), custom_call_target="tpu_custom_call" | custom-call | flops 1048576 | bytes 1048576 | tf_op jit(solution)/shard_map/pallas_call | solution.py:461
  23.9 0.9 %collective-permute-start.5 = (f32[4,8,128]{2,1,0:T(8,128)S(1)}, f32[4,8,128]{2,1,0:T(8,128)S(1)}, u32[]{:S(2)}, u32[]{:S(2)}) collective-permute-start(f32[4,8,128]{2,1,0:T(8,128)S(1)} %get-tuple-element.33), channel_id=1, source_target_pairs={{0,8},{8,0},{16,24},{24,16},{1,9},{9,1},{17,25},{25,17},{2,10},{10... | collective-permute-start | bytes 49160 | tf_op jit(solution)/shard_map/ppermute | solution.py:504
  24.8 2.5 %collective-permute-start.6 = (f32[4,8,128]{2,1,0:T(8,128)S(1)}, f32[4,8,128]{2,1,0:T(8,128)S(1)}, u32[]{:S(2)}, u32[]{:S(2)}) collective-permute-start(f32[4,8,128]{2,1,0:T(8,128)S(1)} %get-tuple-element.32), channel_id=1, source_target_pairs={{0,24},{8,16},{16,0},{24,8},{1,25},{9,17},{17,1},{25,9},{2,26},{10... | collective-permute-start | bytes 49160 | tf_op jit(solution)/shard_map/ppermute | solution.py:504
  27.3 0.4 %collective-permute-start.7 = (f32[4,8,128]{2,1,0:T(8,128)S(1)}, f32[4,8,128]{2,1,0:T(8,128)S(1)}, u32[]{:S(2)}, u32[]{:S(2)}) collective-permute-start(f32[4,8,128]{2,1,0:T(8,128)S(1)} %get-tuple-element.31), channel_id=1, source_target_pairs={{0,16},{8,24},{16,8},{24,0},{1,17},{9,25},{17,9},{25,1},{2,18},{10... | collective-permute-start | bytes 49160 | tf_op jit(solution)/shard_map/ppermute | solution.py:504
  27.7 0.0 collective-permute-done.5.refs_1_
  27.8 1.7 %collective-permute-done.6.refs_2_ = f32[4,8,128]{2,1,0:T(8,128)S(1)} collective-permute-done((f32[4,8,128]{2,1,0:T(8,128)S(1)}, f32[4,8,128]{2,1,0:T(8,128)S(1)}, u32[]{:S(2)}, u32[]{:S(2)}) %collective-permute-start.6) | collective-permute-done | bytes 16416 | tf_op jit(solution)/shard_map/ppermute | solution.py:504
  29.5 3.4 %collective-permute-done.7.refs_3_ = f32[4,8,128]{2,1,0:T(8,128)S(1)} collective-permute-done((f32[4,8,128]{2,1,0:T(8,128)S(1)}, f32[4,8,128]{2,1,0:T(8,128)S(1)}, u32[]{:S(2)}, u32[]{:S(2)}) %collective-permute-start.7) | collective-permute-done | bytes 16416 | tf_op jit(solution)/shard_map/ppermute | solution.py:504
  32.8 0.6 %shard_map.53 = f32[1,1,4,8,128]{4,3,2,1,0:T(8,128)} custom-call(f32[4,8,128]{2,1,0:T(8,128)S(1)} %get-tuple-element.34.refs_0_, f32[4,8,128]{2,1,0:T(8,128)S(1)} %collective-permute-done.5.refs_1_, f32[4,8,128]{2,1,0:T(8,128)S(1)} %collective-permute-done.6.refs_2_, f32[4,8,128]{2,1,0:T(8,128)S(1)} %collective-permute-done.7.refs_3_), custom_call_target="tpu_custom_call" | custom-call | flops 1048576 | bytes 1048576 | tf_op jit(solution)/shard_map/pallas_call | solution.py:526
  (1 shorter events, 0.0 us)
Async XLA Ops:
  1.0 14.4 %copy-start = (s32[4,16,1]{1,2,0:T(1,128)S(1)}, s32[4,16,1]{1,2,0:T(1,128)}, u32[]{:S(2)}) copy-start(s32[4,16,1]{1,2,0:T(1,128)} %param.5) | copy-start | bytes 772
  1.0 22.1 %collective-permute-start.3 = (f32[3,2,128,128]{3,2,1,0:T(8,128)S(1)}, f32[3,2,128,128]{3,2,1,0:T(8,128)S(1)}, u32[]{:S(2)}, u32[]{:S(2)}) collective-permute-start(f32[3,2,128,128]{3,2,1,0:T(8,128)S(1)} %shard_map.49), channel_id=1, source_target_pairs={{0,2},{2,4},{4,6},{6,0},{1,3},{3,5},{5,7},{7,1},{8,10},{10,12},{12... | collective-permute-start | bytes 1179656 | tf_op jit(solution)/shard_map/ppermute | solution.py:474
  5.0 18.5 %collective-permute-start.4 = (f32[3,2,128,128]{3,2,1,0:T(8,128)S(1)}, f32[3,2,128,128]{3,2,1,0:T(8,128)S(1)}, u32[]{:S(2)}, u32[]{:S(2)}) collective-permute-start(f32[3,2,128,128]{3,2,1,0:T(8,128)S(1)} %shard_map.51), channel_id=1, source_target_pairs={{0,6},{2,0},{4,2},{6,4},{1,7},{3,1},{5,3},{7,5},{8,14},{10,8},{12,... | collective-permute-start | bytes 1179656 | tf_op jit(solution)/shard_map/ppermute | solution.py:474
  9.8 5.6 %collective-permute-start = (f32[3,32,4,128]{3,2,1,0:T(4,128)S(1)}, f32[3,32,4,128]{3,2,1,0:T(4,128)S(1)}, u32[]{:S(2)}, u32[]{:S(2)}) collective-permute-start(f32[3,32,4,128]{3,2,1,0:T(4,128)S(1)} %get-tuple-element.20), channel_id=1, source_target_pairs={{0,1},{1,0},{2,3},{3,2},{4,5},{5,4},{6,7},{7,6},{8,9},{9,8},{10,11... | collective-permute-start | bytes 589832 | tf_op jit(solution)/shard_map/ppermute | solution.py:474
  9.9 10.3 %collective-permute-start.1 = (f32[192,128]{1,0:T(8,128)S(1)}, f32[192,128]{1,0:T(8,128)S(1)}, u32[]{:S(2)}, u32[]{:S(2)}) collective-permute-start(f32[192,128]{1,0:T(8,128)S(1)} %get-tuple-element.24), channel_id=1, source_target_pairs={{0,8},{8,16},{16,24},{24,0},{1,9},{9,17},{17,25},{25,1},{2,10},{10... | collective-permute-start | bytes 294920 | tf_op jit(solution)/shard_map/ppermute | solution.py:474
  12.0 8.2 %collective-permute-start.2 = (f32[192,128]{1,0:T(8,128)S(1)}, f32[192,128]{1,0:T(8,128)S(1)}, u32[]{:S(2)}, u32[]{:S(2)}) collective-permute-start(f32[192,128]{1,0:T(8,128)S(1)} %get-tuple-element.25), channel_id=1, source_target_pairs={{0,24},{8,0},{16,8},{24,16},{1,25},{9,1},{17,9},{25,17},{2,26},{10... | collective-permute-start | bytes 294920 | tf_op jit(solution)/shard_map/ppermute | solution.py:474
  23.9 3.8 %collective-permute-start.5 = (f32[4,8,128]{2,1,0:T(8,128)S(1)}, f32[4,8,128]{2,1,0:T(8,128)S(1)}, u32[]{:S(2)}, u32[]{:S(2)}) collective-permute-start(f32[4,8,128]{2,1,0:T(8,128)S(1)} %get-tuple-element.33), channel_id=1, source_target_pairs={{0,8},{8,0},{16,24},{24,16},{1,9},{9,1},{17,25},{25,17},{2,10},{10... | collective-permute-start | bytes 49160 | tf_op jit(solution)/shard_map/ppermute | solution.py:504
  24.8 4.6 %collective-permute-start.6 = (f32[4,8,128]{2,1,0:T(8,128)S(1)}, f32[4,8,128]{2,1,0:T(8,128)S(1)}, u32[]{:S(2)}, u32[]{:S(2)}) collective-permute-start(f32[4,8,128]{2,1,0:T(8,128)S(1)} %get-tuple-element.32), channel_id=1, source_target_pairs={{0,24},{8,16},{16,0},{24,8},{1,25},{9,17},{17,1},{25,9},{2,26},{10... | collective-permute-start | bytes 49160 | tf_op jit(solution)/shard_map/ppermute | solution.py:504
  27.3 5.5 %collective-permute-start.7 = (f32[4,8,128]{2,1,0:T(8,128)S(1)}, f32[4,8,128]{2,1,0:T(8,128)S(1)}, u32[]{:S(2)}, u32[]{:S(2)}) collective-permute-start(f32[4,8,128]{2,1,0:T(8,128)S(1)} %get-tuple-element.31), channel_id=1, source_target_pairs={{0,16},{8,24},{16,8},{24,0},{1,17},{9,25},{17,9},{25,1},{2,18},{10... | collective-permute-start | bytes 49160 | tf_op jit(solution)/shard_map/ppermute | solution.py:504

commit v9 on v8

--- a/solution.py
+++ b/solution.py
@@ -481,9 +481,9 @@
 
 def exchange(count):
     if count == 4:
-        return [(1, 0, 3, 2), (3, 2, 0, 1), (2, 3, 1, 0)]
+        return [(2, 3, 1, 0), (3, 2, 0, 1), (1, 0, 3, 2)]
     if count & (count - 1) == 0:
-        return [tuple(i ^ step for i in range(count)) for step in range(1, count)]
+        return [tuple(i ^ step for i in range(count)) for step in range(count - 1, 0, -1)]
     return [tuple((i + step) % count for i in range(count)) for step in range(1, count)]
 
 

time: 33.7 us -> 32.4 us (0.961)
  waiting for transfers between devices: 5.1 us -> 3.75 us
    ppermute x3, waiting for transfers between devices: 5.09 us -> 3.73 us  [exchanged(): lax.ppermute(blocks[k], axis, list(enumerate(route)))]
  transfers between devices with their start and end apart: 8 -> 8, of which waited for: 2 -> 3; matrix products, arithmetic and copies ran while one was open for 0% -> 0% of each run, Pallas kernels for 38% -> 40%
where the time goes in v9:
time: 32.4 us; the launch traced here: 32.2 us
  Pallas kernels  14.8 us (46%)
  starting transfers between devices  12.2 us (38%)
  waiting for transfers between devices  3.75 us (12%)
  between operations  1.42 us (4%)
    ppermute x5, starting transfers between devices, turn(): lax.ppermute(block, axis, [(i, (i + by) % count) for i in range(count)])  8.29 us
    pallas_call x1, Pallas kernels, shaded(): pl.pallas_call(shade_kernel, out_shape=(jax.ShapeDtypeStruct((nx, ny, nz)...  4.76 us
    ppermute x3, starting transfers between devices, exchanged(): lax.ppermute(blocks[k], axis, list(enumerate(route)))  3.88 us
    pallas_call x1, Pallas kernels, faces(): pl.pallas_call(faces_kernel, out_shape=(jax.ShapeDtypeStruct(u.shape, jnp...  3.78 us
    ppermute x3, waiting for transfers between devices, exchanged(): lax.ppermute(blocks[k], axis, list(enumerate(route)))  3.73 us
    pallas_call x1, Pallas kernels, blended(): pl.pallas_call(functools.partial(blend_kernel, density), out_shape=(jax.S...  2.84 us
    pallas_call x2, Pallas kernels, layers(): pl.pallas_call(functools.partial(layers_kernel, start), out_shape=jax.Sha...  2.01 us
    pallas_call x2, Pallas kernels, edged(): pl.pallas_call(functools.partial(kernel, density), out_shape=jax.ShapeDty...  0.79 us
  transfers between devices with their start and end apart: 8, of which 3 were waited for; matrix products, arithmetic and copies ran while one was open for 0% of the time, Pallas kernels for 40%

profile of v9, /device:TPU:0, one launch (start us, length us, event | category | flops | bytes accessed | tf_op | source)
XLA Modules:
  0.0 32.2 jit_solution(8847909917566543730)
XLA Ops:
  0.0 1.0 %shard_map.49 = f32[3,2,128,128]{3,2,1,0:T(8,128)S(1)} custom-call(f32[3,32,128,128]{3,2,1,0:T(8,128)} %u_hbm.5), custom_call_target="tpu_custom_call" | custom-call | flops 1048576 | bytes 1048576 | tf_op jit(solution)/shard_map/pallas_call | solution.py:37
  1.0 0.0 copy-start
  1.0 3.0 %collective-permute-start.3 = (f32[3,2,128,128]{3,2,1,0:T(8,128)S(1)}, f32[3,2,128,128]{3,2,1,0:T(8,128)S(1)}, u32[]{:S(2)}, u32[]{:S(2)}) collective-permute-start(f32[3,2,128,128]{3,2,1,0:T(8,128)S(1)} %shard_map.49), channel_id=1, source_target_pairs={{0,2},{2,4},{4,6},{6,0},{1,3},{3,5},{5,7},{7,1},{8,10},{10,12},{12... | collective-permute-start | bytes 1179656 | tf_op jit(solution)/shard_map/ppermute | solution.py:474
  4.0 1.0 %shard_map.51 = f32[3,2,128,128]{3,2,1,0:T(8,128)S(1)} custom-call(f32[3,32,128,128]{3,2,1,0:T(8,128)} %u_hbm.5), custom_call_target="tpu_custom_call" | custom-call | flops 1048576 | bytes 1048576 | tf_op jit(solution)/shard_map/pallas_call | solution.py:37
  5.0 1.0 %collective-permute-start.4 = (f32[3,2,128,128]{3,2,1,0:T(8,128)S(1)}, f32[3,2,128,128]{3,2,1,0:T(8,128)S(1)}, u32[]{:S(2)}, u32[]{:S(2)}) collective-permute-start(f32[3,2,128,128]{3,2,1,0:T(8,128)S(1)} %shard_map.51), channel_id=1, source_target_pairs={{0,6},{2,0},{4,2},{6,4},{1,7},{3,1},{5,3},{7,5},{8,14},{10,8},{12,... | collective-permute-start | bytes 1179656 | tf_op jit(solution)/shard_map/ppermute | solution.py:474
  6.1 3.8 %shard_map.46 = (f32[3,32,128,128]{3,2,1,0:T(8,128)S(1)}, bf16[3,32,128,256]{3,2,1,0:T(8,128)(2,1)S(1)}, f32[3,32,4,128]{3,2,1,0:T(4,128)S(1)}, f32[192,128]{1,0:T(8,128)S(1)}, f32[192,128]{1,0:T(8,128)S(1)}) custom-call(f32[3,32,128,128]{3,2,1,0:T(8,128)} %u_hbm.5), custom_call_target="tpu_custom_call" | custom-call | flops 1048576 | bytes 1048576 | tf_op jit(solution)/shard_map/pallas_call | solution.py:116
  9.8 0.1 collective-permute-start
  9.9 2.1 %collective-permute-start.1 = (f32[192,128]{1,0:T(8,128)S(1)}, f32[192,128]{1,0:T(8,128)S(1)}, u32[]{:S(2)}, u32[]{:S(2)}) collective-permute-start(f32[192,128]{1,0:T(8,128)S(1)} %get-tuple-element.24), channel_id=1, source_target_pairs={{0,8},{8,16},{16,24},{24,0},{1,9},{9,17},{17,25},{25,1},{2,10},{10... | collective-permute-start | bytes 294920 | tf_op jit(solution)/shard_map/ppermute | solution.py:474
  12.0 2.1 %collective-permute-start.2 = (f32[192,128]{1,0:T(8,128)S(1)}, f32[192,128]{1,0:T(8,128)S(1)}, u32[]{:S(2)}, u32[]{:S(2)}) collective-permute-start(f32[192,128]{1,0:T(8,128)S(1)} %get-tuple-element.25), channel_id=1, source_target_pairs={{0,24},{8,0},{16,8},{24,16},{1,25},{9,1},{17,9},{25,17},{2,26},{10... | collective-permute-start | bytes 294920 | tf_op jit(solution)/shard_map/ppermute | solution.py:474
  15.4 0.0 collective-permute-done.yleft_ref.yright_ref
  15.4 0.0 copy-done
  15.4 4.8 %shard_map.47 = (f32[32,128,128]{2,1,0:T(8,128)S(1)}, f32[3,128,128]{2,1,0:T(8,128)S(1)}, f32[4,3,128,128]{3,2,1,0:T(8,128)S(1)}, f32[4,128,128]{2,1,0:T(8,128)S(1)}) custom-call(f32[3,32,128,128]{3,2,1,0:T(8,128)S(1)} %get-tuple-element.18.u_ref, bf16[3,32,128,256]{3,2,1,0:T(8,128)(2,1)S(1)} %get-tuple-element.19.parts_ref, ...), custom_call_target="tpu_custom_call" | custom-call | flops 1048576 | bytes 1048576 | tf_op jit(solution)/shard_map/pallas_call | solution.py:257
  20.2 0.0 collective-permute-done.1.zleft_ref
  20.2 0.0 collective-permute-done.2.zright_ref
  20.2 2.8 %shard_map.48 = (f32[4,4,8,128]{3,2,1,0:T(8,128)S(1)}, f32[128,128]{1,0:T(8,128)S(1)}, f32[128,128]{1,0:T(8,128)S(1)}, bf16[256,384]{1,0:T(8,128)(2,1)S(1)}) custom-call(f32[32,128,128]{2,1,0:T(8,128)S(1)} %get-tuple-element.21.raw_ref, f32[3,128,128]{2,1,0:T(8,128)S(1)} %get-tuple-element.22.pack_ref, f32[4,128,128]{2,1,0:T(8,128)S(1)} %get-tuple-element.23.scale_ref, ...), custom_call_target="tpu_custom_call" | custom-call | flops 1048576 | bytes 1048576 | tf_op jit(solution)/shard_map/pallas_call | solution.py:402
  23.1 0.0 collective-permute-done.3.xleft_ref
  23.1 0.4 %shard_map.50.image_in_ref = f32[4,4,8,128]{3,2,1,0:T(8,128)S(1)} custom-call(f32[4,4,8,128]{3,2,1,0:T(8,128)S(1)} %get-tuple-element.26.image_in_ref, f32[32,128,128]{2,1,0:T(8,128)S(1)} %get-tuple-element.21.raw_ref, f32[4,3,128,128]{3,2,1,0:T(8,128)S(1)} %get-tuple-element.27.kept_ref, f32[4,128,128]{2,1,0:T(8,128)S(1)} %get-tuple-element.23.scale_ref, ...), custom_call_target="tpu_custom_call" | custom-call | flops 1048576 | bytes 1048576 | tf_op jit(solution)/shard_map/pallas_call | solution.py:461
  23.5 0.0 collective-permute-done.4.xright_ref
  23.5 0.4 %shard_map.52 = f32[4,4,8,128]{3,2,1,0:T(8,128)S(1)} custom-call(f32[4,4,8,128]{3,2,1,0:T(8,128)S(1)} %shard_map.50.image_in_ref, f32[32,128,128]{2,1,0:T(8,128)S(1)} %get-tuple-element.21.raw_ref, f32[4,3,128,128]{3,2,1,0:T(8,128)S(1)} %get-tuple-element.27.kept_ref, f32[4,128,128]{2,1,0:T(8,128)S(1)} %get-tuple-element.23.scale_ref, ...), custom_call_target="tpu_custom_call" | custom-call | flops 1048576 | bytes 1048576 | tf_op jit(solution)/shard_map/pallas_call | solution.py:461
  23.9 1.9 %collective-permute-start.5 = (f32[4,8,128]{2,1,0:T(8,128)S(1)}, f32[4,8,128]{2,1,0:T(8,128)S(1)}, u32[]{:S(2)}, u32[]{:S(2)}) collective-permute-start(f32[4,8,128]{2,1,0:T(8,128)S(1)} %get-tuple-element.33), channel_id=1, source_target_pairs={{0,16},{8,24},{16,8},{24,0},{1,17},{9,25},{17,9},{25,1},{2,18},{10... | collective-permute-start | bytes 49160 | tf_op jit(solution)/shard_map/ppermute | solution.py:504
  25.8 2.0 %collective-permute-start.6 = (f32[4,8,128]{2,1,0:T(8,128)S(1)}, f32[4,8,128]{2,1,0:T(8,128)S(1)}, u32[]{:S(2)}, u32[]{:S(2)}) collective-permute-start(f32[4,8,128]{2,1,0:T(8,128)S(1)} %get-tuple-element.32), channel_id=1, source_target_pairs={{0,24},{8,16},{16,0},{24,8},{1,25},{9,17},{17,1},{25,9},{2,26},{10... | collective-permute-start | bytes 49160 | tf_op jit(solution)/shard_map/ppermute | solution.py:504
  27.8 0.0 collective-permute-start.7
  27.8 1.7 %collective-permute-done.5.refs_1_ = f32[4,8,128]{2,1,0:T(8,128)S(1)} collective-permute-done((f32[4,8,128]{2,1,0:T(8,128)S(1)}, f32[4,8,128]{2,1,0:T(8,128)S(1)}, u32[]{:S(2)}, u32[]{:S(2)}) %collective-permute-start.5) | collective-permute-done | bytes 16416 | tf_op jit(solution)/shard_map/ppermute | solution.py:504
  29.5 0.9 %collective-permute-done.6.refs_2_ = f32[4,8,128]{2,1,0:T(8,128)S(1)} collective-permute-done((f32[4,8,128]{2,1,0:T(8,128)S(1)}, f32[4,8,128]{2,1,0:T(8,128)S(1)}, u32[]{:S(2)}, u32[]{:S(2)}) %collective-permute-start.6) | collective-permute-done | bytes 16416 | tf_op jit(solution)/shard_map/ppermute | solution.py:504
  30.5 1.1 %collective-permute-done.7.refs_3_ = f32[4,8,128]{2,1,0:T(8,128)S(1)} collective-permute-done((f32[4,8,128]{2,1,0:T(8,128)S(1)}, f32[4,8,128]{2,1,0:T(8,128)S(1)}, u32[]{:S(2)}, u32[]{:S(2)}) %collective-permute-start.7) | collective-permute-done | bytes 16416 | tf_op jit(solution)/shard_map/ppermute | solution.py:504
  31.5 0.6 %shard_map.53 = f32[1,1,4,8,128]{4,3,2,1,0:T(8,128)} custom-call(f32[4,8,128]{2,1,0:T(8,128)S(1)} %get-tuple-element.34.refs_0_, f32[4,8,128]{2,1,0:T(8,128)S(1)} %collective-permute-done.5.refs_1_, f32[4,8,128]{2,1,0:T(8,128)S(1)} %collective-permute-done.6.refs_2_, f32[4,8,128]{2,1,0:T(8,128)S(1)} %collective-permute-done.7.refs_3_), custom_call_target="tpu_custom_call" | custom-call | flops 1048576 | bytes 1048576 | tf_op jit(solution)/shard_map/pallas_call | solution.py:526
  (1 shorter events, 0.0 us)
Async XLA Ops:
  1.0 14.4 %copy-start = (s32[4,16,1]{1,2,0:T(1,128)S(1)}, s32[4,16,1]{1,2,0:T(1,128)}, u32[]{:S(2)}) copy-start(s32[4,16,1]{1,2,0:T(1,128)} %param.5) | copy-start | bytes 772
  1.0 22.1 %collective-permute-start.3 = (f32[3,2,128,128]{3,2,1,0:T(8,128)S(1)}, f32[3,2,128,128]{3,2,1,0:T(8,128)S(1)}, u32[]{:S(2)}, u32[]{:S(2)}) collective-permute-start(f32[3,2,128,128]{3,2,1,0:T(8,128)S(1)} %shard_map.49), channel_id=1, source_target_pairs={{0,2},{2,4},{4,6},{6,0},{1,3},{3,5},{5,7},{7,1},{8,10},{10,12},{12... | collective-permute-start | bytes 1179656 | tf_op jit(solution)/shard_map/ppermute | solution.py:474
  5.0 18.5 %collective-permute-start.4 = (f32[3,2,128,128]{3,2,1,0:T(8,128)S(1)}, f32[3,2,128,128]{3,2,1,0:T(8,128)S(1)}, u32[]{:S(2)}, u32[]{:S(2)}) collective-permute-start(f32[3,2,128,128]{3,2,1,0:T(8,128)S(1)} %shard_map.51), channel_id=1, source_target_pairs={{0,6},{2,0},{4,2},{6,4},{1,7},{3,1},{5,3},{7,5},{8,14},{10,8},{12,... | collective-permute-start | bytes 1179656 | tf_op jit(solution)/shard_map/ppermute | solution.py:474
  9.8 5.6 %collective-permute-start = (f32[3,32,4,128]{3,2,1,0:T(4,128)S(1)}, f32[3,32,4,128]{3,2,1,0:T(4,128)S(1)}, u32[]{:S(2)}, u32[]{:S(2)}) collective-permute-start(f32[3,32,4,128]{3,2,1,0:T(4,128)S(1)} %get-tuple-element.20), channel_id=1, source_target_pairs={{0,1},{1,0},{2,3},{3,2},{4,5},{5,4},{6,7},{7,6},{8,9},{9,8},{10,11... | collective-permute-start | bytes 589832 | tf_op jit(solution)/shard_map/ppermute | solution.py:474
  9.9 10.3 %collective-permute-start.1 = (f32[192,128]{1,0:T(8,128)S(1)}, f32[192,128]{1,0:T(8,128)S(1)}, u32[]{:S(2)}, u32[]{:S(2)}) collective-permute-start(f32[192,128]{1,0:T(8,128)S(1)} %get-tuple-element.24), channel_id=1, source_target_pairs={{0,8},{8,16},{16,24},{24,0},{1,9},{9,17},{17,25},{25,1},{2,10},{10... | collective-permute-start | bytes 294920 | tf_op jit(solution)/shard_map/ppermute | solution.py:474
  12.0 8.2 %collective-permute-start.2 = (f32[192,128]{1,0:T(8,128)S(1)}, f32[192,128]{1,0:T(8,128)S(1)}, u32[]{:S(2)}, u32[]{:S(2)}) collective-permute-start(f32[192,128]{1,0:T(8,128)S(1)} %get-tuple-element.25), channel_id=1, source_target_pairs={{0,24},{8,0},{16,8},{24,16},{1,25},{9,1},{17,9},{25,17},{2,26},{10... | collective-permute-start | bytes 294920 | tf_op jit(solution)/shard_map/ppermute | solution.py:474
  23.9 5.6 %collective-permute-start.5 = (f32[4,8,128]{2,1,0:T(8,128)S(1)}, f32[4,8,128]{2,1,0:T(8,128)S(1)}, u32[]{:S(2)}, u32[]{:S(2)}) collective-permute-start(f32[4,8,128]{2,1,0:T(8,128)S(1)} %get-tuple-element.33), channel_id=1, source_target_pairs={{0,16},{8,24},{16,8},{24,0},{1,17},{9,25},{17,9},{25,1},{2,18},{10... | collective-permute-start | bytes 49160 | tf_op jit(solution)/shard_map/ppermute | solution.py:504
  25.8 4.6 %collective-permute-start.6 = (f32[4,8,128]{2,1,0:T(8,128)S(1)}, f32[4,8,128]{2,1,0:T(8,128)S(1)}, u32[]{:S(2)}, u32[]{:S(2)}) collective-permute-start(f32[4,8,128]{2,1,0:T(8,128)S(1)} %get-tuple-element.32), channel_id=1, source_target_pairs={{0,24},{8,16},{16,0},{24,8},{1,25},{9,17},{17,1},{25,9},{2,26},{10... | collective-permute-start | bytes 49160 | tf_op jit(solution)/shard_map/ppermute | solution.py:504
  27.8 3.7 %collective-permute-start.7 = (f32[4,8,128]{2,1,0:T(8,128)S(1)}, f32[4,8,128]{2,1,0:T(8,128)S(1)}, u32[]{:S(2)}, u32[]{:S(2)}) collective-permute-start(f32[4,8,128]{2,1,0:T(8,128)S(1)} %get-tuple-element.31), channel_id=1, source_target_pairs={{0,8},{8,0},{16,24},{24,16},{1,9},{9,1},{17,25},{25,17},{2,10},{10... | collective-permute-start | bytes 49160 | tf_op jit(solution)/shard_map/ppermute | solution.py:504

commit v10 on v9

--- a/solution.py
+++ b/solution.py
@@ -24,25 +24,6 @@
 
 def iota(shape, dim):
     return lax.broadcasted_iota(jnp.int32, shape, dim)
-
-
-def layers_kernel(start, u_hbm, out_ref, sem):
-    copy = pltpu.make_async_copy(u_hbm.at[:, pl.ds(start, 2)], out_ref, sem)
-    copy.start()
-    copy.wait()
-
-
-def layers(u, start):
-    comps, _, ny, nz = u.shape
-    return pl.pallas_call(
-        functools.partial(layers_kernel, start),
-        out_shape=jax.ShapeDtypeStruct((comps, 2, ny, nz), jnp.float32),
-        in_specs=[HBM],
-        out_specs=VMEM,
-        scratch_shapes=[pltpu.SemaphoreType.DMA],
-        compiler_params=pltpu.CompilerParams(vmem_limit_bytes=50 << 20),
-        cost_estimate=COST,
-    )(u)
 
 
 def faces_kernel(u_hbm, u_ref, parts_ref, yface_ref, tail_ref, head_ref, packed_ref, sems):
@@ -537,8 +518,9 @@
     comps, nx, ny, nz = velocity.shape
     views = lax.axis_size("view")
     density = 5.0 / (nz * views)
-    xleft = turn(layers(velocity, nx - 2), "gx", 1)
-    xright = turn(layers(velocity, 0), "gx", -1)
+    xtail, later = lax.optimization_barrier((velocity[:, nx - 2 :], velocity))
+    xleft = turn(xtail, "gx", 1)
+    xright = turn(later[:, :2], "gx", -1)
     u, parts, yface, ztail, zhead = faces(velocity)
     zleft = turn(ztail, "view", 1)
     zright = turn(zhead, "view", -1)

time: 32.4 us -> 32.4 us (level)
  local copies, waits for them, and re-layouts: 0.01 us -> 2.07 us
  Pallas kernels: 14.8 us -> 12.8 us
    slice x0 -> x2, local copies, waits for them, and re-layouts: none -> 2.06 us  [the longest x1 1.04 us: local(): xtail, later = lax.optimization_barrier((velocity[:, nx - 2:], velocity))]
    pallas_call x2 -> x0, Pallas kernels: 2.01 us -> none  [layers(): pl.pallas_call(functools.partial(layers_kernel, start), out_shape=jax.Sha...]
  transfers between devices with their start and end apart: 8 -> 8, of which waited for: 3 -> 3; matrix products, arithmetic and copies ran while one was open for 0% -> 3% of each run, Pallas kernels for 40% -> 37%
where the time goes in v10:
time: 32.4 us; the launch traced here: 32.2 us
  Pallas kernels  12.8 us (40%)
  starting transfers between devices  12.2 us (38%)
  waiting for transfers between devices  3.75 us (12%)
  local copies, waits for them, and re-layouts  2.07 us (6%)
  between operations  1.4 us (4%)
    ppermute x5, starting transfers between devices, turn(): lax.ppermute(block, axis, [(i, (i + by) % count) for i in range(count)])  8.29 us
    pallas_call x1, Pallas kernels, shaded(): pl.pallas_call(shade_kernel, out_shape=(jax.ShapeDtypeStruct((nx, ny, nz)...  4.75 us
    ppermute x3, starting transfers between devices, exchanged(): lax.ppermute(blocks[k], axis, list(enumerate(route)))  3.88 us
    pallas_call x1, Pallas kernels, faces(): pl.pallas_call(faces_kernel, out_shape=(jax.ShapeDtypeStruct(u.shape, jnp...  3.78 us
    ppermute x3, waiting for transfers between devices, exchanged(): lax.ppermute(blocks[k], axis, list(enumerate(route)))  3.73 us
    pallas_call x1, Pallas kernels, blended(): pl.pallas_call(functools.partial(blend_kernel, density), out_shape=(jax.S...  2.84 us
    slice x1, local copies, waits for them, and re-layouts, local(): xtail, later = lax.optimization_barrier((velocity[:, nx - 2:], velocity))  1.04 us
    slice x1, local copies, waits for them, and re-layouts, local(): xright = turn(later[:, :2], 'gx', -1)  1.02 us
  transfers between devices with their start and end apart: 8, of which 3 were waited for; matrix products, arithmetic and copies ran while one was open for 3% of the time, Pallas kernels for 37%

profile of v10, /device:TPU:0, one launch (start us, length us, event | category | flops | bytes accessed | tf_op | source)
XLA Modules:
  0.0 32.2 jit_solution(3558925026797717815)
XLA Ops:
  0.0 0.0 copy-start
  0.0 1.0 %slice.18 = f32[3,2,128,128]{3,2,1,0:T(8,128)S(1)} slice(f32[3,32,128,128]{3,2,1,0:T(8,128)} %u_hbm.1), slice={[0:3], [30:32], [0:128], [0:128]} | slice | bytes 786432 | tf_op jit(solution)/shard_map/slice | solution.py:521
  1.0 3.0 %collective-permute-start.3 = (f32[3,2,128,128]{3,2,1,0:T(8,128)S(1)}, f32[3,2,128,128]{3,2,1,0:T(8,128)S(1)}, u32[]{:S(2)}, u32[]{:S(2)}) collective-permute-start(f32[3,2,128,128]{3,2,1,0:T(8,128)S(1)} %slice.18), channel_id=1, source_target_pairs={{0,2},{2,4},{4,6},{6,0},{1,3},{3,5},{5,7},{7,1},{8,10},{10,12},{12... | collective-permute-start | bytes 1179656 | tf_op jit(solution)/shard_map/ppermute | solution.py:455
  4.0 1.0 %slice.19 = f32[3,2,128,128]{3,2,1,0:T(8,128)S(1)} slice(f32[3,32,128,128]{3,2,1,0:T(8,128)} %u_hbm.1), slice={[0:3], [0:2], [0:128], [0:128]} | slice | bytes 786432 | tf_op jit(solution)/shard_map/slice | solution.py:523
  5.1 1.0 %collective-permute-start.4 = (f32[3,2,128,128]{3,2,1,0:T(8,128)S(1)}, f32[3,2,128,128]{3,2,1,0:T(8,128)S(1)}, u32[]{:S(2)}, u32[]{:S(2)}) collective-permute-start(f32[3,2,128,128]{3,2,1,0:T(8,128)S(1)} %slice.19), channel_id=1, source_target_pairs={{0,6},{2,0},{4,2},{6,4},{1,7},{3,1},{5,3},{7,5},{8,14},{10,8},{12,... | collective-permute-start | bytes 1179656 | tf_op jit(solution)/shard_map/ppermute | solution.py:455
  6.1 3.8 %shard_map.46 = (f32[3,32,128,128]{3,2,1,0:T(8,128)S(1)}, bf16[3,32,128,256]{3,2,1,0:T(8,128)(2,1)S(1)}, f32[3,32,4,128]{3,2,1,0:T(4,128)S(1)}, f32[192,128]{1,0:T(8,128)S(1)}, f32[192,128]{1,0:T(8,128)S(1)}) custom-call(f32[3,32,128,128]{3,2,1,0:T(8,128)} %u_hbm.1), custom_call_target="tpu_custom_call" | custom-call | flops 1048576 | bytes 1048576 | tf_op jit(solution)/shard_map/pallas_call | solution.py:97
  9.9 0.1 collective-permute-start
  10.0 2.1 %collective-permute-start.1 = (f32[192,128]{1,0:T(8,128)S(1)}, f32[192,128]{1,0:T(8,128)S(1)}, u32[]{:S(2)}, u32[]{:S(2)}) collective-permute-start(f32[192,128]{1,0:T(8,128)S(1)} %get-tuple-element.26), channel_id=1, source_target_pairs={{0,8},{8,16},{16,24},{24,0},{1,9},{9,17},{17,25},{25,1},{2,10},{10... | collective-permute-start | bytes 294920 | tf_op jit(solution)/shard_map/ppermute | solution.py:455
  12.0 2.1 %collective-permute-start.2 = (f32[192,128]{1,0:T(8,128)S(1)}, f32[192,128]{1,0:T(8,128)S(1)}, u32[]{:S(2)}, u32[]{:S(2)}) collective-permute-start(f32[192,128]{1,0:T(8,128)S(1)} %get-tuple-element.27), channel_id=1, source_target_pairs={{0,24},{8,0},{16,8},{24,16},{1,25},{9,1},{17,9},{25,17},{2,26},{10... | collective-permute-start | bytes 294920 | tf_op jit(solution)/shard_map/ppermute | solution.py:455
  15.5 0.0 collective-permute-done.yleft_ref.yright_ref
  15.5 0.0 copy-done
  15.5 4.8 %shard_map.47 = (f32[32,128,128]{2,1,0:T(8,128)S(1)}, f32[3,128,128]{2,1,0:T(8,128)S(1)}, f32[4,3,128,128]{3,2,1,0:T(8,128)S(1)}, f32[4,128,128]{2,1,0:T(8,128)S(1)}) custom-call(f32[3,32,128,128]{3,2,1,0:T(8,128)S(1)} %get-tuple-element.20.u_ref, bf16[3,32,128,256]{3,2,1,0:T(8,128)(2,1)S(1)} %get-tuple-element.21.parts_ref, ...), custom_call_target="tpu_custom_call" | custom-call | flops 1048576 | bytes 1048576 | tf_op jit(solution)/shard_map/pallas_call | solution.py:238
  20.2 0.0 collective-permute-done.1.zleft_ref
  20.2 0.0 collective-permute-done.2.zright_ref
  20.3 2.8 %shard_map.48 = (f32[4,4,8,128]{3,2,1,0:T(8,128)S(1)}, f32[128,128]{1,0:T(8,128)S(1)}, f32[128,128]{1,0:T(8,128)S(1)}, bf16[256,384]{1,0:T(8,128)(2,1)S(1)}) custom-call(f32[32,128,128]{2,1,0:T(8,128)S(1)} %get-tuple-element.23.raw_ref, f32[3,128,128]{2,1,0:T(8,128)S(1)} %get-tuple-element.24.pack_ref, f32[4,128,128]{2,1,0:T(8,128)S(1)} %get-tuple-element.25.scale_ref, ...), custom_call_target="tpu_custom_call" | custom-call | flops 1048576 | bytes 1048576 | tf_op jit(solution)/shard_map/pallas_call | solution.py:383
  23.1 0.0 collective-permute-done.3.xleft_ref
  23.1 0.4 %shard_map.49.image_in_ref = f32[4,4,8,128]{3,2,1,0:T(8,128)S(1)} custom-call(f32[4,4,8,128]{3,2,1,0:T(8,128)S(1)} %get-tuple-element.28.image_in_ref, f32[32,128,128]{2,1,0:T(8,128)S(1)} %get-tuple-element.23.raw_ref, f32[4,3,128,128]{3,2,1,0:T(8,128)S(1)} %get-tuple-element.29.kept_ref, f32[4,128,128]{2,1,0:T(8,128)S(1)} %get-tuple-element.25.scale_ref, ...), custom_call_target="tpu_custom_call" | custom-call | flops 1048576 | bytes 1048576 | tf_op jit(solution)/shard_map/pallas_call | solution.py:442
  23.5 0.0 collective-permute-done.4.xright_ref
  23.5 0.4 %shard_map.50 = f32[4,4,8,128]{3,2,1,0:T(8,128)S(1)} custom-call(f32[4,4,8,128]{3,2,1,0:T(8,128)S(1)} %shard_map.49.image_in_ref, f32[32,128,128]{2,1,0:T(8,128)S(1)} %get-tuple-element.23.raw_ref, f32[4,3,128,128]{3,2,1,0:T(8,128)S(1)} %get-tuple-element.29.kept_ref, f32[4,128,128]{2,1,0:T(8,128)S(1)} %get-tuple-element.25.scale_ref, ...), custom_call_target="tpu_custom_call" | custom-call | flops 1048576 | bytes 1048576 | tf_op jit(solution)/shard_map/pallas_call | solution.py:442
  23.9 1.9 %collective-permute-start.5 = (f32[4,8,128]{2,1,0:T(8,128)S(1)}, f32[4,8,128]{2,1,0:T(8,128)S(1)}, u32[]{:S(2)}, u32[]{:S(2)}) collective-permute-start(f32[4,8,128]{2,1,0:T(8,128)S(1)} %get-tuple-element.37), channel_id=1, source_target_pairs={{0,16},{8,24},{16,8},{24,0},{1,17},{9,25},{17,9},{25,1},{2,18},{10... | collective-permute-start | bytes 49160 | tf_op jit(solution)/shard_map/ppermute | solution.py:485
  25.8 2.0 %collective-permute-start.6 = (f32[4,8,128]{2,1,0:T(8,128)S(1)}, f32[4,8,128]{2,1,0:T(8,128)S(1)}, u32[]{:S(2)}, u32[]{:S(2)}) collective-permute-start(f32[4,8,128]{2,1,0:T(8,128)S(1)} %get-tuple-element.36), channel_id=1, source_target_pairs={{0,24},{8,16},{16,0},{24,8},{1,25},{9,17},{17,1},{25,9},{2,26},{10... | collective-permute-start | bytes 49160 | tf_op jit(solution)/shard_map/ppermute | solution.py:485
  27.8 0.0 collective-permute-start.7
  27.8 1.7 %collective-permute-done.5.refs_1_ = f32[4,8,128]{2,1,0:T(8,128)S(1)} collective-permute-done((f32[4,8,128]{2,1,0:T(8,128)S(1)}, f32[4,8,128]{2,1,0:T(8,128)S(1)}, u32[]{:S(2)}, u32[]{:S(2)}) %collective-permute-start.5) | collective-permute-done | bytes 16416 | tf_op jit(solution)/shard_map/ppermute | solution.py:485
  29.6 0.9 %collective-permute-done.6.refs_2_ = f32[4,8,128]{2,1,0:T(8,128)S(1)} collective-permute-done((f32[4,8,128]{2,1,0:T(8,128)S(1)}, f32[4,8,128]{2,1,0:T(8,128)S(1)}, u32[]{:S(2)}, u32[]{:S(2)}) %collective-permute-start.6) | collective-permute-done | bytes 16416 | tf_op jit(solution)/shard_map/ppermute | solution.py:485
  30.5 1.1 %collective-permute-done.7.refs_3_ = f32[4,8,128]{2,1,0:T(8,128)S(1)} collective-permute-done((f32[4,8,128]{2,1,0:T(8,128)S(1)}, f32[4,8,128]{2,1,0:T(8,128)S(1)}, u32[]{:S(2)}, u32[]{:S(2)}) %collective-permute-start.7) | collective-permute-done | bytes 16416 | tf_op jit(solution)/shard_map/ppermute | solution.py:485
  31.6 0.6 %shard_map.51 = f32[1,1,4,8,128]{4,3,2,1,0:T(8,128)} custom-call(f32[4,8,128]{2,1,0:T(8,128)S(1)} %get-tuple-element.38.refs_0_, f32[4,8,128]{2,1,0:T(8,128)S(1)} %collective-permute-done.5.refs_1_, f32[4,8,128]{2,1,0:T(8,128)S(1)} %collective-permute-done.6.refs_2_, f32[4,8,128]{2,1,0:T(8,128)S(1)} %collective-permute-done.7.refs_3_), custom_call_target="tpu_custom_call" | custom-call | flops 1048576 | bytes 1048576 | tf_op jit(solution)/shard_map/pallas_call | solution.py:507
  (1 shorter events, 0.0 us)
Async XLA Ops:
  0.0 15.5 %copy-start = (s32[4,16,1]{1,2,0:T(1,128)S(1)}, s32[4,16,1]{1,2,0:T(1,128)}, u32[]{:S(2)}) copy-start(s32[4,16,1]{1,2,0:T(1,128)} %param.5) | copy-start | bytes 772
  1.0 22.1 %collective-permute-start.3 = (f32[3,2,128,128]{3,2,1,0:T(8,128)S(1)}, f32[3,2,128,128]{3,2,1,0:T(8,128)S(1)}, u32[]{:S(2)}, u32[]{:S(2)}) collective-permute-start(f32[3,2,128,128]{3,2,1,0:T(8,128)S(1)} %slice.18), channel_id=1, source_target_pairs={{0,2},{2,4},{4,6},{6,0},{1,3},{3,5},{5,7},{7,1},{8,10},{10,12},{12... | collective-permute-start | bytes 1179656 | tf_op jit(solution)/shard_map/ppermute | solution.py:455
  5.1 18.4 %collective-permute-start.4 = (f32[3,2,128,128]{3,2,1,0:T(8,128)S(1)}, f32[3,2,128,128]{3,2,1,0:T(8,128)S(1)}, u32[]{:S(2)}, u32[]{:S(2)}) collective-permute-start(f32[3,2,128,128]{3,2,1,0:T(8,128)S(1)} %slice.19), channel_id=1, source_target_pairs={{0,6},{2,0},{4,2},{6,4},{1,7},{3,1},{5,3},{7,5},{8,14},{10,8},{12,... | collective-permute-start | bytes 1179656 | tf_op jit(solution)/shard_map/ppermute | solution.py:455
  9.9 5.6 %collective-permute-start = (f32[3,32,4,128]{3,2,1,0:T(4,128)S(1)}, f32[3,32,4,128]{3,2,1,0:T(4,128)S(1)}, u32[]{:S(2)}, u32[]{:S(2)}) collective-permute-start(f32[3,32,4,128]{3,2,1,0:T(4,128)S(1)} %get-tuple-element.22), channel_id=1, source_target_pairs={{0,1},{1,0},{2,3},{3,2},{4,5},{5,4},{6,7},{7,6},{8,9},{9,8},{10,11... | collective-permute-start | bytes 589832 | tf_op jit(solution)/shard_map/ppermute | solution.py:455
  10.0 10.3 %collective-permute-start.1 = (f32[192,128]{1,0:T(8,128)S(1)}, f32[192,128]{1,0:T(8,128)S(1)}, u32[]{:S(2)}, u32[]{:S(2)}) collective-permute-start(f32[192,128]{1,0:T(8,128)S(1)} %get-tuple-element.26), channel_id=1, source_target_pairs={{0,8},{8,16},{16,24},{24,0},{1,9},{9,17},{17,25},{25,1},{2,10},{10... | collective-permute-start | bytes 294920 | tf_op jit(solution)/shard_map/ppermute | solution.py:455
  12.0 8.2 %collective-permute-start.2 = (f32[192,128]{1,0:T(8,128)S(1)}, f32[192,128]{1,0:T(8,128)S(1)}, u32[]{:S(2)}, u32[]{:S(2)}) collective-permute-start(f32[192,128]{1,0:T(8,128)S(1)} %get-tuple-element.27), channel_id=1, source_target_pairs={{0,24},{8,0},{16,8},{24,16},{1,25},{9,1},{17,9},{25,17},{2,26},{10... | collective-permute-start | bytes 294920 | tf_op jit(solution)/shard_map/ppermute | solution.py:455
  23.9 5.6 %collective-permute-start.5 = (f32[4,8,128]{2,1,0:T(8,128)S(1)}, f32[4,8,128]{2,1,0:T(8,128)S(1)}, u32[]{:S(2)}, u32[]{:S(2)}) collective-permute-start(f32[4,8,128]{2,1,0:T(8,128)S(1)} %get-tuple-element.37), channel_id=1, source_target_pairs={{0,16},{8,24},{16,8},{24,0},{1,17},{9,25},{17,9},{25,1},{2,18},{10... | collective-permute-start | bytes 49160 | tf_op jit(solution)/shard_map/ppermute | solution.py:485
  25.8 4.6 %collective-permute-start.6 = (f32[4,8,128]{2,1,0:T(8,128)S(1)}, f32[4,8,128]{2,1,0:T(8,128)S(1)}, u32[]{:S(2)}, u32[]{:S(2)}) collective-permute-start(f32[4,8,128]{2,1,0:T(8,128)S(1)} %get-tuple-element.36), channel_id=1, source_target_pairs={{0,24},{8,16},{16,0},{24,8},{1,25},{9,17},{17,1},{25,9},{2,26},{10... | collective-permute-start | bytes 49160 | tf_op jit(solution)/shard_map/ppermute | solution.py:485
  27.8 3.7 %collective-permute-start.7 = (f32[4,8,128]{2,1,0:T(8,128)S(1)}, f32[4,8,128]{2,1,0:T(8,128)S(1)}, u32[]{:S(2)}, u32[]{:S(2)}) collective-permute-start(f32[4,8,128]{2,1,0:T(8,128)S(1)} %get-tuple-element.35), channel_id=1, source_target_pairs={{0,8},{8,0},{16,24},{24,16},{1,9},{9,1},{17,25},{25,17},{2,10},{10... | collective-permute-start | bytes 49160 | tf_op jit(solution)/shard_map/ppermute | solution.py:485

commit v11 on v10

--- a/solution.py
+++ b/solution.py
@@ -304,7 +304,7 @@
         totals = [jnp.where(lane_group == group, part, total) for part, total in zip((red, square, whole), totals)]
     red, square, whole = [jnp.sum(jnp.where(eye, total, 0.0), axis=0, keepdims=True) for total in totals]
     through = jnp.exp2(whole)
-    store(red, 4.0 * (red - square), 1.0 - through - red, through)
+    store(red, square, through)
 
 
 def put(image_ref, x, slot=lambda view: view):
@@ -383,7 +383,7 @@
     return pl.pallas_call(
         functools.partial(blend_kernel, density),
         out_shape=(
-            jax.ShapeDtypeStruct((views, 4, nx // views, ny), jnp.float32),
+            jax.ShapeDtypeStruct((views, 3, nx // views, ny), jnp.float32),
             jax.ShapeDtypeStruct((ny, nz), jnp.float32),
             jax.ShapeDtypeStruct((ny, nz), jnp.float32),
             jax.ShapeDtypeStruct((2 * nz, 2 * nz + ny), jnp.bfloat16),
@@ -490,23 +490,23 @@
     count = len(image_refs)
     me = lax.axis_index("view")
     sources = [me] + [looked_up(me, [route.index(i) for i in range(count)]) for route in exchange(count)]
-    colour = [0.0] * 3
+    red = square = 0.0
     through = 1.0
     for source, image_ref in zip(sources, image_refs):
         passing = 1.0
         for other, front_ref in zip(sources, image_refs):
-            passing = passing * jnp.where(other < source, front_ref[3], 1.0)
-        colour = [total + passing * image_ref[k] for k, total in enumerate(colour)]
-        through = through * image_ref[3]
-    for k in range(3):
-        out_ref[0, 0, k] = colour[k]
-    out_ref[0, 0, 3] = 1.0 - through
+            passing = passing * jnp.where(other < source, front_ref[2], 1.0)
+        red = red + passing * image_ref[0]
+        square = square + passing * image_ref[1]
+        through = through * image_ref[2]
+    for k, values in enumerate((red, 4.0 * (red - square), 1.0 - through - red, 1.0 - through)):
+        out_ref[0, 0, k] = values
 
 
 def composited(images):
     return pl.pallas_call(
         composite_kernel,
-        out_shape=jax.ShapeDtypeStruct((1, 1) + images[0].shape, jnp.float32),
+        out_shape=jax.ShapeDtypeStruct((1, 1, 4) + images[0].shape[1:], jnp.float32),
         in_specs=[VMEM] * len(images),
         out_specs=VMEM,
         compiler_params=PARAMS,
@@ -518,9 +518,8 @@
     comps, nx, ny, nz = velocity.shape
     views = lax.axis_size("view")
     density = 5.0 / (nz * views)
-    xtail, later = lax.optimization_barrier((velocity[:, nx - 2 :], velocity))
-    xleft = turn(xtail, "gx", 1)
-    xright = turn(later[:, :2], "gx", -1)
+    xleft = turn(velocity[:, nx - 2 :], "gx", 1)
+    xright = turn(velocity[:, :2], "gx", -1)
     u, parts, yface, ztail, zhead = faces(velocity)
     zleft = turn(ztail, "view", 1)
     zright = turn(zhead, "view", -1)

time: 32.4 us -> 31.7 us (0.978)
  local copies, waits for them, and re-layouts: 2.07 us -> 1.19 us
    slice x2 -> x1, local copies, waits for them, and re-layouts: 2.06 us -> 1.18 us  [local(): xright = turn(velocity[:, :2], 'gx', -1)]
    ppermute x5, waiting for transfers between devices: 0.01 us -> 0.53 us  [turn(): lax.ppermute(block, axis, [(i, (i + by) % count) for i in range(count)])]
    ppermute x3, waiting for transfers between devices: 3.73 us -> 3.35 us  [exchanged(): lax.ppermute(blocks[k], axis, list(enumerate(route)))]
    ppermute x3, starting transfers between devices: 3.88 us -> 4.22 us  [exchanged(): lax.ppermute(blocks[k], axis, list(enumerate(route)))]
  transfers between devices with their start and end apart: 8 -> 8, of which waited for: 3 -> 4; matrix products, arithmetic and copies ran while one was open for 3% -> 0% of each run, Pallas kernels for 37% -> 37%
where the time goes in v11:
time: 31.7 us; the launch traced here: 31.5 us
  Pallas kernels  12.6 us (40%)
  starting transfers between devices  12.5 us (39%)
  waiting for transfers between devices  3.88 us (12%)
  between operations  1.39 us (4%)
  local copies, waits for them, and re-layouts  1.19 us (4%)
    ppermute x5, starting transfers between devices, turn(): lax.ppermute(block, axis, [(i, (i + by) % count) for i in range(count)])  8.24 us
    pallas_call x1, Pallas kernels, shaded(): pl.pallas_call(shade_kernel, out_shape=(jax.ShapeDtypeStruct((nx, ny, nz)...  4.61 us
    ppermute x3, starting transfers between devices, exchanged(): lax.ppermute(blocks[k], axis, list(enumerate(route)))  4.22 us
    pallas_call x1, Pallas kernels, faces(): pl.pallas_call(faces_kernel, out_shape=(jax.ShapeDtypeStruct(u.shape, jnp...  3.78 us
    ppermute x3, waiting for transfers between devices, exchanged(): lax.ppermute(blocks[k], axis, list(enumerate(route)))  3.35 us
    pallas_call x1, Pallas kernels, blended(): pl.pallas_call(functools.partial(blend_kernel, density), out_shape=(jax.S...  2.81 us
    slice x1, local copies, waits for them, and re-layouts, local(): xright = turn(velocity[:, :2], 'gx', -1)  1.18 us
    pallas_call x2, Pallas kernels, edged(): pl.pallas_call(functools.partial(kernel, density), out_shape=jax.ShapeDty...  0.8 us
  transfers between devices with their start and end apart: 8, of which 4 were waited for; matrix products, arithmetic and copies ran while one was open for 0% of the time, Pallas kernels for 37%

profile of v11, /device:TPU:0, one launch (start us, length us, event | category | flops | bytes accessed | tf_op | source)
XLA Modules:
  0.0 31.5 jit_solution(12318796499539891566)
XLA Ops:
  0.0 0.0 copy-start
  0.0 1.2 %fusion = (f32[3,2,128,128]{3,2,1,0:T(8,128)S(1)}, f32[3,2,128,128]{3,2,1,0:T(8,128)S(1)}) fusion(f32[3,32,128,128]{3,2,1,0:T(8,128)} %u_hbm.1), kind=kLoop, calls=%fused_computation.4 | loop fusion | bytes 1572864 | tf_op jit(solution)/shard_map/slice | solution.py:522
  1.2 3.0 %collective-permute-start.3 = (f32[3,2,128,128]{3,2,1,0:T(8,128)S(1)}, f32[3,2,128,128]{3,2,1,0:T(8,128)S(1)}, u32[]{:S(2)}, u32[]{:S(2)}) collective-permute-start(f32[3,2,128,128]{3,2,1,0:T(8,128)S(1)} %get-tuple-element.32), channel_id=1, source_target_pairs={{0,2},{2,4},{4,6},{6,0},{1,3},{3,5},{5,7},{7,1},{8,10},{10,12},{12... | collective-permute-start | bytes 1179656 | tf_op jit(solution)/shard_map/ppermute | solution.py:455
  4.2 1.0 %collective-permute-start.4 = (f32[3,2,128,128]{3,2,1,0:T(8,128)S(1)}, f32[3,2,128,128]{3,2,1,0:T(8,128)S(1)}, u32[]{:S(2)}, u32[]{:S(2)}) collective-permute-start(f32[3,2,128,128]{3,2,1,0:T(8,128)S(1)} %get-tuple-element.31), channel_id=1, source_target_pairs={{0,6},{2,0},{4,2},{6,4},{1,7},{3,1},{5,3},{7,5},{8,14},{10,8},{12,... | collective-permute-start | bytes 1179656 | tf_op jit(solution)/shard_map/ppermute | solution.py:455
  5.2 3.8 %shard_map.46 = (f32[3,32,128,128]{3,2,1,0:T(8,128)S(1)}, bf16[3,32,128,256]{3,2,1,0:T(8,128)(2,1)S(1)}, f32[3,32,4,128]{3,2,1,0:T(4,128)S(1)}, f32[192,128]{1,0:T(8,128)S(1)}, f32[192,128]{1,0:T(8,128)S(1)}) custom-call(f32[3,32,128,128]{3,2,1,0:T(8,128)} %u_hbm.1), custom_call_target="tpu_custom_call" | custom-call | flops 1048576 | bytes 1048576 | tf_op jit(solution)/shard_map/pallas_call | solution.py:97
  9.0 0.1 collective-permute-start
  9.1 2.0 %collective-permute-start.1 = (f32[192,128]{1,0:T(8,128)S(1)}, f32[192,128]{1,0:T(8,128)S(1)}, u32[]{:S(2)}, u32[]{:S(2)}) collective-permute-start(f32[192,128]{1,0:T(8,128)S(1)} %get-tuple-element.24), channel_id=1, source_target_pairs={{0,8},{8,16},{16,24},{24,0},{1,9},{9,17},{17,25},{25,1},{2,10},{10... | collective-permute-start | bytes 294920 | tf_op jit(solution)/shard_map/ppermute | solution.py:455
  11.1 2.1 %collective-permute-start.2 = (f32[192,128]{1,0:T(8,128)S(1)}, f32[192,128]{1,0:T(8,128)S(1)}, u32[]{:S(2)}, u32[]{:S(2)}) collective-permute-start(f32[192,128]{1,0:T(8,128)S(1)} %get-tuple-element.25), channel_id=1, source_target_pairs={{0,24},{8,0},{16,8},{24,16},{1,25},{9,1},{17,9},{25,17},{2,26},{10... | collective-permute-start | bytes 294920 | tf_op jit(solution)/shard_map/ppermute | solution.py:455
  14.5 0.0 collective-permute-done.yleft_ref.yright_ref
  14.5 0.0 copy-done
  14.5 4.6 %shard_map.47 = (f32[32,128,128]{2,1,0:T(8,128)S(1)}, f32[3,128,128]{2,1,0:T(8,128)S(1)}, f32[4,3,128,128]{3,2,1,0:T(8,128)S(1)}, f32[4,128,128]{2,1,0:T(8,128)S(1)}) custom-call(f32[3,32,128,128]{3,2,1,0:T(8,128)S(1)} %get-tuple-element.18.u_ref, bf16[3,32,128,256]{3,2,1,0:T(8,128)(2,1)S(1)} %get-tuple-element.19.parts_ref, ...), custom_call_target="tpu_custom_call" | custom-call | flops 1048576 | bytes 1048576 | tf_op jit(solution)/shard_map/pallas_call | solution.py:238
  19.2 0.0 collective-permute-done.1.zleft_ref
  19.2 0.0 collective-permute-done.2.zright_ref
  19.2 2.8 %shard_map.48 = (f32[4,3,8,128]{3,2,1,0:T(8,128)S(1)}, f32[128,128]{1,0:T(8,128)S(1)}, f32[128,128]{1,0:T(8,128)S(1)}, bf16[256,384]{1,0:T(8,128)(2,1)S(1)}) custom-call(f32[32,128,128]{2,1,0:T(8,128)S(1)} %get-tuple-element.21.raw_ref, f32[3,128,128]{2,1,0:T(8,128)S(1)} %get-tuple-element.22.pack_ref, f32[4,128,128]{2,1,0:T(8,128)S(1)} %get-tuple-element.23.scale_ref, ...), custom_call_target="tpu_custom_call" | custom-call | flops 1048576 | bytes 1048576 | tf_op jit(solution)/shard_map/pallas_call | solution.py:383
  22.0 0.0 collective-permute-done.3.xleft_ref
  22.0 0.4 %shard_map.49.image_in_ref = f32[4,3,8,128]{3,2,1,0:T(8,128)S(1)} custom-call(f32[4,3,8,128]{3,2,1,0:T(8,128)S(1)} %get-tuple-element.26.image_in_ref, f32[32,128,128]{2,1,0:T(8,128)S(1)} %get-tuple-element.21.raw_ref, f32[4,3,128,128]{3,2,1,0:T(8,128)S(1)} %get-tuple-element.27.kept_ref, f32[4,128,128]{2,1,0:T(8,128)S(1)} %get-tuple-element.23.scale_ref, ...), custom_call_target="tpu_custom_call" | custom-call | flops 1048576 | bytes 1048576 | tf_op jit(solution)/shard_map/pallas_call | solution.py:442
  22.4 0.5 %collective-permute-done.4.xright_ref = f32[3,2,128,128]{3,2,1,0:T(8,128)S(1)} collective-permute-done((f32[3,2,128,128]{3,2,1,0:T(8,128)S(1)}, f32[3,2,128,128]{3,2,1,0:T(8,128)S(1)}, u32[]{:S(2)}, u32[]{:S(2)}) %collective-permute-start.4) | collective-permute-done | bytes 393248 | tf_op jit(solution)/shard_map/ppermute | solution.py:455
  22.9 0.4 %shard_map.50 = f32[4,3,8,128]{3,2,1,0:T(8,128)S(1)} custom-call(f32[4,3,8,128]{3,2,1,0:T(8,128)S(1)} %shard_map.49.image_in_ref, f32[32,128,128]{2,1,0:T(8,128)S(1)} %get-tuple-element.21.raw_ref, f32[4,3,128,128]{3,2,1,0:T(8,128)S(1)} %get-tuple-element.27.kept_ref, f32[4,128,128]{2,1,0:T(8,128)S(1)} %get-tuple-element.23.scale_ref, ...), custom_call_target="tpu_custom_call" | custom-call | flops 1048576 | bytes 1048576 | tf_op jit(solution)/shard_map/pallas_call | solution.py:442
  23.3 2.6 %collective-permute-start.5 = (f32[3,8,128]{2,1,0:T(8,128)S(1)}, f32[3,8,128]{2,1,0:T(8,128)S(1)}, u32[]{:S(2)}, u32[]{:S(2)}) collective-permute-start(f32[3,8,128]{2,1,0:T(8,128)S(1)} %get-tuple-element.35), channel_id=1, source_target_pairs={{0,16},{8,24},{16,8},{24,0},{1,17},{9,25},{17,9},{25,1},{2,18},{10... | collective-permute-start | bytes 36872 | tf_op jit(solution)/shard_map/ppermute | solution.py:485
  26.0 1.2 %collective-permute-start.6 = (f32[3,8,128]{2,1,0:T(8,128)S(1)}, f32[3,8,128]{2,1,0:T(8,128)S(1)}, u32[]{:S(2)}, u32[]{:S(2)}) collective-permute-start(f32[3,8,128]{2,1,0:T(8,128)S(1)} %get-tuple-element.34), channel_id=1, source_target_pairs={{0,24},{8,16},{16,0},{24,8},{1,25},{9,17},{17,1},{25,9},{2,26},{10... | collective-permute-start | bytes 36872 | tf_op jit(solution)/shard_map/ppermute | solution.py:485
  27.2 0.3 %collective-permute-start.7 = (f32[3,8,128]{2,1,0:T(8,128)S(1)}, f32[3,8,128]{2,1,0:T(8,128)S(1)}, u32[]{:S(2)}, u32[]{:S(2)}) collective-permute-start(f32[3,8,128]{2,1,0:T(8,128)S(1)} %get-tuple-element.33), channel_id=1, source_target_pairs={{0,8},{8,0},{16,24},{24,16},{1,9},{9,1},{17,25},{25,17},{2,10},{10... | collective-permute-start | bytes 36872 | tf_op jit(solution)/shard_map/ppermute | solution.py:485
  27.6 1.3 %collective-permute-done.5.refs_1_ = f32[3,8,128]{2,1,0:T(8,128)S(1)} collective-permute-done((f32[3,8,128]{2,1,0:T(8,128)S(1)}, f32[3,8,128]{2,1,0:T(8,128)S(1)}, u32[]{:S(2)}, u32[]{:S(2)}) %collective-permute-start.5) | collective-permute-done | bytes 12320 | tf_op jit(solution)/shard_map/ppermute | solution.py:485
  28.9 1.7 %collective-permute-done.6.refs_2_ = f32[3,8,128]{2,1,0:T(8,128)S(1)} collective-permute-done((f32[3,8,128]{2,1,0:T(8,128)S(1)}, f32[3,8,128]{2,1,0:T(8,128)S(1)}, u32[]{:S(2)}, u32[]{:S(2)}) %collective-permute-start.6) | collective-permute-done | bytes 12320 | tf_op jit(solution)/shard_map/ppermute | solution.py:485
  30.6 0.3 %collective-permute-done.7.refs_3_ = f32[3,8,128]{2,1,0:T(8,128)S(1)} collective-permute-done((f32[3,8,128]{2,1,0:T(8,128)S(1)}, f32[3,8,128]{2,1,0:T(8,128)S(1)}, u32[]{:S(2)}, u32[]{:S(2)}) %collective-permute-start.7) | collective-permute-done | bytes 12320 | tf_op jit(solution)/shard_map/ppermute | solution.py:485
  30.9 0.6 %shard_map.51 = f32[1,1,4,8,128]{4,3,2,1,0:T(8,128)} custom-call(f32[3,8,128]{2,1,0:T(8,128)S(1)} %get-tuple-element.36.refs_0_, f32[3,8,128]{2,1,0:T(8,128)S(1)} %collective-permute-done.5.refs_1_, f32[3,8,128]{2,1,0:T(8,128)S(1)} %collective-permute-done.6.refs_2_, f32[3,8,128]{2,1,0:T(8,128)S(1)} %collective-permute-done.7.refs_3_), custom_call_target="tpu_custom_call" | custom-call | flops 1048576 | bytes 1048576 | tf_op jit(solution)/shard_map/pallas_call | solution.py:507
  (1 shorter events, 0.0 us)
Async XLA Ops:
  0.0 14.5 %copy-start = (s32[4,16,1]{1,2,0:T(1,128)S(1)}, s32[4,16,1]{1,2,0:T(1,128)}, u32[]{:S(2)}) copy-start(s32[4,16,1]{1,2,0:T(1,128)} %param.5) | copy-start | bytes 772
  1.2 20.8 %collective-permute-start.3 = (f32[3,2,128,128]{3,2,1,0:T(8,128)S(1)}, f32[3,2,128,128]{3,2,1,0:T(8,128)S(1)}, u32[]{:S(2)}, u32[]{:S(2)}) collective-permute-start(f32[3,2,128,128]{3,2,1,0:T(8,128)S(1)} %get-tuple-element.32), channel_id=1, source_target_pairs={{0,2},{2,4},{4,6},{6,0},{1,3},{3,5},{5,7},{7,1},{8,10},{10,12},{12... | collective-permute-start | bytes 1179656 | tf_op jit(solution)/shard_map/ppermute | solution.py:455
  4.2 18.7 %collective-permute-start.4 = (f32[3,2,128,128]{3,2,1,0:T(8,128)S(1)}, f32[3,2,128,128]{3,2,1,0:T(8,128)S(1)}, u32[]{:S(2)}, u32[]{:S(2)}) collective-permute-start(f32[3,2,128,128]{3,2,1,0:T(8,128)S(1)} %get-tuple-element.31), channel_id=1, source_target_pairs={{0,6},{2,0},{4,2},{6,4},{1,7},{3,1},{5,3},{7,5},{8,14},{10,8},{12,... | collective-permute-start | bytes 1179656 | tf_op jit(solution)/shard_map/ppermute | solution.py:455
  9.0 5.5 %collective-permute-start = (f32[3,32,4,128]{3,2,1,0:T(4,128)S(1)}, f32[3,32,4,128]{3,2,1,0:T(4,128)S(1)}, u32[]{:S(2)}, u32[]{:S(2)}) collective-permute-start(f32[3,32,4,128]{3,2,1,0:T(4,128)S(1)} %get-tuple-element.20), channel_id=1, source_target_pairs={{0,1},{1,0},{2,3},{3,2},{4,5},{5,4},{6,7},{7,6},{8,9},{9,8},{10,11... | collective-permute-start | bytes 589832 | tf_op jit(solution)/shard_map/ppermute | solution.py:455
  9.1 10.1 %collective-permute-start.1 = (f32[192,128]{1,0:T(8,128)S(1)}, f32[192,128]{1,0:T(8,128)S(1)}, u32[]{:S(2)}, u32[]{:S(2)}) collective-permute-start(f32[192,128]{1,0:T(8,128)S(1)} %get-tuple-element.24), channel_id=1, source_target_pairs={{0,8},{8,16},{16,24},{24,0},{1,9},{9,17},{17,25},{25,1},{2,10},{10... | collective-permute-start | bytes 294920 | tf_op jit(solution)/shard_map/ppermute | solution.py:455
  11.1 8.1 %collective-permute-start.2 = (f32[192,128]{1,0:T(8,128)S(1)}, f32[192,128]{1,0:T(8,128)S(1)}, u32[]{:S(2)}, u32[]{:S(2)}) collective-permute-start(f32[192,128]{1,0:T(8,128)S(1)} %get-tuple-element.25), channel_id=1, source_target_pairs={{0,24},{8,0},{16,8},{24,16},{1,25},{9,1},{17,9},{25,17},{2,26},{10... | collective-permute-start | bytes 294920 | tf_op jit(solution)/shard_map/ppermute | solution.py:455
  23.3 5.5 %collective-permute-start.5 = (f32[3,8,128]{2,1,0:T(8,128)S(1)}, f32[3,8,128]{2,1,0:T(8,128)S(1)}, u32[]{:S(2)}, u32[]{:S(2)}) collective-permute-start(f32[3,8,128]{2,1,0:T(8,128)S(1)} %get-tuple-element.35), channel_id=1, source_target_pairs={{0,16},{8,24},{16,8},{24,0},{1,17},{9,25},{17,9},{25,1},{2,18},{10... | collective-permute-start | bytes 36872 | tf_op jit(solution)/shard_map/ppermute | solution.py:485
  26.0 4.6 %collective-permute-start.6 = (f32[3,8,128]{2,1,0:T(8,128)S(1)}, f32[3,8,128]{2,1,0:T(8,128)S(1)}, u32[]{:S(2)}, u32[]{:S(2)}) collective-permute-start(f32[3,8,128]{2,1,0:T(8,128)S(1)} %get-tuple-element.34), channel_id=1, source_target_pairs={{0,24},{8,16},{16,0},{24,8},{1,25},{9,17},{17,1},{25,9},{2,26},{10... | collective-permute-start | bytes 36872 | tf_op jit(solution)/shard_map/ppermute | solution.py:485
  27.2 3.7 %collective-permute-start.7 = (f32[3,8,128]{2,1,0:T(8,128)S(1)}, f32[3,8,128]{2,1,0:T(8,128)S(1)}, u32[]{:S(2)}, u32[]{:S(2)}) collective-permute-start(f32[3,8,128]{2,1,0:T(8,128)S(1)} %get-tuple-element.33), channel_id=1, source_target_pairs={{0,8},{8,0},{16,24},{24,16},{1,9},{9,1},{17,25},{25,17},{2,10},{10... | collective-permute-start | bytes 36872 | tf_op jit(solution)/shard_map/ppermute | solution.py:485

commit v12 on v11

--- a/solution.py
+++ b/solution.py
@@ -396,58 +396,95 @@
     )(raw, *rest)
 
 
-def edge_raw(x, place, ghost, raw_ref, kept_ref, scale_ref, fix_ref, first_ref):
-    depth = kept_ref[place, 2] + on_border(first_ref[...], x)
-    more = ghost[0] * (0.5 * ghost[0] + kept_ref[place, 0]) + ghost[1] * kept_ref[place, 1] + ghost[2] * depth
-    return raw_ref[x] + on_border(fix_ref[...], x) + more * scale_ref[x // SUB]
+def two_rows(density, raws, level_ref, sums_ref, sum_ref, stores):
+    ny, nz = raws[0].shape
+    binary = density / math.log(2.0)
+    parts = []
+    for k, raw in enumerate(raws):
+        level = jnp.clip(raw, 0.0, 1.0)
+        level_ref[k] = level
+        parts.append(jnp.concatenate(split(binary * level), axis=1))
+    sums = jnp.dot(
+        jnp.concatenate(parts, axis=0), sum_ref[:, pl.ds(nz, nz)], preferred_element_type=jnp.float32
+    )
+    lane_group = iota((8, ny), 1) // 8
+    eye = iota((8, ny), 1) % 8 == iota((8, ny), 0)
+    last = iota((8, nz), 1) == nz - 1
+    for k, store in enumerate(stores):
+        sums_ref[k] = sums[k * ny : (k + 1) * ny]
+        totals = [jnp.zeros((8, ny), jnp.float32)] * 3
+        for group in range(ny // 8):
+            rows = pl.ds(8 * group, 8)
+            level, behind = level_ref[k, rows, :], sums_ref[k, rows, :]
+            left = jnp.exp2(behind)
+            first = (jnp.exp2(behind + binary * level) - left) * level
+            found = [jnp.sum(cells, axis=1, keepdims=True) for cells in (first, first * level, jnp.where(last, left, 0.0))]
+            totals = [jnp.where(lane_group == group, part, total) for part, total in zip(found, totals)]
+        store(*[jnp.sum(jnp.where(eye, total, 0.0), axis=0, keepdims=True) for total in totals])
+
+
+def ghost_terms(ghost, kept, deep):
+    return ghost[0] * (0.5 * ghost[0] + kept[0]) + ghost[1] * kept[1] + ghost[2] * deep
+
+
+def slots(views):
+    me = lax.axis_index("view")
+    return lambda view: step_to(me, view, views)
 
 
 def first_kernel(
     density, image_in_ref, raw_ref, kept_ref, scale_ref, fix_ref, first_ref, sum_ref, xleft_ref,
-    image_ref, level_ref, sums_ref,
-):
-    image_ref[...] = image_in_ref[...]
-    near = [xleft_ref[c, 1] for c in range(3)]
-    far = [xleft_ref[c, 0] - 8.0 * cells for c, cells in enumerate(near)]
-    edge_refs = (raw_ref, kept_ref, scale_ref, fix_ref, first_ref)
-    gather(density, [edge_raw(0, 0, far, *edge_refs), edge_raw(1, 1, near, *edge_refs)], level_ref, sums_ref, sum_ref)
-    for x in range(2):
-        blend(level_ref, sums_ref, x, put(image_ref, x))
-
-
-def last_kernel(
-    density, image_in_ref, raw_ref, kept_ref, scale_ref, fix_ref, first_ref, sum_ref, xright_ref,
-    image_ref, level_ref, sums_ref,
+    image_ref, base_ref, deep_ref, level_ref, sums_ref,
 ):
     nx = raw_ref.shape[0]
     views = image_ref.shape[0]
-    me = lax.axis_index("view")
-
-    def slot(view):
-        return step_to(me, view, views)
-
+    slot = slots(views)
     for view in range(views):
         image_ref[slot(view)] = image_in_ref[view]
+    near = [xleft_ref[c, 1] for c in range(3)]
+    far = [xleft_ref[c, 0] - 8.0 * cells for c, cells in enumerate(near)]
+
+    def prepared(x, place):
+        return raw_ref[x] + on_border(fix_ref[...], x), kept_ref[place, 2] + on_border(first_ref[...], x)
+
+    raws = []
+    for x, ghost in enumerate((far, near)):
+        base, deep = prepared(x, x)
+        raws.append(base + ghost_terms(ghost, kept_ref[x], deep) * scale_ref[0])
+    two_rows(density, raws, level_ref, sums_ref, sum_ref, [put(image_ref, x, slot) for x in range(2)])
+    for k in range(2):
+        base_ref[k], deep_ref[k] = prepared(nx - 2 + k, 2 + k)
+
+
+def last_kernel(
+    density, image_in_ref, base_ref, deep_ref, kept_ref, scale_ref, sum_ref, xright_ref,
+    image_ref, level_ref, sums_ref,
+):
+    views, _, per_view, _ = image_ref.shape
+    nx = views * per_view
+    slot = slots(views)
+    image_ref[...] = image_in_ref[...]
     near = [-xright_ref[c, 0] for c in range(3)]
     far = [-8.0 * cells - xright_ref[c, 1] for c, cells in enumerate(near)]
-    edge_refs = (raw_ref, kept_ref, scale_ref, fix_ref, first_ref)
-    raws = [edge_raw(nx - 2, 2, near, *edge_refs), edge_raw(nx - 1, 3, far, *edge_refs)]
-    gather(density, raws, level_ref, sums_ref, sum_ref)
-    for k in range(2):
-        blend(level_ref, sums_ref, k, put(image_ref, nx - 2 + k, slot))
-
-
-def edged(kernel, density, image, raw, *rest):
-    nx, ny, nz = raw.shape
+    raws = [
+        base_ref[k] + ghost_terms(ghost, kept_ref[2 + k], deep_ref[k]) * scale_ref[scale_ref.shape[0] - 1]
+        for k, ghost in enumerate((near, far))
+    ]
+    two_rows(density, raws, level_ref, sums_ref, sum_ref, [put(image_ref, nx - 2 + k, slot) for k in range(2)])
+
+
+def edged(kernel, density, out_shape, image, *rest):
+    ny = image.shape[3]
+    nz = out_shape[-1].shape[-1] if len(out_shape) > 1 else rest[0].shape[-1]
     return pl.pallas_call(
         functools.partial(kernel, density),
-        out_shape=jax.ShapeDtypeStruct(image.shape, jnp.float32),
-        in_specs=[VMEM] * 8,
-        out_specs=VMEM,
-        scratch_shapes=row_tables(2, ny, nz, 1),
+        out_shape=out_shape,
+        in_specs=[VMEM] * (1 + len(rest)),
+        out_specs=(VMEM,) * len(out_shape),
+        scratch_shapes=[pltpu.VMEM((2, ny, nz), jnp.float32), pltpu.VMEM((2, ny, nz), jnp.float32)],
         compiler_params=PARAMS,
         cost_estimate=COST,
-    )(image, raw, *rest)
+    )(image, *rest)
 
 
 def turn(block, axis, by):
@@ -526,9 +563,12 @@
     yleft, yright = both_sides(yface, "gy")
     raw, pack, kept, scale = shaded(u, parts, yleft, yright, occupied[:, :, 0], q_floor, q_span)
     image, fix, first, summer = blended(density, views, raw, pack, scale, zleft, zright)
-    shared = (raw, kept, scale, fix, first, summer)
-    image = edged(first_kernel, density, image, *shared, xleft)
-    blocks = edged(last_kernel, density, image, *shared, xright)
+    drawn = jax.ShapeDtypeStruct(image.shape, jnp.float32)
+    two = jax.ShapeDtypeStruct((2, ny, nz), jnp.float32)
+    image, base, deep = edged(
+        first_kernel, density, (drawn, two, two), image, raw, kept, scale, fix, first, summer, xleft
+    )
+    (blocks,) = edged(last_kernel, density, (drawn,), image, base, deep, kept, scale, summer, xright)
     return composited(exchanged(blocks, "view"))
 
 

time: 31.7 us -> 31.6 us (level)
  no operation moved by 1% of the time
where the time goes in v12:
time: 31.6 us; the launch traced here: 31.5 us
  Pallas kernels  12.8 us (41%)
  starting transfers between devices  12.5 us (40%)
  waiting for transfers between devices  3.68 us (12%)
  between operations  1.4 us (4%)
  local copies, waits for them, and re-layouts  1.19 us (4%)
    ppermute x5, starting transfers between devices, turn(): lax.ppermute(block, axis, [(i, (i + by) % count) for i in range(count)])  8.24 us
    pallas_call x1, Pallas kernels, shaded(): pl.pallas_call(shade_kernel, out_shape=(jax.ShapeDtypeStruct((nx, ny, nz)...  4.76 us
    ppermute x3, starting transfers between devices, exchanged(): lax.ppermute(blocks[k], axis, list(enumerate(route)))  4.22 us
    pallas_call x1, Pallas kernels, faces(): pl.pallas_call(faces_kernel, out_shape=(jax.ShapeDtypeStruct(u.shape, jnp...  3.78 us
    ppermute x3, waiting for transfers between devices, exchanged(): lax.ppermute(blocks[k], axis, list(enumerate(route)))  3.35 us
    pallas_call x1, Pallas kernels, blended(): pl.pallas_call(functools.partial(blend_kernel, density), out_shape=(jax.S...  2.8 us
    slice x1, local copies, waits for them, and re-layouts, local(): xright = turn(velocity[:, :2], 'gx', -1)  1.18 us
    pallas_call x2, Pallas kernels, edged(): pl.pallas_call(functools.partial(kernel, density), out_shape=out_shape, i...  0.78 us
  transfers between devices with their start and end apart: 8, of which 4 were waited for; matrix products, arithmetic and copies ran while one was open for 0% of the time, Pallas kernels for 37%

profile of v12, /device:TPU:0, one launch (start us, length us, event | category | flops | bytes accessed | tf_op | source)
XLA Modules:
  0.0 31.5 jit_solution(10126928147851350656)
XLA Ops:
  0.0 0.0 copy-start
  0.0 1.2 %fusion = (f32[3,2,128,128]{3,2,1,0:T(8,128)S(1)}, f32[3,2,128,128]{3,2,1,0:T(8,128)S(1)}) fusion(f32[3,32,128,128]{3,2,1,0:T(8,128)} %u_hbm.1), kind=kLoop, calls=%fused_computation.4 | loop fusion | bytes 1572864 | tf_op jit(solution)/shard_map/slice | solution.py:559
  1.2 3.0 %collective-permute-start.3 = (f32[3,2,128,128]{3,2,1,0:T(8,128)S(1)}, f32[3,2,128,128]{3,2,1,0:T(8,128)S(1)}, u32[]{:S(2)}, u32[]{:S(2)}) collective-permute-start(f32[3,2,128,128]{3,2,1,0:T(8,128)S(1)} %get-tuple-element.38), channel_id=1, source_target_pairs={{0,2},{2,4},{4,6},{6,0},{1,3},{3,5},{5,7},{7,1},{8,10},{10,12},{12... | collective-permute-start | bytes 1179656 | tf_op jit(solution)/shard_map/ppermute | solution.py:492
  4.2 1.0 %collective-permute-start.4 = (f32[3,2,128,128]{3,2,1,0:T(8,128)S(1)}, f32[3,2,128,128]{3,2,1,0:T(8,128)S(1)}, u32[]{:S(2)}, u32[]{:S(2)}) collective-permute-start(f32[3,2,128,128]{3,2,1,0:T(8,128)S(1)} %get-tuple-element.37), channel_id=1, source_target_pairs={{0,6},{2,0},{4,2},{6,4},{1,7},{3,1},{5,3},{7,5},{8,14},{10,8},{12,... | collective-permute-start | bytes 1179656 | tf_op jit(solution)/shard_map/ppermute | solution.py:492
  5.2 3.8 %shard_map.46 = (f32[3,32,128,128]{3,2,1,0:T(8,128)S(1)}, bf16[3,32,128,256]{3,2,1,0:T(8,128)(2,1)S(1)}, f32[3,32,4,128]{3,2,1,0:T(4,128)S(1)}, f32[192,128]{1,0:T(8,128)S(1)}, f32[192,128]{1,0:T(8,128)S(1)}) custom-call(f32[3,32,128,128]{3,2,1,0:T(8,128)} %u_hbm.1), custom_call_target="tpu_custom_call" | custom-call | flops 1048576 | bytes 1048576 | tf_op jit(solution)/shard_map/pallas_call | solution.py:97
  9.0 0.1 collective-permute-start
  9.1 2.0 %collective-permute-start.1 = (f32[192,128]{1,0:T(8,128)S(1)}, f32[192,128]{1,0:T(8,128)S(1)}, u32[]{:S(2)}, u32[]{:S(2)}) collective-permute-start(f32[192,128]{1,0:T(8,128)S(1)} %get-tuple-element.27), channel_id=1, source_target_pairs={{0,8},{8,16},{16,24},{24,0},{1,9},{9,17},{17,25},{25,1},{2,10},{10... | collective-permute-start | bytes 294920 | tf_op jit(solution)/shard_map/ppermute | solution.py:492
  11.1 2.1 %collective-permute-start.2 = (f32[192,128]{1,0:T(8,128)S(1)}, f32[192,128]{1,0:T(8,128)S(1)}, u32[]{:S(2)}, u32[]{:S(2)}) collective-permute-start(f32[192,128]{1,0:T(8,128)S(1)} %get-tuple-element.28), channel_id=1, source_target_pairs={{0,24},{8,0},{16,8},{24,16},{1,25},{9,1},{17,9},{25,17},{2,26},{10... | collective-permute-start | bytes 294920 | tf_op jit(solution)/shard_map/ppermute | solution.py:492
  14.5 0.0 collective-permute-done.yleft_ref.yright_ref
  14.5 0.0 copy-done
  14.5 4.8 %shard_map.47 = (f32[32,128,128]{2,1,0:T(8,128)S(1)}, f32[3,128,128]{2,1,0:T(8,128)S(1)}, f32[4,3,128,128]{3,2,1,0:T(8,128)S(1)}, f32[4,128,128]{2,1,0:T(8,128)S(1)}) custom-call(f32[3,32,128,128]{3,2,1,0:T(8,128)S(1)} %get-tuple-element.21.u_ref, bf16[3,32,128,256]{3,2,1,0:T(8,128)(2,1)S(1)} %get-tuple-element.22.parts_ref, ...), custom_call_target="tpu_custom_call" | custom-call | flops 1048576 | bytes 1048576 | tf_op jit(solution)/shard_map/pallas_call | solution.py:238
  19.3 0.0 collective-permute-done.1.zleft_ref
  19.3 0.0 collective-permute-done.2.zright_ref
  19.3 2.8 %shard_map.48 = (f32[4,3,8,128]{3,2,1,0:T(8,128)S(1)}, f32[128,128]{1,0:T(8,128)S(1)}, f32[128,128]{1,0:T(8,128)S(1)}, bf16[256,384]{1,0:T(8,128)(2,1)S(1)}) custom-call(f32[32,128,128]{2,1,0:T(8,128)S(1)} %get-tuple-element.24.raw_ref, f32[3,128,128]{2,1,0:T(8,128)S(1)} %get-tuple-element.25.pack_ref, f32[4,128,128]{2,1,0:T(8,128)S(1)} %get-tuple-element.26.scale_ref, ...), custom_call_target="tpu_custom_call" | custom-call | flops 1048576 | bytes 1048576 | tf_op jit(solution)/shard_map/pallas_call | solution.py:383
  22.1 0.0 collective-permute-done.3.xleft_ref
  22.2 0.4 %shard_map.49 = (f32[4,3,8,128]{3,2,1,0:T(8,128)S(1)}, f32[2,128,128]{2,1,0:T(8,128)S(1)}, f32[2,128,128]{2,1,0:T(8,128)S(1)}) custom-call(f32[4,3,8,128]{3,2,1,0:T(8,128)S(1)} %get-tuple-element.29.image_in_ref, f32[32,128,128]{2,1,0:T(8,128)S(1)} %get-tuple-element.24.raw_ref, f32[4,3,128,128]{3,2,1,0:T(8,128)S(1)} %get-tuple-element.30.kept_ref, ...), custom_call_target="tpu_custom_call" | custom-call | flops 1048576 | bytes 1048576 | tf_op jit(solution)/shard_map/pallas_call | solution.py:479
  22.6 0.3 %collective-permute-done.4.xright_ref = f32[3,2,128,128]{3,2,1,0:T(8,128)S(1)} collective-permute-done((f32[3,2,128,128]{3,2,1,0:T(8,128)S(1)}, f32[3,2,128,128]{3,2,1,0:T(8,128)S(1)}, u32[]{:S(2)}, u32[]{:S(2)}) %collective-permute-start.4) | collective-permute-done | bytes 393248 | tf_op jit(solution)/shard_map/ppermute | solution.py:492
  22.9 0.3 %shard_map.50 = f32[4,3,8,128]{3,2,1,0:T(8,128)S(1)} custom-call(f32[4,3,8,128]{3,2,1,0:T(8,128)S(1)} %get-tuple-element.34.image_in_ref, f32[2,128,128]{2,1,0:T(8,128)S(1)} %get-tuple-element.35.base_ref, f32[2,128,128]{2,1,0:T(8,128)S(1)} %get-tuple-element.36.deep_ref, f32[4,3,128,128]{3,2,1,0:T(8,128)S(1)} %get-tuple-element.30.kept_ref, ...), custom_call_target="tpu_custom_call" | custom-call | flops 1048576 | bytes 1048576 | tf_op jit(solution)/shard_map/pallas_call | solution.py:479
  23.3 2.6 %collective-permute-start.5 = (f32[3,8,128]{2,1,0:T(8,128)S(1)}, f32[3,8,128]{2,1,0:T(8,128)S(1)}, u32[]{:S(2)}, u32[]{:S(2)}) collective-permute-start(f32[3,8,128]{2,1,0:T(8,128)S(1)} %get-tuple-element.41), channel_id=1, source_target_pairs={{0,16},{8,24},{16,8},{24,0},{1,17},{9,25},{17,9},{25,1},{2,18},{10... | collective-permute-start | bytes 36872 | tf_op jit(solution)/shard_map/ppermute | solution.py:522
  25.9 1.2 %collective-permute-start.6 = (f32[3,8,128]{2,1,0:T(8,128)S(1)}, f32[3,8,128]{2,1,0:T(8,128)S(1)}, u32[]{:S(2)}, u32[]{:S(2)}) collective-permute-start(f32[3,8,128]{2,1,0:T(8,128)S(1)} %get-tuple-element.40), channel_id=1, source_target_pairs={{0,24},{8,16},{16,0},{24,8},{1,25},{9,17},{17,1},{25,9},{2,26},{10... | collective-permute-start | bytes 36872 | tf_op jit(solution)/shard_map/ppermute | solution.py:522
  27.2 0.3 %collective-permute-start.7 = (f32[3,8,128]{2,1,0:T(8,128)S(1)}, f32[3,8,128]{2,1,0:T(8,128)S(1)}, u32[]{:S(2)}, u32[]{:S(2)}) collective-permute-start(f32[3,8,128]{2,1,0:T(8,128)S(1)} %get-tuple-element.39), channel_id=1, source_target_pairs={{0,8},{8,0},{16,24},{24,16},{1,9},{9,1},{17,25},{25,17},{2,10},{10... | collective-permute-start | bytes 36872 | tf_op jit(solution)/shard_map/ppermute | solution.py:522
  27.5 1.3 %collective-permute-done.5.refs_1_ = f32[3,8,128]{2,1,0:T(8,128)S(1)} collective-permute-done((f32[3,8,128]{2,1,0:T(8,128)S(1)}, f32[3,8,128]{2,1,0:T(8,128)S(1)}, u32[]{:S(2)}, u32[]{:S(2)}) %collective-permute-start.5) | collective-permute-done | bytes 12320 | tf_op jit(solution)/shard_map/ppermute | solution.py:522
  28.8 1.7 %collective-permute-done.6.refs_2_ = f32[3,8,128]{2,1,0:T(8,128)S(1)} collective-permute-done((f32[3,8,128]{2,1,0:T(8,128)S(1)}, f32[3,8,128]{2,1,0:T(8,128)S(1)}, u32[]{:S(2)}, u32[]{:S(2)}) %collective-permute-start.6) | collective-permute-done | bytes 12320 | tf_op jit(solution)/shard_map/ppermute | solution.py:522
  30.5 0.3 %collective-permute-done.7.refs_3_ = f32[3,8,128]{2,1,0:T(8,128)S(1)} collective-permute-done((f32[3,8,128]{2,1,0:T(8,128)S(1)}, f32[3,8,128]{2,1,0:T(8,128)S(1)}, u32[]{:S(2)}, u32[]{:S(2)}) %collective-permute-start.7) | collective-permute-done | bytes 12320 | tf_op jit(solution)/shard_map/ppermute | solution.py:522
  30.9 0.6 %shard_map.51 = f32[1,1,4,8,128]{4,3,2,1,0:T(8,128)} custom-call(f32[3,8,128]{2,1,0:T(8,128)S(1)} %get-tuple-element.42.refs_0_, f32[3,8,128]{2,1,0:T(8,128)S(1)} %collective-permute-done.5.refs_1_, f32[3,8,128]{2,1,0:T(8,128)S(1)} %collective-permute-done.6.refs_2_, f32[3,8,128]{2,1,0:T(8,128)S(1)} %collective-permute-done.7.refs_3_), custom_call_target="tpu_custom_call" | custom-call | flops 1048576 | bytes 1048576 | tf_op jit(solution)/shard_map/pallas_call | solution.py:544
  (1 shorter events, 0.0 us)
Async XLA Ops:
  0.0 14.5 %copy-start = (s32[4,16,1]{1,2,0:T(1,128)S(1)}, s32[4,16,1]{1,2,0:T(1,128)}, u32[]{:S(2)}) copy-start(s32[4,16,1]{1,2,0:T(1,128)} %param.5) | copy-start | bytes 772
  1.2 21.0 %collective-permute-start.3 = (f32[3,2,128,128]{3,2,1,0:T(8,128)S(1)}, f32[3,2,128,128]{3,2,1,0:T(8,128)S(1)}, u32[]{:S(2)}, u32[]{:S(2)}) collective-permute-start(f32[3,2,128,128]{3,2,1,0:T(8,128)S(1)} %get-tuple-element.38), channel_id=1, source_target_pairs={{0,2},{2,4},{4,6},{6,0},{1,3},{3,5},{5,7},{7,1},{8,10},{10,12},{12... | collective-permute-start | bytes 1179656 | tf_op jit(solution)/shard_map/ppermute | solution.py:492
  4.2 18.7 %collective-permute-start.4 = (f32[3,2,128,128]{3,2,1,0:T(8,128)S(1)}, f32[3,2,128,128]{3,2,1,0:T(8,128)S(1)}, u32[]{:S(2)}, u32[]{:S(2)}) collective-permute-start(f32[3,2,128,128]{3,2,1,0:T(8,128)S(1)} %get-tuple-element.37), channel_id=1, source_target_pairs={{0,6},{2,0},{4,2},{6,4},{1,7},{3,1},{5,3},{7,5},{8,14},{10,8},{12,... | collective-permute-start | bytes 1179656 | tf_op jit(solution)/shard_map/ppermute | solution.py:492
  9.0 5.5 %collective-permute-start = (f32[3,32,4,128]{3,2,1,0:T(4,128)S(1)}, f32[3,32,4,128]{3,2,1,0:T(4,128)S(1)}, u32[]{:S(2)}, u32[]{:S(2)}) collective-permute-start(f32[3,32,4,128]{3,2,1,0:T(4,128)S(1)} %get-tuple-element.23), channel_id=1, source_target_pairs={{0,1},{1,0},{2,3},{3,2},{4,5},{5,4},{6,7},{7,6},{8,9},{9,8},{10,11... | collective-permute-start | bytes 589832 | tf_op jit(solution)/shard_map/ppermute | solution.py:492
  9.1 10.2 %collective-permute-start.1 = (f32[192,128]{1,0:T(8,128)S(1)}, f32[192,128]{1,0:T(8,128)S(1)}, u32[]{:S(2)}, u32[]{:S(2)}) collective-permute-start(f32[192,128]{1,0:T(8,128)S(1)} %get-tuple-element.27), channel_id=1, source_target_pairs={{0,8},{8,16},{16,24},{24,0},{1,9},{9,17},{17,25},{25,1},{2,10},{10... | collective-permute-start | bytes 294920 | tf_op jit(solution)/shard_map/ppermute | solution.py:492
  11.1 8.2 %collective-permute-start.2 = (f32[192,128]{1,0:T(8,128)S(1)}, f32[192,128]{1,0:T(8,128)S(1)}, u32[]{:S(2)}, u32[]{:S(2)}) collective-permute-start(f32[192,128]{1,0:T(8,128)S(1)} %get-tuple-element.28), channel_id=1, source_target_pairs={{0,24},{8,0},{16,8},{24,16},{1,25},{9,1},{17,9},{25,17},{2,26},{10... | collective-permute-start | bytes 294920 | tf_op jit(solution)/shard_map/ppermute | solution.py:492
  23.3 5.5 %collective-permute-start.5 = (f32[3,8,128]{2,1,0:T(8,128)S(1)}, f32[3,8,128]{2,1,0:T(8,128)S(1)}, u32[]{:S(2)}, u32[]{:S(2)}) collective-permute-start(f32[3,8,128]{2,1,0:T(8,128)S(1)} %get-tuple-element.41), channel_id=1, source_target_pairs={{0,16},{8,24},{16,8},{24,0},{1,17},{9,25},{17,9},{25,1},{2,18},{10... | collective-permute-start | bytes 36872 | tf_op jit(solution)/shard_map/ppermute | solution.py:522
  25.9 4.6 %collective-permute-start.6 = (f32[3,8,128]{2,1,0:T(8,128)S(1)}, f32[3,8,128]{2,1,0:T(8,128)S(1)}, u32[]{:S(2)}, u32[]{:S(2)}) collective-permute-start(f32[3,8,128]{2,1,0:T(8,128)S(1)} %get-tuple-element.40), channel_id=1, source_target_pairs={{0,24},{8,16},{16,0},{24,8},{1,25},{9,17},{17,1},{25,9},{2,26},{10... | collective-permute-start | bytes 36872 | tf_op jit(solution)/shard_map/ppermute | solution.py:522
  27.2 3.7 %collective-permute-start.7 = (f32[3,8,128]{2,1,0:T(8,128)S(1)}, f32[3,8,128]{2,1,0:T(8,128)S(1)}, u32[]{:S(2)}, u32[]{:S(2)}) collective-permute-start(f32[3,8,128]{2,1,0:T(8,128)S(1)} %get-tuple-element.39), channel_id=1, source_target_pairs={{0,8},{8,0},{16,24},{24,16},{1,9},{9,1},{17,25},{25,17},{2,10},{10... | collective-permute-start | bytes 36872 | tf_op jit(solution)/shard_map/ppermute | solution.py:522

commit v13 on v12

--- a/solution.py
+++ b/solution.py
@@ -26,7 +26,7 @@
     return lax.broadcasted_iota(jnp.int32, shape, dim)
 
 
-def faces_kernel(u_hbm, u_ref, parts_ref, yface_ref, tail_ref, head_ref, packed_ref, sems):
+def faces_kernel(u_hbm, u_ref, parts_ref, xhead_ref, yface_ref, tail_ref, head_ref, packed_ref, sems):
     comps, nx, ny, nz = u_ref.shape
     quarters = sems.shape[1]
     rows = ny // quarters
@@ -60,6 +60,7 @@
         lax.fori_loop(0, quarters, quarter, 0)
     sub = iota((8, nz), 0)
     for c in range(comps):
+        xhead_ref[c] = u_ref[c, pl.ds(0, 2)]
         for x in range(nx):
             lines = jnp.where(sub >= 6, u_ref[c, x, pl.ds(ny - 8, 8), :], u_ref[c, x, pl.ds(0, 8), :])
             yface_ref[c, x] = pltpu.roll(lines, 2, 0)[:4]
@@ -99,12 +100,13 @@
         out_shape=(
             jax.ShapeDtypeStruct(u.shape, jnp.float32),
             jax.ShapeDtypeStruct((comps, nx, ny, 2 * nz), jnp.bfloat16),
+            jax.ShapeDtypeStruct((comps, 2, ny, nz), jnp.float32),
             jax.ShapeDtypeStruct((comps, nx, 4, nz), jnp.float32),
             message,
             message,
         ),
         in_specs=[HBM],
-        out_specs=(VMEM,) * 5,
+        out_specs=(VMEM,) * 6,
         scratch_shapes=[pltpu.VMEM((comps, ny, nz), jnp.float32), pltpu.SemaphoreType.DMA((comps, 4))],
         compiler_params=pltpu.CompilerParams(vmem_limit_bytes=37 << 20),
         cost_estimate=COST,
@@ -556,8 +558,8 @@
     views = lax.axis_size("view")
     density = 5.0 / (nz * views)
     xleft = turn(velocity[:, nx - 2 :], "gx", 1)
-    xright = turn(velocity[:, :2], "gx", -1)
-    u, parts, yface, ztail, zhead = faces(velocity)
+    u, parts, xhead, yface, ztail, zhead = faces(velocity)
+    xright = turn(xhead, "gx", -1)
     zleft = turn(ztail, "view", 1)
     zright = turn(zhead, "view", -1)
     yleft, yright = both_sides(yface, "gy")

time: 31.6 us -> 31.5 us (level)
  transfers between devices with their start and end apart: 8 -> 8, of which waited for: 4 -> 4; matrix products, arithmetic and copies ran while one was open for 0% -> 0% of each run, Pallas kernels for 37% -> 38%
where the time goes in v13:
time: 31.5 us; the launch traced here: 31.3 us
  Pallas kernels  12.8 us (41%)
  starting transfers between devices  12.3 us (39%)
  waiting for transfers between devices  3.84 us (12%)
  between operations  1.39 us (4%)
  local copies, waits for them, and re-layouts  1.05 us (3%)
    ppermute x5, starting transfers between devices, turn(): lax.ppermute(block, axis, [(i, (i + by) % count) for i in range(count)])  8.08 us
    pallas_call x1, Pallas kernels, shaded(): pl.pallas_call(shade_kernel, out_shape=(jax.ShapeDtypeStruct((nx, ny, nz)...  4.76 us
    ppermute x3, starting transfers between devices, exchanged(): lax.ppermute(blocks[k], axis, list(enumerate(route)))  4.22 us
    pallas_call x1, Pallas kernels, faces(): pl.pallas_call(faces_kernel, out_shape=(jax.ShapeDtypeStruct(u.shape, jnp...  3.78 us
    ppermute x3, waiting for transfers between devices, exchanged(): lax.ppermute(blocks[k], axis, list(enumerate(route)))  3.35 us
    pallas_call x1, Pallas kernels, blended(): pl.pallas_call(functools.partial(blend_kernel, density), out_shape=(jax.S...  2.8 us
    slice x1, local copies, waits for them, and re-layouts, local(): xleft = turn(velocity[:, nx - 2:], 'gx', 1)  1.04 us
    pallas_call x2, Pallas kernels, edged(): pl.pallas_call(functools.partial(kernel, density), out_shape=out_shape, i...  0.78 us
  transfers between devices with their start and end apart: 8, of which 4 were waited for; matrix products, arithmetic and copies ran while one was open for 0% of the time, Pallas kernels for 38%

profile of v13, /device:TPU:0, one launch (start us, length us, event | category | flops | bytes accessed | tf_op | source)
XLA Modules:
  0.0 31.3 jit_solution(12095574664731965991)
XLA Ops:
  0.0 0.0 copy-start
  0.0 1.0 %slice.15 = f32[3,2,128,128]{3,2,1,0:T(8,128)S(1)} slice(f32[3,32,128,128]{3,2,1,0:T(8,128)} %u_hbm.1), slice={[0:3], [30:32], [0:128], [0:128]} | slice | bytes 786432 | tf_op jit(solution)/shard_map/slice | solution.py:560
  1.0 3.0 %collective-permute-start.3 = (f32[3,2,128,128]{3,2,1,0:T(8,128)S(1)}, f32[3,2,128,128]{3,2,1,0:T(8,128)S(1)}, u32[]{:S(2)}, u32[]{:S(2)}) collective-permute-start(f32[3,2,128,128]{3,2,1,0:T(8,128)S(1)} %slice.15), channel_id=1, source_target_pairs={{0,2},{2,4},{4,6},{6,0},{1,3},{3,5},{5,7},{7,1},{8,10},{10,12},{12... | collective-permute-start | bytes 1179656 | tf_op jit(solution)/shard_map/ppermute | solution.py:494
  4.0 3.8 %shard_map.46 = (f32[3,32,128,128]{3,2,1,0:T(8,128)S(1)}, bf16[3,32,128,256]{3,2,1,0:T(8,128)(2,1)S(1)}, f32[3,2,128,128]{3,2,1,0:T(8,128)S(1)}, f32[3,32,4,128]...) custom-call(f32[3,32,128,128]{3,2,1,0:T(8,128)} %u_hbm.1), custom_call_target="tpu_custom_call" | custom-call | flops 1048576 | bytes 1048576 | tf_op jit(solution)/shard_map/pallas_call | solution.py:98
  7.8 1.0 %collective-permute-start.4 = (f32[3,2,128,128]{3,2,1,0:T(8,128)S(1)}, f32[3,2,128,128]{3,2,1,0:T(8,128)S(1)}, u32[]{:S(2)}, u32[]{:S(2)}) collective-permute-start(f32[3,2,128,128]{3,2,1,0:T(8,128)S(1)} %get-tuple-element.38), channel_id=1, source_target_pairs={{0,6},{2,0},{4,2},{6,4},{1,7},{3,1},{5,3},{7,5},{8,14},{10,8},{12,... | collective-permute-start | bytes 1179656 | tf_op jit(solution)/shard_map/ppermute | solution.py:494
  8.8 0.0 collective-permute-start
  8.9 2.0 %collective-permute-start.1 = (f32[192,128]{1,0:T(8,128)S(1)}, f32[192,128]{1,0:T(8,128)S(1)}, u32[]{:S(2)}, u32[]{:S(2)}) collective-permute-start(f32[192,128]{1,0:T(8,128)S(1)} %get-tuple-element.28), channel_id=1, source_target_pairs={{0,8},{8,16},{16,24},{24,0},{1,9},{9,17},{17,25},{25,1},{2,10},{10... | collective-permute-start | bytes 294920 | tf_op jit(solution)/shard_map/ppermute | solution.py:494
  10.9 2.0 %collective-permute-start.2 = (f32[192,128]{1,0:T(8,128)S(1)}, f32[192,128]{1,0:T(8,128)S(1)}, u32[]{:S(2)}, u32[]{:S(2)}) collective-permute-start(f32[192,128]{1,0:T(8,128)S(1)} %get-tuple-element.29), channel_id=1, source_target_pairs={{0,24},{8,0},{16,8},{24,16},{1,25},{9,1},{17,9},{25,17},{2,26},{10... | collective-permute-start | bytes 294920 | tf_op jit(solution)/shard_map/ppermute | solution.py:494
  14.2 0.0 collective-permute-done.yleft_ref.yright_ref
  14.2 0.0 copy-done
  14.2 4.8 %shard_map.47 = (f32[32,128,128]{2,1,0:T(8,128)S(1)}, f32[3,128,128]{2,1,0:T(8,128)S(1)}, f32[4,3,128,128]{3,2,1,0:T(8,128)S(1)}, f32[4,128,128]{2,1,0:T(8,128)S(1)}) custom-call(f32[3,32,128,128]{3,2,1,0:T(8,128)S(1)} %get-tuple-element.22.u_ref, bf16[3,32,128,256]{3,2,1,0:T(8,128)(2,1)S(1)} %get-tuple-element.23.parts_ref, ...), custom_call_target="tpu_custom_call" | custom-call | flops 1048576 | bytes 1048576 | tf_op jit(solution)/shard_map/pallas_call | solution.py:240
  19.0 0.0 collective-permute-done.1.zleft_ref
  19.0 0.0 collective-permute-done.2.zright_ref
  19.0 2.8 %shard_map.48 = (f32[4,3,8,128]{3,2,1,0:T(8,128)S(1)}, f32[128,128]{1,0:T(8,128)S(1)}, f32[128,128]{1,0:T(8,128)S(1)}, bf16[256,384]{1,0:T(8,128)(2,1)S(1)}) custom-call(f32[32,128,128]{2,1,0:T(8,128)S(1)} %get-tuple-element.25.raw_ref, f32[3,128,128]{2,1,0:T(8,128)S(1)} %get-tuple-element.26.pack_ref, f32[4,128,128]{2,1,0:T(8,128)S(1)} %get-tuple-element.27.scale_ref, ...), custom_call_target="tpu_custom_call" | custom-call | flops 1048576 | bytes 1048576 | tf_op jit(solution)/shard_map/pallas_call | solution.py:385
  21.8 0.0 collective-permute-done.3.xleft_ref
  21.8 0.4 %shard_map.49 = (f32[4,3,8,128]{3,2,1,0:T(8,128)S(1)}, f32[2,128,128]{2,1,0:T(8,128)S(1)}, f32[2,128,128]{2,1,0:T(8,128)S(1)}) custom-call(f32[4,3,8,128]{3,2,1,0:T(8,128)S(1)} %get-tuple-element.30.image_in_ref, f32[32,128,128]{2,1,0:T(8,128)S(1)} %get-tuple-element.25.raw_ref, f32[4,3,128,128]{3,2,1,0:T(8,128)S(1)} %get-tuple-element.31.kept_ref, ...), custom_call_target="tpu_custom_call" | custom-call | flops 1048576 | bytes 1048576 | tf_op jit(solution)/shard_map/pallas_call | solution.py:481
  22.3 0.5 %collective-permute-done.4.xright_ref = f32[3,2,128,128]{3,2,1,0:T(8,128)S(1)} collective-permute-done((f32[3,2,128,128]{3,2,1,0:T(8,128)S(1)}, f32[3,2,128,128]{3,2,1,0:T(8,128)S(1)}, u32[]{:S(2)}, u32[]{:S(2)}) %collective-permute-start.4) | collective-permute-done | bytes 393248 | tf_op jit(solution)/shard_map/ppermute | solution.py:494
  22.8 0.3 %shard_map.50 = f32[4,3,8,128]{3,2,1,0:T(8,128)S(1)} custom-call(f32[4,3,8,128]{3,2,1,0:T(8,128)S(1)} %get-tuple-element.35.image_in_ref, f32[2,128,128]{2,1,0:T(8,128)S(1)} %get-tuple-element.36.base_ref, f32[2,128,128]{2,1,0:T(8,128)S(1)} %get-tuple-element.37.deep_ref, f32[4,3,128,128]{3,2,1,0:T(8,128)S(1)} %get-tuple-element.31.kept_ref, ...), custom_call_target="tpu_custom_call" | custom-call | flops 1048576 | bytes 1048576 | tf_op jit(solution)/shard_map/pallas_call | solution.py:481
  23.1 2.6 %collective-permute-start.5 = (f32[3,8,128]{2,1,0:T(8,128)S(1)}, f32[3,8,128]{2,1,0:T(8,128)S(1)}, u32[]{:S(2)}, u32[]{:S(2)}) collective-permute-start(f32[3,8,128]{2,1,0:T(8,128)S(1)} %get-tuple-element.41), channel_id=1, source_target_pairs={{0,16},{8,24},{16,8},{24,0},{1,17},{9,25},{17,9},{25,1},{2,18},{10... | collective-permute-start | bytes 36872 | tf_op jit(solution)/shard_map/ppermute | solution.py:524
  25.8 1.2 %collective-permute-start.6 = (f32[3,8,128]{2,1,0:T(8,128)S(1)}, f32[3,8,128]{2,1,0:T(8,128)S(1)}, u32[]{:S(2)}, u32[]{:S(2)}) collective-permute-start(f32[3,8,128]{2,1,0:T(8,128)S(1)} %get-tuple-element.40), channel_id=1, source_target_pairs={{0,24},{8,16},{16,0},{24,8},{1,25},{9,17},{17,1},{25,9},{2,26},{10... | collective-permute-start | bytes 36872 | tf_op jit(solution)/shard_map/ppermute | solution.py:524
  27.0 0.3 %collective-permute-start.7 = (f32[3,8,128]{2,1,0:T(8,128)S(1)}, f32[3,8,128]{2,1,0:T(8,128)S(1)}, u32[]{:S(2)}, u32[]{:S(2)}) collective-permute-start(f32[3,8,128]{2,1,0:T(8,128)S(1)} %get-tuple-element.39), channel_id=1, source_target_pairs={{0,8},{8,0},{16,24},{24,16},{1,9},{9,1},{17,25},{25,17},{2,10},{10... | collective-permute-start | bytes 36872 | tf_op jit(solution)/shard_map/ppermute | solution.py:524
  27.4 1.3 %collective-permute-done.5.refs_1_ = f32[3,8,128]{2,1,0:T(8,128)S(1)} collective-permute-done((f32[3,8,128]{2,1,0:T(8,128)S(1)}, f32[3,8,128]{2,1,0:T(8,128)S(1)}, u32[]{:S(2)}, u32[]{:S(2)}) %collective-permute-start.5) | collective-permute-done | bytes 12320 | tf_op jit(solution)/shard_map/ppermute | solution.py:524
  28.7 1.7 %collective-permute-done.6.refs_2_ = f32[3,8,128]{2,1,0:T(8,128)S(1)} collective-permute-done((f32[3,8,128]{2,1,0:T(8,128)S(1)}, f32[3,8,128]{2,1,0:T(8,128)S(1)}, u32[]{:S(2)}, u32[]{:S(2)}) %collective-permute-start.6) | collective-permute-done | bytes 12320 | tf_op jit(solution)/shard_map/ppermute | solution.py:524
  30.4 0.3 %collective-permute-done.7.refs_3_ = f32[3,8,128]{2,1,0:T(8,128)S(1)} collective-permute-done((f32[3,8,128]{2,1,0:T(8,128)S(1)}, f32[3,8,128]{2,1,0:T(8,128)S(1)}, u32[]{:S(2)}, u32[]{:S(2)}) %collective-permute-start.7) | collective-permute-done | bytes 12320 | tf_op jit(solution)/shard_map/ppermute | solution.py:524
  30.7 0.6 %shard_map.51 = f32[1,1,4,8,128]{4,3,2,1,0:T(8,128)} custom-call(f32[3,8,128]{2,1,0:T(8,128)S(1)} %get-tuple-element.42.refs_0_, f32[3,8,128]{2,1,0:T(8,128)S(1)} %collective-permute-done.5.refs_1_, f32[3,8,128]{2,1,0:T(8,128)S(1)} %collective-permute-done.6.refs_2_, f32[3,8,128]{2,1,0:T(8,128)S(1)} %collective-permute-done.7.refs_3_), custom_call_target="tpu_custom_call" | custom-call | flops 1048576 | bytes 1048576 | tf_op jit(solution)/shard_map/pallas_call | solution.py:546
  (1 shorter events, 0.0 us)
Async XLA Ops:
  0.0 14.2 %copy-start = (s32[4,16,1]{1,2,0:T(1,128)S(1)}, s32[4,16,1]{1,2,0:T(1,128)}, u32[]{:S(2)}) copy-start(s32[4,16,1]{1,2,0:T(1,128)} %param.5) | copy-start | bytes 772
  1.0 20.8 %collective-permute-start.3 = (f32[3,2,128,128]{3,2,1,0:T(8,128)S(1)}, f32[3,2,128,128]{3,2,1,0:T(8,128)S(1)}, u32[]{:S(2)}, u32[]{:S(2)}) collective-permute-start(f32[3,2,128,128]{3,2,1,0:T(8,128)S(1)} %slice.15), channel_id=1, source_target_pairs={{0,2},{2,4},{4,6},{6,0},{1,3},{3,5},{5,7},{7,1},{8,10},{10,12},{12... | collective-permute-start | bytes 1179656 | tf_op jit(solution)/shard_map/ppermute | solution.py:494
  7.8 15.0 %collective-permute-start.4 = (f32[3,2,128,128]{3,2,1,0:T(8,128)S(1)}, f32[3,2,128,128]{3,2,1,0:T(8,128)S(1)}, u32[]{:S(2)}, u32[]{:S(2)}) collective-permute-start(f32[3,2,128,128]{3,2,1,0:T(8,128)S(1)} %get-tuple-element.38), channel_id=1, source_target_pairs={{0,6},{2,0},{4,2},{6,4},{1,7},{3,1},{5,3},{7,5},{8,14},{10,8},{12,... | collective-permute-start | bytes 1179656 | tf_op jit(solution)/shard_map/ppermute | solution.py:494
  8.8 5.4 %collective-permute-start = (f32[3,32,4,128]{3,2,1,0:T(4,128)S(1)}, f32[3,32,4,128]{3,2,1,0:T(4,128)S(1)}, u32[]{:S(2)}, u32[]{:S(2)}) collective-permute-start(f32[3,32,4,128]{3,2,1,0:T(4,128)S(1)} %get-tuple-element.24), channel_id=1, source_target_pairs={{0,1},{1,0},{2,3},{3,2},{4,5},{5,4},{6,7},{7,6},{8,9},{9,8},{10,11... | collective-permute-start | bytes 589832 | tf_op jit(solution)/shard_map/ppermute | solution.py:494
  8.9 10.2 %collective-permute-start.1 = (f32[192,128]{1,0:T(8,128)S(1)}, f32[192,128]{1,0:T(8,128)S(1)}, u32[]{:S(2)}, u32[]{:S(2)}) collective-permute-start(f32[192,128]{1,0:T(8,128)S(1)} %get-tuple-element.28), channel_id=1, source_target_pairs={{0,8},{8,16},{16,24},{24,0},{1,9},{9,17},{17,25},{25,1},{2,10},{10... | collective-permute-start | bytes 294920 | tf_op jit(solution)/shard_map/ppermute | solution.py:494
  10.9 8.1 %collective-permute-start.2 = (f32[192,128]{1,0:T(8,128)S(1)}, f32[192,128]{1,0:T(8,128)S(1)}, u32[]{:S(2)}, u32[]{:S(2)}) collective-permute-start(f32[192,128]{1,0:T(8,128)S(1)} %get-tuple-element.29), channel_id=1, source_target_pairs={{0,24},{8,0},{16,8},{24,16},{1,25},{9,1},{17,9},{25,17},{2,26},{10... | collective-permute-start | bytes 294920 | tf_op jit(solution)/shard_map/ppermute | solution.py:494
  23.1 5.5 %collective-permute-start.5 = (f32[3,8,128]{2,1,0:T(8,128)S(1)}, f32[3,8,128]{2,1,0:T(8,128)S(1)}, u32[]{:S(2)}, u32[]{:S(2)}) collective-permute-start(f32[3,8,128]{2,1,0:T(8,128)S(1)} %get-tuple-element.41), channel_id=1, source_target_pairs={{0,16},{8,24},{16,8},{24,0},{1,17},{9,25},{17,9},{25,1},{2,18},{10... | collective-permute-start | bytes 36872 | tf_op jit(solution)/shard_map/ppermute | solution.py:524
  25.8 4.6 %collective-permute-start.6 = (f32[3,8,128]{2,1,0:T(8,128)S(1)}, f32[3,8,128]{2,1,0:T(8,128)S(1)}, u32[]{:S(2)}, u32[]{:S(2)}) collective-permute-start(f32[3,8,128]{2,1,0:T(8,128)S(1)} %get-tuple-element.40), channel_id=1, source_target_pairs={{0,24},{8,16},{16,0},{24,8},{1,25},{9,17},{17,1},{25,9},{2,26},{10... | collective-permute-start | bytes 36872 | tf_op jit(solution)/shard_map/ppermute | solution.py:524
  27.0 3.7 %collective-permute-start.7 = (f32[3,8,128]{2,1,0:T(8,128)S(1)}, f32[3,8,128]{2,1,0:T(8,128)S(1)}, u32[]{:S(2)}, u32[]{:S(2)}) collective-permute-start(f32[3,8,128]{2,1,0:T(8,128)S(1)} %get-tuple-element.39), channel_id=1, source_target_pairs={{0,8},{8,0},{16,24},{24,16},{1,9},{9,1},{17,25},{25,17},{2,10},{10... | collective-permute-start | bytes 36872 | tf_op jit(solution)/shard_map/ppermute | solution.py:524

commit v14 on v13

--- a/solution.py
+++ b/solution.py
@@ -439,7 +439,7 @@
     image_ref, base_ref, deep_ref, level_ref, sums_ref,
 ):
     nx = raw_ref.shape[0]
-    views = image_ref.shape[0]
+    views = image_in_ref.shape[0]
     slot = slots(views)
     for view in range(views):
         image_ref[slot(view)] = image_in_ref[view]
@@ -459,11 +459,10 @@
 
 
 def last_kernel(
-    density, image_in_ref, base_ref, deep_ref, kept_ref, scale_ref, sum_ref, xright_ref,
+    views, density, image_in_ref, base_ref, deep_ref, kept_ref, scale_ref, sum_ref, xright_ref,
     image_ref, level_ref, sums_ref,
 ):
-    views, _, per_view, _ = image_ref.shape
-    nx = views * per_view
+    nx = views * image_ref.shape[2]
     slot = slots(views)
     image_ref[...] = image_in_ref[...]
     near = [-xright_ref[c, 0] for c in range(3)]
@@ -501,7 +500,7 @@
 
 def exchange(count):
     if count == 4:
-        return [(2, 3, 1, 0), (3, 2, 0, 1), (1, 0, 3, 2)]
+        return [(1, 2, 0, 3), (2, 1, 3, 0), (3, 0, 2, 1), (0, 3, 1, 2)]
     if count & (count - 1) == 0:
         return [tuple(i ^ step for i in range(count)) for step in range(count - 1, 0, -1)]
     return [tuple((i + step) % count for i in range(count)) for step in range(1, count)]
@@ -524,27 +523,31 @@
     return [blocks[0]] + [lax.ppermute(blocks[k], axis, list(enumerate(route))) for k, route in enumerate(routes, 1)]
 
 
-def composite_kernel(*refs):
+def composite_kernel(count, *refs):
     *image_refs, out_ref = refs
-    count = len(image_refs)
     me = lax.axis_index("view")
     sources = [me] + [looked_up(me, [route.index(i) for i in range(count)]) for route in exchange(count)]
+    idle = [False] + [source == me for source in sources[1:]]
+    images = [
+        [image_ref[k] if sits is False else jnp.where(sits, float(k == 2), image_ref[k]) for k in range(3)]
+        for image_ref, sits in zip(image_refs, idle)
+    ]
     red = square = 0.0
     through = 1.0
-    for source, image_ref in zip(sources, image_refs):
+    for source, image in zip(sources, images):
         passing = 1.0
-        for other, front_ref in zip(sources, image_refs):
-            passing = passing * jnp.where(other < source, front_ref[2], 1.0)
-        red = red + passing * image_ref[0]
-        square = square + passing * image_ref[1]
-        through = through * image_ref[2]
+        for other, front in zip(sources, images):
+            passing = passing * jnp.where(other < source, front[2], 1.0)
+        red = red + passing * image[0]
+        square = square + passing * image[1]
+        through = through * image[2]
     for k, values in enumerate((red, 4.0 * (red - square), 1.0 - through - red, 1.0 - through)):
         out_ref[0, 0, k] = values
 
 
-def composited(images):
+def composited(count, images):
     return pl.pallas_call(
-        composite_kernel,
+        functools.partial(composite_kernel, count),
         out_shape=jax.ShapeDtypeStruct((1, 1, 4) + images[0].shape[1:], jnp.float32),
         in_specs=[VMEM] * len(images),
         out_specs=VMEM,
@@ -565,13 +568,13 @@
     yleft, yright = both_sides(yface, "gy")
     raw, pack, kept, scale = shaded(u, parts, yleft, yright, occupied[:, :, 0], q_floor, q_span)
     image, fix, first, summer = blended(density, views, raw, pack, scale, zleft, zright)
-    drawn = jax.ShapeDtypeStruct(image.shape, jnp.float32)
+    drawn = jax.ShapeDtypeStruct((1 + len(exchange(views)),) + image.shape[1:], jnp.float32)
     two = jax.ShapeDtypeStruct((2, ny, nz), jnp.float32)
     image, base, deep = edged(
         first_kernel, density, (drawn, two, two), image, raw, kept, scale, fix, first, summer, xleft
     )
-    (blocks,) = edged(last_kernel, density, (drawn,), image, base, deep, kept, scale, summer, xright)
-    return composited(exchanged(blocks, "view"))
+    (blocks,) = edged(functools.partial(last_kernel, views), density, (drawn,), image, base, deep, kept, scale, summer, xright)
+    return composited(views, exchanged(blocks, "view"))
 
 
 def solution(mesh):

time: 31.5 us -> 37.3 us (1.18)
  the two profiles are of different devices: /device:TPU:0 before, /device:TPU:8 now
where the time goes in v14:
time: 37.3 us; the launch traced here: 37 us
  starting transfers between devices  17.1 us (46%)
  Pallas kernels  12.8 us (34%)
  waiting for transfers between devices  4.69 us (13%)
  between operations  1.43 us (4%)
  local copies, waits for them, and re-layouts  1.05 us (3%)
    ppermute x4, starting transfers between devices, exchanged(): lax.ppermute(blocks[k], axis, list(enumerate(route)))  12 us
    ppermute x5, starting transfers between devices, turn(): lax.ppermute(block, axis, [(i, (i + by) % count) for i in range(count)])  5.06 us
    pallas_call x1, Pallas kernels, shaded(): pl.pallas_call(shade_kernel, out_shape=(jax.ShapeDtypeStruct((nx, ny, nz)...  4.76 us
    pallas_call x1, Pallas kernels, faces(): pl.pallas_call(faces_kernel, out_shape=(jax.ShapeDtypeStruct(u.shape, jnp...  3.78 us
    pallas_call x1, Pallas kernels, blended(): pl.pallas_call(functools.partial(blend_kernel, density), out_shape=(jax.S...  2.81 us
    ppermute x4, waiting for transfers between devices, exchanged(): lax.ppermute(blocks[k], axis, list(enumerate(route)))  2.62 us
    ppermute x5, waiting for transfers between devices, turn(): lax.ppermute(block, axis, [(i, (i + by) % count) for i in range(count)])  2.07 us
    slice x1, local copies, waits for them, and re-layouts, local(): xleft = turn(velocity[:, nx - 2:], 'gx', 1)  1.04 us
  transfers between devices with their start and end apart: 9, of which 2 were waited for; matrix products, arithmetic and copies ran while one was open for 0% of the time, Pallas kernels for 32%

profile of v14, /device:TPU:8, one launch (start us, length us, event | category | flops | bytes accessed | tf_op | source)
XLA Modules:
  0.0 37.0 jit_solution(5835032595171938761)
XLA Ops:
  0.0 0.0 copy-start
  0.0 1.0 %slice.18 = f32[3,2,128,128]{3,2,1,0:T(8,128)S(1)} slice(f32[3,32,128,128]{3,2,1,0:T(8,128)} %u_hbm.1), slice={[0:3], [30:32], [0:128], [0:128]} | slice | bytes 786432 | tf_op jit(solution)/shard_map/slice | solution.py:563
  1.0 1.5 %collective-permute-start.3 = (f32[3,2,128,128]{3,2,1,0:T(8,128)S(1)}, f32[3,2,128,128]{3,2,1,0:T(8,128)S(1)}, u32[]{:S(2)}, u32[]{:S(2)}) collective-permute-start(f32[3,2,128,128]{3,2,1,0:T(8,128)S(1)} %slice.18), channel_id=1, source_target_pairs={{0,2},{2,4},{4,6},{6,0},{1,3},{3,5},{5,7},{7,1},{8,10},{10,12},{12... | collective-permute-start | bytes 1179656 | tf_op jit(solution)/shard_map/ppermute | solution.py:493
  2.6 3.8 %shard_map.46 = (f32[3,32,128,128]{3,2,1,0:T(8,128)S(1)}, bf16[3,32,128,256]{3,2,1,0:T(8,128)(2,1)S(1)}, f32[3,2,128,128]{3,2,1,0:T(8,128)S(1)}, f32[3,32,4,128]...) custom-call(f32[3,32,128,128]{3,2,1,0:T(8,128)} %u_hbm.1), custom_call_target="tpu_custom_call" | custom-call | flops 1048576 | bytes 1048576 | tf_op jit(solution)/shard_map/pallas_call | solution.py:98
  6.4 1.5 %collective-permute-start.4 = (f32[3,2,128,128]{3,2,1,0:T(8,128)S(1)}, f32[3,2,128,128]{3,2,1,0:T(8,128)S(1)}, u32[]{:S(2)}, u32[]{:S(2)}) collective-permute-start(f32[3,2,128,128]{3,2,1,0:T(8,128)S(1)} %get-tuple-element.38), channel_id=1, source_target_pairs={{0,6},{2,0},{4,2},{6,4},{1,7},{3,1},{5,3},{7,5},{8,14},{10,8},{12,... | collective-permute-start | bytes 1179656 | tf_op jit(solution)/shard_map/ppermute | solution.py:493
  7.9 0.0 collective-permute-start
  7.9 1.6 %collective-permute-start.1 = (f32[192,128]{1,0:T(8,128)S(1)}, f32[192,128]{1,0:T(8,128)S(1)}, u32[]{:S(2)}, u32[]{:S(2)}) collective-permute-start(f32[192,128]{1,0:T(8,128)S(1)} %get-tuple-element.28), channel_id=1, source_target_pairs={{0,8},{8,16},{16,24},{24,0},{1,9},{9,17},{17,25},{25,1},{2,10},{10... | collective-permute-start | bytes 294920 | tf_op jit(solution)/shard_map/ppermute | solution.py:493
  9.4 0.4 %collective-permute-start.2 = (f32[192,128]{1,0:T(8,128)S(1)}, f32[192,128]{1,0:T(8,128)S(1)}, u32[]{:S(2)}, u32[]{:S(2)}) collective-permute-start(f32[192,128]{1,0:T(8,128)S(1)} %get-tuple-element.29), channel_id=1, source_target_pairs={{0,24},{8,0},{16,8},{24,16},{1,25},{9,1},{17,9},{25,17},{2,26},{10... | collective-permute-start | bytes 294920 | tf_op jit(solution)/shard_map/ppermute | solution.py:493
  11.2 0.0 collective-permute-done.yleft_ref.yright_ref
  11.2 0.0 copy-done
  11.2 4.8 %shard_map.47 = (f32[32,128,128]{2,1,0:T(8,128)S(1)}, f32[3,128,128]{2,1,0:T(8,128)S(1)}, f32[4,3,128,128]{3,2,1,0:T(8,128)S(1)}, f32[4,128,128]{2,1,0:T(8,128)S(1)}) custom-call(f32[3,32,128,128]{3,2,1,0:T(8,128)S(1)} %get-tuple-element.22.u_ref, bf16[3,32,128,256]{3,2,1,0:T(8,128)(2,1)S(1)} %get-tuple-element.23.parts_ref, ...), custom_call_target="tpu_custom_call" | custom-call | flops 1048576 | bytes 1048576 | tf_op jit(solution)/shard_map/pallas_call | solution.py:240
  16.0 0.0 collective-permute-done.1.zleft_ref
  16.0 0.0 collective-permute-done.2.zright_ref
  16.0 2.8 %shard_map.48 = (f32[4,3,8,128]{3,2,1,0:T(8,128)S(1)}, f32[128,128]{1,0:T(8,128)S(1)}, f32[128,128]{1,0:T(8,128)S(1)}, bf16[256,384]{1,0:T(8,128)(2,1)S(1)}) custom-call(f32[32,128,128]{2,1,0:T(8,128)S(1)} %get-tuple-element.25.raw_ref, f32[3,128,128]{2,1,0:T(8,128)S(1)} %get-tuple-element.26.pack_ref, f32[4,128,128]{2,1,0:T(8,128)S(1)} %get-tuple-element.27.scale_ref, ...), custom_call_target="tpu_custom_call" | custom-call | flops 1048576 | bytes 1048576 | tf_op jit(solution)/shard_map/pallas_call | solution.py:385
  18.8 0.0 collective-permute-done.3.xleft_ref
  18.9 0.4 %shard_map.49 = (f32[5,3,8,128]{3,2,1,0:T(8,128)S(1)}, f32[2,128,128]{2,1,0:T(8,128)S(1)}, f32[2,128,128]{2,1,0:T(8,128)S(1)}) custom-call(f32[4,3,8,128]{3,2,1,0:T(8,128)S(1)} %get-tuple-element.30.image_in_ref, f32[32,128,128]{2,1,0:T(8,128)S(1)} %get-tuple-element.25.raw_ref, f32[4,3,128,128]{3,2,1,0:T(8,128)S(1)} %get-tuple-element.31.kept_ref, ...), custom_call_target="tpu_custom_call" | custom-call | flops 1048576 | bytes 1048576 | tf_op jit(solution)/shard_map/pallas_call | solution.py:480
  19.3 2.0 %collective-permute-done.4.xright_ref = f32[3,2,128,128]{3,2,1,0:T(8,128)S(1)} collective-permute-done((f32[3,2,128,128]{3,2,1,0:T(8,128)S(1)}, f32[3,2,128,128]{3,2,1,0:T(8,128)S(1)}, u32[]{:S(2)}, u32[]{:S(2)}) %collective-permute-start.4) | collective-permute-done | bytes 393248 | tf_op jit(solution)/shard_map/ppermute | solution.py:493
  21.3 0.3 shard_map.50
  21.7 3.5 %collective-permute-start.5 = (f32[3,8,128]{2,1,0:T(8,128)S(1)}, f32[3,8,128]{2,1,0:T(8,128)S(1)}, u32[]{:S(2)}, u32[]{:S(2)}) collective-permute-start(f32[3,8,128]{2,1,0:T(8,128)S(1)} %get-tuple-element.42), channel_id=1, source_target_pairs={{0,8},{8,16},{16,0},{24,24},{1,9},{9,17},{17,1},{25,25},{2,10},{10... | collective-permute-start | bytes 36872 | tf_op jit(solution)/shard_map/ppermute | solution.py:523
  25.2 0.7 %collective-permute-start.6 = (f32[3,8,128]{2,1,0:T(8,128)S(1)}, f32[3,8,128]{2,1,0:T(8,128)S(1)}, u32[]{:S(2)}, u32[]{:S(2)}) collective-permute-start(f32[3,8,128]{2,1,0:T(8,128)S(1)} %get-tuple-element.41), channel_id=1, source_target_pairs={{0,16},{8,8},{16,24},{24,0},{1,17},{9,9},{17,25},{25,1},{2,18},{10... | collective-permute-start | bytes 36872 | tf_op jit(solution)/shard_map/ppermute | solution.py:523
  25.9 5.0 %collective-permute-start.7 = (f32[3,8,128]{2,1,0:T(8,128)S(1)}, f32[3,8,128]{2,1,0:T(8,128)S(1)}, u32[]{:S(2)}, u32[]{:S(2)}) collective-permute-start(f32[3,8,128]{2,1,0:T(8,128)S(1)} %get-tuple-element.40), channel_id=1, source_target_pairs={{0,24},{8,0},{16,16},{24,8},{1,25},{9,1},{17,17},{25,9},{2,26},{10... | collective-permute-start | bytes 36872 | tf_op jit(solution)/shard_map/ppermute | solution.py:523
  30.8 2.9 %collective-permute-start.8 = (f32[3,8,128]{2,1,0:T(8,128)S(1)}, f32[3,8,128]{2,1,0:T(8,128)S(1)}, u32[]{:S(2)}, u32[]{:S(2)}) collective-permute-start(f32[3,8,128]{2,1,0:T(8,128)S(1)} %get-tuple-element.39), channel_id=1, source_target_pairs={{0,0},{8,24},{16,8},{24,16},{1,1},{9,25},{17,9},{25,17},{2,2},{10,... | collective-permute-start | bytes 36872 | tf_op jit(solution)/shard_map/ppermute | solution.py:523
  33.8 0.0 collective-permute-done.5.refs_1_
  33.8 0.0 collective-permute-done.6.refs_2_
  33.8 0.0 collective-permute-done.7.refs_3_
  33.8 2.6 %collective-permute-done.8.refs_4_ = f32[3,8,128]{2,1,0:T(8,128)S(1)} collective-permute-done((f32[3,8,128]{2,1,0:T(8,128)S(1)}, f32[3,8,128]{2,1,0:T(8,128)S(1)}, u32[]{:S(2)}, u32[]{:S(2)}) %collective-permute-start.8) | collective-permute-done | bytes 12320 | tf_op jit(solution)/shard_map/ppermute | solution.py:523
  36.4 0.6 %shard_map.51 = f32[1,1,4,8,128]{4,3,2,1,0:T(8,128)} custom-call(f32[3,8,128]{2,1,0:T(8,128)S(1)} %get-tuple-element.43.refs_0_, f32[3,8,128]{2,1,0:T(8,128)S(1)} %collective-permute-done.5.refs_1_, f32[3,8,128]{2,1,0:T(8,128)S(1)} %collective-permute-done.6.refs_2_, f32[3,8,128]{2,1,0:T(8,128)S(1)} %collective-permute-done.7.refs_3_, ...), custom_call_target="tpu_custom_call" | custom-call | flops 1048576 | bytes 1048576 | tf_op jit(solution)/shard_map/pallas_call | solution.py:549
  (1 shorter events, 0.0 us)
Async XLA Ops:
  0.0 11.2 %copy-start = (s32[4,16,1]{1,2,0:T(1,128)S(1)}, s32[4,16,1]{1,2,0:T(1,128)}, u32[]{:S(2)}) copy-start(s32[4,16,1]{1,2,0:T(1,128)} %param.5) | copy-start | bytes 772
  1.0 17.8 %collective-permute-start.3 = (f32[3,2,128,128]{3,2,1,0:T(8,128)S(1)}, f32[3,2,128,128]{3,2,1,0:T(8,128)S(1)}, u32[]{:S(2)}, u32[]{:S(2)}) collective-permute-start(f32[3,2,128,128]{3,2,1,0:T(8,128)S(1)} %slice.18), channel_id=1, source_target_pairs={{0,2},{2,4},{4,6},{6,0},{1,3},{3,5},{5,7},{7,1},{8,10},{10,12},{12... | collective-permute-start | bytes 1179656 | tf_op jit(solution)/shard_map/ppermute | solution.py:493
  6.4 15.0 %collective-permute-start.4 = (f32[3,2,128,128]{3,2,1,0:T(8,128)S(1)}, f32[3,2,128,128]{3,2,1,0:T(8,128)S(1)}, u32[]{:S(2)}, u32[]{:S(2)}) collective-permute-start(f32[3,2,128,128]{3,2,1,0:T(8,128)S(1)} %get-tuple-element.38), channel_id=1, source_target_pairs={{0,6},{2,0},{4,2},{6,4},{1,7},{3,1},{5,3},{7,5},{8,14},{10,8},{12,... | collective-permute-start | bytes 1179656 | tf_op jit(solution)/shard_map/ppermute | solution.py:493
  7.9 3.3 %collective-permute-start = (f32[3,32,4,128]{3,2,1,0:T(4,128)S(1)}, f32[3,32,4,128]{3,2,1,0:T(4,128)S(1)}, u32[]{:S(2)}, u32[]{:S(2)}) collective-permute-start(f32[3,32,4,128]{3,2,1,0:T(4,128)S(1)} %get-tuple-element.24), channel_id=1, source_target_pairs={{0,1},{1,0},{2,3},{3,2},{4,5},{5,4},{6,7},{7,6},{8,9},{9,8},{10,11... | collective-permute-start | bytes 589832 | tf_op jit(solution)/shard_map/ppermute | solution.py:493
  7.9 8.1 %collective-permute-start.1 = (f32[192,128]{1,0:T(8,128)S(1)}, f32[192,128]{1,0:T(8,128)S(1)}, u32[]{:S(2)}, u32[]{:S(2)}) collective-permute-start(f32[192,128]{1,0:T(8,128)S(1)} %get-tuple-element.28), channel_id=1, source_target_pairs={{0,8},{8,16},{16,24},{24,0},{1,9},{9,17},{17,25},{25,1},{2,10},{10... | collective-permute-start | bytes 294920 | tf_op jit(solution)/shard_map/ppermute | solution.py:493
  9.4 6.6 %collective-permute-start.2 = (f32[192,128]{1,0:T(8,128)S(1)}, f32[192,128]{1,0:T(8,128)S(1)}, u32[]{:S(2)}, u32[]{:S(2)}) collective-permute-start(f32[192,128]{1,0:T(8,128)S(1)} %get-tuple-element.29), channel_id=1, source_target_pairs={{0,24},{8,0},{16,8},{24,16},{1,25},{9,1},{17,9},{25,17},{2,26},{10... | collective-permute-start | bytes 294920 | tf_op jit(solution)/shard_map/ppermute | solution.py:493
  21.7 12.1 %collective-permute-start.5 = (f32[3,8,128]{2,1,0:T(8,128)S(1)}, f32[3,8,128]{2,1,0:T(8,128)S(1)}, u32[]{:S(2)}, u32[]{:S(2)}) collective-permute-start(f32[3,8,128]{2,1,0:T(8,128)S(1)} %get-tuple-element.42), channel_id=1, source_target_pairs={{0,8},{8,16},{16,0},{24,24},{1,9},{9,17},{17,1},{25,25},{2,10},{10... | collective-permute-start | bytes 36872 | tf_op jit(solution)/shard_map/ppermute | solution.py:523
  25.2 8.6 %collective-permute-start.6 = (f32[3,8,128]{2,1,0:T(8,128)S(1)}, f32[3,8,128]{2,1,0:T(8,128)S(1)}, u32[]{:S(2)}, u32[]{:S(2)}) collective-permute-start(f32[3,8,128]{2,1,0:T(8,128)S(1)} %get-tuple-element.41), channel_id=1, source_target_pairs={{0,16},{8,8},{16,24},{24,0},{1,17},{9,9},{17,25},{25,1},{2,18},{10... | collective-permute-start | bytes 36872 | tf_op jit(solution)/shard_map/ppermute | solution.py:523
  25.9 7.9 %collective-permute-start.7 = (f32[3,8,128]{2,1,0:T(8,128)S(1)}, f32[3,8,128]{2,1,0:T(8,128)S(1)}, u32[]{:S(2)}, u32[]{:S(2)}) collective-permute-start(f32[3,8,128]{2,1,0:T(8,128)S(1)} %get-tuple-element.40), channel_id=1, source_target_pairs={{0,24},{8,0},{16,16},{24,8},{1,25},{9,1},{17,17},{25,9},{2,26},{10... | collective-permute-start | bytes 36872 | tf_op jit(solution)/shard_map/ppermute | solution.py:523
  30.8 5.6 %collective-permute-start.8 = (f32[3,8,128]{2,1,0:T(8,128)S(1)}, f32[3,8,128]{2,1,0:T(8,128)S(1)}, u32[]{:S(2)}, u32[]{:S(2)}) collective-permute-start(f32[3,8,128]{2,1,0:T(8,128)S(1)} %get-tuple-element.39), channel_id=1, source_target_pairs={{0,0},{8,24},{16,8},{24,16},{1,1},{9,25},{17,9},{25,17},{2,2},{10,... | collective-permute-start | bytes 36872 | tf_op jit(solution)/shard_map/ppermute | solution.py:523

commit v15 on v13

--- a/solution.py
+++ b/solution.py
@@ -24,6 +24,38 @@
 
 def iota(shape, dim):
     return lax.broadcasted_iota(jnp.int32, shape, dim)
+
+
+def tail_kernel(u_hbm, out_ref, sems):
+    comps, nx, ny, _ = u_hbm.shape
+    half = ny // 2
+    copies = [
+        pltpu.make_async_copy(
+            u_hbm.at[c, nx - 2 + layer, pl.ds(part * half, half)],
+            out_ref.at[c, layer, pl.ds(part * half, half)],
+            sems.at[c, layer, part],
+        )
+        for c in range(comps)
+        for layer in range(2)
+        for part in range(2)
+    ]
+    for copy in copies:
+        copy.start()
+    for copy in copies:
+        copy.wait()
+
+
+def tail(u):
+    comps, _, ny, nz = u.shape
+    return pl.pallas_call(
+        tail_kernel,
+        out_shape=jax.ShapeDtypeStruct((comps, 2, ny, nz), jnp.float32),
+        in_specs=[HBM],
+        out_specs=VMEM,
+        scratch_shapes=[pltpu.SemaphoreType.DMA((comps, 2, 2))],
+        compiler_params=pltpu.CompilerParams(vmem_limit_bytes=50 << 20),
+        cost_estimate=COST,
+    )(u)
 
 
 def faces_kernel(u_hbm, u_ref, parts_ref, xhead_ref, yface_ref, tail_ref, head_ref, packed_ref, sems):
@@ -557,7 +589,7 @@
     comps, nx, ny, nz = velocity.shape
     views = lax.axis_size("view")
     density = 5.0 / (nz * views)
-    xleft = turn(velocity[:, nx - 2 :], "gx", 1)
+    xleft = turn(tail(velocity), "gx", 1)
     u, parts, xhead, yface, ztail, zhead = faces(velocity)
     xright = turn(xhead, "gx", -1)
     zleft = turn(ztail, "view", 1)

time: 31.5 us -> 31.6 us (level)
  local copies, waits for them, and re-layouts: 1.05 us -> 0.01 us
  Pallas kernels: 12.8 us -> 13.8 us
    pallas_call x0 -> x1, Pallas kernels: none -> 1.05 us  [tail(): pl.pallas_call(tail_kernel, out_shape=jax.ShapeDtypeStruct((comps, 2, ny,...]
    slice x1 -> x0, local copies, waits for them, and re-layouts: 1.04 us -> none  [local(): xleft = turn(velocity[:, nx - 2:], 'gx', 1)]
where the time goes in v15:
time: 31.6 us; the launch traced here: 31.4 us
  Pallas kernels  13.8 us (44%)
  starting transfers between devices  12.3 us (39%)
  waiting for transfers between devices  3.84 us (12%)
  between operations  1.39 us (4%)
    ppermute x5, starting transfers between devices, turn(): lax.ppermute(block, axis, [(i, (i + by) % count) for i in range(count)])  8.08 us
    pallas_call x1, Pallas kernels, shaded(): pl.pallas_call(shade_kernel, out_shape=(jax.ShapeDtypeStruct((nx, ny, nz)...  4.76 us
    ppermute x3, starting transfers between devices, exchanged(): lax.ppermute(blocks[k], axis, list(enumerate(route)))  4.22 us
    pallas_call x1, Pallas kernels, faces(): pl.pallas_call(faces_kernel, out_shape=(jax.ShapeDtypeStruct(u.shape, jnp...  3.78 us
    ppermute x3, waiting for transfers between devices, exchanged(): lax.ppermute(blocks[k], axis, list(enumerate(route)))  3.35 us
    pallas_call x1, Pallas kernels, blended(): pl.pallas_call(functools.partial(blend_kernel, density), out_shape=(jax.S...  2.8 us
    pallas_call x1, Pallas kernels, tail(): pl.pallas_call(tail_kernel, out_shape=jax.ShapeDtypeStruct((comps, 2, ny,...  1.05 us
    pallas_call x2, Pallas kernels, edged(): pl.pallas_call(functools.partial(kernel, density), out_shape=out_shape, i...  0.78 us
  transfers between devices with their start and end apart: 8, of which 4 were waited for; matrix products, arithmetic and copies ran while one was open for 0% of the time, Pallas kernels for 38%

profile of v15, /device:TPU:0, one launch (start us, length us, event | category | flops | bytes accessed | tf_op | source)
XLA Modules:
  0.0 31.4 jit_solution(6088859876406323648)
XLA Ops:
  0.0 0.0 copy-start
  0.0 1.0 %shard_map.49 = f32[3,2,128,128]{3,2,1,0:T(8,128)S(1)} custom-call(f32[3,32,128,128]{3,2,1,0:T(8,128)} %u_hbm.3), custom_call_target="tpu_custom_call" | custom-call | flops 1048576 | bytes 1048576 | tf_op jit(solution)/shard_map/pallas_call | solution.py:50
  1.1 3.0 %collective-permute-start.3 = (f32[3,2,128,128]{3,2,1,0:T(8,128)S(1)}, f32[3,2,128,128]{3,2,1,0:T(8,128)S(1)}, u32[]{:S(2)}, u32[]{:S(2)}) collective-permute-start(f32[3,2,128,128]{3,2,1,0:T(8,128)S(1)} %shard_map.49), channel_id=1, source_target_pairs={{0,2},{2,4},{4,6},{6,0},{1,3},{3,5},{5,7},{7,1},{8,10},{10,12},{12... | collective-permute-start | bytes 1179656 | tf_op jit(solution)/shard_map/ppermute | solution.py:526
  4.1 3.8 %shard_map.46 = (f32[3,32,128,128]{3,2,1,0:T(8,128)S(1)}, bf16[3,32,128,256]{3,2,1,0:T(8,128)(2,1)S(1)}, f32[3,2,128,128]{3,2,1,0:T(8,128)S(1)}, f32[3,32,4,128]...) custom-call(f32[3,32,128,128]{3,2,1,0:T(8,128)} %u_hbm.3), custom_call_target="tpu_custom_call" | custom-call | flops 1048576 | bytes 1048576 | tf_op jit(solution)/shard_map/pallas_call | solution.py:130
  7.8 1.0 %collective-permute-start.4 = (f32[3,2,128,128]{3,2,1,0:T(8,128)S(1)}, f32[3,2,128,128]{3,2,1,0:T(8,128)S(1)}, u32[]{:S(2)}, u32[]{:S(2)}) collective-permute-start(f32[3,2,128,128]{3,2,1,0:T(8,128)S(1)} %get-tuple-element.38), channel_id=1, source_target_pairs={{0,6},{2,0},{4,2},{6,4},{1,7},{3,1},{5,3},{7,5},{8,14},{10,8},{12,... | collective-permute-start | bytes 1179656 | tf_op jit(solution)/shard_map/ppermute | solution.py:526
  8.9 0.0 collective-permute-start
  8.9 2.0 %collective-permute-start.1 = (f32[192,128]{1,0:T(8,128)S(1)}, f32[192,128]{1,0:T(8,128)S(1)}, u32[]{:S(2)}, u32[]{:S(2)}) collective-permute-start(f32[192,128]{1,0:T(8,128)S(1)} %get-tuple-element.28), channel_id=1, source_target_pairs={{0,8},{8,16},{16,24},{24,0},{1,9},{9,17},{17,25},{25,1},{2,10},{10... | collective-permute-start | bytes 294920 | tf_op jit(solution)/shard_map/ppermute | solution.py:526
  10.9 2.0 %collective-permute-start.2 = (f32[192,128]{1,0:T(8,128)S(1)}, f32[192,128]{1,0:T(8,128)S(1)}, u32[]{:S(2)}, u32[]{:S(2)}) collective-permute-start(f32[192,128]{1,0:T(8,128)S(1)} %get-tuple-element.29), channel_id=1, source_target_pairs={{0,24},{8,0},{16,8},{24,16},{1,25},{9,1},{17,9},{25,17},{2,26},{10... | collective-permute-start | bytes 294920 | tf_op jit(solution)/shard_map/ppermute | solution.py:526
  14.2 0.0 collective-permute-done.yleft_ref.yright_ref
  14.2 0.0 copy-done
  14.3 4.8 %shard_map.47 = (f32[32,128,128]{2,1,0:T(8,128)S(1)}, f32[3,128,128]{2,1,0:T(8,128)S(1)}, f32[4,3,128,128]{3,2,1,0:T(8,128)S(1)}, f32[4,128,128]{2,1,0:T(8,128)S(1)}) custom-call(f32[3,32,128,128]{3,2,1,0:T(8,128)S(1)} %get-tuple-element.22.u_ref, bf16[3,32,128,256]{3,2,1,0:T(8,128)(2,1)S(1)} %get-tuple-element.23.parts_ref, ...), custom_call_target="tpu_custom_call" | custom-call | flops 1048576 | bytes 1048576 | tf_op jit(solution)/shard_map/pallas_call | solution.py:272
  19.0 0.0 collective-permute-done.1.zleft_ref
  19.0 0.0 collective-permute-done.2.zright_ref
  19.0 2.8 %shard_map.48 = (f32[4,3,8,128]{3,2,1,0:T(8,128)S(1)}, f32[128,128]{1,0:T(8,128)S(1)}, f32[128,128]{1,0:T(8,128)S(1)}, bf16[256,384]{1,0:T(8,128)(2,1)S(1)}) custom-call(f32[32,128,128]{2,1,0:T(8,128)S(1)} %get-tuple-element.25.raw_ref, f32[3,128,128]{2,1,0:T(8,128)S(1)} %get-tuple-element.26.pack_ref, f32[4,128,128]{2,1,0:T(8,128)S(1)} %get-tuple-element.27.scale_ref, ...), custom_call_target="tpu_custom_call" | custom-call | flops 1048576 | bytes 1048576 | tf_op jit(solution)/shard_map/pallas_call | solution.py:417
  21.9 0.0 collective-permute-done.3.xleft_ref
  21.9 0.4 %shard_map.50 = (f32[4,3,8,128]{3,2,1,0:T(8,128)S(1)}, f32[2,128,128]{2,1,0:T(8,128)S(1)}, f32[2,128,128]{2,1,0:T(8,128)S(1)}) custom-call(f32[4,3,8,128]{3,2,1,0:T(8,128)S(1)} %get-tuple-element.30.image_in_ref, f32[32,128,128]{2,1,0:T(8,128)S(1)} %get-tuple-element.25.raw_ref, f32[4,3,128,128]{3,2,1,0:T(8,128)S(1)} %get-tuple-element.31.kept_ref, ...), custom_call_target="tpu_custom_call" | custom-call | flops 1048576 | bytes 1048576 | tf_op jit(solution)/shard_map/pallas_call | solution.py:513
  22.3 0.5 %collective-permute-done.4.xright_ref = f32[3,2,128,128]{3,2,1,0:T(8,128)S(1)} collective-permute-done((f32[3,2,128,128]{3,2,1,0:T(8,128)S(1)}, f32[3,2,128,128]{3,2,1,0:T(8,128)S(1)}, u32[]{:S(2)}, u32[]{:S(2)}) %collective-permute-start.4) | collective-permute-done | bytes 393248 | tf_op jit(solution)/shard_map/ppermute | solution.py:526
  22.8 0.3 %shard_map.51 = f32[4,3,8,128]{3,2,1,0:T(8,128)S(1)} custom-call(f32[4,3,8,128]{3,2,1,0:T(8,128)S(1)} %get-tuple-element.35.image_in_ref, f32[2,128,128]{2,1,0:T(8,128)S(1)} %get-tuple-element.36.base_ref, f32[2,128,128]{2,1,0:T(8,128)S(1)} %get-tuple-element.37.deep_ref, f32[4,3,128,128]{3,2,1,0:T(8,128)S(1)} %get-tuple-element.31.kept_ref, ...), custom_call_target="tpu_custom_call" | custom-call | flops 1048576 | bytes 1048576 | tf_op jit(solution)/shard_map/pallas_call | solution.py:513
  23.2 2.6 %collective-permute-start.5 = (f32[3,8,128]{2,1,0:T(8,128)S(1)}, f32[3,8,128]{2,1,0:T(8,128)S(1)}, u32[]{:S(2)}, u32[]{:S(2)}) collective-permute-start(f32[3,8,128]{2,1,0:T(8,128)S(1)} %get-tuple-element.41), channel_id=1, source_target_pairs={{0,16},{8,24},{16,8},{24,0},{1,17},{9,25},{17,9},{25,1},{2,18},{10... | collective-permute-start | bytes 36872 | tf_op jit(solution)/shard_map/ppermute | solution.py:556
  25.8 1.2 %collective-permute-start.6 = (f32[3,8,128]{2,1,0:T(8,128)S(1)}, f32[3,8,128]{2,1,0:T(8,128)S(1)}, u32[]{:S(2)}, u32[]{:S(2)}) collective-permute-start(f32[3,8,128]{2,1,0:T(8,128)S(1)} %get-tuple-element.40), channel_id=1, source_target_pairs={{0,24},{8,16},{16,0},{24,8},{1,25},{9,17},{17,1},{25,9},{2,26},{10... | collective-permute-start | bytes 36872 | tf_op jit(solution)/shard_map/ppermute | solution.py:556
  27.0 0.3 %collective-permute-start.7 = (f32[3,8,128]{2,1,0:T(8,128)S(1)}, f32[3,8,128]{2,1,0:T(8,128)S(1)}, u32[]{:S(2)}, u32[]{:S(2)}) collective-permute-start(f32[3,8,128]{2,1,0:T(8,128)S(1)} %get-tuple-element.39), channel_id=1, source_target_pairs={{0,8},{8,0},{16,24},{24,16},{1,9},{9,1},{17,25},{25,17},{2,10},{10... | collective-permute-start | bytes 36872 | tf_op jit(solution)/shard_map/ppermute | solution.py:556
  27.4 1.3 %collective-permute-done.5.refs_1_ = f32[3,8,128]{2,1,0:T(8,128)S(1)} collective-permute-done((f32[3,8,128]{2,1,0:T(8,128)S(1)}, f32[3,8,128]{2,1,0:T(8,128)S(1)}, u32[]{:S(2)}, u32[]{:S(2)}) %collective-permute-start.5) | collective-permute-done | bytes 12320 | tf_op jit(solution)/shard_map/ppermute | solution.py:556
  28.7 1.7 %collective-permute-done.6.refs_2_ = f32[3,8,128]{2,1,0:T(8,128)S(1)} collective-permute-done((f32[3,8,128]{2,1,0:T(8,128)S(1)}, f32[3,8,128]{2,1,0:T(8,128)S(1)}, u32[]{:S(2)}, u32[]{:S(2)}) %collective-permute-start.6) | collective-permute-done | bytes 12320 | tf_op jit(solution)/shard_map/ppermute | solution.py:556
  30.4 0.3 %collective-permute-done.7.refs_3_ = f32[3,8,128]{2,1,0:T(8,128)S(1)} collective-permute-done((f32[3,8,128]{2,1,0:T(8,128)S(1)}, f32[3,8,128]{2,1,0:T(8,128)S(1)}, u32[]{:S(2)}, u32[]{:S(2)}) %collective-permute-start.7) | collective-permute-done | bytes 12320 | tf_op jit(solution)/shard_map/ppermute | solution.py:556
  30.7 0.6 %shard_map.52 = f32[1,1,4,8,128]{4,3,2,1,0:T(8,128)} custom-call(f32[3,8,128]{2,1,0:T(8,128)S(1)} %get-tuple-element.42.refs_0_, f32[3,8,128]{2,1,0:T(8,128)S(1)} %collective-permute-done.5.refs_1_, f32[3,8,128]{2,1,0:T(8,128)S(1)} %collective-permute-done.6.refs_2_, f32[3,8,128]{2,1,0:T(8,128)S(1)} %collective-permute-done.7.refs_3_), custom_call_target="tpu_custom_call" | custom-call | flops 1048576 | bytes 1048576 | tf_op jit(solution)/shard_map/pallas_call | solution.py:578
  (1 shorter events, 0.0 us)
Async XLA Ops:
  0.0 14.2 %copy-start = (s32[4,16,1]{1,2,0:T(1,128)S(1)}, s32[4,16,1]{1,2,0:T(1,128)}, u32[]{:S(2)}) copy-start(s32[4,16,1]{1,2,0:T(1,128)} %param.5) | copy-start | bytes 772
  1.1 20.8 %collective-permute-start.3 = (f32[3,2,128,128]{3,2,1,0:T(8,128)S(1)}, f32[3,2,128,128]{3,2,1,0:T(8,128)S(1)}, u32[]{:S(2)}, u32[]{:S(2)}) collective-permute-start(f32[3,2,128,128]{3,2,1,0:T(8,128)S(1)} %shard_map.49), channel_id=1, source_target_pairs={{0,2},{2,4},{4,6},{6,0},{1,3},{3,5},{5,7},{7,1},{8,10},{10,12},{12... | collective-permute-start | bytes 1179656 | tf_op jit(solution)/shard_map/ppermute | solution.py:526
  7.8 15.0 %collective-permute-start.4 = (f32[3,2,128,128]{3,2,1,0:T(8,128)S(1)}, f32[3,2,128,128]{3,2,1,0:T(8,128)S(1)}, u32[]{:S(2)}, u32[]{:S(2)}) collective-permute-start(f32[3,2,128,128]{3,2,1,0:T(8,128)S(1)} %get-tuple-element.38), channel_id=1, source_target_pairs={{0,6},{2,0},{4,2},{6,4},{1,7},{3,1},{5,3},{7,5},{8,14},{10,8},{12,... | collective-permute-start | bytes 1179656 | tf_op jit(solution)/shard_map/ppermute | solution.py:526
  8.9 5.4 %collective-permute-start = (f32[3,32,4,128]{3,2,1,0:T(4,128)S(1)}, f32[3,32,4,128]{3,2,1,0:T(4,128)S(1)}, u32[]{:S(2)}, u32[]{:S(2)}) collective-permute-start(f32[3,32,4,128]{3,2,1,0:T(4,128)S(1)} %get-tuple-element.24), channel_id=1, source_target_pairs={{0,1},{1,0},{2,3},{3,2},{4,5},{5,4},{6,7},{7,6},{8,9},{9,8},{10,11... | collective-permute-start | bytes 589832 | tf_op jit(solution)/shard_map/ppermute | solution.py:526
  8.9 10.2 %collective-permute-start.1 = (f32[192,128]{1,0:T(8,128)S(1)}, f32[192,128]{1,0:T(8,128)S(1)}, u32[]{:S(2)}, u32[]{:S(2)}) collective-permute-start(f32[192,128]{1,0:T(8,128)S(1)} %get-tuple-element.28), channel_id=1, source_target_pairs={{0,8},{8,16},{16,24},{24,0},{1,9},{9,17},{17,25},{25,1},{2,10},{10... | collective-permute-start | bytes 294920 | tf_op jit(solution)/shard_map/ppermute | solution.py:526
  10.9 8.1 %collective-permute-start.2 = (f32[192,128]{1,0:T(8,128)S(1)}, f32[192,128]{1,0:T(8,128)S(1)}, u32[]{:S(2)}, u32[]{:S(2)}) collective-permute-start(f32[192,128]{1,0:T(8,128)S(1)} %get-tuple-element.29), channel_id=1, source_target_pairs={{0,24},{8,0},{16,8},{24,16},{1,25},{9,1},{17,9},{25,17},{2,26},{10... | collective-permute-start | bytes 294920 | tf_op jit(solution)/shard_map/ppermute | solution.py:526
  23.2 5.5 %collective-permute-start.5 = (f32[3,8,128]{2,1,0:T(8,128)S(1)}, f32[3,8,128]{2,1,0:T(8,128)S(1)}, u32[]{:S(2)}, u32[]{:S(2)}) collective-permute-start(f32[3,8,128]{2,1,0:T(8,128)S(1)} %get-tuple-element.41), channel_id=1, source_target_pairs={{0,16},{8,24},{16,8},{24,0},{1,17},{9,25},{17,9},{25,1},{2,18},{10... | collective-permute-start | bytes 36872 | tf_op jit(solution)/shard_map/ppermute | solution.py:556
  25.8 4.6 %collective-permute-start.6 = (f32[3,8,128]{2,1,0:T(8,128)S(1)}, f32[3,8,128]{2,1,0:T(8,128)S(1)}, u32[]{:S(2)}, u32[]{:S(2)}) collective-permute-start(f32[3,8,128]{2,1,0:T(8,128)S(1)} %get-tuple-element.40), channel_id=1, source_target_pairs={{0,24},{8,16},{16,0},{24,8},{1,25},{9,17},{17,1},{25,9},{2,26},{10... | collective-permute-start | bytes 36872 | tf_op jit(solution)/shard_map/ppermute | solution.py:556
  27.0 3.7 %collective-permute-start.7 = (f32[3,8,128]{2,1,0:T(8,128)S(1)}, f32[3,8,128]{2,1,0:T(8,128)S(1)}, u32[]{:S(2)}, u32[]{:S(2)}) collective-permute-start(f32[3,8,128]{2,1,0:T(8,128)S(1)} %get-tuple-element.39), channel_id=1, source_target_pairs={{0,8},{8,0},{16,24},{24,16},{1,9},{9,1},{17,25},{25,17},{2,10},{10... | collective-permute-start | bytes 36872 | tf_op jit(solution)/shard_map/ppermute | solution.py:556

commit v16 on v13

--- a/solution.py
+++ b/solution.py
@@ -328,8 +328,9 @@
 
 
 def blend_kernel(
-    density, raw_ref, pack_ref, scale_ref, zleft_ref, zright_ref,
-    image_ref, fix_ref, first_ref, sum_ref, level0_ref, level1_ref, sums0_ref, sums1_ref,
+    density, raw_ref, pack_ref, kept_ref, scale_ref, zleft_ref, zright_ref, xleft_ref,
+    image_ref, base_ref, deep_ref, sum_ref, level0_ref, level1_ref, sums0_ref, sums1_ref,
+    fix_ref, first_ref, edge_level_ref, edge_sums_ref,
 ):
     nx, ny, nz = raw_ref.shape
     summing(sum_ref)
@@ -345,6 +346,19 @@
     image_ref[...] = jnp.zeros(image_ref.shape, jnp.float32)
     batch = level0_ref.shape[0]
 
+    near = [xleft_ref[c, 1] for c in range(3)]
+    far = [xleft_ref[c, 0] - 8.0 * cells for c, cells in enumerate(near)]
+
+    def prepared(x, place):
+        return raw_ref[x] + on_border(fix_ref[...], x), kept_ref[place, 2] + on_border(first_ref[...], x)
+
+    raws = []
+    for x, ghost in enumerate((far, near)):
+        base, deep = prepared(x, x)
+        raws.append(base + ghost_terms(ghost, kept_ref[x], deep) * scale_ref[0])
+    for k in range(2):
+        base_ref[k], deep_ref[k] = prepared(nx - 2 + k, 2 + k)
+
     def load(x, level_ref, sums_ref):
         raws = [raw_ref[x + k] + on_border(fix_ref[...], x + k) for k in range(batch)]
         gather(density, raws, level_ref, sums_ref, sum_ref)
@@ -354,6 +368,7 @@
             blend(level_ref, sums_ref, k, put(image_ref, x + k))
 
     load(2, level0_ref, sums0_ref)
+    two_rows(density, raws, edge_level_ref, edge_sums_ref, sum_ref, [put(image_ref, x) for x in range(2)])
 
     def batches(i, carry):
         x = 2 * batch * i + 2
@@ -386,13 +401,15 @@
         functools.partial(blend_kernel, density),
         out_shape=(
             jax.ShapeDtypeStruct((views, 3, nx // views, ny), jnp.float32),
-            jax.ShapeDtypeStruct((ny, nz), jnp.float32),
-            jax.ShapeDtypeStruct((ny, nz), jnp.float32),
+            jax.ShapeDtypeStruct((2, ny, nz), jnp.float32),
+            jax.ShapeDtypeStruct((2, ny, nz), jnp.float32),
             jax.ShapeDtypeStruct((2 * nz, 2 * nz + ny), jnp.bfloat16),
         ),
-        in_specs=[VMEM] * 5,
+        in_specs=[VMEM] * 7,
         out_specs=(VMEM,) * 4,
-        scratch_shapes=row_tables(4, ny, nz, 2),
+        scratch_shapes=row_tables(4, ny, nz, 2)
+        + [pltpu.VMEM((ny, nz), jnp.float32)] * 2
+        + [pltpu.VMEM((2, ny, nz), jnp.float32)] * 2,
         compiler_params=PARAMS,
         cost_estimate=COST,
     )(raw, *rest)
@@ -434,30 +451,6 @@
     return lambda view: step_to(me, view, views)
 
 
-def first_kernel(
-    density, image_in_ref, raw_ref, kept_ref, scale_ref, fix_ref, first_ref, sum_ref, xleft_ref,
-    image_ref, base_ref, deep_ref, level_ref, sums_ref,
-):
-    nx = raw_ref.shape[0]
-    views = image_ref.shape[0]
-    slot = slots(views)
-    for view in range(views):
-        image_ref[slot(view)] = image_in_ref[view]
-    near = [xleft_ref[c, 1] for c in range(3)]
-    far = [xleft_ref[c, 0] - 8.0 * cells for c, cells in enumerate(near)]
-
-    def prepared(x, place):
-        return raw_ref[x] + on_border(fix_ref[...], x), kept_ref[place, 2] + on_border(first_ref[...], x)
-
-    raws = []
-    for x, ghost in enumerate((far, near)):
-        base, deep = prepared(x, x)
-        raws.append(base + ghost_terms(ghost, kept_ref[x], deep) * scale_ref[0])
-    two_rows(density, raws, level_ref, sums_ref, sum_ref, [put(image_ref, x, slot) for x in range(2)])
-    for k in range(2):
-        base_ref[k], deep_ref[k] = prepared(nx - 2 + k, 2 + k)
-
-
 def last_kernel(
     density, image_in_ref, base_ref, deep_ref, kept_ref, scale_ref, sum_ref, xright_ref,
     image_ref, level_ref, sums_ref,
@@ -465,7 +458,8 @@
     views, _, per_view, _ = image_ref.shape
     nx = views * per_view
     slot = slots(views)
-    image_ref[...] = image_in_ref[...]
+    for view in range(views):
+        image_ref[slot(view)] = image_in_ref[view]
     near = [-xright_ref[c, 0] for c in range(3)]
     far = [-8.0 * cells - xright_ref[c, 1] for c, cells in enumerate(near)]
     raws = [
@@ -475,18 +469,16 @@
     two_rows(density, raws, level_ref, sums_ref, sum_ref, [put(image_ref, nx - 2 + k, slot) for k in range(2)])
 
 
-def edged(kernel, density, out_shape, image, *rest):
-    ny = image.shape[3]
-    nz = out_shape[-1].shape[-1] if len(out_shape) > 1 else rest[0].shape[-1]
+def edged(density, image, base, *rest):
     return pl.pallas_call(
-        functools.partial(kernel, density),
-        out_shape=out_shape,
-        in_specs=[VMEM] * (1 + len(rest)),
-        out_specs=(VMEM,) * len(out_shape),
-        scratch_shapes=[pltpu.VMEM((2, ny, nz), jnp.float32), pltpu.VMEM((2, ny, nz), jnp.float32)],
+        functools.partial(last_kernel, density),
+        out_shape=jax.ShapeDtypeStruct(image.shape, jnp.float32),
+        in_specs=[VMEM] * (2 + len(rest)),
+        out_specs=VMEM,
+        scratch_shapes=[pltpu.VMEM(base.shape, jnp.float32)] * 2,
         compiler_params=PARAMS,
         cost_estimate=COST,
-    )(image, *rest)
+    )(image, base, *rest)
 
 
 def turn(block, axis, by):
@@ -564,13 +556,8 @@
     zright = turn(zhead, "view", -1)
     yleft, yright = both_sides(yface, "gy")
     raw, pack, kept, scale = shaded(u, parts, yleft, yright, occupied[:, :, 0], q_floor, q_span)
-    image, fix, first, summer = blended(density, views, raw, pack, scale, zleft, zright)
-    drawn = jax.ShapeDtypeStruct(image.shape, jnp.float32)
-    two = jax.ShapeDtypeStruct((2, ny, nz), jnp.float32)
-    image, base, deep = edged(
-        first_kernel, density, (drawn, two, two), image, raw, kept, scale, fix, first, summer, xleft
-    )
-    (blocks,) = edged(last_kernel, density, (drawn,), image, base, deep, kept, scale, summer, xright)
+    image, base, deep, summer = blended(density, views, raw, pack, kept, scale, zleft, zright, xleft)
+    blocks = edged(density, image, base, deep, kept, scale, summer, xright)
     return composited(exchanged(blocks, "view"))
 
 

time: 31.5 us -> 31.5 us (level)
  Pallas kernels: 12.8 us -> 12.3 us
  waiting for transfers between devices: 3.84 us -> 4.31 us
    ppermute x5, waiting for transfers between devices: 0.49 us -> 0.96 us  [turn(): lax.ppermute(block, axis, [(i, (i + by) % count) for i in range(count)])]
    pallas_call x2 -> x1, Pallas kernels: 0.78 us -> 0.33 us  [edged(): pl.pallas_call(functools.partial(last_kernel, density), out_shape=jax.Sha...]
  transfers between devices with their start and end apart: 8 -> 8, of which waited for: 4 -> 4; matrix products, arithmetic and copies ran while one was open for 0% -> 0% of each run, Pallas kernels for 38% -> 36%
where the time goes in v16:
time: 31.5 us; the launch traced here: 31.3 us
  starting transfers between devices  12.3 us (39%)
  Pallas kernels  12.3 us (39%)
  waiting for transfers between devices  4.31 us (14%)
  between operations  1.38 us (4%)
  local copies, waits for them, and re-layouts  1.05 us (3%)
    ppermute x5, starting transfers between devices, turn(): lax.ppermute(block, axis, [(i, (i + by) % count) for i in range(count)])  8.08 us
    pallas_call x1, Pallas kernels, shaded(): pl.pallas_call(shade_kernel, out_shape=(jax.ShapeDtypeStruct((nx, ny, nz)...  4.59 us
    ppermute x3, starting transfers between devices, exchanged(): lax.ppermute(blocks[k], axis, list(enumerate(route)))  4.22 us
    pallas_call x1, Pallas kernels, faces(): pl.pallas_call(faces_kernel, out_shape=(jax.ShapeDtypeStruct(u.shape, jnp...  3.78 us
    ppermute x3, waiting for transfers between devices, exchanged(): lax.ppermute(blocks[k], axis, list(enumerate(route)))  3.35 us
    pallas_call x1, Pallas kernels, blended(): pl.pallas_call(functools.partial(blend_kernel, density), out_shape=(jax.S...  2.96 us
    slice x1, local copies, waits for them, and re-layouts, local(): xleft = turn(velocity[:, nx - 2:], 'gx', 1)  1.04 us
    ppermute x5, waiting for transfers between devices, turn(): lax.ppermute(block, axis, [(i, (i + by) % count) for i in range(count)])  0.96 us
  transfers between devices with their start and end apart: 8, of which 4 were waited for; matrix products, arithmetic and copies ran while one was open for 0% of the time, Pallas kernels for 36%

profile of v16, /device:TPU:0, one launch (start us, length us, event | category | flops | bytes accessed | tf_op | source)
XLA Modules:
  0.0 31.3 jit_solution(5200601507737571635)
XLA Ops:
  0.0 0.0 copy-start
  0.0 1.0 %slice.15 = f32[3,2,128,128]{3,2,1,0:T(8,128)S(1)} slice(f32[3,32,128,128]{3,2,1,0:T(8,128)} %u_hbm.1), slice={[0:3], [30:32], [0:128], [0:128]} | slice | bytes 786432 | tf_op jit(solution)/shard_map/slice | solution.py:552
  1.0 3.0 %collective-permute-start.3 = (f32[3,2,128,128]{3,2,1,0:T(8,128)S(1)}, f32[3,2,128,128]{3,2,1,0:T(8,128)S(1)}, u32[]{:S(2)}, u32[]{:S(2)}) collective-permute-start(f32[3,2,128,128]{3,2,1,0:T(8,128)S(1)} %slice.15), channel_id=1, source_target_pairs={{0,2},{2,4},{4,6},{6,0},{1,3},{3,5},{5,7},{7,1},{8,10},{10,12},{12... | collective-permute-start | bytes 1179656 | tf_op jit(solution)/shard_map/ppermute | solution.py:486
  4.0 3.8 %shard_map.46 = (f32[3,32,128,128]{3,2,1,0:T(8,128)S(1)}, bf16[3,32,128,256]{3,2,1,0:T(8,128)(2,1)S(1)}, f32[3,2,128,128]{3,2,1,0:T(8,128)S(1)}, f32[3,32,4,128]...) custom-call(f32[3,32,128,128]{3,2,1,0:T(8,128)} %u_hbm.1), custom_call_target="tpu_custom_call" | custom-call | flops 1048576 | bytes 1048576 | tf_op jit(solution)/shard_map/pallas_call | solution.py:98
  7.8 1.0 %collective-permute-start.4 = (f32[3,2,128,128]{3,2,1,0:T(8,128)S(1)}, f32[3,2,128,128]{3,2,1,0:T(8,128)S(1)}, u32[]{:S(2)}, u32[]{:S(2)}) collective-permute-start(f32[3,2,128,128]{3,2,1,0:T(8,128)S(1)} %get-tuple-element.32), channel_id=1, source_target_pairs={{0,6},{2,0},{4,2},{6,4},{1,7},{3,1},{5,3},{7,5},{8,14},{10,8},{12,... | collective-permute-start | bytes 1179656 | tf_op jit(solution)/shard_map/ppermute | solution.py:486
  8.9 0.0 collective-permute-start
  8.9 2.0 %collective-permute-start.1 = (f32[192,128]{1,0:T(8,128)S(1)}, f32[192,128]{1,0:T(8,128)S(1)}, u32[]{:S(2)}, u32[]{:S(2)}) collective-permute-start(f32[192,128]{1,0:T(8,128)S(1)} %get-tuple-element.26), channel_id=1, source_target_pairs={{0,8},{8,16},{16,24},{24,0},{1,9},{9,17},{17,25},{25,1},{2,10},{10... | collective-permute-start | bytes 294920 | tf_op jit(solution)/shard_map/ppermute | solution.py:486
  10.9 2.0 %collective-permute-start.2 = (f32[192,128]{1,0:T(8,128)S(1)}, f32[192,128]{1,0:T(8,128)S(1)}, u32[]{:S(2)}, u32[]{:S(2)}) collective-permute-start(f32[192,128]{1,0:T(8,128)S(1)} %get-tuple-element.27), channel_id=1, source_target_pairs={{0,24},{8,0},{16,8},{24,16},{1,25},{9,1},{17,9},{25,17},{2,26},{10... | collective-permute-start | bytes 294920 | tf_op jit(solution)/shard_map/ppermute | solution.py:486
  14.2 0.0 collective-permute-done.yleft_ref.yright_ref
  14.2 0.0 copy-done
  14.2 4.6 %shard_map.47 = (f32[32,128,128]{2,1,0:T(8,128)S(1)}, f32[3,128,128]{2,1,0:T(8,128)S(1)}, f32[4,3,128,128]{3,2,1,0:T(8,128)S(1)}, f32[4,128,128]{2,1,0:T(8,128)S(1)}) custom-call(f32[3,32,128,128]{3,2,1,0:T(8,128)S(1)} %get-tuple-element.19.u_ref, bf16[3,32,128,256]{3,2,1,0:T(8,128)(2,1)S(1)} %get-tuple-element.20.parts_ref, ...), custom_call_target="tpu_custom_call" | custom-call | flops 1048576 | bytes 1048576 | tf_op jit(solution)/shard_map/pallas_call | solution.py:240
  18.8 0.0 collective-permute-done.1.zleft_ref
  18.8 0.0 collective-permute-done.2.zright_ref
  18.9 0.0 collective-permute-done.3.xleft_ref
  18.9 3.0 %shard_map.48 = (f32[4,3,8,128]{3,2,1,0:T(8,128)S(1)}, f32[2,128,128]{2,1,0:T(8,128)S(1)}, f32[2,128,128]{2,1,0:T(8,128)S(1)}, bf16[256,384]{1,0:T(8,128)(2,1)S(1)}) custom-call(f32[32,128,128]{2,1,0:T(8,128)S(1)} %get-tuple-element.22.raw_ref, f32[3,128,128]{2,1,0:T(8,128)S(1)} %get-tuple-element.23.pack_ref, ...), custom_call_target="tpu_custom_call" | custom-call | flops 1048576 | bytes 1048576 | tf_op jit(solution)/shard_map/pallas_call | solution.py:400
  21.8 0.9 %collective-permute-done.4.xright_ref = f32[3,2,128,128]{3,2,1,0:T(8,128)S(1)} collective-permute-done((f32[3,2,128,128]{3,2,1,0:T(8,128)S(1)}, f32[3,2,128,128]{3,2,1,0:T(8,128)S(1)}, u32[]{:S(2)}, u32[]{:S(2)}) %collective-permute-start.4) | collective-permute-done | bytes 393248 | tf_op jit(solution)/shard_map/ppermute | solution.py:486
  22.8 0.3 %shard_map.49 = f32[4,3,8,128]{3,2,1,0:T(8,128)S(1)} custom-call(f32[4,3,8,128]{3,2,1,0:T(8,128)S(1)} %get-tuple-element.28.image_in_ref, f32[2,128,128]{2,1,0:T(8,128)S(1)} %get-tuple-element.29.base_ref, f32[2,128,128]{2,1,0:T(8,128)S(1)} %get-tuple-element.30.deep_ref, f32[4,3,128,128]{3,2,1,0:T(8,128)S(1)} %get-tuple-element.24.kept_ref, ...), custom_call_target="tpu_custom_call" | custom-call | flops 1048576 | bytes 1048576 | tf_op jit(solution)/shard_map/pallas_call | solution.py:473
  23.1 2.6 %collective-permute-start.5 = (f32[3,8,128]{2,1,0:T(8,128)S(1)}, f32[3,8,128]{2,1,0:T(8,128)S(1)}, u32[]{:S(2)}, u32[]{:S(2)}) collective-permute-start(f32[3,8,128]{2,1,0:T(8,128)S(1)} %get-tuple-element.35), channel_id=1, source_target_pairs={{0,16},{8,24},{16,8},{24,0},{1,17},{9,25},{17,9},{25,1},{2,18},{10... | collective-permute-start | bytes 36872 | tf_op jit(solution)/shard_map/ppermute | solution.py:516
  25.8 1.2 %collective-permute-start.6 = (f32[3,8,128]{2,1,0:T(8,128)S(1)}, f32[3,8,128]{2,1,0:T(8,128)S(1)}, u32[]{:S(2)}, u32[]{:S(2)}) collective-permute-start(f32[3,8,128]{2,1,0:T(8,128)S(1)} %get-tuple-element.34), channel_id=1, source_target_pairs={{0,24},{8,16},{16,0},{24,8},{1,25},{9,17},{17,1},{25,9},{2,26},{10... | collective-permute-start | bytes 36872 | tf_op jit(solution)/shard_map/ppermute | solution.py:516
  27.0 0.3 %collective-permute-start.7 = (f32[3,8,128]{2,1,0:T(8,128)S(1)}, f32[3,8,128]{2,1,0:T(8,128)S(1)}, u32[]{:S(2)}, u32[]{:S(2)}) collective-permute-start(f32[3,8,128]{2,1,0:T(8,128)S(1)} %get-tuple-element.33), channel_id=1, source_target_pairs={{0,8},{8,0},{16,24},{24,16},{1,9},{9,1},{17,25},{25,17},{2,10},{10... | collective-permute-start | bytes 36872 | tf_op jit(solution)/shard_map/ppermute | solution.py:516
  27.4 1.3 %collective-permute-done.5.refs_1_ = f32[3,8,128]{2,1,0:T(8,128)S(1)} collective-permute-done((f32[3,8,128]{2,1,0:T(8,128)S(1)}, f32[3,8,128]{2,1,0:T(8,128)S(1)}, u32[]{:S(2)}, u32[]{:S(2)}) %collective-permute-start.5) | collective-permute-done | bytes 12320 | tf_op jit(solution)/shard_map/ppermute | solution.py:516
  28.7 1.7 %collective-permute-done.6.refs_2_ = f32[3,8,128]{2,1,0:T(8,128)S(1)} collective-permute-done((f32[3,8,128]{2,1,0:T(8,128)S(1)}, f32[3,8,128]{2,1,0:T(8,128)S(1)}, u32[]{:S(2)}, u32[]{:S(2)}) %collective-permute-start.6) | collective-permute-done | bytes 12320 | tf_op jit(solution)/shard_map/ppermute | solution.py:516
  30.4 0.3 %collective-permute-done.7.refs_3_ = f32[3,8,128]{2,1,0:T(8,128)S(1)} collective-permute-done((f32[3,8,128]{2,1,0:T(8,128)S(1)}, f32[3,8,128]{2,1,0:T(8,128)S(1)}, u32[]{:S(2)}, u32[]{:S(2)}) %collective-permute-start.7) | collective-permute-done | bytes 12320 | tf_op jit(solution)/shard_map/ppermute | solution.py:516
  30.7 0.6 %shard_map.50 = f32[1,1,4,8,128]{4,3,2,1,0:T(8,128)} custom-call(f32[3,8,128]{2,1,0:T(8,128)S(1)} %get-tuple-element.36.refs_0_, f32[3,8,128]{2,1,0:T(8,128)S(1)} %collective-permute-done.5.refs_1_, f32[3,8,128]{2,1,0:T(8,128)S(1)} %collective-permute-done.6.refs_2_, f32[3,8,128]{2,1,0:T(8,128)S(1)} %collective-permute-done.7.refs_3_), custom_call_target="tpu_custom_call" | custom-call | flops 1048576 | bytes 1048576 | tf_op jit(solution)/shard_map/pallas_call | solution.py:538
  (1 shorter events, 0.0 us)
Async XLA Ops:
  0.0 14.2 %copy-start = (s32[4,16,1]{1,2,0:T(1,128)S(1)}, s32[4,16,1]{1,2,0:T(1,128)}, u32[]{:S(2)}) copy-start(s32[4,16,1]{1,2,0:T(1,128)} %param.5) | copy-start | bytes 772
  1.0 17.8 %collective-permute-start.3 = (f32[3,2,128,128]{3,2,1,0:T(8,128)S(1)}, f32[3,2,128,128]{3,2,1,0:T(8,128)S(1)}, u32[]{:S(2)}, u32[]{:S(2)}) collective-permute-start(f32[3,2,128,128]{3,2,1,0:T(8,128)S(1)} %slice.15), channel_id=1, source_target_pairs={{0,2},{2,4},{4,6},{6,0},{1,3},{3,5},{5,7},{7,1},{8,10},{10,12},{12... | collective-permute-start | bytes 1179656 | tf_op jit(solution)/shard_map/ppermute | solution.py:486
  7.8 15.0 %collective-permute-start.4 = (f32[3,2,128,128]{3,2,1,0:T(8,128)S(1)}, f32[3,2,128,128]{3,2,1,0:T(8,128)S(1)}, u32[]{:S(2)}, u32[]{:S(2)}) collective-permute-start(f32[3,2,128,128]{3,2,1,0:T(8,128)S(1)} %get-tuple-element.32), channel_id=1, source_target_pairs={{0,6},{2,0},{4,2},{6,4},{1,7},{3,1},{5,3},{7,5},{8,14},{10,8},{12,... | collective-permute-start | bytes 1179656 | tf_op jit(solution)/shard_map/ppermute | solution.py:486
  8.9 5.4 %collective-permute-start = (f32[3,32,4,128]{3,2,1,0:T(4,128)S(1)}, f32[3,32,4,128]{3,2,1,0:T(4,128)S(1)}, u32[]{:S(2)}, u32[]{:S(2)}) collective-permute-start(f32[3,32,4,128]{3,2,1,0:T(4,128)S(1)} %get-tuple-element.21), channel_id=1, source_target_pairs={{0,1},{1,0},{2,3},{3,2},{4,5},{5,4},{6,7},{7,6},{8,9},{9,8},{10,11... | collective-permute-start | bytes 589832 | tf_op jit(solution)/shard_map/ppermute | solution.py:486
  8.9 10.0 %collective-permute-start.1 = (f32[192,128]{1,0:T(8,128)S(1)}, f32[192,128]{1,0:T(8,128)S(1)}, u32[]{:S(2)}, u32[]{:S(2)}) collective-permute-start(f32[192,128]{1,0:T(8,128)S(1)} %get-tuple-element.26), channel_id=1, source_target_pairs={{0,8},{8,16},{16,24},{24,0},{1,9},{9,17},{17,25},{25,1},{2,10},{10... | collective-permute-start | bytes 294920 | tf_op jit(solution)/shard_map/ppermute | solution.py:486
  10.9 8.0 %collective-permute-start.2 = (f32[192,128]{1,0:T(8,128)S(1)}, f32[192,128]{1,0:T(8,128)S(1)}, u32[]{:S(2)}, u32[]{:S(2)}) collective-permute-start(f32[192,128]{1,0:T(8,128)S(1)} %get-tuple-element.27), channel_id=1, source_target_pairs={{0,24},{8,0},{16,8},{24,16},{1,25},{9,1},{17,9},{25,17},{2,26},{10... | collective-permute-start | bytes 294920 | tf_op jit(solution)/shard_map/ppermute | solution.py:486
  23.1 5.5 %collective-permute-start.5 = (f32[3,8,128]{2,1,0:T(8,128)S(1)}, f32[3,8,128]{2,1,0:T(8,128)S(1)}, u32[]{:S(2)}, u32[]{:S(2)}) collective-permute-start(f32[3,8,128]{2,1,0:T(8,128)S(1)} %get-tuple-element.35), channel_id=1, source_target_pairs={{0,16},{8,24},{16,8},{24,0},{1,17},{9,25},{17,9},{25,1},{2,18},{10... | collective-permute-start | bytes 36872 | tf_op jit(solution)/shard_map/ppermute | solution.py:516
  25.8 4.6 %collective-permute-start.6 = (f32[3,8,128]{2,1,0:T(8,128)S(1)}, f32[3,8,128]{2,1,0:T(8,128)S(1)}, u32[]{:S(2)}, u32[]{:S(2)}) collective-permute-start(f32[3,8,128]{2,1,0:T(8,128)S(1)} %get-tuple-element.34), channel_id=1, source_target_pairs={{0,24},{8,16},{16,0},{24,8},{1,25},{9,17},{17,1},{25,9},{2,26},{10... | collective-permute-start | bytes 36872 | tf_op jit(solution)/shard_map/ppermute | solution.py:516
  27.0 3.7 %collective-permute-start.7 = (f32[3,8,128]{2,1,0:T(8,128)S(1)}, f32[3,8,128]{2,1,0:T(8,128)S(1)}, u32[]{:S(2)}, u32[]{:S(2)}) collective-permute-start(f32[3,8,128]{2,1,0:T(8,128)S(1)} %get-tuple-element.33), channel_id=1, source_target_pairs={{0,8},{8,0},{16,24},{24,16},{1,9},{9,1},{17,25},{25,17},{2,10},{10... | collective-permute-start | bytes 36872 | tf_op jit(solution)/shard_map/ppermute | solution.py:516

commit v17 on v16

--- a/solution.py
+++ b/solution.py
@@ -24,6 +24,34 @@
 
 def iota(shape, dim):
     return lax.broadcasted_iota(jnp.int32, shape, dim)
+
+
+def tail_kernel(u_hbm, out_ref, sems):
+    comps, nx, ny, _ = u_hbm.shape
+    copies = [
+        pltpu.make_async_copy(
+            u_hbm.at[c, nx - 2 + layer], out_ref.at[pl.ds((2 * c + layer) * ny, ny)], sems.at[c, layer]
+        )
+        for c in range(comps)
+        for layer in range(2)
+    ]
+    for copy in copies:
+        copy.start()
+    for copy in copies:
+        copy.wait()
+
+
+def tail(u):
+    comps, _, ny, nz = u.shape
+    return pl.pallas_call(
+        tail_kernel,
+        out_shape=jax.ShapeDtypeStruct((2 * comps * ny + 2 * SUB, nz), jnp.float32),
+        in_specs=[HBM],
+        out_specs=VMEM,
+        scratch_shapes=[pltpu.SemaphoreType.DMA((comps, 2))],
+        compiler_params=pltpu.CompilerParams(vmem_limit_bytes=50 << 20),
+        cost_estimate=COST,
+    )(u)
 
 
 def faces_kernel(u_hbm, u_ref, parts_ref, xhead_ref, yface_ref, tail_ref, head_ref, packed_ref, sems):
@@ -63,7 +91,7 @@
         xhead_ref[c] = u_ref[c, pl.ds(0, 2)]
         for x in range(nx):
             lines = jnp.where(sub >= 6, u_ref[c, x, pl.ds(ny - 8, 8), :], u_ref[c, x, pl.ds(0, 8), :])
-            yface_ref[c, x] = pltpu.roll(lines, 2, 0)[:4]
+            yface_ref[c * nx + x] = lines
     tails, heads = fold([packed_ref[c] for c in range(comps)], ny, nz)
     tail_ref[...] = tails
     head_ref[...] = heads
@@ -101,7 +129,7 @@
             jax.ShapeDtypeStruct(u.shape, jnp.float32),
             jax.ShapeDtypeStruct((comps, nx, ny, 2 * nz), jnp.bfloat16),
             jax.ShapeDtypeStruct((comps, 2, ny, nz), jnp.float32),
-            jax.ShapeDtypeStruct((comps, nx, 4, nz), jnp.float32),
+            jax.ShapeDtypeStruct((comps * nx + 1, 8, nz), jnp.float32),
             message,
             message,
         ),
@@ -139,15 +167,16 @@
 def slopes(parts_ref, x, tables, slope_ref):
     yleft_ref, yright_ref, dz_ref, dy_ref = tables
     comps, ny, nz = slope_ref.shape[2:]
+    rows = parts_ref.shape[1]
     sub = iota((8, nz), 0)
 
     def top(left):
-        lines = jnp.concatenate([left, left], axis=0)
-        return jnp.where(sub < 2, lines - jnp.where(sub == 0, 8.0 * pltpu.roll(lines, 7, 0), 0.0), 0.0)
+        lines = pltpu.roll(left, 2, 0)
+        return jnp.where(sub < 2, lines - jnp.where(sub == 0, 8.0 * pltpu.roll(left, 1, 0), 0.0), 0.0)
 
     def low(right):
-        lines = jnp.concatenate([right, right], axis=0)
-        return jnp.where(sub >= 6, jnp.where(sub == 7, 8.0 * pltpu.roll(lines, 1, 0), 0.0) - lines, 0.0)
+        lines = pltpu.roll(right, 6, 0)
+        return jnp.where(sub >= 6, jnp.where(sub == 7, 8.0 * pltpu.roll(right, 7, 0), 0.0) - lines, 0.0)
 
     parts = [[parts_ref[c, x + k] for k in range(2)] for c in range(comps)]
     depth = jnp.dot(
@@ -163,9 +192,9 @@
         for k in range(2):
             slope_ref[1, k, c] = depth[(2 * c + k) * ny : (2 * c + k + 1) * ny]
             mine = down[:, k * nz : (k + 1) * nz]
-            slope_ref[0, k, c, pl.ds(0, 8), :] = mine[:8] + top(yleft_ref[c, x + k])
+            slope_ref[0, k, c, pl.ds(0, 8), :] = mine[:8] + top(yleft_ref[c * rows + x + k])
             slope_ref[0, k, c, pl.ds(8, ny - 16), :] = mine[8 : ny - 8]
-            slope_ref[0, k, c, pl.ds(ny - 8, 8), :] = mine[ny - 8 :] + low(yright_ref[c, x + k])
+            slope_ref[0, k, c, pl.ds(ny - 8, 8), :] = mine[ny - 8 :] + low(yright_ref[c * rows + x + k])
 
 
 def shade(u_ref, x, slope_ref, scale_ref, offset_ref, raw_ref, pack_ref, kept_ref=None, place=None):
@@ -346,8 +375,8 @@
     image_ref[...] = jnp.zeros(image_ref.shape, jnp.float32)
     batch = level0_ref.shape[0]
 
-    near = [xleft_ref[c, 1] for c in range(3)]
-    far = [xleft_ref[c, 0] - 8.0 * cells for c, cells in enumerate(near)]
+    near = [xleft_ref[pl.ds((2 * c + 1) * ny, ny), :] for c in range(3)]
+    far = [xleft_ref[pl.ds(2 * c * ny, ny), :] - 8.0 * cells for c, cells in enumerate(near)]
 
     def prepared(x, place):
         return raw_ref[x] + on_border(fix_ref[...], x), kept_ref[place, 2] + on_border(first_ref[...], x)
@@ -549,7 +578,7 @@
     comps, nx, ny, nz = velocity.shape
     views = lax.axis_size("view")
     density = 5.0 / (nz * views)
-    xleft = turn(velocity[:, nx - 2 :], "gx", 1)
+    xleft = turn(tail(velocity), "gx", 1)
     u, parts, xhead, yface, ztail, zhead = faces(velocity)
     xright = turn(xhead, "gx", -1)
     zleft = turn(ztail, "view", 1)

time: 31.5 us -> 31.7 us (level)
  Pallas kernels: 12.3 us -> 13.5 us
  local copies, waits for them, and re-layouts: 1.05 us -> 0.01 us
    pallas_call x0 -> x1, Pallas kernels: none -> 1.06 us  [tail(): pl.pallas_call(tail_kernel, out_shape=jax.ShapeDtypeStruct((2 * comps * n...]
    slice x1 -> x0, local copies, waits for them, and re-layouts: 1.04 us -> none  [local(): xleft = turn(velocity[:, nx - 2:], 'gx', 1)]
where the time goes in v17:
time: 31.7 us; the launch traced here: 31.5 us
  Pallas kernels  13.5 us (43%)
  starting transfers between devices  12.4 us (39%)
  waiting for transfers between devices  4.29 us (14%)
  between operations  1.4 us (4%)
    ppermute x5, starting transfers between devices, turn(): lax.ppermute(block, axis, [(i, (i + by) % count) for i in range(count)])  8.15 us
    pallas_call x1, Pallas kernels, shaded(): pl.pallas_call(shade_kernel, out_shape=(jax.ShapeDtypeStruct((nx, ny, nz)...  4.64 us
    ppermute x3, starting transfers between devices, exchanged(): lax.ppermute(blocks[k], axis, list(enumerate(route)))  4.22 us
    pallas_call x1, Pallas kernels, faces(): pl.pallas_call(faces_kernel, out_shape=(jax.ShapeDtypeStruct(u.shape, jnp...  3.79 us
    ppermute x3, waiting for transfers between devices, exchanged(): lax.ppermute(blocks[k], axis, list(enumerate(route)))  3.35 us
    pallas_call x1, Pallas kernels, blended(): pl.pallas_call(functools.partial(blend_kernel, density), out_shape=(jax.S...  3.03 us
    pallas_call x1, Pallas kernels, tail(): pl.pallas_call(tail_kernel, out_shape=jax.ShapeDtypeStruct((2 * comps * n...  1.06 us
    ppermute x5, waiting for transfers between devices, turn(): lax.ppermute(block, axis, [(i, (i + by) % count) for i in range(count)])  0.94 us
  transfers between devices with their start and end apart: 8, of which 4 were waited for; matrix products, arithmetic and copies ran while one was open for 0% of the time, Pallas kernels for 36%

profile of v17, /device:TPU:0, one launch (start us, length us, event | category | flops | bytes accessed | tf_op | source)
XLA Modules:
  0.0 31.5 jit_solution(17281707300082228738)
XLA Ops:
  0.0 0.0 copy-start
  0.0 1.1 %shard_map.48 = f32[784,128]{1,0:T(8,128)S(1)} custom-call(f32[3,32,128,128]{3,2,1,0:T(8,128)} %u_hbm.3), custom_call_target="tpu_custom_call" | custom-call | flops 1048576 | bytes 1048576 | tf_op jit(solution)/shard_map/pallas_call | solution.py:46
  1.1 3.0 %collective-permute-start.3 = (f32[784,128]{1,0:T(8,128)S(1)}, f32[784,128]{1,0:T(8,128)S(1)}, u32[]{:S(2)}, u32[]{:S(2)}) collective-permute-start(f32[784,128]{1,0:T(8,128)S(1)} %shard_map.48), channel_id=1, source_target_pairs={{0,2},{2,4},{4,6},{6,0},{1,3},{3,5},{5,7},{7,1},{8,10},{10,12},{12... | collective-permute-start | bytes 1204232 | tf_op jit(solution)/shard_map/ppermute | solution.py:515
  4.1 3.8 %shard_map.46 = (f32[3,32,128,128]{3,2,1,0:T(8,128)S(1)}, bf16[3,32,128,256]{3,2,1,0:T(8,128)(2,1)S(1)}, f32[3,2,128,128]{3,2,1,0:T(8,128)S(1)}, f32[97,8,128]{2...) custom-call(f32[3,32,128,128]{3,2,1,0:T(8,128)} %u_hbm.3), custom_call_target="tpu_custom_call" | custom-call | flops 1048576 | bytes 1048576 | tf_op jit(solution)/shard_map/pallas_call | solution.py:126
  7.9 0.1 collective-permute-start
  7.9 1.0 %collective-permute-start.4 = (f32[3,2,128,128]{3,2,1,0:T(8,128)S(1)}, f32[3,2,128,128]{3,2,1,0:T(8,128)S(1)}, u32[]{:S(2)}, u32[]{:S(2)}) collective-permute-start(f32[3,2,128,128]{3,2,1,0:T(8,128)S(1)} %get-tuple-element.32), channel_id=1, source_target_pairs={{0,6},{2,0},{4,2},{6,4},{1,7},{3,1},{5,3},{7,5},{8,14},{10,8},{12,... | collective-permute-start | bytes 1179656 | tf_op jit(solution)/shard_map/ppermute | solution.py:515
  9.0 2.0 %collective-permute-start.1 = (f32[192,128]{1,0:T(8,128)S(1)}, f32[192,128]{1,0:T(8,128)S(1)}, u32[]{:S(2)}, u32[]{:S(2)}) collective-permute-start(f32[192,128]{1,0:T(8,128)S(1)} %get-tuple-element.26), channel_id=1, source_target_pairs={{0,8},{8,16},{16,24},{24,0},{1,9},{9,17},{17,25},{25,1},{2,10},{10... | collective-permute-start | bytes 294920 | tf_op jit(solution)/shard_map/ppermute | solution.py:515
  11.0 2.0 %collective-permute-start.2 = (f32[192,128]{1,0:T(8,128)S(1)}, f32[192,128]{1,0:T(8,128)S(1)}, u32[]{:S(2)}, u32[]{:S(2)}) collective-permute-start(f32[192,128]{1,0:T(8,128)S(1)} %get-tuple-element.27), channel_id=1, source_target_pairs={{0,24},{8,0},{16,8},{24,16},{1,25},{9,1},{17,9},{25,17},{2,26},{10... | collective-permute-start | bytes 294920 | tf_op jit(solution)/shard_map/ppermute | solution.py:515
  14.3 0.0 collective-permute-done.yleft_ref.yright_ref
  14.3 0.0 copy-done
  14.3 4.6 %shard_map.47 = (f32[32,128,128]{2,1,0:T(8,128)S(1)}, f32[3,128,128]{2,1,0:T(8,128)S(1)}, f32[4,3,128,128]{3,2,1,0:T(8,128)S(1)}, f32[4,128,128]{2,1,0:T(8,128)S(1)}) custom-call(f32[3,32,128,128]{3,2,1,0:T(8,128)S(1)} %get-tuple-element.19.u_ref, bf16[3,32,128,256]{3,2,1,0:T(8,128)(2,1)S(1)} %get-tuple-element.20.parts_ref, ...), custom_call_target="tpu_custom_call" | custom-call | flops 1048576 | bytes 1048576 | tf_op jit(solution)/shard_map/pallas_call | solution.py:269
  19.0 0.0 collective-permute-done.1.zleft_ref
  19.0 0.0 collective-permute-done.2.zright_ref
  19.0 0.0 collective-permute-done.3.xleft_ref
  19.0 3.0 %shard_map.49 = (f32[4,3,8,128]{3,2,1,0:T(8,128)S(1)}, f32[2,128,128]{2,1,0:T(8,128)S(1)}, f32[2,128,128]{2,1,0:T(8,128)S(1)}, bf16[256,384]{1,0:T(8,128)(2,1)S(1)}) custom-call(f32[32,128,128]{2,1,0:T(8,128)S(1)} %get-tuple-element.22.raw_ref, f32[3,128,128]{2,1,0:T(8,128)S(1)} %get-tuple-element.23.pack_ref, ...), custom_call_target="tpu_custom_call" | custom-call | flops 1048576 | bytes 1048576 | tf_op jit(solution)/shard_map/pallas_call | solution.py:429
  22.1 0.9 %collective-permute-done.4.xright_ref = f32[3,2,128,128]{3,2,1,0:T(8,128)S(1)} collective-permute-done((f32[3,2,128,128]{3,2,1,0:T(8,128)S(1)}, f32[3,2,128,128]{3,2,1,0:T(8,128)S(1)}, u32[]{:S(2)}, u32[]{:S(2)}) %collective-permute-start.4) | collective-permute-done | bytes 393248 | tf_op jit(solution)/shard_map/ppermute | solution.py:515
  23.0 0.3 %shard_map.50 = f32[4,3,8,128]{3,2,1,0:T(8,128)S(1)} custom-call(f32[4,3,8,128]{3,2,1,0:T(8,128)S(1)} %get-tuple-element.28.image_in_ref, f32[2,128,128]{2,1,0:T(8,128)S(1)} %get-tuple-element.29.base_ref, f32[2,128,128]{2,1,0:T(8,128)S(1)} %get-tuple-element.30.deep_ref, f32[4,3,128,128]{3,2,1,0:T(8,128)S(1)} %get-tuple-element.24.kept_ref, ...), custom_call_target="tpu_custom_call" | custom-call | flops 1048576 | bytes 1048576 | tf_op jit(solution)/shard_map/pallas_call | solution.py:502
  23.3 2.6 %collective-permute-start.5 = (f32[3,8,128]{2,1,0:T(8,128)S(1)}, f32[3,8,128]{2,1,0:T(8,128)S(1)}, u32[]{:S(2)}, u32[]{:S(2)}) collective-permute-start(f32[3,8,128]{2,1,0:T(8,128)S(1)} %get-tuple-element.35), channel_id=1, source_target_pairs={{0,16},{8,24},{16,8},{24,0},{1,17},{9,25},{17,9},{25,1},{2,18},{10... | collective-permute-start | bytes 36872 | tf_op jit(solution)/shard_map/ppermute | solution.py:545
  26.0 1.2 %collective-permute-start.6 = (f32[3,8,128]{2,1,0:T(8,128)S(1)}, f32[3,8,128]{2,1,0:T(8,128)S(1)}, u32[]{:S(2)}, u32[]{:S(2)}) collective-permute-start(f32[3,8,128]{2,1,0:T(8,128)S(1)} %get-tuple-element.34), channel_id=1, source_target_pairs={{0,24},{8,16},{16,0},{24,8},{1,25},{9,17},{17,1},{25,9},{2,26},{10... | collective-permute-start | bytes 36872 | tf_op jit(solution)/shard_map/ppermute | solution.py:545
  27.2 0.3 %collective-permute-start.7 = (f32[3,8,128]{2,1,0:T(8,128)S(1)}, f32[3,8,128]{2,1,0:T(8,128)S(1)}, u32[]{:S(2)}, u32[]{:S(2)}) collective-permute-start(f32[3,8,128]{2,1,0:T(8,128)S(1)} %get-tuple-element.33), channel_id=1, source_target_pairs={{0,8},{8,0},{16,24},{24,16},{1,9},{9,1},{17,25},{25,17},{2,10},{10... | collective-permute-start | bytes 36872 | tf_op jit(solution)/shard_map/ppermute | solution.py:545
  27.6 1.3 %collective-permute-done.5.refs_1_ = f32[3,8,128]{2,1,0:T(8,128)S(1)} collective-permute-done((f32[3,8,128]{2,1,0:T(8,128)S(1)}, f32[3,8,128]{2,1,0:T(8,128)S(1)}, u32[]{:S(2)}, u32[]{:S(2)}) %collective-permute-start.5) | collective-permute-done | bytes 12320 | tf_op jit(solution)/shard_map/ppermute | solution.py:545
  28.9 1.7 %collective-permute-done.6.refs_2_ = f32[3,8,128]{2,1,0:T(8,128)S(1)} collective-permute-done((f32[3,8,128]{2,1,0:T(8,128)S(1)}, f32[3,8,128]{2,1,0:T(8,128)S(1)}, u32[]{:S(2)}, u32[]{:S(2)}) %collective-permute-start.6) | collective-permute-done | bytes 12320 | tf_op jit(solution)/shard_map/ppermute | solution.py:545
  30.6 0.3 %collective-permute-done.7.refs_3_ = f32[3,8,128]{2,1,0:T(8,128)S(1)} collective-permute-done((f32[3,8,128]{2,1,0:T(8,128)S(1)}, f32[3,8,128]{2,1,0:T(8,128)S(1)}, u32[]{:S(2)}, u32[]{:S(2)}) %collective-permute-start.7) | collective-permute-done | bytes 12320 | tf_op jit(solution)/shard_map/ppermute | solution.py:545
  30.9 0.6 %shard_map.51 = f32[1,1,4,8,128]{4,3,2,1,0:T(8,128)} custom-call(f32[3,8,128]{2,1,0:T(8,128)S(1)} %get-tuple-element.36.refs_0_, f32[3,8,128]{2,1,0:T(8,128)S(1)} %collective-permute-done.5.refs_1_, f32[3,8,128]{2,1,0:T(8,128)S(1)} %collective-permute-done.6.refs_2_, f32[3,8,128]{2,1,0:T(8,128)S(1)} %collective-permute-done.7.refs_3_), custom_call_target="tpu_custom_call" | custom-call | flops 1048576 | bytes 1048576 | tf_op jit(solution)/shard_map/pallas_call | solution.py:567
  (1 shorter events, 0.0 us)
Async XLA Ops:
  0.0 14.3 %copy-start = (s32[4,16,1]{1,2,0:T(1,128)S(1)}, s32[4,16,1]{1,2,0:T(1,128)}, u32[]{:S(2)}) copy-start(s32[4,16,1]{1,2,0:T(1,128)} %param.5) | copy-start | bytes 772
  1.1 17.9 %collective-permute-start.3 = (f32[784,128]{1,0:T(8,128)S(1)}, f32[784,128]{1,0:T(8,128)S(1)}, u32[]{:S(2)}, u32[]{:S(2)}) collective-permute-start(f32[784,128]{1,0:T(8,128)S(1)} %shard_map.48), channel_id=1, source_target_pairs={{0,2},{2,4},{4,6},{6,0},{1,3},{3,5},{5,7},{7,1},{8,10},{10,12},{12... | collective-permute-start | bytes 1204232 | tf_op jit(solution)/shard_map/ppermute | solution.py:515
  7.9 6.5 %collective-permute-start = (f32[97,8,128]{2,1,0:T(8,128)S(1)}, f32[97,8,128]{2,1,0:T(8,128)S(1)}, u32[]{:S(2)}, u32[]{:S(2)}) collective-permute-start(f32[97,8,128]{2,1,0:T(8,128)S(1)} %get-tuple-element.21), channel_id=1, source_target_pairs={{0,1},{1,0},{2,3},{3,2},{4,5},{5,4},{6,7},{7,6},{8,9},{9,8},{10,11... | collective-permute-start | bytes 1191944 | tf_op jit(solution)/shard_map/ppermute | solution.py:515
  7.9 15.0 %collective-permute-start.4 = (f32[3,2,128,128]{3,2,1,0:T(8,128)S(1)}, f32[3,2,128,128]{3,2,1,0:T(8,128)S(1)}, u32[]{:S(2)}, u32[]{:S(2)}) collective-permute-start(f32[3,2,128,128]{3,2,1,0:T(8,128)S(1)} %get-tuple-element.32), channel_id=1, source_target_pairs={{0,6},{2,0},{4,2},{6,4},{1,7},{3,1},{5,3},{7,5},{8,14},{10,8},{12,... | collective-permute-start | bytes 1179656 | tf_op jit(solution)/shard_map/ppermute | solution.py:515
  9.0 10.0 %collective-permute-start.1 = (f32[192,128]{1,0:T(8,128)S(1)}, f32[192,128]{1,0:T(8,128)S(1)}, u32[]{:S(2)}, u32[]{:S(2)}) collective-permute-start(f32[192,128]{1,0:T(8,128)S(1)} %get-tuple-element.26), channel_id=1, source_target_pairs={{0,8},{8,16},{16,24},{24,0},{1,9},{9,17},{17,25},{25,1},{2,10},{10... | collective-permute-start | bytes 294920 | tf_op jit(solution)/shard_map/ppermute | solution.py:515
  11.0 8.0 %collective-permute-start.2 = (f32[192,128]{1,0:T(8,128)S(1)}, f32[192,128]{1,0:T(8,128)S(1)}, u32[]{:S(2)}, u32[]{:S(2)}) collective-permute-start(f32[192,128]{1,0:T(8,128)S(1)} %get-tuple-element.27), channel_id=1, source_target_pairs={{0,24},{8,0},{16,8},{24,16},{1,25},{9,1},{17,9},{25,17},{2,26},{10... | collective-permute-start | bytes 294920 | tf_op jit(solution)/shard_map/ppermute | solution.py:515
  23.3 5.5 %collective-permute-start.5 = (f32[3,8,128]{2,1,0:T(8,128)S(1)}, f32[3,8,128]{2,1,0:T(8,128)S(1)}, u32[]{:S(2)}, u32[]{:S(2)}) collective-permute-start(f32[3,8,128]{2,1,0:T(8,128)S(1)} %get-tuple-element.35), channel_id=1, source_target_pairs={{0,16},{8,24},{16,8},{24,0},{1,17},{9,25},{17,9},{25,1},{2,18},{10... | collective-permute-start | bytes 36872 | tf_op jit(solution)/shard_map/ppermute | solution.py:545
  26.0 4.6 %collective-permute-start.6 = (f32[3,8,128]{2,1,0:T(8,128)S(1)}, f32[3,8,128]{2,1,0:T(8,128)S(1)}, u32[]{:S(2)}, u32[]{:S(2)}) collective-permute-start(f32[3,8,128]{2,1,0:T(8,128)S(1)} %get-tuple-element.34), channel_id=1, source_target_pairs={{0,24},{8,16},{16,0},{24,8},{1,25},{9,17},{17,1},{25,9},{2,26},{10... | collective-permute-start | bytes 36872 | tf_op jit(solution)/shard_map/ppermute | solution.py:545
  27.2 3.7 %collective-permute-start.7 = (f32[3,8,128]{2,1,0:T(8,128)S(1)}, f32[3,8,128]{2,1,0:T(8,128)S(1)}, u32[]{:S(2)}, u32[]{:S(2)}) collective-permute-start(f32[3,8,128]{2,1,0:T(8,128)S(1)} %get-tuple-element.33), channel_id=1, source_target_pairs={{0,8},{8,0},{16,24},{24,16},{1,9},{9,1},{17,25},{25,17},{2,10},{10... | collective-permute-start | bytes 36872 | tf_op jit(solution)/shard_map/ppermute | solution.py:545

commit v18 on v16

--- a/solution.py
+++ b/solution.py
@@ -493,7 +493,7 @@
 
 def exchange(count):
     if count == 4:
-        return [(2, 3, 1, 0), (3, 2, 0, 1), (1, 0, 3, 2)]
+        return [(2, 3, 0, 1), (3, 2, 1, 0), (1, 0, 3, 2)]
     if count & (count - 1) == 0:
         return [tuple(i ^ step for i in range(count)) for step in range(count - 1, 0, -1)]
     return [tuple((i + step) % count for i in range(count)) for step in range(1, count)]

time: 31.5 us -> 32.1 us (1.019)
  waiting for transfers between devices: 4.31 us -> 4.87 us
    ppermute x3, waiting for transfers between devices: 3.35 us -> 3.92 us  [exchanged(): lax.ppermute(blocks[k], axis, list(enumerate(route)))]
  transfers between devices with their start and end apart: 8 -> 8, of which waited for: 4 -> 3; matrix products, arithmetic and copies ran while one was open for 0% -> 0% of each run, Pallas kernels for 36% -> 36%
where the time goes in v18:
time: 32.1 us; the launch traced here: 31.9 us
  starting transfers between devices  12.3 us (38%)
  Pallas kernels  12.3 us (38%)
  waiting for transfers between devices  4.87 us (15%)
  between operations  1.38 us (4%)
  local copies, waits for them, and re-layouts  1.05 us (3%)
    ppermute x5, starting transfers between devices, turn(): lax.ppermute(block, axis, [(i, (i + by) % count) for i in range(count)])  8.08 us
    pallas_call x1, Pallas kernels, shaded(): pl.pallas_call(shade_kernel, out_shape=(jax.ShapeDtypeStruct((nx, ny, nz)...  4.59 us
    ppermute x3, starting transfers between devices, exchanged(): lax.ppermute(blocks[k], axis, list(enumerate(route)))  4.23 us
    ppermute x3, waiting for transfers between devices, exchanged(): lax.ppermute(blocks[k], axis, list(enumerate(route)))  3.92 us
    pallas_call x1, Pallas kernels, faces(): pl.pallas_call(faces_kernel, out_shape=(jax.ShapeDtypeStruct(u.shape, jnp...  3.78 us
    pallas_call x1, Pallas kernels, blended(): pl.pallas_call(functools.partial(blend_kernel, density), out_shape=(jax.S...  2.96 us
    slice x1, local copies, waits for them, and re-layouts, local(): xleft = turn(velocity[:, nx - 2:], 'gx', 1)  1.04 us
    ppermute x5, waiting for transfers between devices, turn(): lax.ppermute(block, axis, [(i, (i + by) % count) for i in range(count)])  0.96 us
  transfers between devices with their start and end apart: 8, of which 3 were waited for; matrix products, arithmetic and copies ran while one was open for 0% of the time, Pallas kernels for 36%

profile of v18, /device:TPU:0, one launch (start us, length us, event | category | flops | bytes accessed | tf_op | source)
XLA Modules:
  0.0 31.9 jit_solution(14726027603845483871)
XLA Ops:
  0.0 0.0 copy-start
  0.0 1.0 %slice.15 = f32[3,2,128,128]{3,2,1,0:T(8,128)S(1)} slice(f32[3,32,128,128]{3,2,1,0:T(8,128)} %u_hbm.1), slice={[0:3], [30:32], [0:128], [0:128]} | slice | bytes 786432 | tf_op jit(solution)/shard_map/slice | solution.py:552
  1.0 3.0 %collective-permute-start.3 = (f32[3,2,128,128]{3,2,1,0:T(8,128)S(1)}, f32[3,2,128,128]{3,2,1,0:T(8,128)S(1)}, u32[]{:S(2)}, u32[]{:S(2)}) collective-permute-start(f32[3,2,128,128]{3,2,1,0:T(8,128)S(1)} %slice.15), channel_id=1, source_target_pairs={{0,2},{2,4},{4,6},{6,0},{1,3},{3,5},{5,7},{7,1},{8,10},{10,12},{12... | collective-permute-start | bytes 1179656 | tf_op jit(solution)/shard_map/ppermute | solution.py:486
  4.0 3.8 %shard_map.46 = (f32[3,32,128,128]{3,2,1,0:T(8,128)S(1)}, bf16[3,32,128,256]{3,2,1,0:T(8,128)(2,1)S(1)}, f32[3,2,128,128]{3,2,1,0:T(8,128)S(1)}, f32[3,32,4,128]...) custom-call(f32[3,32,128,128]{3,2,1,0:T(8,128)} %u_hbm.1), custom_call_target="tpu_custom_call" | custom-call | flops 1048576 | bytes 1048576 | tf_op jit(solution)/shard_map/pallas_call | solution.py:98
  7.8 1.0 %collective-permute-start.4 = (f32[3,2,128,128]{3,2,1,0:T(8,128)S(1)}, f32[3,2,128,128]{3,2,1,0:T(8,128)S(1)}, u32[]{:S(2)}, u32[]{:S(2)}) collective-permute-start(f32[3,2,128,128]{3,2,1,0:T(8,128)S(1)} %get-tuple-element.32), channel_id=1, source_target_pairs={{0,6},{2,0},{4,2},{6,4},{1,7},{3,1},{5,3},{7,5},{8,14},{10,8},{12,... | collective-permute-start | bytes 1179656 | tf_op jit(solution)/shard_map/ppermute | solution.py:486
  8.9 0.0 collective-permute-start
  8.9 2.0 %collective-permute-start.1 = (f32[192,128]{1,0:T(8,128)S(1)}, f32[192,128]{1,0:T(8,128)S(1)}, u32[]{:S(2)}, u32[]{:S(2)}) collective-permute-start(f32[192,128]{1,0:T(8,128)S(1)} %get-tuple-element.26), channel_id=1, source_target_pairs={{0,8},{8,16},{16,24},{24,0},{1,9},{9,17},{17,25},{25,1},{2,10},{10... | collective-permute-start | bytes 294920 | tf_op jit(solution)/shard_map/ppermute | solution.py:486
  10.9 2.0 %collective-permute-start.2 = (f32[192,128]{1,0:T(8,128)S(1)}, f32[192,128]{1,0:T(8,128)S(1)}, u32[]{:S(2)}, u32[]{:S(2)}) collective-permute-start(f32[192,128]{1,0:T(8,128)S(1)} %get-tuple-element.27), channel_id=1, source_target_pairs={{0,24},{8,0},{16,8},{24,16},{1,25},{9,1},{17,9},{25,17},{2,26},{10... | collective-permute-start | bytes 294920 | tf_op jit(solution)/shard_map/ppermute | solution.py:486
  14.2 0.0 collective-permute-done.yleft_ref.yright_ref
  14.2 0.0 copy-done
  14.2 4.6 %shard_map.47 = (f32[32,128,128]{2,1,0:T(8,128)S(1)}, f32[3,128,128]{2,1,0:T(8,128)S(1)}, f32[4,3,128,128]{3,2,1,0:T(8,128)S(1)}, f32[4,128,128]{2,1,0:T(8,128)S(1)}) custom-call(f32[3,32,128,128]{3,2,1,0:T(8,128)S(1)} %get-tuple-element.19.u_ref, bf16[3,32,128,256]{3,2,1,0:T(8,128)(2,1)S(1)} %get-tuple-element.20.parts_ref, ...), custom_call_target="tpu_custom_call" | custom-call | flops 1048576 | bytes 1048576 | tf_op jit(solution)/shard_map/pallas_call | solution.py:240
  18.8 0.0 collective-permute-done.1.zleft_ref
  18.8 0.0 collective-permute-done.2.zright_ref
  18.9 0.0 collective-permute-done.3.xleft_ref
  18.9 3.0 %shard_map.48 = (f32[4,3,8,128]{3,2,1,0:T(8,128)S(1)}, f32[2,128,128]{2,1,0:T(8,128)S(1)}, f32[2,128,128]{2,1,0:T(8,128)S(1)}, bf16[256,384]{1,0:T(8,128)(2,1)S(1)}) custom-call(f32[32,128,128]{2,1,0:T(8,128)S(1)} %get-tuple-element.22.raw_ref, f32[3,128,128]{2,1,0:T(8,128)S(1)} %get-tuple-element.23.pack_ref, ...), custom_call_target="tpu_custom_call" | custom-call | flops 1048576 | bytes 1048576 | tf_op jit(solution)/shard_map/pallas_call | solution.py:400
  21.8 0.9 %collective-permute-done.4.xright_ref = f32[3,2,128,128]{3,2,1,0:T(8,128)S(1)} collective-permute-done((f32[3,2,128,128]{3,2,1,0:T(8,128)S(1)}, f32[3,2,128,128]{3,2,1,0:T(8,128)S(1)}, u32[]{:S(2)}, u32[]{:S(2)}) %collective-permute-start.4) | collective-permute-done | bytes 393248 | tf_op jit(solution)/shard_map/ppermute | solution.py:486
  22.8 0.3 %shard_map.49 = f32[4,3,8,128]{3,2,1,0:T(8,128)S(1)} custom-call(f32[4,3,8,128]{3,2,1,0:T(8,128)S(1)} %get-tuple-element.28.image_in_ref, f32[2,128,128]{2,1,0:T(8,128)S(1)} %get-tuple-element.29.base_ref, f32[2,128,128]{2,1,0:T(8,128)S(1)} %get-tuple-element.30.deep_ref, f32[4,3,128,128]{3,2,1,0:T(8,128)S(1)} %get-tuple-element.24.kept_ref, ...), custom_call_target="tpu_custom_call" | custom-call | flops 1048576 | bytes 1048576 | tf_op jit(solution)/shard_map/pallas_call | solution.py:473
  23.1 2.7 %collective-permute-start.5 = (f32[3,8,128]{2,1,0:T(8,128)S(1)}, f32[3,8,128]{2,1,0:T(8,128)S(1)}, u32[]{:S(2)}, u32[]{:S(2)}) collective-permute-start(f32[3,8,128]{2,1,0:T(8,128)S(1)} %get-tuple-element.35), channel_id=1, source_target_pairs={{0,16},{8,24},{16,0},{24,8},{1,17},{9,25},{17,1},{25,9},{2,18},{10... | collective-permute-start | bytes 36872 | tf_op jit(solution)/shard_map/ppermute | solution.py:516
  25.8 1.3 %collective-permute-start.6 = (f32[3,8,128]{2,1,0:T(8,128)S(1)}, f32[3,8,128]{2,1,0:T(8,128)S(1)}, u32[]{:S(2)}, u32[]{:S(2)}) collective-permute-start(f32[3,8,128]{2,1,0:T(8,128)S(1)} %get-tuple-element.34), channel_id=1, source_target_pairs={{0,24},{8,16},{16,8},{24,0},{1,25},{9,17},{17,9},{25,1},{2,26},{10... | collective-permute-start | bytes 36872 | tf_op jit(solution)/shard_map/ppermute | solution.py:516
  27.1 0.2 collective-permute-start.7
  27.4 0.4 %collective-permute-done.5.refs_1_ = f32[3,8,128]{2,1,0:T(8,128)S(1)} collective-permute-done((f32[3,8,128]{2,1,0:T(8,128)S(1)}, f32[3,8,128]{2,1,0:T(8,128)S(1)}, u32[]{:S(2)}, u32[]{:S(2)}) %collective-permute-start.5) | collective-permute-done | bytes 12320 | tf_op jit(solution)/shard_map/ppermute | solution.py:516
  27.8 3.5 %collective-permute-done.6.refs_2_ = f32[3,8,128]{2,1,0:T(8,128)S(1)} collective-permute-done((f32[3,8,128]{2,1,0:T(8,128)S(1)}, f32[3,8,128]{2,1,0:T(8,128)S(1)}, u32[]{:S(2)}, u32[]{:S(2)}) %collective-permute-start.6) | collective-permute-done | bytes 12320 | tf_op jit(solution)/shard_map/ppermute | solution.py:516
  31.3 0.0 collective-permute-done.7.refs_3_
  31.3 0.6 %shard_map.50 = f32[1,1,4,8,128]{4,3,2,1,0:T(8,128)} custom-call(f32[3,8,128]{2,1,0:T(8,128)S(1)} %get-tuple-element.36.refs_0_, f32[3,8,128]{2,1,0:T(8,128)S(1)} %collective-permute-done.5.refs_1_, f32[3,8,128]{2,1,0:T(8,128)S(1)} %collective-permute-done.6.refs_2_, f32[3,8,128]{2,1,0:T(8,128)S(1)} %collective-permute-done.7.refs_3_), custom_call_target="tpu_custom_call" | custom-call | flops 1048576 | bytes 1048576 | tf_op jit(solution)/shard_map/pallas_call | solution.py:538
  (1 shorter events, 0.0 us)
Async XLA Ops:
  0.0 14.2 %copy-start = (s32[4,16,1]{1,2,0:T(1,128)S(1)}, s32[4,16,1]{1,2,0:T(1,128)}, u32[]{:S(2)}) copy-start(s32[4,16,1]{1,2,0:T(1,128)} %param.5) | copy-start | bytes 772
  1.0 17.8 %collective-permute-start.3 = (f32[3,2,128,128]{3,2,1,0:T(8,128)S(1)}, f32[3,2,128,128]{3,2,1,0:T(8,128)S(1)}, u32[]{:S(2)}, u32[]{:S(2)}) collective-permute-start(f32[3,2,128,128]{3,2,1,0:T(8,128)S(1)} %slice.15), channel_id=1, source_target_pairs={{0,2},{2,4},{4,6},{6,0},{1,3},{3,5},{5,7},{7,1},{8,10},{10,12},{12... | collective-permute-start | bytes 1179656 | tf_op jit(solution)/shard_map/ppermute | solution.py:486
  7.8 15.0 %collective-permute-start.4 = (f32[3,2,128,128]{3,2,1,0:T(8,128)S(1)}, f32[3,2,128,128]{3,2,1,0:T(8,128)S(1)}, u32[]{:S(2)}, u32[]{:S(2)}) collective-permute-start(f32[3,2,128,128]{3,2,1,0:T(8,128)S(1)} %get-tuple-element.32), channel_id=1, source_target_pairs={{0,6},{2,0},{4,2},{6,4},{1,7},{3,1},{5,3},{7,5},{8,14},{10,8},{12,... | collective-permute-start | bytes 1179656 | tf_op jit(solution)/shard_map/ppermute | solution.py:486
  8.9 5.4 %collective-permute-start = (f32[3,32,4,128]{3,2,1,0:T(4,128)S(1)}, f32[3,32,4,128]{3,2,1,0:T(4,128)S(1)}, u32[]{:S(2)}, u32[]{:S(2)}) collective-permute-start(f32[3,32,4,128]{3,2,1,0:T(4,128)S(1)} %get-tuple-element.21), channel_id=1, source_target_pairs={{0,1},{1,0},{2,3},{3,2},{4,5},{5,4},{6,7},{7,6},{8,9},{9,8},{10,11... | collective-permute-start | bytes 589832 | tf_op jit(solution)/shard_map/ppermute | solution.py:486
  8.9 10.0 %collective-permute-start.1 = (f32[192,128]{1,0:T(8,128)S(1)}, f32[192,128]{1,0:T(8,128)S(1)}, u32[]{:S(2)}, u32[]{:S(2)}) collective-permute-start(f32[192,128]{1,0:T(8,128)S(1)} %get-tuple-element.26), channel_id=1, source_target_pairs={{0,8},{8,16},{16,24},{24,0},{1,9},{9,17},{17,25},{25,1},{2,10},{10... | collective-permute-start | bytes 294920 | tf_op jit(solution)/shard_map/ppermute | solution.py:486
  10.9 8.0 %collective-permute-start.2 = (f32[192,128]{1,0:T(8,128)S(1)}, f32[192,128]{1,0:T(8,128)S(1)}, u32[]{:S(2)}, u32[]{:S(2)}) collective-permute-start(f32[192,128]{1,0:T(8,128)S(1)} %get-tuple-element.27), channel_id=1, source_target_pairs={{0,24},{8,0},{16,8},{24,16},{1,25},{9,1},{17,9},{25,17},{2,26},{10... | collective-permute-start | bytes 294920 | tf_op jit(solution)/shard_map/ppermute | solution.py:486
  23.1 4.7 %collective-permute-start.5 = (f32[3,8,128]{2,1,0:T(8,128)S(1)}, f32[3,8,128]{2,1,0:T(8,128)S(1)}, u32[]{:S(2)}, u32[]{:S(2)}) collective-permute-start(f32[3,8,128]{2,1,0:T(8,128)S(1)} %get-tuple-element.35), channel_id=1, source_target_pairs={{0,16},{8,24},{16,0},{24,8},{1,17},{9,25},{17,1},{25,9},{2,18},{10... | collective-permute-start | bytes 36872 | tf_op jit(solution)/shard_map/ppermute | solution.py:516
  25.8 5.5 %collective-permute-start.6 = (f32[3,8,128]{2,1,0:T(8,128)S(1)}, f32[3,8,128]{2,1,0:T(8,128)S(1)}, u32[]{:S(2)}, u32[]{:S(2)}) collective-permute-start(f32[3,8,128]{2,1,0:T(8,128)S(1)} %get-tuple-element.34), channel_id=1, source_target_pairs={{0,24},{8,16},{16,8},{24,0},{1,25},{9,17},{17,9},{25,1},{2,26},{10... | collective-permute-start | bytes 36872 | tf_op jit(solution)/shard_map/ppermute | solution.py:516
  27.1 4.1 %collective-permute-start.7 = (f32[3,8,128]{2,1,0:T(8,128)S(1)}, f32[3,8,128]{2,1,0:T(8,128)S(1)}, u32[]{:S(2)}, u32[]{:S(2)}) collective-permute-start(f32[3,8,128]{2,1,0:T(8,128)S(1)} %get-tuple-element.33), channel_id=1, source_target_pairs={{0,8},{8,0},{16,24},{24,16},{1,9},{9,1},{17,25},{25,17},{2,10},{10... | collective-permute-start | bytes 36872 | tf_op jit(solution)/shard_map/ppermute | solution.py:516

commit v19 on v16

--- a/solution.py
+++ b/solution.py
@@ -423,14 +423,11 @@
         level = jnp.clip(raw, 0.0, 1.0)
         level_ref[k] = level
         parts.append(jnp.concatenate(split(binary * level), axis=1))
-    sums = jnp.dot(
-        jnp.concatenate(parts, axis=0), sum_ref[:, pl.ds(nz, nz)], preferred_element_type=jnp.float32
-    )
     lane_group = iota((8, ny), 1) // 8
     eye = iota((8, ny), 1) % 8 == iota((8, ny), 0)
     last = iota((8, nz), 1) == nz - 1
     for k, store in enumerate(stores):
-        sums_ref[k] = sums[k * ny : (k + 1) * ny]
+        sums_ref[k] = jnp.dot(parts[k], sum_ref[:, pl.ds(nz, nz)], preferred_element_type=jnp.float32)
         totals = [jnp.zeros((8, ny), jnp.float32)] * 3
         for group in range(ny // 8):
             rows = pl.ds(8 * group, 8)

time: 31.5 us -> 31.5 us (level)
  no operation moved by 1% of the time
where the time goes in v19:
time: 31.5 us; the launch traced here: 31.3 us
  starting transfers between devices  12.3 us (39%)
  Pallas kernels  12.3 us (39%)
  waiting for transfers between devices  4.34 us (14%)
  between operations  1.38 us (4%)
  local copies, waits for them, and re-layouts  1.05 us (3%)
    ppermute x5, starting transfers between devices, turn(): lax.ppermute(block, axis, [(i, (i + by) % count) for i in range(count)])  8.08 us
    pallas_call x1, Pallas kernels, shaded(): pl.pallas_call(shade_kernel, out_shape=(jax.ShapeDtypeStruct((nx, ny, nz)...  4.59 us
    ppermute x3, starting transfers between devices, exchanged(): lax.ppermute(blocks[k], axis, list(enumerate(route)))  4.22 us
    pallas_call x1, Pallas kernels, faces(): pl.pallas_call(faces_kernel, out_shape=(jax.ShapeDtypeStruct(u.shape, jnp...  3.78 us
    ppermute x3, waiting for transfers between devices, exchanged(): lax.ppermute(blocks[k], axis, list(enumerate(route)))  3.35 us
    pallas_call x1, Pallas kernels, blended(): pl.pallas_call(functools.partial(blend_kernel, density), out_shape=(jax.S...  2.92 us
    slice x1, local copies, waits for them, and re-layouts, local(): xleft = turn(velocity[:, nx - 2:], 'gx', 1)  1.04 us
    ppermute x5, waiting for transfers between devices, turn(): lax.ppermute(block, axis, [(i, (i + by) % count) for i in range(count)])  0.99 us
  transfers between devices with their start and end apart: 8, of which 4 were waited for; matrix products, arithmetic and copies ran while one was open for 0% of the time, Pallas kernels for 36%

profile of v19, /device:TPU:0, one launch (start us, length us, event | category | flops | bytes accessed | tf_op | source)
XLA Modules:
  0.0 31.3 jit_solution(14021410802825668454)
XLA Ops:
  0.0 0.0 copy-start
  0.0 1.0 %slice.15 = f32[3,2,128,128]{3,2,1,0:T(8,128)S(1)} slice(f32[3,32,128,128]{3,2,1,0:T(8,128)} %u_hbm.1), slice={[0:3], [30:32], [0:128], [0:128]} | slice | bytes 786432 | tf_op jit(solution)/shard_map/slice | solution.py:549
  1.0 3.0 %collective-permute-start.3 = (f32[3,2,128,128]{3,2,1,0:T(8,128)S(1)}, f32[3,2,128,128]{3,2,1,0:T(8,128)S(1)}, u32[]{:S(2)}, u32[]{:S(2)}) collective-permute-start(f32[3,2,128,128]{3,2,1,0:T(8,128)S(1)} %slice.15), channel_id=1, source_target_pairs={{0,2},{2,4},{4,6},{6,0},{1,3},{3,5},{5,7},{7,1},{8,10},{10,12},{12... | collective-permute-start | bytes 1179656 | tf_op jit(solution)/shard_map/ppermute | solution.py:483
  4.0 3.8 %shard_map.46 = (f32[3,32,128,128]{3,2,1,0:T(8,128)S(1)}, bf16[3,32,128,256]{3,2,1,0:T(8,128)(2,1)S(1)}, f32[3,2,128,128]{3,2,1,0:T(8,128)S(1)}, f32[3,32,4,128]...) custom-call(f32[3,32,128,128]{3,2,1,0:T(8,128)} %u_hbm.1), custom_call_target="tpu_custom_call" | custom-call | flops 1048576 | bytes 1048576 | tf_op jit(solution)/shard_map/pallas_call | solution.py:98
  7.8 1.0 %collective-permute-start.4 = (f32[3,2,128,128]{3,2,1,0:T(8,128)S(1)}, f32[3,2,128,128]{3,2,1,0:T(8,128)S(1)}, u32[]{:S(2)}, u32[]{:S(2)}) collective-permute-start(f32[3,2,128,128]{3,2,1,0:T(8,128)S(1)} %get-tuple-element.32), channel_id=1, source_target_pairs={{0,6},{2,0},{4,2},{6,4},{1,7},{3,1},{5,3},{7,5},{8,14},{10,8},{12,... | collective-permute-start | bytes 1179656 | tf_op jit(solution)/shard_map/ppermute | solution.py:483
  8.9 0.0 collective-permute-start
  8.9 2.0 %collective-permute-start.1 = (f32[192,128]{1,0:T(8,128)S(1)}, f32[192,128]{1,0:T(8,128)S(1)}, u32[]{:S(2)}, u32[]{:S(2)}) collective-permute-start(f32[192,128]{1,0:T(8,128)S(1)} %get-tuple-element.26), channel_id=1, source_target_pairs={{0,8},{8,16},{16,24},{24,0},{1,9},{9,17},{17,25},{25,1},{2,10},{10... | collective-permute-start | bytes 294920 | tf_op jit(solution)/shard_map/ppermute | solution.py:483
  10.9 2.0 %collective-permute-start.2 = (f32[192,128]{1,0:T(8,128)S(1)}, f32[192,128]{1,0:T(8,128)S(1)}, u32[]{:S(2)}, u32[]{:S(2)}) collective-permute-start(f32[192,128]{1,0:T(8,128)S(1)} %get-tuple-element.27), channel_id=1, source_target_pairs={{0,24},{8,0},{16,8},{24,16},{1,25},{9,1},{17,9},{25,17},{2,26},{10... | collective-permute-start | bytes 294920 | tf_op jit(solution)/shard_map/ppermute | solution.py:483
  14.2 0.0 collective-permute-done.yleft_ref.yright_ref
  14.2 0.0 copy-done
  14.2 4.6 %shard_map.47 = (f32[32,128,128]{2,1,0:T(8,128)S(1)}, f32[3,128,128]{2,1,0:T(8,128)S(1)}, f32[4,3,128,128]{3,2,1,0:T(8,128)S(1)}, f32[4,128,128]{2,1,0:T(8,128)S(1)}) custom-call(f32[3,32,128,128]{3,2,1,0:T(8,128)S(1)} %get-tuple-element.19.u_ref, bf16[3,32,128,256]{3,2,1,0:T(8,128)(2,1)S(1)} %get-tuple-element.20.parts_ref, ...), custom_call_target="tpu_custom_call" | custom-call | flops 1048576 | bytes 1048576 | tf_op jit(solution)/shard_map/pallas_call | solution.py:240
  18.8 0.0 collective-permute-done.1.zleft_ref
  18.8 0.0 collective-permute-done.2.zright_ref
  18.9 0.0 collective-permute-done.3.xleft_ref
  18.9 2.9 %shard_map.48 = (f32[4,3,8,128]{3,2,1,0:T(8,128)S(1)}, f32[2,128,128]{2,1,0:T(8,128)S(1)}, f32[2,128,128]{2,1,0:T(8,128)S(1)}, bf16[256,384]{1,0:T(8,128)(2,1)S(1)}) custom-call(f32[32,128,128]{2,1,0:T(8,128)S(1)} %get-tuple-element.22.raw_ref, f32[3,128,128]{2,1,0:T(8,128)S(1)} %get-tuple-element.23.pack_ref, ...), custom_call_target="tpu_custom_call" | custom-call | flops 1048576 | bytes 1048576 | tf_op jit(solution)/shard_map/pallas_call | solution.py:400
  21.8 1.0 %collective-permute-done.4.xright_ref = f32[3,2,128,128]{3,2,1,0:T(8,128)S(1)} collective-permute-done((f32[3,2,128,128]{3,2,1,0:T(8,128)S(1)}, f32[3,2,128,128]{3,2,1,0:T(8,128)S(1)}, u32[]{:S(2)}, u32[]{:S(2)}) %collective-permute-start.4) | collective-permute-done | bytes 393248 | tf_op jit(solution)/shard_map/ppermute | solution.py:483
  22.8 0.3 %shard_map.49 = f32[4,3,8,128]{3,2,1,0:T(8,128)S(1)} custom-call(f32[4,3,8,128]{3,2,1,0:T(8,128)S(1)} %get-tuple-element.28.image_in_ref, f32[2,128,128]{2,1,0:T(8,128)S(1)} %get-tuple-element.29.base_ref, f32[2,128,128]{2,1,0:T(8,128)S(1)} %get-tuple-element.30.deep_ref, f32[4,3,128,128]{3,2,1,0:T(8,128)S(1)} %get-tuple-element.24.kept_ref, ...), custom_call_target="tpu_custom_call" | custom-call | flops 1048576 | bytes 1048576 | tf_op jit(solution)/shard_map/pallas_call | solution.py:470
  23.1 2.6 %collective-permute-start.5 = (f32[3,8,128]{2,1,0:T(8,128)S(1)}, f32[3,8,128]{2,1,0:T(8,128)S(1)}, u32[]{:S(2)}, u32[]{:S(2)}) collective-permute-start(f32[3,8,128]{2,1,0:T(8,128)S(1)} %get-tuple-element.35), channel_id=1, source_target_pairs={{0,16},{8,24},{16,8},{24,0},{1,17},{9,25},{17,9},{25,1},{2,18},{10... | collective-permute-start | bytes 36872 | tf_op jit(solution)/shard_map/ppermute | solution.py:513
  25.8 1.2 %collective-permute-start.6 = (f32[3,8,128]{2,1,0:T(8,128)S(1)}, f32[3,8,128]{2,1,0:T(8,128)S(1)}, u32[]{:S(2)}, u32[]{:S(2)}) collective-permute-start(f32[3,8,128]{2,1,0:T(8,128)S(1)} %get-tuple-element.34), channel_id=1, source_target_pairs={{0,24},{8,16},{16,0},{24,8},{1,25},{9,17},{17,1},{25,9},{2,26},{10... | collective-permute-start | bytes 36872 | tf_op jit(solution)/shard_map/ppermute | solution.py:513
  27.0 0.3 %collective-permute-start.7 = (f32[3,8,128]{2,1,0:T(8,128)S(1)}, f32[3,8,128]{2,1,0:T(8,128)S(1)}, u32[]{:S(2)}, u32[]{:S(2)}) collective-permute-start(f32[3,8,128]{2,1,0:T(8,128)S(1)} %get-tuple-element.33), channel_id=1, source_target_pairs={{0,8},{8,0},{16,24},{24,16},{1,9},{9,1},{17,25},{25,17},{2,10},{10... | collective-permute-start | bytes 36872 | tf_op jit(solution)/shard_map/ppermute | solution.py:513
  27.4 1.3 %collective-permute-done.5.refs_1_ = f32[3,8,128]{2,1,0:T(8,128)S(1)} collective-permute-done((f32[3,8,128]{2,1,0:T(8,128)S(1)}, f32[3,8,128]{2,1,0:T(8,128)S(1)}, u32[]{:S(2)}, u32[]{:S(2)}) %collective-permute-start.5) | collective-permute-done | bytes 12320 | tf_op jit(solution)/shard_map/ppermute | solution.py:513
  28.7 1.7 %collective-permute-done.6.refs_2_ = f32[3,8,128]{2,1,0:T(8,128)S(1)} collective-permute-done((f32[3,8,128]{2,1,0:T(8,128)S(1)}, f32[3,8,128]{2,1,0:T(8,128)S(1)}, u32[]{:S(2)}, u32[]{:S(2)}) %collective-permute-start.6) | collective-permute-done | bytes 12320 | tf_op jit(solution)/shard_map/ppermute | solution.py:513
  30.4 0.3 %collective-permute-done.7.refs_3_ = f32[3,8,128]{2,1,0:T(8,128)S(1)} collective-permute-done((f32[3,8,128]{2,1,0:T(8,128)S(1)}, f32[3,8,128]{2,1,0:T(8,128)S(1)}, u32[]{:S(2)}, u32[]{:S(2)}) %collective-permute-start.7) | collective-permute-done | bytes 12320 | tf_op jit(solution)/shard_map/ppermute | solution.py:513
  30.7 0.6 %shard_map.50 = f32[1,1,4,8,128]{4,3,2,1,0:T(8,128)} custom-call(f32[3,8,128]{2,1,0:T(8,128)S(1)} %get-tuple-element.36.refs_0_, f32[3,8,128]{2,1,0:T(8,128)S(1)} %collective-permute-done.5.refs_1_, f32[3,8,128]{2,1,0:T(8,128)S(1)} %collective-permute-done.6.refs_2_, f32[3,8,128]{2,1,0:T(8,128)S(1)} %collective-permute-done.7.refs_3_), custom_call_target="tpu_custom_call" | custom-call | flops 1048576 | bytes 1048576 | tf_op jit(solution)/shard_map/pallas_call | solution.py:535
  (1 shorter events, 0.0 us)
Async XLA Ops:
  0.0 14.2 %copy-start = (s32[4,16,1]{1,2,0:T(1,128)S(1)}, s32[4,16,1]{1,2,0:T(1,128)}, u32[]{:S(2)}) copy-start(s32[4,16,1]{1,2,0:T(1,128)} %param.5) | copy-start | bytes 772
  1.0 17.8 %collective-permute-start.3 = (f32[3,2,128,128]{3,2,1,0:T(8,128)S(1)}, f32[3,2,128,128]{3,2,1,0:T(8,128)S(1)}, u32[]{:S(2)}, u32[]{:S(2)}) collective-permute-start(f32[3,2,128,128]{3,2,1,0:T(8,128)S(1)} %slice.15), channel_id=1, source_target_pairs={{0,2},{2,4},{4,6},{6,0},{1,3},{3,5},{5,7},{7,1},{8,10},{10,12},{12... | collective-permute-start | bytes 1179656 | tf_op jit(solution)/shard_map/ppermute | solution.py:483
  7.8 15.0 %collective-permute-start.4 = (f32[3,2,128,128]{3,2,1,0:T(8,128)S(1)}, f32[3,2,128,128]{3,2,1,0:T(8,128)S(1)}, u32[]{:S(2)}, u32[]{:S(2)}) collective-permute-start(f32[3,2,128,128]{3,2,1,0:T(8,128)S(1)} %get-tuple-element.32), channel_id=1, source_target_pairs={{0,6},{2,0},{4,2},{6,4},{1,7},{3,1},{5,3},{7,5},{8,14},{10,8},{12,... | collective-permute-start | bytes 1179656 | tf_op jit(solution)/shard_map/ppermute | solution.py:483
  8.9 5.4 %collective-permute-start = (f32[3,32,4,128]{3,2,1,0:T(4,128)S(1)}, f32[3,32,4,128]{3,2,1,0:T(4,128)S(1)}, u32[]{:S(2)}, u32[]{:S(2)}) collective-permute-start(f32[3,32,4,128]{3,2,1,0:T(4,128)S(1)} %get-tuple-element.21), channel_id=1, source_target_pairs={{0,1},{1,0},{2,3},{3,2},{4,5},{5,4},{6,7},{7,6},{8,9},{9,8},{10,11... | collective-permute-start | bytes 589832 | tf_op jit(solution)/shard_map/ppermute | solution.py:483
  8.9 10.0 %collective-permute-start.1 = (f32[192,128]{1,0:T(8,128)S(1)}, f32[192,128]{1,0:T(8,128)S(1)}, u32[]{:S(2)}, u32[]{:S(2)}) collective-permute-start(f32[192,128]{1,0:T(8,128)S(1)} %get-tuple-element.26), channel_id=1, source_target_pairs={{0,8},{8,16},{16,24},{24,0},{1,9},{9,17},{17,25},{25,1},{2,10},{10... | collective-permute-start | bytes 294920 | tf_op jit(solution)/shard_map/ppermute | solution.py:483
  10.9 8.0 %collective-permute-start.2 = (f32[192,128]{1,0:T(8,128)S(1)}, f32[192,128]{1,0:T(8,128)S(1)}, u32[]{:S(2)}, u32[]{:S(2)}) collective-permute-start(f32[192,128]{1,0:T(8,128)S(1)} %get-tuple-element.27), channel_id=1, source_target_pairs={{0,24},{8,0},{16,8},{24,16},{1,25},{9,1},{17,9},{25,17},{2,26},{10... | collective-permute-start | bytes 294920 | tf_op jit(solution)/shard_map/ppermute | solution.py:483
  23.1 5.5 %collective-permute-start.5 = (f32[3,8,128]{2,1,0:T(8,128)S(1)}, f32[3,8,128]{2,1,0:T(8,128)S(1)}, u32[]{:S(2)}, u32[]{:S(2)}) collective-permute-start(f32[3,8,128]{2,1,0:T(8,128)S(1)} %get-tuple-element.35), channel_id=1, source_target_pairs={{0,16},{8,24},{16,8},{24,0},{1,17},{9,25},{17,9},{25,1},{2,18},{10... | collective-permute-start | bytes 36872 | tf_op jit(solution)/shard_map/ppermute | solution.py:513
  25.8 4.6 %collective-permute-start.6 = (f32[3,8,128]{2,1,0:T(8,128)S(1)}, f32[3,8,128]{2,1,0:T(8,128)S(1)}, u32[]{:S(2)}, u32[]{:S(2)}) collective-permute-start(f32[3,8,128]{2,1,0:T(8,128)S(1)} %get-tuple-element.34), channel_id=1, source_target_pairs={{0,24},{8,16},{16,0},{24,8},{1,25},{9,17},{17,1},{25,9},{2,26},{10... | collective-permute-start | bytes 36872 | tf_op jit(solution)/shard_map/ppermute | solution.py:513
  27.0 3.7 %collective-permute-start.7 = (f32[3,8,128]{2,1,0:T(8,128)S(1)}, f32[3,8,128]{2,1,0:T(8,128)S(1)}, u32[]{:S(2)}, u32[]{:S(2)}) collective-permute-start(f32[3,8,128]{2,1,0:T(8,128)S(1)} %get-tuple-element.33), channel_id=1, source_target_pairs={{0,8},{8,0},{16,24},{24,16},{1,9},{9,1},{17,25},{25,17},{2,10},{10... | collective-permute-start | bytes 36872 | tf_op jit(solution)/shard_map/ppermute | solution.py:513

commit v20 on v16

--- a/solution.py
+++ b/solution.py
@@ -24,6 +24,38 @@
 
 def iota(shape, dim):
     return lax.broadcasted_iota(jnp.int32, shape, dim)
+
+
+def tail_kernel(u_hbm, out_ref, sems):
+    comps, nx, ny, _ = u_hbm.shape
+    half = ny // 2
+    copies = [
+        pltpu.make_async_copy(
+            u_hbm.at[c, nx - 2 + layer, pl.ds(part * half, half)],
+            out_ref.at[c, layer, pl.ds(part * half, half)],
+            sems.at[c, layer, part],
+        )
+        for c in range(comps)
+        for layer in range(2)
+        for part in range(2)
+    ]
+    for copy in copies:
+        copy.start()
+    for copy in copies:
+        copy.wait()
+
+
+def tail(u):
+    comps, _, ny, nz = u.shape
+    return pl.pallas_call(
+        tail_kernel,
+        out_shape=jax.ShapeDtypeStruct((comps, 2, ny, nz), jnp.float32),
+        in_specs=[HBM],
+        out_specs=VMEM,
+        scratch_shapes=[pltpu.SemaphoreType.DMA((comps, 2, 2))],
+        compiler_params=pltpu.CompilerParams(vmem_limit_bytes=50 << 20),
+        cost_estimate=COST,
+    )(u)
 
 
 def faces_kernel(u_hbm, u_ref, parts_ref, xhead_ref, yface_ref, tail_ref, head_ref, packed_ref, sems):
@@ -549,7 +581,7 @@
     comps, nx, ny, nz = velocity.shape
     views = lax.axis_size("view")
     density = 5.0 / (nz * views)
-    xleft = turn(velocity[:, nx - 2 :], "gx", 1)
+    xleft = turn(tail(velocity), "gx", 1)
     u, parts, xhead, yface, ztail, zhead = faces(velocity)
     xright = turn(xhead, "gx", -1)
     zleft = turn(ztail, "view", 1)

time: 31.5 us -> 31.6 us (level)
  local copies, waits for them, and re-layouts: 1.05 us -> 0.01 us
  Pallas kernels: 12.3 us -> 13.3 us
    pallas_call x0 -> x1, Pallas kernels: none -> 1.05 us  [tail(): pl.pallas_call(tail_kernel, out_shape=jax.ShapeDtypeStruct((comps, 2, ny,...]
    slice x1 -> x0, local copies, waits for them, and re-layouts: 1.04 us -> none  [local(): xleft = turn(velocity[:, nx - 2:], 'gx', 1)]
where the time goes in v20:
time: 31.6 us; the launch traced here: 31.3 us
  Pallas kernels  13.3 us (42%)
  starting transfers between devices  12.3 us (39%)
  waiting for transfers between devices  4.33 us (14%)
  between operations  1.39 us (4%)
    ppermute x5, starting transfers between devices, turn(): lax.ppermute(block, axis, [(i, (i + by) % count) for i in range(count)])  8.08 us
    pallas_call x1, Pallas kernels, shaded(): pl.pallas_call(shade_kernel, out_shape=(jax.ShapeDtypeStruct((nx, ny, nz)...  4.59 us
    ppermute x3, starting transfers between devices, exchanged(): lax.ppermute(blocks[k], axis, list(enumerate(route)))  4.22 us
    pallas_call x1, Pallas kernels, faces(): pl.pallas_call(faces_kernel, out_shape=(jax.ShapeDtypeStruct(u.shape, jnp...  3.78 us
    ppermute x3, waiting for transfers between devices, exchanged(): lax.ppermute(blocks[k], axis, list(enumerate(route)))  3.35 us
    pallas_call x1, Pallas kernels, blended(): pl.pallas_call(functools.partial(blend_kernel, density), out_shape=(jax.S...  2.94 us
    pallas_call x1, Pallas kernels, tail(): pl.pallas_call(tail_kernel, out_shape=jax.ShapeDtypeStruct((comps, 2, ny,...  1.05 us
    ppermute x5, waiting for transfers between devices, turn(): lax.ppermute(block, axis, [(i, (i + by) % count) for i in range(count)])  0.98 us
  transfers between devices with their start and end apart: 8, of which 4 were waited for; matrix products, arithmetic and copies ran while one was open for 0% of the time, Pallas kernels for 36%

profile of v20, /device:TPU:0, one launch (start us, length us, event | category | flops | bytes accessed | tf_op | source)
XLA Modules:
  0.0 31.3 jit_solution(16502570553094830235)
XLA Ops:
  0.0 0.0 copy-start
  0.0 1.0 %shard_map.48 = f32[3,2,128,128]{3,2,1,0:T(8,128)S(1)} custom-call(f32[3,32,128,128]{3,2,1,0:T(8,128)} %u_hbm.3), custom_call_target="tpu_custom_call" | custom-call | flops 1048576 | bytes 1048576 | tf_op jit(solution)/shard_map/pallas_call | solution.py:50
  1.1 3.0 %collective-permute-start.3 = (f32[3,2,128,128]{3,2,1,0:T(8,128)S(1)}, f32[3,2,128,128]{3,2,1,0:T(8,128)S(1)}, u32[]{:S(2)}, u32[]{:S(2)}) collective-permute-start(f32[3,2,128,128]{3,2,1,0:T(8,128)S(1)} %shard_map.48), channel_id=1, source_target_pairs={{0,2},{2,4},{4,6},{6,0},{1,3},{3,5},{5,7},{7,1},{8,10},{10,12},{12... | collective-permute-start | bytes 1179656 | tf_op jit(solution)/shard_map/ppermute | solution.py:518
  4.1 3.8 %shard_map.46 = (f32[3,32,128,128]{3,2,1,0:T(8,128)S(1)}, bf16[3,32,128,256]{3,2,1,0:T(8,128)(2,1)S(1)}, f32[3,2,128,128]{3,2,1,0:T(8,128)S(1)}, f32[3,32,4,128]...) custom-call(f32[3,32,128,128]{3,2,1,0:T(8,128)} %u_hbm.3), custom_call_target="tpu_custom_call" | custom-call | flops 1048576 | bytes 1048576 | tf_op jit(solution)/shard_map/pallas_call | solution.py:130
  7.8 1.0 %collective-permute-start.4 = (f32[3,2,128,128]{3,2,1,0:T(8,128)S(1)}, f32[3,2,128,128]{3,2,1,0:T(8,128)S(1)}, u32[]{:S(2)}, u32[]{:S(2)}) collective-permute-start(f32[3,2,128,128]{3,2,1,0:T(8,128)S(1)} %get-tuple-element.32), channel_id=1, source_target_pairs={{0,6},{2,0},{4,2},{6,4},{1,7},{3,1},{5,3},{7,5},{8,14},{10,8},{12,... | collective-permute-start | bytes 1179656 | tf_op jit(solution)/shard_map/ppermute | solution.py:518
  8.9 0.0 collective-permute-start
  8.9 2.0 %collective-permute-start.1 = (f32[192,128]{1,0:T(8,128)S(1)}, f32[192,128]{1,0:T(8,128)S(1)}, u32[]{:S(2)}, u32[]{:S(2)}) collective-permute-start(f32[192,128]{1,0:T(8,128)S(1)} %get-tuple-element.26), channel_id=1, source_target_pairs={{0,8},{8,16},{16,24},{24,0},{1,9},{9,17},{17,25},{25,1},{2,10},{10... | collective-permute-start | bytes 294920 | tf_op jit(solution)/shard_map/ppermute | solution.py:518
  10.9 2.0 %collective-permute-start.2 = (f32[192,128]{1,0:T(8,128)S(1)}, f32[192,128]{1,0:T(8,128)S(1)}, u32[]{:S(2)}, u32[]{:S(2)}) collective-permute-start(f32[192,128]{1,0:T(8,128)S(1)} %get-tuple-element.27), channel_id=1, source_target_pairs={{0,24},{8,0},{16,8},{24,16},{1,25},{9,1},{17,9},{25,17},{2,26},{10... | collective-permute-start | bytes 294920 | tf_op jit(solution)/shard_map/ppermute | solution.py:518
  14.2 0.0 collective-permute-done.yleft_ref.yright_ref
  14.2 0.0 copy-done
  14.3 4.6 %shard_map.47 = (f32[32,128,128]{2,1,0:T(8,128)S(1)}, f32[3,128,128]{2,1,0:T(8,128)S(1)}, f32[4,3,128,128]{3,2,1,0:T(8,128)S(1)}, f32[4,128,128]{2,1,0:T(8,128)S(1)}) custom-call(f32[3,32,128,128]{3,2,1,0:T(8,128)S(1)} %get-tuple-element.19.u_ref, bf16[3,32,128,256]{3,2,1,0:T(8,128)(2,1)S(1)} %get-tuple-element.20.parts_ref, ...), custom_call_target="tpu_custom_call" | custom-call | flops 1048576 | bytes 1048576 | tf_op jit(solution)/shard_map/pallas_call | solution.py:272
  18.9 0.0 collective-permute-done.1.zleft_ref
  18.9 0.0 collective-permute-done.2.zright_ref
  18.9 0.0 collective-permute-done.3.xleft_ref
  18.9 2.9 %shard_map.49 = (f32[4,3,8,128]{3,2,1,0:T(8,128)S(1)}, f32[2,128,128]{2,1,0:T(8,128)S(1)}, f32[2,128,128]{2,1,0:T(8,128)S(1)}, bf16[256,384]{1,0:T(8,128)(2,1)S(1)}) custom-call(f32[32,128,128]{2,1,0:T(8,128)S(1)} %get-tuple-element.22.raw_ref, f32[3,128,128]{2,1,0:T(8,128)S(1)} %get-tuple-element.23.pack_ref, ...), custom_call_target="tpu_custom_call" | custom-call | flops 1048576 | bytes 1048576 | tf_op jit(solution)/shard_map/pallas_call | solution.py:432
  21.8 1.0 %collective-permute-done.4.xright_ref = f32[3,2,128,128]{3,2,1,0:T(8,128)S(1)} collective-permute-done((f32[3,2,128,128]{3,2,1,0:T(8,128)S(1)}, f32[3,2,128,128]{3,2,1,0:T(8,128)S(1)}, u32[]{:S(2)}, u32[]{:S(2)}) %collective-permute-start.4) | collective-permute-done | bytes 393248 | tf_op jit(solution)/shard_map/ppermute | solution.py:518
  22.8 0.3 %shard_map.50 = f32[4,3,8,128]{3,2,1,0:T(8,128)S(1)} custom-call(f32[4,3,8,128]{3,2,1,0:T(8,128)S(1)} %get-tuple-element.28.image_in_ref, f32[2,128,128]{2,1,0:T(8,128)S(1)} %get-tuple-element.29.base_ref, f32[2,128,128]{2,1,0:T(8,128)S(1)} %get-tuple-element.30.deep_ref, f32[4,3,128,128]{3,2,1,0:T(8,128)S(1)} %get-tuple-element.24.kept_ref, ...), custom_call_target="tpu_custom_call" | custom-call | flops 1048576 | bytes 1048576 | tf_op jit(solution)/shard_map/pallas_call | solution.py:505
  23.1 2.6 %collective-permute-start.5 = (f32[3,8,128]{2,1,0:T(8,128)S(1)}, f32[3,8,128]{2,1,0:T(8,128)S(1)}, u32[]{:S(2)}, u32[]{:S(2)}) collective-permute-start(f32[3,8,128]{2,1,0:T(8,128)S(1)} %get-tuple-element.35), channel_id=1, source_target_pairs={{0,16},{8,24},{16,8},{24,0},{1,17},{9,25},{17,9},{25,1},{2,18},{10... | collective-permute-start | bytes 36872 | tf_op jit(solution)/shard_map/ppermute | solution.py:548
  25.8 1.2 %collective-permute-start.6 = (f32[3,8,128]{2,1,0:T(8,128)S(1)}, f32[3,8,128]{2,1,0:T(8,128)S(1)}, u32[]{:S(2)}, u32[]{:S(2)}) collective-permute-start(f32[3,8,128]{2,1,0:T(8,128)S(1)} %get-tuple-element.34), channel_id=1, source_target_pairs={{0,24},{8,16},{16,0},{24,8},{1,25},{9,17},{17,1},{25,9},{2,26},{10... | collective-permute-start | bytes 36872 | tf_op jit(solution)/shard_map/ppermute | solution.py:548
  27.0 0.3 %collective-permute-start.7 = (f32[3,8,128]{2,1,0:T(8,128)S(1)}, f32[3,8,128]{2,1,0:T(8,128)S(1)}, u32[]{:S(2)}, u32[]{:S(2)}) collective-permute-start(f32[3,8,128]{2,1,0:T(8,128)S(1)} %get-tuple-element.33), channel_id=1, source_target_pairs={{0,8},{8,0},{16,24},{24,16},{1,9},{9,1},{17,25},{25,17},{2,10},{10... | collective-permute-start | bytes 36872 | tf_op jit(solution)/shard_map/ppermute | solution.py:548
  27.4 1.3 %collective-permute-done.5.refs_1_ = f32[3,8,128]{2,1,0:T(8,128)S(1)} collective-permute-done((f32[3,8,128]{2,1,0:T(8,128)S(1)}, f32[3,8,128]{2,1,0:T(8,128)S(1)}, u32[]{:S(2)}, u32[]{:S(2)}) %collective-permute-start.5) | collective-permute-done | bytes 12320 | tf_op jit(solution)/shard_map/ppermute | solution.py:548
  28.7 1.7 %collective-permute-done.6.refs_2_ = f32[3,8,128]{2,1,0:T(8,128)S(1)} collective-permute-done((f32[3,8,128]{2,1,0:T(8,128)S(1)}, f32[3,8,128]{2,1,0:T(8,128)S(1)}, u32[]{:S(2)}, u32[]{:S(2)}) %collective-permute-start.6) | collective-permute-done | bytes 12320 | tf_op jit(solution)/shard_map/ppermute | solution.py:548
  30.4 0.3 %collective-permute-done.7.refs_3_ = f32[3,8,128]{2,1,0:T(8,128)S(1)} collective-permute-done((f32[3,8,128]{2,1,0:T(8,128)S(1)}, f32[3,8,128]{2,1,0:T(8,128)S(1)}, u32[]{:S(2)}, u32[]{:S(2)}) %collective-permute-start.7) | collective-permute-done | bytes 12320 | tf_op jit(solution)/shard_map/ppermute | solution.py:548
  30.7 0.6 %shard_map.51 = f32[1,1,4,8,128]{4,3,2,1,0:T(8,128)} custom-call(f32[3,8,128]{2,1,0:T(8,128)S(1)} %get-tuple-element.36.refs_0_, f32[3,8,128]{2,1,0:T(8,128)S(1)} %collective-permute-done.5.refs_1_, f32[3,8,128]{2,1,0:T(8,128)S(1)} %collective-permute-done.6.refs_2_, f32[3,8,128]{2,1,0:T(8,128)S(1)} %collective-permute-done.7.refs_3_), custom_call_target="tpu_custom_call" | custom-call | flops 1048576 | bytes 1048576 | tf_op jit(solution)/shard_map/pallas_call | solution.py:570
  (1 shorter events, 0.0 us)
Async XLA Ops:
  0.0 14.2 %copy-start = (s32[4,16,1]{1,2,0:T(1,128)S(1)}, s32[4,16,1]{1,2,0:T(1,128)}, u32[]{:S(2)}) copy-start(s32[4,16,1]{1,2,0:T(1,128)} %param.5) | copy-start | bytes 772
  1.1 17.8 %collective-permute-start.3 = (f32[3,2,128,128]{3,2,1,0:T(8,128)S(1)}, f32[3,2,128,128]{3,2,1,0:T(8,128)S(1)}, u32[]{:S(2)}, u32[]{:S(2)}) collective-permute-start(f32[3,2,128,128]{3,2,1,0:T(8,128)S(1)} %shard_map.48), channel_id=1, source_target_pairs={{0,2},{2,4},{4,6},{6,0},{1,3},{3,5},{5,7},{7,1},{8,10},{10,12},{12... | collective-permute-start | bytes 1179656 | tf_op jit(solution)/shard_map/ppermute | solution.py:518
  7.8 15.0 %collective-permute-start.4 = (f32[3,2,128,128]{3,2,1,0:T(8,128)S(1)}, f32[3,2,128,128]{3,2,1,0:T(8,128)S(1)}, u32[]{:S(2)}, u32[]{:S(2)}) collective-permute-start(f32[3,2,128,128]{3,2,1,0:T(8,128)S(1)} %get-tuple-element.32), channel_id=1, source_target_pairs={{0,6},{2,0},{4,2},{6,4},{1,7},{3,1},{5,3},{7,5},{8,14},{10,8},{12,... | collective-permute-start | bytes 1179656 | tf_op jit(solution)/shard_map/ppermute | solution.py:518
  8.9 5.4 %collective-permute-start = (f32[3,32,4,128]{3,2,1,0:T(4,128)S(1)}, f32[3,32,4,128]{3,2,1,0:T(4,128)S(1)}, u32[]{:S(2)}, u32[]{:S(2)}) collective-permute-start(f32[3,32,4,128]{3,2,1,0:T(4,128)S(1)} %get-tuple-element.21), channel_id=1, source_target_pairs={{0,1},{1,0},{2,3},{3,2},{4,5},{5,4},{6,7},{7,6},{8,9},{9,8},{10,11... | collective-permute-start | bytes 589832 | tf_op jit(solution)/shard_map/ppermute | solution.py:518
  8.9 10.0 %collective-permute-start.1 = (f32[192,128]{1,0:T(8,128)S(1)}, f32[192,128]{1,0:T(8,128)S(1)}, u32[]{:S(2)}, u32[]{:S(2)}) collective-permute-start(f32[192,128]{1,0:T(8,128)S(1)} %get-tuple-element.26), channel_id=1, source_target_pairs={{0,8},{8,16},{16,24},{24,0},{1,9},{9,17},{17,25},{25,1},{2,10},{10... | collective-permute-start | bytes 294920 | tf_op jit(solution)/shard_map/ppermute | solution.py:518
  10.9 8.0 %collective-permute-start.2 = (f32[192,128]{1,0:T(8,128)S(1)}, f32[192,128]{1,0:T(8,128)S(1)}, u32[]{:S(2)}, u32[]{:S(2)}) collective-permute-start(f32[192,128]{1,0:T(8,128)S(1)} %get-tuple-element.27), channel_id=1, source_target_pairs={{0,24},{8,0},{16,8},{24,16},{1,25},{9,1},{17,9},{25,17},{2,26},{10... | collective-permute-start | bytes 294920 | tf_op jit(solution)/shard_map/ppermute | solution.py:518
  23.1 5.5 %collective-permute-start.5 = (f32[3,8,128]{2,1,0:T(8,128)S(1)}, f32[3,8,128]{2,1,0:T(8,128)S(1)}, u32[]{:S(2)}, u32[]{:S(2)}) collective-permute-start(f32[3,8,128]{2,1,0:T(8,128)S(1)} %get-tuple-element.35), channel_id=1, source_target_pairs={{0,16},{8,24},{16,8},{24,0},{1,17},{9,25},{17,9},{25,1},{2,18},{10... | collective-permute-start | bytes 36872 | tf_op jit(solution)/shard_map/ppermute | solution.py:548
  25.8 4.6 %collective-permute-start.6 = (f32[3,8,128]{2,1,0:T(8,128)S(1)}, f32[3,8,128]{2,1,0:T(8,128)S(1)}, u32[]{:S(2)}, u32[]{:S(2)}) collective-permute-start(f32[3,8,128]{2,1,0:T(8,128)S(1)} %get-tuple-element.34), channel_id=1, source_target_pairs={{0,24},{8,16},{16,0},{24,8},{1,25},{9,17},{17,1},{25,9},{2,26},{10... | collective-permute-start | bytes 36872 | tf_op jit(solution)/shard_map/ppermute | solution.py:548
  27.0 3.7 %collective-permute-start.7 = (f32[3,8,128]{2,1,0:T(8,128)S(1)}, f32[3,8,128]{2,1,0:T(8,128)S(1)}, u32[]{:S(2)}, u32[]{:S(2)}) collective-permute-start(f32[3,8,128]{2,1,0:T(8,128)S(1)} %get-tuple-element.33), channel_id=1, source_target_pairs={{0,8},{8,0},{16,24},{24,16},{1,9},{9,1},{17,25},{25,17},{2,10},{10... | collective-permute-start | bytes 36872 | tf_op jit(solution)/shard_map/ppermute | solution.py:548
